TPU v7x, 32 devices: a whole 2x2x4 slice. The times are simulated.
32 devices in a mesh: dp: 4 (over x, core), space: 4 (over z), tm: 2 (over y).
Axes of the slice: x: 2, y: 2, z: 4, core: 2. Of those that a mesh axis runs over, the one named last changes fastest.
Arguments:
- inputs: bfloat16 [4, 20, 64, 1024], P('dp', None, 'space', 'tm'), may hold values from -6 to 6
- out_grad: bfloat16 [4, 20, 64, 1024], P('dp', None, 'space', 'tm'), may hold values from -6 to 6
- norm_gain: float32 [1024], replicated, may hold values from 0.1 to 1.9
- pos_bias: float32 [16, 39], P('tm'), may hold values from -4 to 4
- w_query: bfloat16 [1024, 1024], P(None, 'tm'), may hold values from -0.1875 to 0.1875
- w_key: bfloat16 [1024, 1024], P(None, 'tm'), may hold values from -0.1875 to 0.1875
- w_value: bfloat16 [1024, 1024], P(None, 'tm'), may hold values from -0.1875 to 0.1875
- w_out: bfloat16 [1024, 1024], P('tm'), may hold values from -0.1875 to 0.1875
Outputs:
- block_out: bfloat16 [4, 20, 64, 1024], P('dp', None, 'space', 'tm')
- input_grad: bfloat16 [4, 20, 64, 1024], P('dp', None, 'space', 'tm')
- gain_grad: float32 [1024], P('tm')
- bias_grad: float32 [16, 39], P('tm')
All inputs are finite; a program needn't handle non-finite values.
Results may differ from a plain program's by a relative error of at most 0.0099.
Values may be sent and summed in bfloat16 or wider, within the bound.
No kernel may reach another device: no remote copies, remote signals or barrier semaphores. Data moves between devices by JAX's collectives and lax.ppermute only.
A program may use at most 64 MiB of HBM per device.

v0:
```python
import jax
import jax.numpy as jnp
from jax import lax
from jax.sharding import PartitionSpec as P


def offset_table(frames):
    query_idx = lax.iota(jnp.int32, frames)
    key_idx = lax.iota(jnp.int32, frames)
    offsets = key_idx[None, :] - query_idx[:, None] + frames - 1
    columns = lax.iota(jnp.int32, 2 * frames - 1)
    return (offsets[:, :, None] == columns[None, None, :]).astype(jnp.float32)


def bias_rows(bias, table):
    return jnp.einsum("ho,qko->hqk", bias, table, precision=lax.Precision.HIGHEST)


def bias_back(score_sum, table):
    return jnp.einsum("hqk,qko->ho", score_sum, table, precision=lax.Precision.HIGHEST)


def soft_probs(queries, key_rows, rel_bias, scale):
    scores = jnp.einsum("bqphd,bkphd->bphqk", queries, key_rows, preferred_element_type=jnp.float32)
    scores = scores * scale + rel_bias[None, None]
    log_total = jax.nn.logsumexp(scores, axis=-1, keepdims=True)
    return jnp.exp(scores - log_total).astype(jnp.bfloat16)


def attend(probs, value_rows):
    return jnp.einsum(
        "bphqk,bkphd->bqphd", probs, value_rows, preferred_element_type=jnp.float32
    ).astype(jnp.bfloat16)


def score_grads(probs, grad_att, value_rows, scale):
    grad_prob = jnp.einsum(
        "bqphd,bkphd->bphqk", grad_att, value_rows, preferred_element_type=jnp.float32
    )
    probs_full = probs.astype(jnp.float32)
    row_dot = jnp.sum(probs_full * grad_prob, axis=-1, keepdims=True)
    grad_score = probs_full * (grad_prob - row_dot)
    return (grad_score, (grad_score * scale).astype(jnp.bfloat16))


def contract_keys(grad_scaled, key_rows):
    return jnp.einsum(
        "bphqk,bkphd->bqphd", grad_scaled, key_rows, preferred_element_type=jnp.float32
    ).astype(jnp.bfloat16)


def contract_queries(weights, rows):
    return jnp.einsum(
        "bphqk,bqphd->bkphd", weights, rows, preferred_element_type=jnp.float32
    ).astype(jnp.bfloat16)


def per_device(inputs, out_grad, norm_gain, pos_bias, w_query, w_key, w_value, w_out):
    clips, frames, pixels, width = inputs.shape
    group = pos_bias.shape[0]
    tm_count = lax.axis_size("tm")
    chans = width * tm_count
    head_dim = width // group
    scale = head_dim ** (-0.5)
    col_start = lax.axis_index("tm") * width
    x_local = inputs.astype(jnp.float32)
    x_whole = lax.all_gather(inputs, "tm", axis=3, tiled=True).astype(jnp.float32)
    scale_inv = lax.rsqrt(jnp.mean(x_whole * x_whole, axis=-1, keepdims=True) + 1e-06)
    normed = (x_whole * scale_inv * norm_gain).astype(jnp.bfloat16)

    def project(weight):
        out = jnp.einsum("bfpc,cd->bfpd", normed, weight, preferred_element_type=jnp.float32)
        return out.astype(jnp.bfloat16).reshape(clips, frames, pixels, group, head_dim)

    queries = project(w_query)
    key_rows = project(w_key)
    value_rows = project(w_value)
    table = offset_table(frames)
    probs = soft_probs(queries, key_rows, bias_rows(pos_bias, table), scale)
    attended = attend(probs, value_rows).reshape(clips, frames, pixels, width)
    partial_mix = jnp.einsum("bfpd,dc->bfpc", attended, w_out, preferred_element_type=jnp.float32)
    mixed = lax.psum_scatter(partial_mix, "tm", scatter_dimension=3, tiled=True)
    block_out = (x_local + mixed).astype(jnp.bfloat16)
    grad_att = jnp.einsum(
        "bfpc,dc->bfpd",
        lax.all_gather(out_grad, "tm", axis=3, tiled=True),
        w_out,
        preferred_element_type=jnp.float32,
    )
    grad_att = grad_att.astype(jnp.bfloat16).reshape(clips, frames, pixels, group, head_dim)
    grad_score, grad_scaled = score_grads(probs, grad_att, value_rows, scale)
    grad_query = contract_keys(grad_scaled, key_rows).reshape(clips, frames, pixels, width)
    grad_key = contract_queries(grad_scaled, queries).reshape(clips, frames, pixels, width)
    grad_value = contract_queries(probs, grad_att).reshape(clips, frames, pixels, width)
    gain_local = lax.dynamic_slice_in_dim(norm_gain, col_start, width, 0)

    def back_project(grads, weight):
        return jnp.einsum("bfpd,cd->bfpc", grads, weight, preferred_element_type=jnp.float32)

    partial_grad = (
        back_project(grad_query, w_query)
        + back_project(grad_key, w_key)
        + back_project(grad_value, w_value)
    )
    partial_inner = jnp.sum(partial_grad * norm_gain * x_whole, axis=-1, keepdims=True) / chans
    inner_copies = jnp.broadcast_to(partial_inner, (clips, frames, pixels, tm_count))
    grad_normed, inner = (
        lax.psum_scatter(partial_grad, "tm", scatter_dimension=3, tiled=True),
        lax.psum_scatter(inner_copies, "tm", scatter_dimension=3, tiled=True),
    )
    scale_grad = grad_normed * gain_local
    gain_part = jnp.sum(grad_normed * x_local * scale_inv, axis=(0, 1, 2))
    input_grad = (
        out_grad.astype(jnp.float32) + scale_inv * scale_grad - x_local * scale_inv**3 * inner
    )
    bias_part = bias_back(jnp.sum(grad_score, axis=(0, 1)), table)
    gain_grad, bias_grad = lax.psum((gain_part, bias_part), ("dp", "space"))
    return (block_out, input_grad.astype(jnp.bfloat16), gain_grad, bias_grad)


def solution(mesh):
    return jax.shard_map(
        per_device,
        mesh=mesh,
        in_specs=(
            P("dp", None, "space", "tm"),
            P("dp", None, "space", "tm"),
            P(),
            P("tm", None),
            P(None, "tm"),
            P(None, "tm"),
            P(None, "tm"),
            P("tm", None),
        ),
        out_specs=(
            P("dp", None, "space", "tm"),
            P("dp", None, "space", "tm"),
            P("tm"),
            P("tm", None),
        ),
        check_vma=False,
    )
```

profile of v0, /device:TPU:0, one launch (start us, length us, event | category | flops | bytes accessed | tf_op | source)
XLA Modules:
  0.0 174.3 jit_solution(1682381952775574645)
XLA Ops:
  7.4 1.6 convolution_bitcast_fusion.1
  9.8 11.6 %all_gather.6 = bf16[1,20,16,1024]{3,2,1,0:T(8,128)(2,1)S(1)} all-gather(bf16[1,20,16,512]{3,2,1,0:T(8,128)(2,1)} %param.8), channel_id=1, replica_groups=mesh['dp'=4,'space'=4,'tm'=2] {'tm'}, dimensions={3}, use_global_device_ids=true | all-gather | bytes 983040 | tf_op jit(solution)/shard_map/all_gather | solution.py:67
  22.5 1.8 %convolution_convert_fusion.5 = bf16[20,16,512]{2,1,0:T(8,128)(2,1)S(1)} fusion(bf16[1024,512]{1,0:T(8,128)(2,1)} %param.13, bf16[1,20,16,1024]{3,2,1,0:T(8,128)(2,1)S(1)} %all_gather.6, f32[1024]{0:T(1024)S(1)} %copy-done.15, f32[20,16]{1,0:T(8,128)S(1)} %get-tuple-element.10), kind=kOutput, calls=%fused_computation.26 | convolution fusion | flops 337018880 | bytes 2036992 | tf_op jit(solution)/shard_map/bfpc,cd->bfpd/dot_general | solution.py:72
  24.6 1.3 convolution_convert_fusion.7
  25.9 1.3 reshape.212
  27.3 9.6 %all_gather.7 = bf16[1,20,16,1024]{3,2,1,0:T(8,128)(2,1)S(1)} all-gather(bf16[1,20,16,512]{3,2,1,0:T(8,128)(2,1)S(1)} %copy-done.9), channel_id=1, replica_groups=mesh['dp'=4,'space'=4,'tm'=2] {'tm'}, dimensions={3}, use_global_device_ids=true | all-gather | bytes 983040 | tf_op jit(solution)/shard_map/all_gather | solution.py:86
  36.9 2.5 %convolution_convert_fusion.4 = bf16[20,16,512]{2,1,0:T(8,128)(2,1)} fusion(bf16[512,1024]{1,0:T(8,128)(2,1)} %param.15, bf16[1,20,16,1024]{3,2,1,0:T(8,128)(2,1)S(1)} %all_gather.7), kind=kOutput, calls=%fused_computation.25 | convolution fusion | flops 335708160 | bytes 2031616 | tf_op jit(solution)/shard_map/bfpc,dc->bfpd/dot_general | solution.py:84
  39.4 2.2 %reshape.217 = bf16[20,16,8,64]{3,2,1,0:T(8,128)(2,1)} reshape(bf16[20,16,512]{2,1,0:T(8,128)(2,1)} %convolution_convert_fusion.4) | data formatting | bytes 655360 | tf_op jit(solution)/shard_map/reshape.34
  41.6 1.2 fusion.44
  46.0 3.9 %fusion.45 = (f32[8,20,20]{1,2,0:T(8,128)S(1)}, f32[16,8,20,20]{2,3,1,0:T(8,128)S(1)}) fusion(f32[16,8,20,20]{2,3,1,0:T(8,128)S(1)} %fusion.20, bf16[16,8,20,20]{2,3,1,0:T(8,128)(2,1)S(1)} %exponential_convert_fusion), kind=kOutput, calls=%fused_computation.74 | output fusion | flops 306579 | bytes 524800 | tf_op jit(solution)/shard_map/sub | solution.py:42
  50.0 1.5 fusion.7
  51.5 1.6 fusion.6
  54.1 2.3 %reshape.220 = bf16[20,16,512]{2,1,0:T(8,128)(2,1)} reshape(bf16[1,20,16,8,64]{4,3,2,1,0:T(8,128)(2,1)} %copy.55) | data formatting | bytes 655360 | tf_op jit(solution)/shard_map/reshape.53
  56.4 2.1 %copy.51 = bf16[1,20,16,8,64]{4,3,2,1,0:T(8,128)(2,1)} copy(bf16[1,20,16,8,64]{4,1,3,2,0:T(8,128)(2,1)} %fusion.6) | data formatting | bytes 655360 | tf_op jit(solution)/shard_map/convert_element_type | solution.py:49
  58.5 2.2 %reshape.218 = bf16[20,16,512]{2,1,0:T(8,128)(2,1)} reshape(bf16[1,20,16,8,64]{4,3,2,1,0:T(8,128)(2,1)} %copy.51) | data formatting | bytes 655360 | tf_op jit(solution)/shard_map/reshape.43
  61.7 1.5 reshape.219
  63.2 1.9 %fusion.14 = f32[20,16,1024]{2,1,0:T(8,128)S(1)} fusion(bf16[20,16,512]{2,1,0:T(8,128)(2,1)} %reshape.218, bf16[1024,512]{1,0:T(8,128)(2,1)} %param.12), kind=kOutput, calls=%fused_computation.36 | convolution fusion | flops 335544320 | bytes 2686976 | tf_op jit(solution)/shard_map/bfpd,cd->bfpc/dot_general | solution.py:98
  66.3 1.7 fusion.4
  71.4 1.6 convolution_bitcast_fusion
  73.5 6.3 %reduce-scatter.8.cloned.1.call-done = f32[1,20,16,1]{1,2,0,3:T(8,128)} async-done(((f32[1,20,16,2]{1,2,0,3:T(8,128)}), f32[1,20,16,1]{1,2,0,3:T(8,128)}) %reduce-scatter.8.cloned.1.call-update) | async-done | bytes 1296 | tf_op jit(solution)/shard_map/reduce_scatter | solution.py:109
  80.5 24.7 %reduce-scatter.6.cloned.1.call-done = f32[1,20,16,512]{3,2,1,0:T(8,128)} async-done(((f32[1,20,16,1024]{3,2,1,0:T(8,128)}), f32[1,20,16,512]{3,2,1,0:T(8,128)}) %reduce-scatter.6.cloned.1.call-update) | async-done | bytes 655376 | tf_op jit(solution)/shard_map/reduce_scatter | solution.py:108
  105.2 25.6 %reduce-scatter.4.cloned.1.call-done = f32[1,20,16,512]{3,2,1,0:T(8,128)} async-done(((f32[1,20,16,1024]{3,2,1,0:T(8,128)}), f32[1,20,16,512]{3,2,1,0:T(8,128)}) %reduce-scatter.4.cloned.1.call-update) | async-done | bytes 655376 | tf_op jit(solution)/shard_map/reduce_scatter | solution.py:82
  130.8 2.4 %fusion.33 = (f32[512]{0:T(512)S(1)}, bf16[1,20,16,512]{3,2,1,0:T(8,128)(2,1)}, bf16[1,20,16,512]{3,2,1,0:T(8,128)(2,1)}) fusion(f32[1,20,16,512]{3,2,1,0:T(8,128)} %reduce-scatter.6.cloned.1.call-done, bf16[1,20,16,512]{3,2,1,0:T(8,128)(2,1)S(1)} %copy-done.8, f32[20,16]{1,0:T(8,128)S(1)} %get-tuple-element.10, f32[20,16]{1,0:T(8,128)S(1)} %copy.57, ...), kind=kLoop, calls=%fused_computation.58 | loop fusion | flops 2293248 | bytes 2629376 | tf_op jit(solution)/shard_map/reduce_sum | solution.py:112
  133.2 34.6 %all-reduce = (f32[512]{0:T(512)}, f32[8,39]{1,0:T(8,128)}) all-reduce(f32[512]{0:T(512)S(1)} %get-tuple-element.6, f32[8,39]{1,0:T(8,128)S(1)} %convolution_bitcast_fusion.2), channel_id=1, replica_groups=mesh['dp'=4,'space'=4,'tm'=2] {'dp','space'}, use_global_device_ids=true, to_apply=%region_9.0 | all-reduce | flops 824 | bytes 6592 | tf_op jit(solution)/shard_map/psum | solution.py:117
  (64 shorter events, 13.3 us)
Async XLA Ops:
  7.2 17.5 %copy-start = (bf16[1024,512]{1,0:T(8,128)(2,1)S(1)}, bf16[1024,512]{1,0:T(8,128)(2,1)}, u32[]{:S(2)}) copy-start(bf16[1024,512]{1,0:T(8,128)(2,1)} %param.14) | copy-start | bytes 3145732
  7.2 14.4 %copy-start.15 = (f32[1024]{0:T(1024)S(1)}, f32[1024]{0:T(1024)}, u32[]{:S(2)}) copy-start(f32[1024]{0:T(1024)} %param.10) | copy-start | bytes 12292
  7.2 14.4 %copy-start.11 = (bf16[1024,512]{1,0:T(8,128)(2,1)S(1)}, bf16[1024,512]{1,0:T(8,128)(2,1)}, u32[]{:S(2)}) copy-start(bf16[1024,512]{1,0:T(8,128)(2,1)} %param.12) | copy-start | bytes 3145732
  7.2 72.6 %reduce-scatter.8.cloned.1.call-start = ((), (), s32[]{:S(2)}) async-start(), calls=%async_computation.5 | async-start | bytes 24576 | tf_op jit(solution)/shard_map/reduce_scatter | solution.py:109
  21.4 3.2 %copy-start.4 = (bf16[1,20,16,1024]{3,2,1,0:T(8,128)(2,1)}, bf16[1,20,16,1024]{3,2,1,0:T(8,128)(2,1)S(1)}, u32[]{:S(2)}) copy-start(bf16[1,20,16,1024]{3,2,1,0:T(8,128)(2,1)S(1)} %all_gather.6) | copy-start | bytes 1966084
  24.6 16.9 %copy-start.1 = (bf16[20,16,8,64]{3,2,1,0:T(8,128)(2,1)}, bf16[20,16,8,64]{3,2,1,0:T(8,128)(2,1)S(1)}, u32[]{:S(2)}) copy-start(bf16[20,16,8,64]{3,2,1,0:T(8,128)(2,1)S(1)} %reshape.214) | copy-start | bytes 983044
  24.6 2.6 %copy-start.9 = (bf16[1,20,16,512]{3,2,1,0:T(8,128)(2,1)S(1)}, bf16[1,20,16,512]{3,2,1,0:T(8,128)(2,1)}, u32[]{:S(2)}) copy-start(bf16[1,20,16,512]{3,2,1,0:T(8,128)(2,1)} %param.9) | copy-start | bytes 983044
  36.9 4.7 %copy-start.14 = (f32[8,20,20]{1,2,0:T(8,128)S(1)}, f32[8,20,20]{1,2,0:T(8,128)}, u32[]{:S(2)}) copy-start(f32[8,20,20]{1,2,0:T(8,128)} %copy.43) | copy-start | bytes 38404
  43.3 1.1 copy-start.3
  50.0 1.5 copy-start.2
  54.1 6.7 %copy-start.6 = (bf16[1,20,16,8,64]{4,1,3,2,0:T(8,128)(2,1)S(1)}, bf16[1,20,16,8,64]{4,1,3,2,0:T(8,128)(2,1)}, u32[]{:S(2)}) copy-start(bf16[1,20,16,8,64]{4,1,3,2,0:T(8,128)(2,1)} %fusion.7) | copy-start | bytes 983044
  63.2 2.0 %copy-start.12 = (bf16[1024,512]{1,0:T(8,128)(2,1)S(1)}, bf16[1024,512]{1,0:T(8,128)(2,1)}, u32[]{:S(2)}) copy-start(bf16[1024,512]{1,0:T(8,128)(2,1)} %param.13) | copy-start | bytes 3145732
  65.2 1.1 copy-start.5
  65.2 1.2 copy-start.7
  68.7 36.5 %reduce-scatter.6.cloned.1.call-start = ((), (), s32[]{:S(2)}) async-start(), calls=%async_computation.4 | async-start | bytes 1966080 | tf_op jit(solution)/shard_map/reduce_scatter | solution.py:108
  69.5 61.3 %reduce-scatter.4.cloned.1.call-start = ((), (), s32[]{:S(2)}) async-start(), calls=%async_computation.3 | async-start | bytes 1966080 | tf_op jit(solution)/shard_map/reduce_scatter | solution.py:82
  70.2 1.2 copy-start.13
  71.4 59.4 %copy-start.8 = (bf16[1,20,16,512]{3,2,1,0:T(8,128)(2,1)S(1)}, bf16[1,20,16,512]{3,2,1,0:T(8,128)(2,1)}, u32[]{:S(2)}) copy-start(bf16[1,20,16,512]{3,2,1,0:T(8,128)(2,1)} %param.8) | copy-start | bytes 983044
  71.4 59.4 %copy-start.10 = (bf16[1,20,16,512]{3,2,1,0:T(8,128)(2,1)S(1)}, bf16[1,20,16,512]{3,2,1,0:T(8,128)(2,1)}, u32[]{:S(2)}) copy-start(bf16[1,20,16,512]{3,2,1,0:T(8,128)(2,1)} %param.9) | copy-start | bytes 983044
Sparse Core Ops, SparseCore 0:
  68.9 10.8 reduce-scatter.7
  82.0 23.1 reduce-scatter.5
  107.6 23.1 reduce-scatter.3
where the time goes:
time: 175 us; the launch traced here: 174 us
  waiting for transfers between devices  57.2 us (33%)
  blocking collectives  55.7 us (32%)
  matrix products  20.4 us (12%)
  local copies, waits for them, and re-layouts  19.3 us (11%)
  between operations  14 us (8%)
  other arithmetic  7.44 us (4%)
    psum x1, blocking collectives, per_device(): gain_grad, bias_grad = lax.psum((gain_part, bias_part), ('dp', 'space'))  34.6 us
    reduce_scatter x1, waiting for transfers between devices, per_device(): mixed = lax.psum_scatter(partial_mix, 'tm', scatter_dimension=3, tiled=True)  25.6 us
    reduce_scatter x1, waiting for transfers between devices, per_device(): lax.psum_scatter(partial_grad, 'tm', scatter_dimension=3, tiled=True)  24.7 us
    all_gather x1, blocking collectives, per_device(): lax.all_gather(inputs, 'tm', axis=3, tiled=True).astype(jnp.float32)  11.6 us
    another operation x8, local copies, waits for them, and re-layouts  10.6 us
    all_gather x1, blocking collectives, per_device(): lax.all_gather(out_grad, 'tm', axis=3, tiled=True)  9.57 us
    reduce_scatter x1, waiting for transfers between devices, per_device(): lax.psum_scatter(inner_copies, 'tm', scatter_dimension=3, tiled=True)  6.27 us
    dot_general x3, matrix products, back_project(): jnp.einsum('bfpd,cd->bfpc', grads, weight, preferred_element_type=jnp.flo...  4.17 us
  transfers between devices with their start and end apart: 3, of which 3 were waited for; matrix products, arithmetic and copies ran while one was open for 2% of the time, Pallas kernels for 0%

commit v1 on v0

v1 whole, which is shorter than its diff:
```python
import jax
import jax.numpy as jnp
from jax import lax
from jax.sharding import PartitionSpec as P


def offset_table(frames):
    query_idx = lax.iota(jnp.int32, frames)
    key_idx = lax.iota(jnp.int32, frames)
    offsets = key_idx[None, :] - query_idx[:, None] + frames - 1
    columns = lax.iota(jnp.int32, 2 * frames - 1)
    return (offsets[:, :, None] == columns[None, None, :]).astype(jnp.float32)


def shifted(value, axis, step):
    count = lax.axis_size(axis)
    return lax.ppermute(value, axis, [((i + step) % count, i) for i in range(count)])


def group_sum(value, axis):
    count = lax.axis_size(axis)
    stride = 1
    while stride < count:
        left = count // stride
        radix = 4 if left % 4 == 0 else 2 if left % 2 == 0 else left
        parts = [value]
        for step in range(1, radix):
            pairs = []
            for i in range(count):
                digit = i // stride % radix
                pairs.append((i + ((digit + step) % radix - digit) * stride, i))
            parts.append(lax.ppermute(value, axis, pairs))
        value = sum(parts[1:], parts[0])
        stride *= radix
    return value


def place(parts, axis, me, count):
    if count == 2:
        flip = me == 1
        return jnp.concatenate([jnp.where(flip, parts[1], parts[0]), jnp.where(flip, parts[0], parts[1])], axis)
    whole = jnp.concatenate(parts, axis)
    return jnp.roll(whole, me * parts[0].shape[axis], axis)


def per_device(inputs, out_grad, norm_gain, pos_bias, w_query, w_key, w_value, w_out):
    clips, frames, pixels, width = inputs.shape
    group = pos_bias.shape[0]
    tm = lax.axis_size("tm")
    me = lax.axis_index("tm")
    chans = width * tm
    head_dim = width // group
    scale = head_dim ** (-0.5)
    table = offset_table(frames)
    rel_bias = jnp.einsum("ho,qko->hqk", pos_bias, table, precision=lax.Precision.HIGHEST)
    x_parts = [inputs] + [shifted(inputs, "tm", k) for k in range(1, tm)]
    x_whole = place(x_parts, 3, me, tm).astype(jnp.float32)
    g_parts = [out_grad] + [shifted(out_grad, "tm", k) for k in range(1, tm)]
    g_whole = place(g_parts, 3, me, tm)
    scale_inv = lax.rsqrt(jnp.mean(x_whole * x_whole, axis=-1, keepdims=True) + 1e-06)
    normed = (x_whole * scale_inv * norm_gain).astype(jnp.bfloat16)

    def project(weight):
        out = jnp.einsum("bfpc,cd->bfpd", normed, weight, preferred_element_type=jnp.float32)
        return out.astype(jnp.bfloat16).reshape(clips, frames, pixels, group, head_dim)

    def heads(spec, a, b):
        return jnp.einsum(spec, a, b, preferred_element_type=jnp.float32)

    def scattered(partial):
        own = lax.dynamic_slice_in_dim(partial, me * width, width, 3)
        for k in range(1, tm):
            theirs = lax.dynamic_slice_in_dim(partial, (me + tm - k) % tm * width, width, 3)
            own = own + shifted(theirs.astype(jnp.bfloat16), "tm", k).astype(jnp.float32)
        return own

    queries, key_rows, value_rows = project(w_query), project(w_key), project(w_value)
    scores = heads("bqphd,bkphd->bphqk", queries, key_rows) * scale + rel_bias[None, None]
    log_total = jax.nn.logsumexp(scores, axis=-1, keepdims=True)
    probs = jnp.exp(scores - log_total).astype(jnp.bfloat16)
    attended = heads("bphqk,bkphd->bqphd", probs, value_rows).astype(jnp.bfloat16)
    attended = attended.reshape(clips, frames, pixels, width)
    mixed = scattered(heads("bfpd,dc->bfpc", attended, w_out))
    block_out = (inputs.astype(jnp.float32) + mixed).astype(jnp.bfloat16)

    grad_att = heads("bfpc,dc->bfpd", g_whole, w_out).astype(jnp.bfloat16)
    grad_att = grad_att.reshape(clips, frames, pixels, group, head_dim)
    grad_prob = heads("bqphd,bkphd->bphqk", grad_att, value_rows)
    probs_full = probs.astype(jnp.float32)
    row_dot = jnp.sum(probs_full * grad_prob, axis=-1, keepdims=True)
    grad_score = probs_full * (grad_prob - row_dot)
    grad_scaled = (grad_score * scale).astype(jnp.bfloat16)
    shape = (clips, frames, pixels, width)
    grad_query = heads("bphqk,bkphd->bqphd", grad_scaled, key_rows).astype(jnp.bfloat16).reshape(shape)
    grad_key = heads("bphqk,bqphd->bkphd", grad_scaled, queries).astype(jnp.bfloat16).reshape(shape)
    grad_value = heads("bphqk,bqphd->bkphd", probs, grad_att).astype(jnp.bfloat16).reshape(shape)
    partial = (
        heads("bfpd,cd->bfpc", grad_query, w_query)
        + heads("bfpd,cd->bfpc", grad_key, w_key)
        + heads("bfpd,cd->bfpc", grad_value, w_value)
    )
    scaled = partial * norm_gain
    inner = jnp.sum(scaled * x_whole, axis=-1, keepdims=True) / chans
    term = scale_inv * scaled - x_whole * scale_inv**3 * inner
    input_grad = out_grad.astype(jnp.float32) + scattered(term)

    gain_part = jnp.sum(partial * x_whole * scale_inv, axis=(0, 1, 2)).reshape(tm, width)
    bias_part = jnp.einsum(
        "hqk,qko->ho", jnp.sum(grad_score, axis=(0, 1)), table, precision=lax.Precision.HIGHEST
    )
    gain_own = lax.dynamic_index_in_dim(gain_part, me, 0, keepdims=False)
    for k in range(1, tm):
        gain_own = gain_own + shifted(
            lax.dynamic_index_in_dim(gain_part, (me + tm - k) % tm, 0, keepdims=False), "tm", k
        )
    small = jnp.concatenate([gain_own, bias_part.reshape(-1)])
    small = group_sum(group_sum(small, "dp"), "space")
    gain_grad, bias_grad = small[:width], small[width:].reshape(bias_part.shape)
    return (block_out, input_grad.astype(jnp.bfloat16), gain_grad, bias_grad)


def solution(mesh):
    return jax.shard_map(
        per_device,
        mesh=mesh,
        in_specs=(
            P("dp", None, "space", "tm"),
            P("dp", None, "space", "tm"),
            P(),
            P("tm", None),
            P(None, "tm"),
            P(None, "tm"),
            P(None, "tm"),
            P("tm", None),
        ),
        out_specs=(
            P("dp", None, "space", "tm"),
            P("dp", None, "space", "tm"),
            P("tm"),
            P("tm", None),
        ),
        check_vma=False,
    )
```

time: 175 us -> 88.7 us (0.51)
  blocking collectives: 55.7 us -> 0 us
  waiting for transfers between devices: 57.2 us -> 20.4 us
  starting transfers between devices: 0.12 us -> 15.9 us
  between operations: 14 us -> 0.99 us
  other arithmetic: 7.44 us -> 12.8 us
    reduce_scatter x3 -> x0, waiting for transfers between devices: 56.5 us -> none  [the longest x1 25.6 us: per_device(): mixed = lax.psum_scatter(partial_mix, 'tm', scatter_dimension=3, tiled=True)]
    psum x1 -> x0, blocking collectives: 34.6 us -> none  [per_device(): gain_grad, bias_grad = lax.psum((gain_part, bias_part), ('dp', 'space'))]
    all_gather x2 -> x0, blocking collectives: 21.2 us -> none  [the longest x1 11.6 us: per_device(): lax.all_gather(inputs, 'tm', axis=3, tiled=True).astype(jnp.float32)]
    ppermute x0 -> x11, waiting for transfers between devices: none -> 20.4 us  [the longest x5 19.7 us: shifted(): lax.ppermute(value, axis, [((i + step) % count, i) for i in range(count)])]
    ppermute x0 -> x11, starting transfers between devices: none -> 15.9 us  [the longest x6 8.77 us: group_sum(): parts.append(lax.ppermute(value, axis, pairs))]
    convert_element_type x1 -> x3, other arithmetic: 0.25 us -> 4.17 us  [the longest x1 2.07 us: per_device(): block_out = (inputs.astype(jnp.float32) + mixed).astype(jnp.bfloat16)]
    dot_general x13, matrix products: 16.8 us -> 13.6 us  [the longest x11 11.8 us: heads(): return jnp.einsum(spec, a, b, preferred_element_type=jnp.float32)]
    dot_general x3, matrix products: 3.6 us -> 6.53 us  [project(): jnp.einsum('bfpc,cd->bfpd', normed, weight, preferred_element_type=jnp.fl...]
  transfers between devices with their start and end apart: 3 -> 11, of which waited for: 3 -> 5; matrix products, arithmetic and copies ran while one was open for 2% -> 11% of each run, Pallas kernels for 0% -> 0%
where the time goes in v1:
time: 88.7 us; the launch traced here: 88 us
  waiting for transfers between devices  20.4 us (23%)
  matrix products  20.1 us (23%)
  local copies, waits for them, and re-layouts  17.8 us (20%)
  starting transfers between devices  15.9 us (18%)
  other arithmetic  12.8 us (14%)
  between operations  0.99 us (1%)
    ppermute x5, waiting for transfers between devices, shifted(): lax.ppermute(value, axis, [((i + step) % count, i) for i in range(count)])  19.7 us
    dot_general x11, matrix products, heads(): return jnp.einsum(spec, a, b, preferred_element_type=jnp.float32)  11.8 us
    another operation x8, local copies, waits for them, and re-layouts  10.5 us
    ppermute x6, starting transfers between devices, group_sum(): parts.append(lax.ppermute(value, axis, pairs))  8.77 us
    ppermute x5, starting transfers between devices, shifted(): lax.ppermute(value, axis, [((i + step) % count, i) for i in range(count)])  7.16 us
    dot_general x3, matrix products, project(): jnp.einsum('bfpc,cd->bfpd', normed, weight, preferred_element_type=jnp.fl...  6.53 us
    sub x1, other arithmetic, per_device(): grad_score = probs_full * (grad_prob - row_dot)  4.75 us
    convert_element_type x1, other arithmetic, per_device(): block_out = (inputs.astype(jnp.float32) + mixed).astype(jnp.bfloat16)  2.07 us
  transfers between devices with their start and end apart: 11, of which 5 were waited for; matrix products, arithmetic and copies ran while one was open for 11% of the time, Pallas kernels for 0%

profile of v1, /device:TPU:0, one launch (start us, length us, event | category | flops | bytes accessed | tf_op | source)
XLA Modules:
  0.0 88.0 jit_solution(7756679855788632296)
XLA Ops:
  0.6 3.0 %collective-permute-start = (bf16[1,20,16,512]{3,2,1,0:T(8,128)(2,1)}, bf16[1,20,16,512]{3,2,1,0:T(8,128)(2,1)S(1)}, u32[]{:S(2)}, u32[]{:S(2)}) collective-permute-start(bf16[1,20,16,512]{3,2,1,0:T(8,128)(2,1)} %param.8), channel_id=1, source_target_pairs={{1,0},{0,1},{3,2},{2,3},{5,4},{4,5},{7,6},{6,7},{9,8},{8,9},{11,10... | collective-permute-start | bytes 983048 | tf_op jit(solution)/shard_map/ppermute | solution.py:17
  5.5 6.9 %collective-permute-done = bf16[1,20,16,512]{3,2,1,0:T(8,128)(2,1)S(1)} collective-permute-done((bf16[1,20,16,512]{3,2,1,0:T(8,128)(2,1)}, bf16[1,20,16,512]{3,2,1,0:T(8,128)(2,1)S(1)}, u32[]{:S(2)}, u32[]{:S(2)}) %collective-permute-start) | collective-permute-done | bytes 327712 | tf_op jit(solution)/shard_map/ppermute | solution.py:17
  12.4 6.3 %collective-permute-done.2 = bf16[1,20,16,512]{3,2,1,0:T(8,128)(2,1)} collective-permute-done((bf16[1,20,16,512]{3,2,1,0:T(8,128)(2,1)}, bf16[1,20,16,512]{3,2,1,0:T(8,128)(2,1)}, u32[]{:S(2)}, u32[]{:S(2)}) %collective-permute-start.2) | collective-permute-done | bytes 327712 | tf_op jit(solution)/shard_map/ppermute | solution.py:17
  21.1 1.8 %convolution_convert_fusion.5 = bf16[20,16,512]{2,1,0:T(8,128)(2,1)S(1)} fusion(bf16[1024,512]{1,0:T(8,128)(2,1)} %param.13, f32[1024]{0:T(1024)S(1)} %copy-done.15, f32[20,16]{1,0:T(8,128)S(1)} %get-tuple-element.11, bf16[20,16,512]{2,1,0:T(8,128)(2,1)S(1)} %bitcast.82, bf16[20,16,512]{2,1,0:T(8,128)(2,1)S(1)} %bitcast.87), kind=kOutput, calls=%fused_computation.30 | convolution fusion | flops 338001920 | bytes 2036992 | tf_op jit(solution)/shard_map/bfpc,cd->bfpd/dot_general | solution.py:64
  23.3 2.5 %convolution_convert_fusion.6 = bf16[20,16,512]{2,1,0:T(8,128)(2,1)} fusion(bf16[1024,512]{1,0:T(8,128)(2,1)} %param.12, f32[1024]{0:T(1024)S(1)} %copy-done.15, f32[20,16]{1,0:T(8,128)S(1)} %get-tuple-element.11, bf16[20,16,512]{2,1,0:T(8,128)(2,1)S(1)} %bitcast.83, bf16[20,16,512]{2,1,0:T(8,128)(2,1)S(1)} %bitcast.88), kind=kOutput, calls=%fused_computation.31 | convolution fusion | flops 338001920 | bytes 2036992 | tf_op jit(solution)/shard_map/bfpc,cd->bfpd/dot_general | solution.py:64
  27.1 2.3 %convolution_convert_fusion.7 = bf16[20,16,512]{2,1,0:T(8,128)(2,1)} fusion(bf16[1024,512]{1,0:T(8,128)(2,1)S(1)} %copy-done, f32[1024]{0:T(1024)S(1)} %copy-done.15, f32[20,16]{1,0:T(8,128)S(1)} %get-tuple-element.11, bf16[20,16,512]{2,1,0:T(8,128)(2,1)S(1)} %bitcast.84, bf16[20,16,512]{2,1,0:T(8,128)(2,1)} %bitcast.89), kind=kOutput, calls=%fused_computation.32 | convolution fusion | flops 338001920 | bytes 2036992 | tf_op jit(solution)/shard_map/bfpc,cd->bfpd/dot_general | solution.py:64
  29.4 2.2 %reshape.272 = bf16[20,16,8,64]{3,2,1,0:T(8,128)(2,1)} reshape(bf16[20,16,512]{2,1,0:T(8,128)(2,1)} %convolution_convert_fusion.7) | data formatting | bytes 655360 | tf_op jit(solution)/shard_map/reshape.25
  34.6 1.6 %fusion.8 = bf16[1,20,16,8,64]{4,1,3,2,0:T(8,128)(2,1)} fusion(bf16[16,8,20,20]{2,3,1,0:T(8,128)(2,1)S(1)} %exponential_convert_fusion, bf16[20,16,8,64]{3,2,1,0:T(8,128)(2,1)S(1)} %copy-done.1), kind=kOutput, calls=%fused_computation.25 | convolution fusion | flops 6717440 | bytes 757760 | tf_op jit(solution)/shard_map/bphqk,bkphd->bqphd/dot_general | solution.py:68
  37.2 4.7 %fusion.50 = (f32[8,20,20]{1,2,0:T(8,128)}, f32[16,8,20,20]{2,3,1,0:T(8,128)S(1)}) fusion(f32[16,8,20,20]{2,3,1,0:T(8,128)S(1)} %fusion.24, bf16[16,8,20,20]{2,3,1,0:T(8,128)(2,1)S(1)} %exponential_convert_fusion), kind=kOutput, calls=%fused_computation.92 | output fusion | flops 306579 | bytes 524800 | tf_op jit(solution)/shard_map/sub | solution.py:91
  42.0 1.5 %fusion.10 = bf16[1,20,16,8,64]{4,1,3,2,0:T(8,128)(2,1)} fusion(bf16[20,16,8,64]{3,2,1,0:T(8,128)(2,1)S(1)} %reshape.273, f32[16,8,20,20]{2,3,1,0:T(8,128)S(1)} %get-tuple-element.18), kind=kOutput, calls=%fused_computation.27 | convolution fusion | flops 6819840 | bytes 860160 | tf_op jit(solution)/shard_map/bphqk,bqphd->bkphd/dot_general | solution.py:68
  45.2 2.2 %reshape.280 = bf16[20,16,512]{2,1,0:T(8,128)(2,1)} reshape(bf16[1,20,16,8,64]{4,3,2,1,0:T(8,128)(2,1)} %copy.55) | data formatting | bytes 655360 | tf_op jit(solution)/shard_map/reshape.59
  48.4 2.2 %reshape.275 = bf16[20,16,512]{2,1,0:T(8,128)(2,1)} reshape(bf16[1,20,16,8,64]{4,3,2,1,0:T(8,128)(2,1)} %copy.46) | data formatting | bytes 655360 | tf_op jit(solution)/shard_map/reshape.32
  54.2 1.8 %fusion.14 = f32[20,16,1024]{2,1,0:T(8,128)S(1)} fusion(bf16[20,16,512]{2,1,0:T(8,128)(2,1)S(1)} %copy-done.9, bf16[512,1024]{1,0:T(8,128)(2,1)} %param.15), kind=kOutput, calls=%fused_computation.37 | convolution fusion | flops 335544320 | bytes 2686976 | tf_op jit(solution)/shard_map/bfpd,dc->bfpc/dot_general | solution.py:68
  57.2 1.7 %collective-permute-start.1 = (bf16[1,20,16,512]{3,2,1,0:T(8,128)(2,1)}, bf16[1,20,16,512]{3,2,1,0:T(8,128)(2,1)}, u32[]{:S(2)}, u32[]{:S(2)}) collective-permute-start(bf16[1,20,16,512]{3,2,1,0:T(8,128)(2,1)} %fusion.41), channel_id=1, source_target_pairs={{1,0},{0,1},{3,2},{2,3},{5,4},{4,5},{7,6},{6,7},{9,8},{8,9},{11,10... | collective-permute-start | bytes 983048 | tf_op jit(solution)/shard_map/ppermute | solution.py:17
  60.6 1.8 %fusion.7 = (f32[1024]{0:T(1024)S(1)}, f32[20,16]{1,0:T(8,128)S(1)}, f32[20,16,1024]{2,1,0:T(8,128)}) fusion(f32[20,16]{1,0:T(8,128)S(1)} %get-tuple-element.11, bf16[20,16,512]{2,1,0:T(8,128)(2,1)S(1)} %bitcast.85, bf16[20,16,512]{2,1,0:T(8,128)(2,1)S(1)} %bitcast.90, f32[1024]{0:T(1024)S(1)} %copy-done.15, f32[20,16,1024]{2,1,0:T(8,128)S(1)} %convolution_add_fusion.1, ...), kind=kOutput, calls=%fused_computation.23 | convolution fusion | flops 339147456 | bytes 4663808 | tf_op jit(solution)/shard_map/bfpd,cd->bfpc/dot_general | solution.py:68
  63.5 2.9 %collective-permute-done.4 = f32[512]{0:T(512)S(1)} collective-permute-done((f32[512]{0:T(512)S(1)}, f32[512]{0:T(512)S(1)}, u32[]{:S(2)}, u32[]{:S(2)}) %collective-permute-start.4) | collective-permute-done | bytes 2080 | tf_op jit(solution)/shard_map/ppermute | solution.py:17
  67.9 1.7 %collective-permute-start.5 = (f32[824]{0:T(1024)S(1)}, f32[824]{0:T(1024)S(1)}, u32[]{:S(2)}, u32[]{:S(2)}) collective-permute-start(f32[824]{0:T(1024)S(1)} %pad_maximum_fusion.1), channel_id=1, source_target_pairs={{8,0},{16,8},{24,16},{0,24},{9,1},{17,9},{25,17},{1,25},{10,2},{18... | collective-permute-start | bytes 9896 | tf_op jit(solution)/shard_map/ppermute | solution.py:32
  69.6 1.7 %fusion.4 = f32[20,16,1024]{2,1,0:T(8,128)S(1)} fusion(f32[20,16,1024]{2,1,0:T(8,128)} %get-tuple-element.16, f32[20,16]{1,0:T(8,128)S(1)} %broadcast_multiply_fusion, f32[20,16]{1,0:T(8,128)S(1)} %get-tuple-element.10, f32[1024]{0:T(1024)S(1)} %copy-done.15, f32[20,16]{1,0:T(8,128)S(1)} %get-tuple-element.11, bf16[20,16,512]{2,1,0:T(8,128)(2,1)S(1)} %bitcast.86, ...), kind=kLoop, calls=%fused_computation.20 | loop fusion | flops 2949120 | bytes 3284736 | tf_op jit(solution)/shard_map/sub | solution.py:104
  71.4 1.6 %collective-permute-start.10 = (f32[824]{0:T(1024)S(1)}, f32[824]{0:T(1024)S(1)}, u32[]{:S(2)}, u32[]{:S(2)}) collective-permute-start(f32[824]{0:T(1024)S(1)} %add_add_fusion.1), channel_id=1, source_target_pairs={{6,0},{0,2},{2,4},{4,6},{7,1},{1,3},{3,5},{5,7},{14,8},{8,10},{10,... | collective-permute-start | bytes 9896 | tf_op jit(solution)/shard_map/ppermute | solution.py:32
  73.0 2.6 %collective-permute-start.9 = (f32[824]{0:T(1024)S(1)}, f32[824]{0:T(1024)S(1)}, u32[]{:S(2)}, u32[]{:S(2)}) collective-permute-start(f32[824]{0:T(1024)S(1)} %add_add_fusion.1), channel_id=1, source_target_pairs={{4,0},{6,2},{0,4},{2,6},{5,1},{7,3},{1,5},{3,7},{12,8},{14,10},{8,... | collective-permute-start | bytes 9896 | tf_op jit(solution)/shard_map/ppermute | solution.py:32
  77.0 1.6 %collective-permute-start.3 = (bf16[1,20,16,512]{3,2,1,0:T(8,128)(2,1)S(1)}, bf16[1,20,16,512]{3,2,1,0:T(8,128)(2,1)}, u32[]{:S(2)}, u32[]{:S(2)}) collective-permute-start(bf16[1,20,16,512]{3,2,1,0:T(8,128)(2,1)S(1)} %fusion.42), channel_id=1, source_target_pairs={{1,0},{0,1},{3,2},{2,3},{5,4},{4,5},{7,6},{6,7},{9,8},{8,9},{11,10... | collective-permute-start | bytes 983048 | tf_op jit(solution)/shard_map/ppermute | solution.py:17
  80.5 2.1 %fusion.37 = bf16[1,20,16,512]{3,2,1,0:T(8,128)(2,1)} fusion(bf16[1,20,16,512]{3,2,1,0:T(8,128)(2,1)} %collective-permute-done.1, f32[20,16,1024]{2,1,0:T(8,128)} %copy-done.2, s32[]{:T(128)S(6)} %select_n.61, bf16[1,20,16,512]{3,2,1,0:T(8,128)(2,1)S(1)} %copy-done.7), kind=kLoop, calls=%fused_computation.64 | loop fusion | flops 819200 | bytes 1638404 | tf_op jit(solution)/shard_map/convert_element_type | solution.py:84
  82.6 3.6 %collective-permute-done.3 = bf16[1,20,16,512]{3,2,1,0:T(8,128)(2,1)} collective-permute-done((bf16[1,20,16,512]{3,2,1,0:T(8,128)(2,1)S(1)}, bf16[1,20,16,512]{3,2,1,0:T(8,128)(2,1)}, u32[]{:S(2)}, u32[]{:S(2)}) %collective-permute-start.3) | collective-permute-done | bytes 327712 | tf_op jit(solution)/shard_map/ppermute | solution.py:17
  86.2 1.9 %fusion.35 = bf16[1,20,16,512]{3,2,1,0:T(8,128)(2,1)} fusion(bf16[1,20,16,512]{3,2,1,0:T(8,128)(2,1)} %collective-permute-done.3, f32[20,16,1024]{2,1,0:T(8,128)S(1)} %fusion.4, s32[]{:T(128)S(6)} %select_n.61, bf16[1,20,16,512]{3,2,1,0:T(8,128)(2,1)S(1)} %copy-done.8), kind=kLoop, calls=%fused_computation.61 | loop fusion | flops 819200 | bytes 1638404 | tf_op jit(solution)/shard_map/convert_element_type | solution.py:119
  (85 shorter events, 24.8 us)
Async XLA Ops:
  0.6 26.5 %copy-start = (bf16[1024,512]{1,0:T(8,128)(2,1)S(1)}, bf16[1024,512]{1,0:T(8,128)(2,1)}, u32[]{:S(2)}) copy-start(bf16[1024,512]{1,0:T(8,128)(2,1)} %param.14) | copy-start | bytes 3145732
  0.6 11.8 %collective-permute-start = (bf16[1,20,16,512]{3,2,1,0:T(8,128)(2,1)}, bf16[1,20,16,512]{3,2,1,0:T(8,128)(2,1)S(1)}, u32[]{:S(2)}, u32[]{:S(2)}) collective-permute-start(bf16[1,20,16,512]{3,2,1,0:T(8,128)(2,1)} %param.8), channel_id=1, source_target_pairs={{1,0},{0,1},{3,2},{2,3},{5,4},{4,5},{7,6},{6,7},{9,8},{8,9},{11,10... | collective-permute-start | bytes 983048 | tf_op jit(solution)/shard_map/ppermute | solution.py:17
  3.7 15.1 %collective-permute-start.2 = (bf16[1,20,16,512]{3,2,1,0:T(8,128)(2,1)}, bf16[1,20,16,512]{3,2,1,0:T(8,128)(2,1)}, u32[]{:S(2)}, u32[]{:S(2)}) collective-permute-start(bf16[1,20,16,512]{3,2,1,0:T(8,128)(2,1)} %param.9), channel_id=1, source_target_pairs={{1,0},{0,1},{3,2},{2,3},{5,4},{4,5},{7,6},{6,7},{9,8},{8,9},{11,10... | collective-permute-start | bytes 983048 | tf_op jit(solution)/shard_map/ppermute | solution.py:17
  5.5 14.7 %copy-start.10 = (bf16[512,1024]{1,0:T(8,128)(2,1)S(1)}, bf16[512,1024]{1,0:T(8,128)(2,1)}, u32[]{:S(2)}) copy-start(bf16[512,1024]{1,0:T(8,128)(2,1)} %param.15) | copy-start | bytes 3145732
  20.0 3.3 %copy-start.5 = (bf16[1,20,16,512]{3,2,1,0:T(8,128)(2,1)}, bf16[1,20,16,512]{3,2,1,0:T(8,128)(2,1)S(1)}, u32[]{:S(2)}) copy-start(bf16[1,20,16,512]{3,2,1,0:T(8,128)(2,1)S(1)} %get-tuple-element.20) | copy-start | bytes 983044
  33.6 1.1 %copy-start.1 = (bf16[20,16,8,64]{3,2,1,0:T(8,128)(2,1)S(1)}, bf16[20,16,8,64]{3,2,1,0:T(8,128)(2,1)}, u32[]{:S(2)}) copy-start(bf16[20,16,8,64]{3,2,1,0:T(8,128)(2,1)} %reshape.272) | copy-start | bytes 983044
  44.2 3.2 %copy-start.3 = (bf16[1,20,16,8,64]{4,1,3,2,0:T(8,128)(2,1)S(1)}, bf16[1,20,16,8,64]{4,1,3,2,0:T(8,128)(2,1)}, u32[]{:S(2)}) copy-start(bf16[1,20,16,8,64]{4,1,3,2,0:T(8,128)(2,1)} %fusion.8) | copy-start | bytes 983044
  50.7 2.5 %copy-start.4 = (bf16[1,20,16,8,64]{4,1,3,2,0:T(8,128)(2,1)S(1)}, bf16[1,20,16,8,64]{4,1,3,2,0:T(8,128)(2,1)}, u32[]{:S(2)}) copy-start(bf16[1,20,16,8,64]{4,1,3,2,0:T(8,128)(2,1)} %fusion.10) | copy-start | bytes 983044
  54.2 4.8 %copy-start.11 = (bf16[1024,512]{1,0:T(8,128)(2,1)S(1)}, bf16[1024,512]{1,0:T(8,128)(2,1)}, u32[]{:S(2)}) copy-start(bf16[1024,512]{1,0:T(8,128)(2,1)} %param.12) | copy-start | bytes 3145732
  56.0 1.2 %copy-start.2 = (f32[20,16,1024]{2,1,0:T(8,128)}, f32[20,16,1024]{2,1,0:T(8,128)S(1)}, u32[]{:S(2)}) copy-start(f32[20,16,1024]{2,1,0:T(8,128)S(1)} %fusion.14) | copy-start | bytes 3932164
  57.2 2.3 %copy-start.12 = (bf16[1024,512]{1,0:T(8,128)(2,1)S(1)}, bf16[1024,512]{1,0:T(8,128)(2,1)}, u32[]{:S(2)}) copy-start(bf16[1024,512]{1,0:T(8,128)(2,1)} %param.13) | copy-start | bytes 3145732
  57.2 23.3 %collective-permute-start.1 = (bf16[1,20,16,512]{3,2,1,0:T(8,128)(2,1)}, bf16[1,20,16,512]{3,2,1,0:T(8,128)(2,1)}, u32[]{:S(2)}, u32[]{:S(2)}) collective-permute-start(bf16[1,20,16,512]{3,2,1,0:T(8,128)(2,1)} %fusion.41), channel_id=1, source_target_pairs={{1,0},{0,1},{3,2},{2,3},{5,4},{4,5},{7,6},{6,7},{9,8},{8,9},{11,10... | collective-permute-start | bytes 983048 | tf_op jit(solution)/shard_map/ppermute | solution.py:17
  59.5 1.1 %copy-start.13 = (bf16[20,16,512]{2,1,0:T(8,128)(2,1)S(1)}, bf16[20,16,512]{2,1,0:T(8,128)(2,1)}, u32[]{:S(2)}) copy-start(bf16[20,16,512]{2,1,0:T(8,128)(2,1)} %reshape.280) | copy-start | bytes 983044
  60.6 2.5 %copy-start.14 = (f32[8,20,20]{1,2,0:T(8,128)S(1)}, f32[8,20,20]{1,2,0:T(8,128)}, u32[]{:S(2)}) copy-start(f32[8,20,20]{1,2,0:T(8,128)} %get-tuple-element.17) | copy-start | bytes 38404
  62.3 4.1 %collective-permute-start.4 = (f32[512]{0:T(512)S(1)}, f32[512]{0:T(512)S(1)}, u32[]{:S(2)}, u32[]{:S(2)}) collective-permute-start(f32[512]{0:T(512)S(1)} %bitcast.93), channel_id=1, source_target_pairs={{1,0},{0,1},{3,2},{2,3},{5,4},{4,5},{7,6},{6,7},{9,8},{8,9},{11,10... | collective-permute-start | bytes 6152 | tf_op jit(solution)/shard_map/ppermute | solution.py:17
  66.4 4.9 %collective-permute-start.6 = (f32[824]{0:T(1024)S(1)}, f32[824]{0:T(1024)S(1)}, u32[]{:S(2)}, u32[]{:S(2)}) collective-permute-start(f32[824]{0:T(1024)S(1)} %pad_maximum_fusion.1), channel_id=1, source_target_pairs={{16,0},{24,8},{0,16},{8,24},{17,1},{25,9},{1,17},{9,25},{18,2},{26... | collective-permute-start | bytes 9896 | tf_op jit(solution)/shard_map/ppermute | solution.py:32
  67.9 3.5 %collective-permute-start.7 = (f32[824]{0:T(1024)S(1)}, f32[824]{0:T(1024)S(1)}, u32[]{:S(2)}, u32[]{:S(2)}) collective-permute-start(f32[824]{0:T(1024)S(1)} %pad_maximum_fusion.1), channel_id=1, source_target_pairs={{24,0},{0,8},{8,16},{16,24},{25,1},{1,9},{9,17},{17,25},{26,2},{2,... | collective-permute-start | bytes 9896 | tf_op jit(solution)/shard_map/ppermute | solution.py:32
  67.9 3.5 %collective-permute-start.5 = (f32[824]{0:T(1024)S(1)}, f32[824]{0:T(1024)S(1)}, u32[]{:S(2)}, u32[]{:S(2)}) collective-permute-start(f32[824]{0:T(1024)S(1)} %pad_maximum_fusion.1), channel_id=1, source_target_pairs={{8,0},{16,8},{24,16},{0,24},{9,1},{17,9},{25,17},{1,25},{10,2},{18... | collective-permute-start | bytes 9896 | tf_op jit(solution)/shard_map/ppermute | solution.py:32
  69.6 10.8 %copy-start.7 = (bf16[1,20,16,512]{3,2,1,0:T(8,128)(2,1)S(1)}, bf16[1,20,16,512]{3,2,1,0:T(8,128)(2,1)}, u32[]{:S(2)}) copy-start(bf16[1,20,16,512]{3,2,1,0:T(8,128)(2,1)} %param.8) | copy-start | bytes 983044
  71.3 14.8 %copy-start.8 = (bf16[1,20,16,512]{3,2,1,0:T(8,128)(2,1)S(1)}, bf16[1,20,16,512]{3,2,1,0:T(8,128)(2,1)}, u32[]{:S(2)}) copy-start(bf16[1,20,16,512]{3,2,1,0:T(8,128)(2,1)} %param.9) | copy-start | bytes 983044
  71.4 7.2 %collective-permute-start.10 = (f32[824]{0:T(1024)S(1)}, f32[824]{0:T(1024)S(1)}, u32[]{:S(2)}, u32[]{:S(2)}) collective-permute-start(f32[824]{0:T(1024)S(1)} %add_add_fusion.1), channel_id=1, source_target_pairs={{6,0},{0,2},{2,4},{4,6},{7,1},{1,3},{3,5},{5,7},{14,8},{8,10},{10,... | collective-permute-start | bytes 9896 | tf_op jit(solution)/shard_map/ppermute | solution.py:32
  73.0 5.6 %collective-permute-start.9 = (f32[824]{0:T(1024)S(1)}, f32[824]{0:T(1024)S(1)}, u32[]{:S(2)}, u32[]{:S(2)}) collective-permute-start(f32[824]{0:T(1024)S(1)} %add_add_fusion.1), channel_id=1, source_target_pairs={{4,0},{6,2},{0,4},{2,6},{5,1},{7,3},{1,5},{3,7},{12,8},{14,10},{8,... | collective-permute-start | bytes 9896 | tf_op jit(solution)/shard_map/ppermute | solution.py:32
  75.6 3.6 %collective-permute-start.8 = (f32[824]{0:T(1024)S(1)}, f32[824]{0:T(1024)S(1)}, u32[]{:S(2)}, u32[]{:S(2)}) collective-permute-start(f32[824]{0:T(1024)S(1)} %add_add_fusion.1), channel_id=1, source_target_pairs={{2,0},{4,2},{6,4},{0,6},{3,1},{5,3},{7,5},{1,7},{10,8},{12,10},{14... | collective-permute-start | bytes 9896 | tf_op jit(solution)/shard_map/ppermute | solution.py:32
  77.0 9.1 %collective-permute-start.3 = (bf16[1,20,16,512]{3,2,1,0:T(8,128)(2,1)S(1)}, bf16[1,20,16,512]{3,2,1,0:T(8,128)(2,1)}, u32[]{:S(2)}, u32[]{:S(2)}) collective-permute-start(bf16[1,20,16,512]{3,2,1,0:T(8,128)(2,1)S(1)} %fusion.42), channel_id=1, source_target_pairs={{1,0},{0,1},{3,2},{2,3},{5,4},{4,5},{7,6},{6,7},{9,8},{8,9},{11,10... | collective-permute-start | bytes 983048 | tf_op jit(solution)/shard_map/ppermute | solution.py:17
  (3 other events, 2.8 us)

commit v2 on v1

v2 whole, which is shorter than its diff:
```python
import functools

import jax
import jax.numpy as jnp
from jax import lax
from jax.experimental import pallas as pl
from jax.experimental.pallas import tpu as pltpu
from jax.sharding import PartitionSpec as P

BAND = 8
LANES = 128
FAR = -1e30
F32, BF16 = jnp.float32, jnp.bfloat16
NT = (((1,), (1,)), ((), ()))
NN = (((1,), (0,)), ((), ()))
TN = (((0,), (0,)), ((), ()))
VMEM_LIMIT = 24 * 1024 * 1024


def mm(a, b, dims=NN):
    return lax.dot_general(a, b, dims, preferred_element_type=F32)


def band_rows(value, frames, pixels, band):
    value = value.astype(F32).reshape(frames, pixels // BAND, BAND, value.shape[-1])
    return value[:, band].reshape(frames * BAND, value.shape[-1])


def same_pixel(rows):
    row = lax.broadcasted_iota(jnp.int32, (BAND, rows), 0)
    lane = lax.broadcasted_iota(jnp.int32, (BAND, rows), 1)
    return (lane & (BAND - 1)) == row


def head_lanes(head_dim, rows):
    return lax.broadcasted_iota(jnp.int32, (rows, LANES), 1) // head_dim


def stack_heads(pair, owner, per_pair, factor=None):
    pair = pair if factor is None else pair * jnp.asarray(factor, pair.dtype)
    return jnp.concatenate([jnp.where(owner == h, pair, jnp.zeros_like(pair)) for h in range(per_pair)], 0)


def pick_heads(parts, owner):
    out = parts[0]
    for h in range(1, len(parts)):
        out = jnp.where(owner == h, parts[h], out)
    return out


def forward_kernel(dims, me_ref, *refs):
    tm, frames, pixels, width, group, head_dim, eps = dims
    x_refs = refs[:tm]
    gain_ref, bias_ref, wq_ref, wk_ref, wv_ref, wo_ref = refs[tm:tm + 6]
    q_ref, k_ref, v_ref, p_ref, own_ref = refs[tm + 6:tm + 11]
    msg_refs = refs[tm + 11:tm + 11 + tm - 1]
    xw_ref, mix_ref, rel_ref = refs[tm + 11 + tm - 1:]
    me = me_ref[0]
    rows = frames * BAND
    per_pair = LANES // head_dim
    scale = head_dim ** -0.5

    def place(k):
        return pl.multiple_of(lax.rem(me + k, tm) * width, width)

    for k in range(tm):
        xw_ref[:, pl.ds(place(k), width)] = x_refs[k][...]
    for i in range(frames):
        rel_ref[i] = bias_ref[:, (frames - 1 - i) * BAND:(frames - 1 - i) * BAND + rows]
    same = same_pixel(rows)[None]
    owner = head_lanes(head_dim, rows)
    for band in range(pixels // BAND):
        x = band_rows(xw_ref[...], frames, pixels, band)
        inv = lax.rsqrt(jnp.mean(x * x, axis=-1, keepdims=True) + eps)
        normed = (x * inv * gain_ref[...]).astype(BF16)
        q = mm(normed, wq_ref[...]).astype(BF16)
        k = mm(normed, wk_ref[...]).astype(BF16)
        v = mm(normed, wv_ref[...]).astype(BF16)
        q_ref[band], k_ref[band], v_ref[band] = q, k, v
        att = []
        for pair in range(width // LANES):
            cols = slice(pair * LANES, (pair + 1) * LANES)
            kp, vp = k[:, cols], v[:, cols]
            scores = mm(stack_heads(q[:, cols], owner, per_pair, scale), kp, NT)
            scores = scores.reshape(per_pair, frames, BAND, rows)
            outs = []
            for h in range(per_pair):
                head = pair * per_pair + h
                s = jnp.where(same, scores[h] + rel_ref[:, head:head + 1, :], FAR)
                s = s.reshape(rows, rows)
                e = jnp.exp(s - jnp.max(s, axis=-1, keepdims=True))
                probs = (e * (1.0 / jnp.sum(e, axis=-1, keepdims=True))).astype(BF16)
                p_ref[band, head] = probs
                outs.append(mm(probs, vp))
            att.append(pick_heads(outs, owner).astype(BF16))
        mixed = mm(jnp.concatenate(att, axis=1), wo_ref[...])
        mix_ref[:, band] = mixed.reshape(frames, BAND, mixed.shape[-1])
    total = frames * pixels
    for k in range(1, tm):
        part = mix_ref[:, :, :, pl.ds(place(tm - k), width)]
        msg_refs[k - 1][...] = part.reshape(total, width).astype(BF16)
    own = mix_ref[:, :, :, pl.ds(place(0), width)].reshape(total, width)
    own_ref[...] = own + x_refs[0][...].astype(F32)


def backward_kernel(dims, me_ref, *refs):
    tm, frames, pixels, width, group, head_dim, eps = dims
    x_refs, g_refs = refs[:tm], refs[tm:2 * tm]
    gain_ref, q_ref, k_ref, v_ref, p_ref, wq_ref, wk_ref, wv_ref, wo_ref = refs[2 * tm:2 * tm + 9]
    outs = refs[2 * tm + 9:]
    own_ref, gain_out, bias_out = outs[:3]
    msg_refs = outs[3:3 + tm - 1]
    xw_ref, gw_ref, term_ref = outs[3 + tm - 1:]
    me = me_ref[0]
    rows = frames * BAND
    per_pair = LANES // head_dim
    scale = head_dim ** -0.5
    chans = width * tm

    def place(k):
        return pl.multiple_of(lax.rem(me + k, tm) * width, width)

    for k in range(tm):
        xw_ref[:, pl.ds(place(k), width)] = x_refs[k][...]
        gw_ref[:, pl.ds(place(k), width)] = g_refs[k][...]
    owner = head_lanes(head_dim, rows)
    gain_sum = jnp.zeros((1, chans), F32)
    diag = [0.0] * group
    for band in range(pixels // BAND):
        g = band_rows(gw_ref[...], frames, pixels, band).astype(BF16)
        d_att = mm(g, wo_ref[...], NT).astype(BF16)
        dq, dk, dv = [], [], []
        for pair in range(width // LANES):
            cols = slice(pair * LANES, (pair + 1) * LANES)
            qp, kp, vp = q_ref[band, :, cols], k_ref[band, :, cols], v_ref[band, :, cols]
            da = d_att[:, cols]
            d_prob = mm(stack_heads(da, owner, per_pair), vp, NT)
            q_parts, k_parts, v_parts = [], [], []
            for h in range(per_pair):
                head = pair * per_pair + h
                probs = p_ref[band, head]
                full = probs.astype(F32)
                t = d_prob[h * rows:(h + 1) * rows]
                dot = jnp.sum(full * t, axis=-1, keepdims=True)
                score = full * (t - dot)
                diag[head] = diag[head] + jnp.sum(score.reshape(frames, BAND, rows), axis=1)
                score = (score * scale).astype(BF16)
                q_parts.append(mm(score, kp))
                k_parts.append(mm(score, qp, TN))
                v_parts.append(mm(probs, da, TN))
            dq.append(pick_heads(q_parts, owner).astype(BF16))
            dk.append(pick_heads(k_parts, owner).astype(BF16))
            dv.append(pick_heads(v_parts, owner).astype(BF16))
        grad = mm(jnp.concatenate(dq, axis=1), wq_ref[...], NT)
        grad = grad + mm(jnp.concatenate(dk, axis=1), wk_ref[...], NT)
        grad = grad + mm(jnp.concatenate(dv, axis=1), wv_ref[...], NT)
        x = band_rows(xw_ref[...], frames, pixels, band)
        inv = lax.rsqrt(jnp.mean(x * x, axis=-1, keepdims=True) + eps)
        gain_sum = gain_sum + jnp.sum(grad * x * inv, axis=0, keepdims=True)
        scaled = grad * gain_ref[...]
        inner = jnp.mean(scaled * x, axis=-1, keepdims=True)
        term = inv * scaled - x * (inv * inv * inv * inner)
        term_ref[:, band] = term.reshape(frames, BAND, chans)
    total = frames * pixels
    for k in range(1, tm):
        part = term_ref[:, :, :, pl.ds(place(tm - k), width)]
        msg_refs[k - 1][...] = part.reshape(total, width).astype(BF16)
    own = term_ref[:, :, :, pl.ds(place(0), width)].reshape(total, width)
    own_ref[...] = own + g_refs[0][...].astype(F32)
    gain_out[...] = gain_sum
    for head in range(group):
        row = jnp.zeros((1, (2 * frames - 1) * BAND), F32)
        for i in range(frames):
            row = row + jnp.pad(
                diag[head][i:i + 1], ((0, 0), ((frames - 1 - i) * BAND, i * BAND))
            )
        bias_out[head:head + 1, :] = row


def shifted(value, axis, step):
    count = lax.axis_size(axis)
    return lax.ppermute(value, axis, [((i + step) % count, i) for i in range(count)])


def per_device(inputs, out_grad, norm_gain, pos_bias, w_query, w_key, w_value, w_out):
    clips, frames, pixels, width = inputs.shape
    group = pos_bias.shape[0]
    tm = lax.axis_size("tm")
    me = lax.axis_index("tm")
    chans = width * tm
    head_dim = width // group
    total = frames * pixels
    bands = pixels // BAND
    rows = frames * BAND
    dims = (tm, frames, pixels, width, group, head_dim, 1e-06)
    x0, g0 = inputs.reshape(total, width), out_grad.reshape(total, width)
    x_parts = [x0] + [shifted(x0, "tm", k) for k in range(1, tm)]
    g_parts = [g0] + [shifted(g0, "tm", k) for k in range(1, tm)]
    me1 = me.astype(jnp.int32).reshape(1)
    gain = norm_gain.reshape(1, chans)
    spread = jnp.broadcast_to(pos_bias[:, :, None], (*pos_bias.shape, BAND)).reshape(group, -1)
    smem, vmem = pl.BlockSpec(memory_space=pltpu.SMEM), pl.BlockSpec(memory_space=pltpu.VMEM)
    params = pltpu.CompilerParams(vmem_limit_bytes=VMEM_LIMIT)
    half = jax.ShapeDtypeStruct((bands, rows, width), BF16)
    share = jax.ShapeDtypeStruct((total, width), BF16)
    own = jax.ShapeDtypeStruct((total, width), F32)
    q, k, v, probs, mix_own, *mix_out = pl.pallas_call(
        functools.partial(forward_kernel, dims),
        in_specs=[smem] + [vmem] * (tm + 6),
        out_specs=[vmem] * (5 + tm - 1),
        out_shape=[half, half, half, jax.ShapeDtypeStruct((bands, group, rows, rows), BF16), own] + [share] * (tm - 1),
        scratch_shapes=[
            pltpu.VMEM((total, chans), BF16),
            pltpu.VMEM((frames, bands, BAND, chans), F32),
            pltpu.VMEM((frames, group, rows), F32),
        ],
        compiler_params=params,
        cost_estimate=pl.CostEstimate(flops=8_000_000_000, bytes_accessed=8_000_000, transcendentals=0),
        name="attend",
    )(me1, *x_parts, gain, spread, w_query, w_key, w_value, w_out)
    mix_in = [shifted(mix_out[k - 1], "tm", k) for k in range(1, tm)]
    grad_own, gain_part, bias_part, *grad_out = pl.pallas_call(
        functools.partial(backward_kernel, dims),
        in_specs=[smem] + [vmem] * (2 * tm + 9),
        out_specs=[vmem] * (3 + tm - 1),
        out_shape=[
            own,
            jax.ShapeDtypeStruct((1, chans), F32),
            jax.ShapeDtypeStruct((group, (2 * frames - 1) * BAND), F32),
        ] + [share] * (tm - 1),
        scratch_shapes=[
            pltpu.VMEM((total, chans), BF16),
            pltpu.VMEM((total, chans), BF16),
            pltpu.VMEM((frames, bands, BAND, chans), F32),
        ],
        compiler_params=params,
        cost_estimate=pl.CostEstimate(flops=8_000_000_000, bytes_accessed=8_000_000, transcendentals=0),
        name="attend_back",
    )(me1, *x_parts, *g_parts, gain, q, k, v, probs, w_query, w_key, w_value, w_out)
    grad_in = [shifted(grad_out[k - 1], "tm", k) for k in range(1, tm)]

    bias_sum = jnp.sum(bias_part.reshape(group, -1, BAND), axis=-1)
    small = jnp.concatenate([gain_part.reshape(-1), bias_sum.reshape(-1)])
    length = -(-small.shape[0] // 1024) * 1024
    small = jnp.pad(small, (0, length - small.shape[0])).reshape(-1, LANES)
    everyone = lax.all_gather(small, ("dp", "space", "tm"), axis=0, tiled=True)
    everyone = everyone.reshape(-1, tm, length)
    gain_grad = jnp.sum(
        lax.dynamic_slice_in_dim(everyone[:, :, :chans], me * width, width, 2), axis=(0, 1)
    )
    bias_grad = jnp.sum(lax.dynamic_index_in_dim(everyone, me, 1, keepdims=False), axis=0)
    bias_grad = bias_grad[chans:chans + pos_bias.size]

    def finish(mine, others):
        for part in others:
            mine = mine + part.astype(F32)
        return mine.astype(BF16).reshape(inputs.shape)

    return (finish(mix_own, mix_in), finish(grad_own, grad_in), gain_grad, bias_grad.reshape(pos_bias.shape))


def solution(mesh):
    return jax.shard_map(
        per_device,
        mesh=mesh,
        in_specs=(
            P("dp", None, "space", "tm"),
            P("dp", None, "space", "tm"),
            P(),
            P("tm", None),
            P(None, "tm"),
            P(None, "tm"),
            P(None, "tm"),
            P("tm", None),
        ),
        out_specs=(
            P("dp", None, "space", "tm"),
            P("dp", None, "space", "tm"),
            P("tm"),
            P("tm", None),
        ),
        check_vma=False,
    )
```

time: 88.7 us -> 103 us (1.16)
  blocking collectives: 0 us -> 67.6 us
  matrix products: 20.1 us -> 0 us
  waiting for transfers between devices: 20.4 us -> 7.78 us
  starting transfers between devices: 15.9 us -> 5.34 us
  Pallas kernels: 0 us -> 10.3 us
  other arithmetic: 12.8 us -> 2.53 us
  local copies, waits for them, and re-layouts: 17.8 us -> 8.45 us
    all_gather x0 -> x1, blocking collectives: none -> 67.6 us  [per_device(): everyone = lax.all_gather(small, ('dp', 'space', 'tm'), axis=0, tiled=True)]
    dot_general x16 -> x0, matrix products: 20.1 us -> none  [the longest x11 11.8 us: heads(): return jnp.einsum(spec, a, b, preferred_element_type=jnp.float32)]
    ppermute x5 -> x4, waiting for transfers between devices: 19.7 us -> 7.78 us  [shifted(): lax.ppermute(value, axis, [((i + step) % count, i) for i in range(count)])]
    another operation x8 -> x0, local copies, waits for them, and re-layouts: 10.5 us -> none
    pallas_call x0 -> x2, Pallas kernels: none -> 10.3 us  [the longest x1 6.68 us: per_device(): pl.pallas_call(functools.partial(backward_kernel, dims), in_specs=[smem]...]
    ppermute x6 -> x0, starting transfers between devices: 8.77 us -> none  [group_sum(): parts.append(lax.ppermute(value, axis, pairs))]
    sub x3 -> x0, other arithmetic: 6.45 us -> none  [the longest x1 4.75 us: per_device(): grad_score = probs_full * (grad_prob - row_dot)]
    unnamed x32 -> x16, local copies, waits for them, and re-layouts: 1.8 us -> 6.56 us
  transfers between devices with their start and end apart: 11 -> 4, of which waited for: 5 -> 1; matrix products, arithmetic and copies ran while one was open for 11% -> 3% of each run, Pallas kernels for 0% -> 10%
where the time goes in v2:
time: 103 us
  blocking collectives  67.6 us (66%)
  Pallas kernels  10.3 us (10%)
  local copies, waits for them, and re-layouts  8.45 us (8%)
  waiting for transfers between devices  7.78 us (8%)
  starting transfers between devices  5.34 us (5%)
  other arithmetic  2.53 us (2%)
    all_gather x1, blocking collectives, per_device(): everyone = lax.all_gather(small, ('dp', 'space', 'tm'), axis=0, tiled=True)  67.6 us
    ppermute x4, waiting for transfers between devices, shifted(): lax.ppermute(value, axis, [((i + step) % count, i) for i in range(count)])  7.78 us
    pallas_call x1, Pallas kernels, per_device(): pl.pallas_call(functools.partial(backward_kernel, dims), in_specs=[smem]...  6.68 us
    unnamed x16, local copies, waits for them, and re-layouts  6.56 us
    ppermute x4, starting transfers between devices, shifted(): lax.ppermute(value, axis, [((i + step) % count, i) for i in range(count)])  5.34 us
    pallas_call x1, Pallas kernels, per_device(): pl.pallas_call(functools.partial(forward_kernel, dims), in_specs=[smem] +...  3.66 us
  transfers between devices with their start and end apart: 4, of which 1 were waited for; matrix products, arithmetic and copies ran while one was open for 3% of the time, Pallas kernels for 10%

profile of v2, /device:TPU:0, one launch (start us, length us, event | category | flops | bytes accessed | tf_op | source)
XLA Modules:
  0.0 102.8 jit_solution(14994376421759391726)
XLA Ops:
  0.6 3.0 %collective-permute-start = (bf16[320,512]{1,0:T(8,128)(2,1)}, bf16[320,512]{1,0:T(8,128)(2,1)S(1)}, u32[]{:S(2)}, u32[]{:S(2)}) collective-permute-start(bf16[320,512]{1,0:T(8,128)(2,1)} %bitcast.10), channel_id=1, source_target_pairs={{1,0},{0,1},{3,2},{2,3},{5,4},{4,5},{7,6},{6,7},{9,8},{8,9},{11,10... | collective-permute-start | bytes 983048 | tf_op jit(solution)/shard_map/ppermute | solution.py:182
  3.7 0.1 collective-permute-start.2
  3.7 0.8 broadcast_in_dim.2
  4.5 0.1 reshape.51.refs_3_
  4.6 7.8 %collective-permute-done.refs_1_ = bf16[320,512]{1,0:T(8,128)(2,1)S(1)} collective-permute-done((bf16[320,512]{1,0:T(8,128)(2,1)}, bf16[320,512]{1,0:T(8,128)(2,1)S(1)}, u32[]{:S(2)}, u32[]{:S(2)}) %collective-permute-start) | collective-permute-done | bytes 327712 | tf_op jit(solution)/shard_map/ppermute | solution.py:182
  12.4 1.2 %copy-done = bf16[1024,512]{1,0:T(8,128)(2,1)S(1)} copy-done((bf16[1024,512]{1,0:T(8,128)(2,1)S(1)}, bf16[1024,512]{1,0:T(8,128)(2,1)}, u32[]{:S(2)}) %copy-start) | copy-done | bytes 1048600
  13.6 1.2 %copy-done.1 = bf16[1024,512]{1,0:T(8,128)(2,1)S(1)} copy-done((bf16[1024,512]{1,0:T(8,128)(2,1)S(1)}, bf16[1024,512]{1,0:T(8,128)(2,1)}, u32[]{:S(2)}) %copy-start.1) | copy-done | bytes 1048600
  14.9 1.2 %copy-done.2 = bf16[1024,512]{1,0:T(8,128)(2,1)S(1)} copy-done((bf16[1024,512]{1,0:T(8,128)(2,1)S(1)}, bf16[1024,512]{1,0:T(8,128)(2,1)}, u32[]{:S(2)}) %copy-start.2) | copy-done | bytes 1048600
  16.1 1.2 %copy-done.3 = bf16[512,1024]{1,0:T(8,128)(2,1)S(1)} copy-done((bf16[512,1024]{1,0:T(8,128)(2,1)S(1)}, bf16[512,1024]{1,0:T(8,128)(2,1)}, u32[]{:S(2)}) %copy-start.3) | copy-done | bytes 1048600
  17.3 1.0 copy-done.4
  18.3 0.7 copy-done.6
  19.0 3.7 %attend.1 = (bf16[2,160,512]{2,1,0:T(8,128)(2,1)S(1)}, bf16[2,160,512]{2,1,0:T(8,128)(2,1)S(1)}, bf16[2,160,512]{2,1,0:T(8,128)(2,1)S(1)}, bf16[2,8,160,160]{3,2...) custom-call(s32[1]{0:T(128)} %bitcast.me_ref, bf16[320,512]{1,0:T(8,128)(2,1)S(1)} %bitcast.11, ...), custom_call_target="tpu_custom_call" | custom-call | flops 8000000000 | bytes 8000000 | tf_op jit(solution)/shard_map/attend/pallas_call | solution.py:207
  22.7 2.1 %collective-permute-start.1 = (bf16[320,512]{1,0:T(8,128)(2,1)S(1)}, bf16[320,512]{1,0:T(8,128)(2,1)S(1)}, u32[]{:S(2)}, u32[]{:S(2)}) collective-permute-start(bf16[320,512]{1,0:T(8,128)(2,1)S(1)} %get-tuple-element.15), channel_id=1, source_target_pairs={{1,0},{0,1},{3,2},{2,3},{5,4},{4,5},{7,6},{6,7},{9,8},{8,9},{11,10... | collective-permute-start | bytes 983048 | tf_op jit(solution)/shard_map/ppermute | solution.py:182
  24.8 6.7 %attend_back.1 = (f32[320,512]{1,0:T(8,128)S(1)}, f32[1,1024]{1,0:T(1,128)S(1)}, f32[8,312]{1,0:T(8,128)S(1)}, bf16[320,512]{1,0:T(8,128)(2,1)S(1)}) custom-call(s32[1]{0:T(128)} %bitcast.me_ref, bf16[320,512]{1,0:T(8,128)(2,1)S(1)} %bitcast.12, bf16[320,512]{1,0:T(8,128)(2,1)S(1)} %collective-permute-done.refs_1_, bf16[320,512]{1,0:T(8,128)(2,1)S(1)} %bitcast.14, ...), custom_call_target="tpu_custom_call" | custom-call | flops 8000000000 | bytes 8000000 | tf_op jit(solution)/shard_map/attend_back/pallas_call | solution.py:222
  31.5 0.1 collective-permute-start.3
  31.6 0.1 reshape.56
  31.7 0.1 reduce_sum.27
  31.9 67.6 %all_gather.3 = f32[512,128]{1,0:T(8,128)S(1)} all-gather(f32[16,128]{1,0:T(8,128)S(1)} %fusion), channel_id=1, replica_groups=mesh['dp'=4,'space'=4,'tm'=2] {'dp','space','tm'}, dimensions={0}, use_global_device_ids=true | all-gather | bytes 270336 | tf_op jit(solution)/shard_map/all_gather | solution.py:246
  99.5 0.1 reshape.59
  99.7 0.2 dynamic-slice_reduce_fusion
  99.8 0.7 reshape.60
  100.5 0.6 dynamic-slice_reduce_fusion.1
  101.1 0.8 add_convert_fusion.1
  102.0 0.8 add_convert_fusion
  (17 shorter events, 0.1 us)
Async XLA Ops:
  0.6 11.8 %collective-permute-start = (bf16[320,512]{1,0:T(8,128)(2,1)}, bf16[320,512]{1,0:T(8,128)(2,1)S(1)}, u32[]{:S(2)}, u32[]{:S(2)}) collective-permute-start(bf16[320,512]{1,0:T(8,128)(2,1)} %bitcast.10), channel_id=1, source_target_pairs={{1,0},{0,1},{3,2},{2,3},{5,4},{4,5},{7,6},{6,7},{9,8},{8,9},{11,10... | collective-permute-start | bytes 983048 | tf_op jit(solution)/shard_map/ppermute | solution.py:182
  3.7 21.1 %collective-permute-start.2 = (bf16[320,512]{1,0:T(8,128)(2,1)}, bf16[320,512]{1,0:T(8,128)(2,1)S(1)}, u32[]{:S(2)}, u32[]{:S(2)}) collective-permute-start(bf16[320,512]{1,0:T(8,128)(2,1)} %bitcast.13), channel_id=1, source_target_pairs={{1,0},{0,1},{3,2},{2,3},{5,4},{4,5},{7,6},{6,7},{9,8},{8,9},{11,10... | collective-permute-start | bytes 983048 | tf_op jit(solution)/shard_map/ppermute | solution.py:182
  12.4 1.2 %copy-start = (bf16[1024,512]{1,0:T(8,128)(2,1)S(1)}, bf16[1024,512]{1,0:T(8,128)(2,1)}, u32[]{:S(2)}) copy-start(bf16[1024,512]{1,0:T(8,128)(2,1)} %refs_9_.1) | copy-start | bytes 3145732
  13.6 1.2 %copy-start.1 = (bf16[1024,512]{1,0:T(8,128)(2,1)S(1)}, bf16[1024,512]{1,0:T(8,128)(2,1)}, u32[]{:S(2)}) copy-start(bf16[1024,512]{1,0:T(8,128)(2,1)} %refs_10_.1) | copy-start | bytes 3145732
  14.9 1.2 %copy-start.2 = (bf16[1024,512]{1,0:T(8,128)(2,1)S(1)}, bf16[1024,512]{1,0:T(8,128)(2,1)}, u32[]{:S(2)}) copy-start(bf16[1024,512]{1,0:T(8,128)(2,1)} %refs_11_.1) | copy-start | bytes 3145732
  16.1 1.2 %copy-start.3 = (bf16[512,1024]{1,0:T(8,128)(2,1)S(1)}, bf16[512,1024]{1,0:T(8,128)(2,1)}, u32[]{:S(2)}) copy-start(bf16[512,1024]{1,0:T(8,128)(2,1)} %refs_12_.1) | copy-start | bytes 3145732
  17.3 1.0 copy-start.4
  18.3 0.7 copy-start.6
  19.0 5.8 %copy-start.5 = (bf16[1,20,16,512]{3,2,1,0:T(8,128)(2,1)S(1)}, bf16[1,20,16,512]{3,2,1,0:T(8,128)(2,1)}, u32[]{:S(2)}) copy-start(bf16[1,20,16,512]{3,2,1,0:T(8,128)(2,1)} %param.9) | copy-start | bytes 983044
  19.0 5.8 %copy-start.7 = (f32[1024]{0:T(1024)S(1)}, f32[1024]{0:T(1024)}, u32[]{:S(2)}) copy-start(f32[1024]{0:T(1024)} %param.10) | copy-start | bytes 12292
  22.7 78.5 %collective-permute-start.1 = (bf16[320,512]{1,0:T(8,128)(2,1)S(1)}, bf16[320,512]{1,0:T(8,128)(2,1)S(1)}, u32[]{:S(2)}, u32[]{:S(2)}) collective-permute-start(bf16[320,512]{1,0:T(8,128)(2,1)S(1)} %get-tuple-element.15), channel_id=1, source_target_pairs={{1,0},{0,1},{3,2},{2,3},{5,4},{4,5},{7,6},{6,7},{9,8},{8,9},{11,10... | collective-permute-start | bytes 983048 | tf_op jit(solution)/shard_map/ppermute | solution.py:182
  31.5 70.5 %collective-permute-start.3 = (bf16[320,512]{1,0:T(8,128)(2,1)S(1)}, bf16[320,512]{1,0:T(8,128)(2,1)S(1)}, u32[]{:S(2)}, u32[]{:S(2)}) collective-permute-start(bf16[320,512]{1,0:T(8,128)(2,1)S(1)} %get-tuple-element.21), channel_id=1, source_target_pairs={{1,0},{0,1},{3,2},{2,3},{5,4},{4,5},{7,6},{6,7},{9,8},{8,9},{11,10... | collective-permute-start | bytes 983048 | tf_op jit(solution)/shard_map/ppermute | solution.py:182

commit v3 on v2

--- a/solution.py
+++ b/solution.py
@@ -48,13 +48,26 @@
     return out
 
 
+def stage_kernel(count, frames, bias_ref, *refs):
+    sources, rel_ref, targets, sems = refs[:count], refs[count], refs[count + 1:2 * count + 1], refs[2 * count + 1]
+    copies = [pltpu.make_async_copy(s, t, sems.at[n]) for n, (s, t) in enumerate(zip(sources, targets))]
+    for copy in copies:
+        copy.start()
+    rows = rel_ref.shape[2]
+    for i in range(frames):
+        start = (frames - 1 - i) * BAND
+        rel_ref[i] = bias_ref[:, start:start + rows]
+    for copy in copies:
+        copy.wait()
+
+
 def forward_kernel(dims, me_ref, *refs):
     tm, frames, pixels, width, group, head_dim, eps = dims
     x_refs = refs[:tm]
-    gain_ref, bias_ref, wq_ref, wk_ref, wv_ref, wo_ref = refs[tm:tm + 6]
+    gain_ref, rel_ref, wq_ref, wk_ref, wv_ref, wo_ref = refs[tm:tm + 6]
     q_ref, k_ref, v_ref, p_ref, own_ref = refs[tm + 6:tm + 11]
     msg_refs = refs[tm + 11:tm + 11 + tm - 1]
-    xw_ref, mix_ref, rel_ref = refs[tm + 11 + tm - 1:]
+    xw_ref, mix_ref = refs[tm + 11 + tm - 1:]
     me = me_ref[0]
     rows = frames * BAND
     per_pair = LANES // head_dim
@@ -65,8 +78,6 @@
 
     for k in range(tm):
         xw_ref[:, pl.ds(place(k), width)] = x_refs[k][...]
-    for i in range(frames):
-        rel_ref[i] = bias_ref[:, (frames - 1 - i) * BAND:(frames - 1 - i) * BAND + rows]
     same = same_pixel(rows)[None]
     owner = head_lanes(head_dim, rows)
     for band in range(pixels // BAND):
@@ -108,9 +119,9 @@
     x_refs, g_refs = refs[:tm], refs[tm:2 * tm]
     gain_ref, q_ref, k_ref, v_ref, p_ref, wq_ref, wk_ref, wv_ref, wo_ref = refs[2 * tm:2 * tm + 9]
     outs = refs[2 * tm + 9:]
-    own_ref, gain_out, bias_out = outs[:3]
-    msg_refs = outs[3:3 + tm - 1]
-    xw_ref, gw_ref, term_ref = outs[3 + tm - 1:]
+    own_ref, small_ref = outs[:2]
+    msg_refs = outs[2:2 + tm - 1]
+    xw_ref, gw_ref, term_ref = outs[2 + tm - 1:]
     me = me_ref[0]
     rows = frames * BAND
     per_pair = LANES // head_dim
@@ -167,14 +178,29 @@
         msg_refs[k - 1][...] = part.reshape(total, width).astype(BF16)
     own = term_ref[:, :, :, pl.ds(place(0), width)].reshape(total, width)
     own_ref[...] = own + g_refs[0][...].astype(F32)
-    gain_out[...] = gain_sum
-    for head in range(group):
-        row = jnp.zeros((1, (2 * frames - 1) * BAND), F32)
-        for i in range(frames):
-            row = row + jnp.pad(
-                diag[head][i:i + 1], ((0, 0), ((frames - 1 - i) * BAND, i * BAND))
+    offsets = 2 * frames - 1
+    span = offsets * BAND
+    gain_rows = width // LANES
+    per_row = LANES // offsets
+    small_ref[...] = jnp.zeros_like(small_ref)
+    for t in range(tm):
+        for r in range(gain_rows):
+            start = t * width + r * LANES
+            small_ref[t, r:r + 1, :] = gain_sum[:, start:start + LANES]
+    lane = lax.broadcasted_iota(jnp.int32, (span, LANES), 1)
+    offset = lax.broadcasted_iota(jnp.int32, (span, LANES), 0) // BAND
+    for first in range(0, group, per_row):
+        packed = jnp.zeros((1, LANES), F32)
+        for head in range(first, min(first + per_row, group)):
+            row = jnp.zeros((1, span), F32)
+            for i in range(frames):
+                row = row + jnp.pad(diag[head][i:i + 1], ((0, 0), ((frames - 1 - i) * BAND, i * BAND)))
+            put = (lane == offset + (head - first) * offsets).astype(F32)
+            packed = packed + lax.dot_general(
+                row, put, NN, precision=lax.Precision.HIGHEST, preferred_element_type=F32
             )
-        bias_out[head:head + 1, :] = row
+        line = gain_rows + first // per_row
+        small_ref[pl.ds(me, 1), line:line + 1, :] = packed[None]
 
 
 def shifted(value, axis, step):
@@ -192,6 +218,10 @@
     total = frames * pixels
     bands = pixels // BAND
     rows = frames * BAND
+    offsets = 2 * frames - 1
+    per_row = LANES // offsets
+    gain_rows, bias_rows = width // LANES, -(-group // per_row)
+    lines = -(-(gain_rows + bias_rows) // BAND) * BAND
     dims = (tm, frames, pixels, width, group, head_dim, 1e-06)
     x0, g0 = inputs.reshape(total, width), out_grad.reshape(total, width)
     x_parts = [x0] + [shifted(x0, "tm", k) for k in range(1, tm)]
@@ -201,6 +231,20 @@
     spread = jnp.broadcast_to(pos_bias[:, :, None], (*pos_bias.shape, BAND)).reshape(group, -1)
     smem, vmem = pl.BlockSpec(memory_space=pltpu.SMEM), pl.BlockSpec(memory_space=pltpu.VMEM)
     params = pltpu.CompilerParams(vmem_limit_bytes=VMEM_LIMIT)
+    held = [x0, w_query, w_key, w_value, w_out, g0, gain]
+    rel, *held = pl.pallas_call(
+        functools.partial(stage_kernel, len(held), frames),
+        in_specs=[vmem] + [pl.BlockSpec(memory_space=pltpu.HBM)] * len(held),
+        out_specs=[vmem] * (1 + len(held)),
+        out_shape=[jax.ShapeDtypeStruct((frames, group, rows), F32)]
+        + [jax.ShapeDtypeStruct(h.shape, h.dtype) for h in held],
+        scratch_shapes=[pltpu.SemaphoreType.DMA((len(held),))],
+        compiler_params=params,
+        cost_estimate=pl.CostEstimate(flops=0, bytes_accessed=8_000_000, transcendentals=0),
+        name="stage",
+    )(spread, *held)
+    x0, w_query, w_key, w_value, w_out, g0, gain = held
+    x_parts[0], g_parts[0] = x0, g0
     half = jax.ShapeDtypeStruct((bands, rows, width), BF16)
     share = jax.ShapeDtypeStruct((total, width), BF16)
     own = jax.ShapeDtypeStruct((total, width), F32)
@@ -212,22 +256,17 @@
         scratch_shapes=[
             pltpu.VMEM((total, chans), BF16),
             pltpu.VMEM((frames, bands, BAND, chans), F32),
-            pltpu.VMEM((frames, group, rows), F32),
         ],
         compiler_params=params,
         cost_estimate=pl.CostEstimate(flops=8_000_000_000, bytes_accessed=8_000_000, transcendentals=0),
         name="attend",
-    )(me1, *x_parts, gain, spread, w_query, w_key, w_value, w_out)
+    )(me1, *x_parts, gain, rel, w_query, w_key, w_value, w_out)
     mix_in = [shifted(mix_out[k - 1], "tm", k) for k in range(1, tm)]
-    grad_own, gain_part, bias_part, *grad_out = pl.pallas_call(
+    grad_own, small, *grad_out = pl.pallas_call(
         functools.partial(backward_kernel, dims),
         in_specs=[smem] + [vmem] * (2 * tm + 9),
-        out_specs=[vmem] * (3 + tm - 1),
-        out_shape=[
-            own,
-            jax.ShapeDtypeStruct((1, chans), F32),
-            jax.ShapeDtypeStruct((group, (2 * frames - 1) * BAND), F32),
-        ] + [share] * (tm - 1),
+        out_specs=[vmem] * (2 + tm - 1),
+        out_shape=[own, jax.ShapeDtypeStruct((tm, lines, LANES), F32)] + [share] * (tm - 1),
         scratch_shapes=[
             pltpu.VMEM((total, chans), BF16),
             pltpu.VMEM((total, chans), BF16),
@@ -239,24 +278,20 @@
     )(me1, *x_parts, *g_parts, gain, q, k, v, probs, w_query, w_key, w_value, w_out)
     grad_in = [shifted(grad_out[k - 1], "tm", k) for k in range(1, tm)]
 
-    bias_sum = jnp.sum(bias_part.reshape(group, -1, BAND), axis=-1)
-    small = jnp.concatenate([gain_part.reshape(-1), bias_sum.reshape(-1)])
-    length = -(-small.shape[0] // 1024) * 1024
-    small = jnp.pad(small, (0, length - small.shape[0])).reshape(-1, LANES)
-    everyone = lax.all_gather(small, ("dp", "space", "tm"), axis=0, tiled=True)
-    everyone = everyone.reshape(-1, tm, length)
-    gain_grad = jnp.sum(
-        lax.dynamic_slice_in_dim(everyone[:, :, :chans], me * width, width, 2), axis=(0, 1)
-    )
-    bias_grad = jnp.sum(lax.dynamic_index_in_dim(everyone, me, 1, keepdims=False), axis=0)
-    bias_grad = bias_grad[chans:chans + pos_bias.size]
+    axes = ("dp", "space", "tm")
+    others = lax.axis_size(axes) // tm
+    small = jnp.broadcast_to(small[None], (others, tm, lines, LANES)).reshape(-1, LANES)
+    small = lax.all_to_all(small, axes, split_axis=0, concat_axis=0, tiled=True)
+    small = jnp.sum(small.reshape(-1, lines, LANES), axis=0)
+    gain_grad = small[:gain_rows].reshape(width)
+    bias_grad = small[gain_rows:gain_rows + bias_rows, :per_row * offsets].reshape(-1, offsets)[:group]
 
     def finish(mine, others):
         for part in others:
             mine = mine + part.astype(F32)
         return mine.astype(BF16).reshape(inputs.shape)
 
-    return (finish(mix_own, mix_in), finish(grad_own, grad_in), gain_grad, bias_grad.reshape(pos_bias.shape))
+    return (finish(mix_own, mix_in), finish(grad_own, grad_in), gain_grad, bias_grad)
 
 
 def solution(mesh):

time: 103 us -> 52.1 us (0.51)
  blocking collectives: 67.6 us -> 0 us
  waiting for transfers between devices: 7.78 us -> 16.1 us
  starting transfers between devices: 5.34 us -> 11.3 us
  local copies, waits for them, and re-layouts: 8.45 us -> 10.4 us
  Pallas kernels: 10.3 us -> 11.6 us
    all_gather x1 -> x0, blocking collectives: 67.6 us -> none  [per_device(): everyone = lax.all_gather(small, ('dp', 'space', 'tm'), axis=0, tiled=True)]
    all_to_all x0 -> x1, starting transfers between devices: none -> 6.06 us  [per_device(): small = lax.all_to_all(small, axes, split_axis=0, concat_axis=0, tiled=True)]
    all_to_all x0 -> x1, waiting for transfers between devices: none -> 5.65 us  [per_device(): small = lax.all_to_all(small, axes, split_axis=0, concat_axis=0, tiled=True)]
    ppermute x4, waiting for transfers between devices: 7.78 us -> 10.5 us  [shifted(): lax.ppermute(value, axis, [((i + step) % count, i) for i in range(count)])]
    unnamed x16 -> x14, local copies, waits for them, and re-layouts: 6.56 us -> 7.52 us
  transfers between devices with their start and end apart: 4 -> 5, of which waited for: 1 -> 4; matrix products, arithmetic and copies ran while one was open for 3% -> 6% of each run, Pallas kernels for 10% -> 9%
where the time goes in v3:
time: 52.1 us; the launch traced here: 51.7 us
  waiting for transfers between devices  16.1 us (31%)
  Pallas kernels  11.6 us (22%)
  starting transfers between devices  11.3 us (22%)
  local copies, waits for them, and re-layouts  10.4 us (20%)
  other arithmetic  1.67 us (3%)
  between operations  0.7 us (1%)
    ppermute x4, waiting for transfers between devices, shifted(): lax.ppermute(value, axis, [((i + step) % count, i) for i in range(count)])  10.5 us
    unnamed x14, local copies, waits for them, and re-layouts  7.52 us
    pallas_call x1, Pallas kernels, per_device(): pl.pallas_call(functools.partial(backward_kernel, dims), in_specs=[smem]...  7.17 us
    all_to_all x1, starting transfers between devices, per_device(): small = lax.all_to_all(small, axes, split_axis=0, concat_axis=0, tiled=True)  6.06 us
    all_to_all x1, waiting for transfers between devices, per_device(): small = lax.all_to_all(small, axes, split_axis=0, concat_axis=0, tiled=True)  5.65 us
    ppermute x4, starting transfers between devices, shifted(): lax.ppermute(value, axis, [((i + step) % count, i) for i in range(count)])  5.2 us
    pallas_call x1, Pallas kernels, per_device(): pl.pallas_call(functools.partial(forward_kernel, dims), in_specs=[smem] +...  3.77 us
    convert_element_type x2, other arithmetic, finish(): return mine.astype(BF16).reshape(inputs.shape)  1.63 us
  transfers between devices with their start and end apart: 5, of which 4 were waited for; matrix products, arithmetic and copies ran while one was open for 6% of the time, Pallas kernels for 9%

profile of v3, /device:TPU:0, one launch (start us, length us, event | category | flops | bytes accessed | tf_op | source)
XLA Modules:
  0.0 51.7 jit_solution(2981058580410738703)
XLA Ops:
  0.6 3.0 %collective-permute-start = (bf16[320,512]{1,0:T(8,128)(2,1)}, bf16[320,512]{1,0:T(8,128)(2,1)S(1)}, u32[]{:S(2)}, u32[]{:S(2)}) collective-permute-start(bf16[320,512]{1,0:T(8,128)(2,1)} %bitcast.9), channel_id=1, source_target_pairs={{1,0},{0,1},{3,2},{2,3},{5,4},{4,5},{7,6},{6,7},{9,8},{8,9},{11,10... | collective-permute-start | bytes 983048 | tf_op jit(solution)/shard_map/ppermute | solution.py:208
  3.7 0.8 %broadcast_in_dim.4 = f32[8,39,8]{2,1,0:T(8,128)S(1)} broadcast(f32[8,39]{1,0:T(8,128)} %param.11), dimensions={0,1} | broadcast | bytes 11232 | tf_op jit(solution)/shard_map/broadcast_in_dim | solution.py:231
  4.7 1.2 %copy-done = bf16[1024,512]{1,0:T(8,128)(2,1)S(1)} copy-done((bf16[1024,512]{1,0:T(8,128)(2,1)S(1)}, bf16[1024,512]{1,0:T(8,128)(2,1)}, u32[]{:S(2)}) %copy-start) | copy-done | bytes 1048600
  5.9 1.2 %copy-done.1 = bf16[1024,512]{1,0:T(8,128)(2,1)S(1)} copy-done((bf16[1024,512]{1,0:T(8,128)(2,1)S(1)}, bf16[1024,512]{1,0:T(8,128)(2,1)}, u32[]{:S(2)}) %copy-start.1) | copy-done | bytes 1048600
  7.1 1.2 %copy-done.2 = bf16[1024,512]{1,0:T(8,128)(2,1)S(1)} copy-done((bf16[1024,512]{1,0:T(8,128)(2,1)S(1)}, bf16[1024,512]{1,0:T(8,128)(2,1)}, u32[]{:S(2)}) %copy-start.2) | copy-done | bytes 1048600
  8.3 1.2 %copy-done.3 = bf16[512,1024]{1,0:T(8,128)(2,1)S(1)} copy-done((bf16[512,1024]{1,0:T(8,128)(2,1)S(1)}, bf16[512,1024]{1,0:T(8,128)(2,1)}, u32[]{:S(2)}) %copy-start.3) | copy-done | bytes 1048600
  9.5 1.0 %copy-done.4 = bf16[1,20,16,512]{3,2,1,0:T(8,128)(2,1)S(1)} copy-done((bf16[1,20,16,512]{3,2,1,0:T(8,128)(2,1)S(1)}, bf16[1,20,16,512]{3,2,1,0:T(8,128)(2,1)}, u32[]{:S(2)}) %copy-start.4) | copy-done | bytes 327704
  10.5 1.0 %copy-done.5 = bf16[1,20,16,512]{3,2,1,0:T(8,128)(2,1)S(1)} copy-done((bf16[1,20,16,512]{3,2,1,0:T(8,128)(2,1)S(1)}, bf16[1,20,16,512]{3,2,1,0:T(8,128)(2,1)}, u32[]{:S(2)}) %copy-start.5) | copy-done | bytes 327704
  11.5 0.7 %copy-done.6 = f32[1024]{0:T(1024)S(1)} copy-done((f32[1024]{0:T(1024)S(1)}, f32[1024]{0:T(1024)}, u32[]{:S(2)}) %copy-start.6) | copy-done | bytes 4120
  12.2 0.7 %stage.1 = (f32[20,8,160]{2,1,0:T(8,128)S(1)}, bf16[320,512]{1,0:T(8,128)(2,1)S(1)}, bf16[1024,512]{1,0:T(8,128)(2,1)S(1)}, bf16[1024,512]{1,0:T(8,128)(2,1)S(1)...) custom-call(f32[8,312]{1,0:T(8,128)S(1)} %reshape.44.bias_ref, ...), custom_call_target="tpu_custom_call" | custom-call | bytes 8000000 | tf_op jit(solution)/shard_map/stage/pallas_call | solution.py:235
  12.9 3.8 %attend.1 = (bf16[2,160,512]{2,1,0:T(8,128)(2,1)S(1)}, bf16[2,160,512]{2,1,0:T(8,128)(2,1)S(1)}, bf16[2,160,512]{2,1,0:T(8,128)(2,1)S(1)}, bf16[2,8,160,160]{3,2...) custom-call(s32[1]{0:T(128)} %bitcast.me_ref, ...), custom_call_target="tpu_custom_call" | custom-call | flops 8000000000 | bytes 8000000 | tf_op jit(solution)/shard_map/attend/pallas_call | solution.py:251
  16.6 2.0 %collective-permute-done.2.refs_3_ = bf16[320,512]{1,0:T(8,128)(2,1)S(1)} collective-permute-done((bf16[320,512]{1,0:T(8,128)(2,1)}, bf16[320,512]{1,0:T(8,128)(2,1)S(1)}, u32[]{:S(2)}, u32[]{:S(2)}) %collective-permute-start.2) | collective-permute-done | bytes 327712 | tf_op jit(solution)/shard_map/ppermute | solution.py:208
  18.6 7.2 %attend_back.1 = (f32[320,512]{1,0:T(8,128)S(1)}, f32[2,8,128]{2,1,0:T(8,128)S(1)}, bf16[320,512]{1,0:T(8,128)(2,1)S(1)}) custom-call(s32[1]{0:T(128)} %bitcast.me_ref, bf16[320,512]{1,0:T(8,128)(2,1)S(1)} %get-tuple-element.21.refs_0_, bf16[320,512]{1,0:T(8,128)(2,1)S(1)} %collective-permute-done.refs_1_, bf16[320,512]{1,0:T(8,128)(2,1)S(1)} %get-tuple-element.30.refs_2_, ...), custom_call_target="tpu_custom_call" | custom-call | flops 8000000000 | bytes 8000000 | tf_op jit(solution)/shard_map/attend_back/pallas_call | solution.py:265
  25.8 0.7 %broadcast_in_dim.5 = f32[16,2,8,128]{3,2,1,0:T(8,128)} broadcast(f32[2,8,128]{2,1,0:T(8,128)S(1)} %get-tuple-element.37), dimensions={1,2,3} | broadcast | bytes 139264 | tf_op jit(solution)/shard_map/broadcast_in_dim | solution.py:283
  26.5 6.1 %all-to-all-start = ((f32[32,8,128]{2,1,0:T(8,128)}), f32[32,8,128]{2,1,0:T(8,128)S(1)}, u32[]{:S(2)}, u32[]{:S(2)}) async-start(f32[32,8,128]{2,1,0:T(8,128)} %bitcast.6), calls=%async_computation | async-start | bytes 262144 | tf_op jit(solution)/shard_map/all_to_all | solution.py:284
  32.5 1.8 %collective-permute-start.1 = (bf16[320,512]{1,0:T(8,128)(2,1)S(1)}, bf16[320,512]{1,0:T(8,128)(2,1)S(1)}, u32[]{:S(2)}, u32[]{:S(2)}) collective-permute-start(bf16[320,512]{1,0:T(8,128)(2,1)S(1)} %get-tuple-element.29), channel_id=1, source_target_pairs={{1,0},{0,1},{3,2},{2,3},{5,4},{4,5},{7,6},{6,7},{9,8},{8,9},{11,10... | collective-permute-start | bytes 983048 | tf_op jit(solution)/shard_map/ppermute | solution.py:208
  34.4 0.3 collective-permute-start.3
  34.6 5.6 %all-to-all-done = f32[32,8,128]{2,1,0:T(8,128)S(1)} async-done(((f32[32,8,128]{2,1,0:T(8,128)}), f32[32,8,128]{2,1,0:T(8,128)S(1)}, u32[]{:S(2)}, u32[]{:S(2)}) %all-to-all-start) | async-done | bytes 131104 | tf_op jit(solution)/shard_map/all_to_all | solution.py:284
  40.3 0.6 %slice_bitcast_fusion = f32[512]{0:T(512)} fusion(f32[8,128]{1,0:T(8,128)S(1)} %reduce_sum.9), kind=kLoop, calls=%fused_computation.2 | loop fusion | bytes 4096 | tf_op jit(solution)/shard_map/reshape | solution.py:286
  41.0 0.6 %slice.12 = f32[8,39]{1,0:T(8,128)} slice(f32[9,39]{1,0:T(8,128)S(1)} %reshape.51), slice={[0:8], [0:39]} | slice | bytes 2496 | tf_op jit(solution)/shard_map/slice | solution.py:287
  41.6 2.8 %collective-permute-done.1 = bf16[320,512]{1,0:T(8,128)(2,1)S(1)} collective-permute-done((bf16[320,512]{1,0:T(8,128)(2,1)S(1)}, bf16[320,512]{1,0:T(8,128)(2,1)S(1)}, u32[]{:S(2)}, u32[]{:S(2)}) %collective-permute-start.1) | collective-permute-done | bytes 327712 | tf_op jit(solution)/shard_map/ppermute | solution.py:208
  44.4 0.8 %add_convert_fusion.1 = bf16[320,512]{1,0:T(8,128)(2,1)} fusion(f32[320,512]{1,0:T(8,128)S(1)} %get-tuple-element.28, bf16[320,512]{1,0:T(8,128)(2,1)S(1)} %collective-permute-done.1), kind=kLoop, calls=%fused_computation.1 | loop fusion | flops 491520 | bytes 1310720 | tf_op jit(solution)/shard_map/convert_element_type | solution.py:292
  45.2 5.7 %collective-permute-done.3 = bf16[320,512]{1,0:T(8,128)(2,1)S(1)} collective-permute-done((bf16[320,512]{1,0:T(8,128)(2,1)S(1)}, bf16[320,512]{1,0:T(8,128)(2,1)S(1)}, u32[]{:S(2)}, u32[]{:S(2)}) %collective-permute-start.3) | collective-permute-done | bytes 327712 | tf_op jit(solution)/shard_map/ppermute | solution.py:208
  50.9 0.8 %add_convert_fusion = bf16[320,512]{1,0:T(8,128)(2,1)} fusion(f32[320,512]{1,0:T(8,128)S(1)} %get-tuple-element.35, bf16[320,512]{1,0:T(8,128)(2,1)S(1)} %collective-permute-done.3), kind=kLoop, calls=%fused_computation | loop fusion | flops 491520 | bytes 1310720 | tf_op jit(solution)/shard_map/convert_element_type | solution.py:292
  (13 shorter events, 0.3 us)
Async XLA Ops:
  0.6 12.2 %collective-permute-start = (bf16[320,512]{1,0:T(8,128)(2,1)}, bf16[320,512]{1,0:T(8,128)(2,1)S(1)}, u32[]{:S(2)}, u32[]{:S(2)}) collective-permute-start(bf16[320,512]{1,0:T(8,128)(2,1)} %bitcast.9), channel_id=1, source_target_pairs={{1,0},{0,1},{3,2},{2,3},{5,4},{4,5},{7,6},{6,7},{9,8},{8,9},{11,10... | collective-permute-start | bytes 983048 | tf_op jit(solution)/shard_map/ppermute | solution.py:208
  3.7 14.9 %collective-permute-start.2 = (bf16[320,512]{1,0:T(8,128)(2,1)}, bf16[320,512]{1,0:T(8,128)(2,1)S(1)}, u32[]{:S(2)}, u32[]{:S(2)}) collective-permute-start(bf16[320,512]{1,0:T(8,128)(2,1)} %bitcast.11), channel_id=1, source_target_pairs={{1,0},{0,1},{3,2},{2,3},{5,4},{4,5},{7,6},{6,7},{9,8},{8,9},{11,10... | collective-permute-start | bytes 983048 | tf_op jit(solution)/shard_map/ppermute | solution.py:208
  4.6 1.2 %copy-start = (bf16[1024,512]{1,0:T(8,128)(2,1)S(1)}, bf16[1024,512]{1,0:T(8,128)(2,1)}, u32[]{:S(2)}) copy-start(bf16[1024,512]{1,0:T(8,128)(2,1)} %refs_1_.1) | copy-start | bytes 3145732
  5.9 1.2 %copy-start.1 = (bf16[1024,512]{1,0:T(8,128)(2,1)S(1)}, bf16[1024,512]{1,0:T(8,128)(2,1)}, u32[]{:S(2)}) copy-start(bf16[1024,512]{1,0:T(8,128)(2,1)} %refs_2_.1) | copy-start | bytes 3145732
  7.1 1.2 %copy-start.2 = (bf16[1024,512]{1,0:T(8,128)(2,1)S(1)}, bf16[1024,512]{1,0:T(8,128)(2,1)}, u32[]{:S(2)}) copy-start(bf16[1024,512]{1,0:T(8,128)(2,1)} %refs_3_.1) | copy-start | bytes 3145732
  8.3 1.2 %copy-start.3 = (bf16[512,1024]{1,0:T(8,128)(2,1)S(1)}, bf16[512,1024]{1,0:T(8,128)(2,1)}, u32[]{:S(2)}) copy-start(bf16[512,1024]{1,0:T(8,128)(2,1)} %refs_4_.1) | copy-start | bytes 3145732
  9.5 1.0 %copy-start.4 = (bf16[1,20,16,512]{3,2,1,0:T(8,128)(2,1)S(1)}, bf16[1,20,16,512]{3,2,1,0:T(8,128)(2,1)}, u32[]{:S(2)}) copy-start(bf16[1,20,16,512]{3,2,1,0:T(8,128)(2,1)} %param.8) | copy-start | bytes 983044
  10.5 1.0 %copy-start.5 = (bf16[1,20,16,512]{3,2,1,0:T(8,128)(2,1)S(1)}, bf16[1,20,16,512]{3,2,1,0:T(8,128)(2,1)}, u32[]{:S(2)}) copy-start(bf16[1,20,16,512]{3,2,1,0:T(8,128)(2,1)} %param.9) | copy-start | bytes 983044
  11.5 0.7 %copy-start.6 = (f32[1024]{0:T(1024)S(1)}, f32[1024]{0:T(1024)}, u32[]{:S(2)}) copy-start(f32[1024]{0:T(1024)} %param.10) | copy-start | bytes 12292
  26.5 13.8 %all-to-all-start = ((f32[32,8,128]{2,1,0:T(8,128)}), f32[32,8,128]{2,1,0:T(8,128)S(1)}, u32[]{:S(2)}, u32[]{:S(2)}) async-start(f32[32,8,128]{2,1,0:T(8,128)} %bitcast.6), calls=%async_computation | async-start | bytes 262144 | tf_op jit(solution)/shard_map/all_to_all | solution.py:284
  32.5 11.8 %collective-permute-start.1 = (bf16[320,512]{1,0:T(8,128)(2,1)S(1)}, bf16[320,512]{1,0:T(8,128)(2,1)S(1)}, u32[]{:S(2)}, u32[]{:S(2)}) collective-permute-start(bf16[320,512]{1,0:T(8,128)(2,1)S(1)} %get-tuple-element.29), channel_id=1, source_target_pairs={{1,0},{0,1},{3,2},{2,3},{5,4},{4,5},{7,6},{6,7},{9,8},{8,9},{11,10... | collective-permute-start | bytes 983048 | tf_op jit(solution)/shard_map/ppermute | solution.py:208
  34.4 16.5 %collective-permute-start.3 = (bf16[320,512]{1,0:T(8,128)(2,1)S(1)}, bf16[320,512]{1,0:T(8,128)(2,1)S(1)}, u32[]{:S(2)}, u32[]{:S(2)}) collective-permute-start(bf16[320,512]{1,0:T(8,128)(2,1)S(1)} %get-tuple-element.36), channel_id=1, source_target_pairs={{1,0},{0,1},{3,2},{2,3},{5,4},{4,5},{7,6},{6,7},{9,8},{8,9},{11,10... | collective-permute-start | bytes 983048 | tf_op jit(solution)/shard_map/ppermute | solution.py:208

commit v4 on v3

v4 whole, which is shorter than its diff:
```python
import functools

import jax
import jax.numpy as jnp
from jax import lax
from jax.experimental import pallas as pl
from jax.experimental.pallas import tpu as pltpu
from jax.sharding import PartitionSpec as P

BAND = 8
LANES = 128
FAR = -1e30
F32, BF16 = jnp.float32, jnp.bfloat16
NT = (((1,), (1,)), ((), ()))
NN = (((1,), (0,)), ((), ()))
TN = (((0,), (0,)), ((), ()))
VMEM_LIMIT = 24 * 1024 * 1024


def mm(a, b, dims=NN):
    return lax.dot_general(a, b, dims, preferred_element_type=F32)


def band_rows(value, frames, pixels, band):
    value = value.astype(F32).reshape(frames, pixels // BAND, BAND, value.shape[-1])
    return value[:, band].reshape(frames * BAND, value.shape[-1])


def same_pixel(rows):
    row = lax.broadcasted_iota(jnp.int32, (BAND, rows), 0)
    lane = lax.broadcasted_iota(jnp.int32, (BAND, rows), 1)
    return (lane & (BAND - 1)) == row


def head_lanes(head_dim, rows):
    return lax.broadcasted_iota(jnp.int32, (rows, LANES), 1) // head_dim


def stack_heads(pair, owner, per_pair, factor=None):
    pair = pair if factor is None else pair * jnp.asarray(factor, pair.dtype)
    return jnp.concatenate([jnp.where(owner == h, pair, jnp.zeros_like(pair)) for h in range(per_pair)], 0)


def pick_heads(parts, owner):
    out = parts[0]
    for h in range(1, len(parts)):
        out = jnp.where(owner == h, parts[h], out)
    return out


def stage_kernel(count, frames, bias_ref, *refs):
    sources, rel_ref, targets, sems = refs[:count], refs[count], refs[count + 1:2 * count + 1], refs[2 * count + 1]
    copies = [pltpu.make_async_copy(s, t, sems.at[n]) for n, (s, t) in enumerate(zip(sources, targets))]
    for copy in copies:
        copy.start()
    rows = rel_ref.shape[2]
    for i in range(frames):
        start = (frames - 1 - i) * BAND
        rel_ref[i] = bias_ref[:, start:start + rows]
    for copy in copies:
        copy.wait()


def forward_kernel(dims, me_ref, *refs):
    tm, frames, pixels, width, group, head_dim, eps = dims
    x_refs = refs[:tm]
    gain_ref, rel_ref, wq_ref, wk_ref, wv_ref, wo_ref = refs[tm:tm + 6]
    q_ref, k_ref, v_ref, p_ref, xb_ref, inv_ref, own_ref = refs[tm + 6:tm + 13]
    msg_refs = refs[tm + 13:tm + 13 + tm - 1]
    xw_ref, mix_ref = refs[tm + 13 + tm - 1:]
    me = me_ref[0]
    rows = frames * BAND
    per_pair = LANES // head_dim
    scale = head_dim ** -0.5

    def place(k):
        return pl.multiple_of(lax.rem(me + k, tm) * width, width)

    for k in range(tm):
        xw_ref[:, pl.ds(place(k), width)] = x_refs[k][...]
    same = same_pixel(rows)[None]
    owner = head_lanes(head_dim, rows)
    for band in range(pixels // BAND):
        x = band_rows(xw_ref[...], frames, pixels, band)
        inv = lax.rsqrt(jnp.mean(x * x, axis=-1, keepdims=True) + eps)
        normed = (x * inv * gain_ref[...]).astype(BF16)
        xb_ref[band] = x.astype(BF16)
        inv_ref[band] = jnp.broadcast_to(inv, (rows, LANES))
        q = mm(normed, wq_ref[...]).astype(BF16)
        k = mm(normed, wk_ref[...]).astype(BF16)
        v = mm(normed, wv_ref[...]).astype(BF16)
        q_ref[band], k_ref[band], v_ref[band] = q, k, v
        att = []
        for pair in range(width // LANES):
            cols = slice(pair * LANES, (pair + 1) * LANES)
            kp, vp = k[:, cols], v[:, cols]
            scores = mm(stack_heads(q[:, cols], owner, per_pair, scale), kp, NT)
            scores = scores.reshape(per_pair, frames, BAND, rows)
            outs = []
            for h in range(per_pair):
                head = pair * per_pair + h
                s = jnp.where(same, scores[h] + rel_ref[:, head:head + 1, :], FAR)
                s = s.reshape(rows, rows)
                e = jnp.exp(s - jnp.max(s, axis=-1, keepdims=True))
                probs = (e * (1.0 / jnp.sum(e, axis=-1, keepdims=True))).astype(BF16)
                p_ref[band, head] = probs
                outs.append(mm(probs, vp))
            att.append(pick_heads(outs, owner).astype(BF16))
        mixed = mm(jnp.concatenate(att, axis=1), wo_ref[...])
        mix_ref[:, band] = mixed.reshape(frames, BAND, mixed.shape[-1])
    total = frames * pixels
    for k in range(1, tm):
        part = mix_ref[:, :, :, pl.ds(place(tm - k), width)]
        msg_refs[k - 1][...] = part.reshape(total, width).astype(BF16)
    own = mix_ref[:, :, :, pl.ds(place(0), width)].reshape(total, width)
    own_ref[...] = own + x_refs[0][...].astype(F32)


def backward_kernel(dims, band, last, me_ref, *refs):
    tm, frames, pixels, width, group, head_dim, eps = dims
    g_refs = refs[:tm]
    gain_ref, q_ref, k_ref, v_ref, p_ref, xb_ref, inv_ref, wq_ref, wk_ref, wv_ref, wo_ref = refs[tm:tm + 11]
    rest = list(refs[tm + 11:])
    carried = (rest.pop(0), rest.pop(0)) if band else None
    own_ref = rest.pop(0)
    msg_refs = [rest.pop(0) for _ in range(tm - 1)]
    outs = [rest.pop(0)] if last else [rest.pop(0), rest.pop(0)]
    gw_ref, term_ref = rest
    me = me_ref[0]
    rows = frames * BAND
    per_pair = LANES // head_dim
    scale = head_dim ** -0.5

    def place(k):
        return pl.multiple_of(lax.rem(me + k, tm) * width, width)

    for k in range(tm):
        gw_ref[:, pl.ds(place(k), width)] = g_refs[k][...]
    owner = head_lanes(head_dim, rows)
    d_att = mm(gw_ref[...], wo_ref[...], NT).astype(BF16)
    dq, dk, dv, diag = [], [], [], []
    for pair in range(width // LANES):
        cols = slice(pair * LANES, (pair + 1) * LANES)
        qp, kp, vp = q_ref[band, :, cols], k_ref[band, :, cols], v_ref[band, :, cols]
        da = d_att[:, cols]
        d_prob = mm(stack_heads(da, owner, per_pair), vp, NT)
        q_parts, k_parts, v_parts = [], [], []
        for h in range(per_pair):
            head = pair * per_pair + h
            probs = p_ref[band, head]
            full = probs.astype(F32)
            t = d_prob[h * rows:(h + 1) * rows]
            dot = jnp.sum(full * t, axis=-1, keepdims=True)
            score = full * (t - dot)
            part = jnp.sum(score.reshape(frames, BAND, rows), axis=1)
            diag.append(part if carried is None else part + carried[1][head])
            score = (score * scale).astype(BF16)
            q_parts.append(mm(score, kp))
            k_parts.append(mm(score, qp, TN))
            v_parts.append(mm(probs, da, TN))
        dq.append(pick_heads(q_parts, owner).astype(BF16))
        dk.append(pick_heads(k_parts, owner).astype(BF16))
        dv.append(pick_heads(v_parts, owner).astype(BF16))
    grad = mm(jnp.concatenate(dq, axis=1), wq_ref[...], NT)
    grad = grad + mm(jnp.concatenate(dk, axis=1), wk_ref[...], NT)
    grad = grad + mm(jnp.concatenate(dv, axis=1), wv_ref[...], NT)
    x = xb_ref[band].astype(F32)
    inv = inv_ref[band][:, :1]
    gain_sum = jnp.sum(grad * x * inv, axis=0, keepdims=True)
    if carried is not None:
        gain_sum = gain_sum + carried[0][...]
    scaled = grad * gain_ref[...]
    inner = jnp.mean(scaled * x, axis=-1, keepdims=True)
    term_ref[...] = inv * scaled - x * (inv * inv * inv * inner)
    for k in range(1, tm):
        msg_refs[k - 1][...] = term_ref[:, pl.ds(place(tm - k), width)].astype(BF16)
    own_ref[...] = term_ref[:, pl.ds(place(0), width)] + g_refs[0][...].astype(F32)
    if not last:
        outs[0][...] = gain_sum
        for head in range(group):
            outs[1][head] = diag[head]
        return
    small_ref = outs[0]
    copies, lines = small_ref.shape[0], small_ref.shape[2]
    offsets = 2 * frames - 1
    span = offsets * BAND
    gain_rows = width // LANES
    per_row = LANES // offsets
    lane = lax.broadcasted_iota(jnp.int32, (span, LANES), 1)
    offset = lax.broadcasted_iota(jnp.int32, (span, LANES), 0) // BAND
    packed_rows = []
    for first in range(0, group, per_row):
        packed = jnp.zeros((1, LANES), F32)
        for head in range(first, min(first + per_row, group)):
            row = jnp.zeros((1, span), F32)
            for i in range(frames):
                row = row + jnp.pad(diag[head][i:i + 1], ((0, 0), ((frames - 1 - i) * BAND, i * BAND)))
            put = (lane == offset + (head - first) * offsets).astype(F32)
            packed = packed + lax.dot_general(
                row, put, NN, precision=lax.Precision.HIGHEST, preferred_element_type=F32
            )
        packed_rows.append(packed)
    filler = [jnp.zeros((1, LANES), F32)] * (lines - gain_rows - len(packed_rows))
    for t in range(tm):
        block = [gain_sum[:, t * width + r * LANES:t * width + (r + 1) * LANES] for r in range(gain_rows)]
        block += [jnp.where(me == t, row, 0.0) for row in packed_rows] + filler
        block = jnp.concatenate(block, axis=0)
        for c in range(copies):
            small_ref[c, t] = block


def finish_kernel(bands, frames, *refs):
    own_refs, in_refs, out_ref = refs[:bands], refs[bands:-1], refs[-1]
    each = len(in_refs) // bands
    parts = []
    for band in range(bands):
        value = own_refs[band][...]
        for ref in in_refs[band * each:(band + 1) * each]:
            value = value + ref[...].astype(F32)
        parts.append(value.reshape(frames, 1, BAND, value.shape[-1]))
    value = jnp.concatenate(parts, axis=1)
    out_ref[...] = value.reshape(out_ref.shape).astype(out_ref.dtype)


def sums_kernel(gain_rows, bias_rows, *refs):
    *block_refs, gain_ref, bias_ref = refs
    total = block_refs[0][...]
    for ref in block_refs[1:]:
        total = total + ref[...]
    for r in range(gain_rows):
        gain_ref[:, r * LANES:(r + 1) * LANES] = total[r:r + 1]
    group, offsets = bias_ref.shape
    per_row = LANES // offsets
    for head in range(group):
        line, start = gain_rows + head // per_row, head % per_row * offsets
        bias_ref[head:head + 1, :] = total[line:line + 1, start:start + offsets]


def shifted(value, axis, step):
    count = lax.axis_size(axis)
    return lax.ppermute(value, axis, [((i + step) % count, i) for i in range(count)])


def per_device(inputs, out_grad, norm_gain, pos_bias, w_query, w_key, w_value, w_out):
    clips, frames, pixels, width = inputs.shape
    group = pos_bias.shape[0]
    tm = lax.axis_size("tm")
    me = lax.axis_index("tm")
    chans = width * tm
    head_dim = width // group
    total = frames * pixels
    bands = pixels // BAND
    rows = frames * BAND
    offsets = 2 * frames - 1
    per_row = LANES // offsets
    gain_rows, bias_rows = width // LANES, -(-group // per_row)
    lines = -(-(gain_rows + bias_rows) // BAND) * BAND
    dims = (tm, frames, pixels, width, group, head_dim, 1e-06)
    x0 = inputs.reshape(total, width)
    g_bands = [out_grad[:, :, n * BAND:(n + 1) * BAND].reshape(rows, width) for n in range(bands)]
    x_parts = [x0] + [shifted(x0, "tm", k) for k in range(1, tm)]
    g_parts = [[g] + [shifted(g, "tm", k) for k in range(1, tm)] for g in g_bands]
    me1 = me.astype(jnp.int32).reshape(1)
    gain = norm_gain.reshape(1, chans)
    spread = jnp.broadcast_to(pos_bias[:, :, None], (*pos_bias.shape, BAND)).reshape(group, -1)
    smem, vmem = pl.BlockSpec(memory_space=pltpu.SMEM), pl.BlockSpec(memory_space=pltpu.VMEM)
    params = pltpu.CompilerParams(vmem_limit_bytes=VMEM_LIMIT)
    held = [x0, w_query, w_key, w_value, w_out, gain]
    held = [pltpu.with_memory_space_constraint(h, pltpu.HBM) for h in held]
    rel, x0, *weights, gain = pl.pallas_call(
        functools.partial(stage_kernel, len(held), frames),
        in_specs=[vmem] + [pl.BlockSpec(memory_space=pltpu.HBM)] * len(held),
        out_specs=[vmem] * (1 + len(held)),
        out_shape=[jax.ShapeDtypeStruct((frames, group, rows), F32)]
        + [jax.ShapeDtypeStruct(h.shape, h.dtype) for h in held],
        scratch_shapes=[pltpu.SemaphoreType.DMA((len(held),))],
        compiler_params=params,
        cost_estimate=pl.CostEstimate(flops=0, bytes_accessed=8_000_000, transcendentals=0),
        name="stage",
    )(spread, *held)
    x_parts[0] = x0
    half = jax.ShapeDtypeStruct((bands, rows, width), BF16)
    share = jax.ShapeDtypeStruct((total, width), BF16)
    q, k, v, probs, xb, inv, mix_own, *mix_out = pl.pallas_call(
        functools.partial(forward_kernel, dims),
        in_specs=[smem] + [vmem] * (tm + 6),
        out_specs=[vmem] * (7 + tm - 1),
        out_shape=[
            half, half, half,
            jax.ShapeDtypeStruct((bands, group, rows, rows), BF16),
            jax.ShapeDtypeStruct((bands, rows, chans), BF16),
            jax.ShapeDtypeStruct((bands, rows, LANES), F32),
            jax.ShapeDtypeStruct((total, width), F32),
        ] + [share] * (tm - 1),
        scratch_shapes=[
            pltpu.VMEM((total, chans), BF16),
            pltpu.VMEM((frames, bands, BAND, chans), F32),
        ],
        compiler_params=params,
        cost_estimate=pl.CostEstimate(flops=4_000_000_000, bytes_accessed=8_000_000, transcendentals=0),
        name="attend",
    )(me1, *x_parts, gain, rel, *weights)
    mix_in = [shifted(mix_out[k - 1], "tm", k) for k in range(1, tm)]

    others = lax.axis_size(("dp", "space"))
    copies = others if others <= 64 else 1
    owns, ins, carry = [], [], []
    for band in range(bands):
        last = band == bands - 1
        if last:
            extra = [jax.ShapeDtypeStruct((copies, tm, lines, LANES), F32)]
        else:
            extra = [jax.ShapeDtypeStruct((1, chans), F32), jax.ShapeDtypeStruct((group, frames, rows), F32)]
        own, *rest = pl.pallas_call(
            functools.partial(backward_kernel, dims, band, last),
            in_specs=[smem] + [vmem] * (tm + 11 + len(carry)),
            out_specs=[vmem] * (tm + len(extra)),
            out_shape=[jax.ShapeDtypeStruct((rows, width), F32)]
            + [jax.ShapeDtypeStruct((rows, width), BF16)] * (tm - 1) + extra,
            scratch_shapes=[pltpu.VMEM((rows, chans), BF16), pltpu.VMEM((rows, chans), F32)],
            compiler_params=params,
            cost_estimate=pl.CostEstimate(flops=4_000_000_000, bytes_accessed=4_000_000, transcendentals=0),
            name="attend_back",
        )(me1, *g_parts[band], gain, q, k, v, probs, xb, inv, *weights, *carry)
        sent, carry = rest[:tm - 1], rest[tm - 1:]
        if last:
            sent, mix_in = lax.optimization_barrier((sent, mix_in))
        owns.append(own)
        ins += [shifted(sent[k - 1], "tm", k) for k in range(1, tm)]

    small = carry[0]
    if copies < others:
        small = jnp.broadcast_to(small, (others, *small.shape[1:]))
    small = lax.all_to_all(small.reshape(-1, LANES), ("dp", "space"), split_axis=0, concat_axis=0, tiled=True)
    small = jnp.sum(small.reshape(others, tm, lines, LANES), axis=0)
    blocks = [lax.dynamic_index_in_dim(small, me, 0, keepdims=False)]
    for k in range(1, tm):
        theirs = lax.dynamic_index_in_dim(small, (me + tm - k) % tm, 0, keepdims=False)
        blocks.append(shifted(theirs, "tm", k))
    gain_grad, bias_grad = pl.pallas_call(
        functools.partial(sums_kernel, gain_rows, bias_rows),
        in_specs=[vmem] * tm,
        out_specs=[vmem] * 2,
        out_shape=[jax.ShapeDtypeStruct((1, width), F32), jax.ShapeDtypeStruct((group, offsets), F32)],
        name="sums",
    )(*blocks)
    input_grad = pl.pallas_call(
        functools.partial(finish_kernel, bands, frames),
        in_specs=[vmem] * (bands * tm),
        out_specs=vmem,
        out_shape=jax.ShapeDtypeStruct((total, width), BF16),
        compiler_params=params,
        name="finish",
    )(*owns, *ins)
    mixed = mix_own
    for part in mix_in:
        mixed = mixed + part.astype(F32)
    return (
        mixed.astype(BF16).reshape(inputs.shape),
        input_grad.reshape(inputs.shape),
        gain_grad.reshape(width),
        bias_grad,
    )


def solution(mesh):
    return jax.shard_map(
        per_device,
        mesh=mesh,
        in_specs=(
            P("dp", None, "space", "tm"),
            P("dp", None, "space", "tm"),
            P(),
            P("tm", None),
            P(None, "tm"),
            P(None, "tm"),
            P(None, "tm"),
            P("tm", None),
        ),
        out_specs=(
            P("dp", None, "space", "tm"),
            P("dp", None, "space", "tm"),
            P("tm"),
            P("tm", None),
        ),
        check_vma=False,
    )
```

time: 52.1 us -> 51 us (0.979)
  local copies, waits for them, and re-layouts: 10.4 us -> 3.09 us
  starting transfers between devices: 11.3 us -> 16.7 us
  Pallas kernels: 11.6 us -> 16.6 us
  waiting for transfers between devices: 16.1 us -> 12.8 us
  other arithmetic: 1.67 us -> 0.83 us
    unnamed x14 -> x2, local copies, waits for them, and re-layouts: 7.52 us -> 0.59 us
    ppermute x4 -> x7, starting transfers between devices: 5.2 us -> 10.3 us  [shifted(): lax.ppermute(value, axis, [((i + step) % count, i) for i in range(count)])]
    ppermute x4 -> x7, waiting for transfers between devices: 10.5 us -> 7.02 us  [shifted(): lax.ppermute(value, axis, [((i + step) % count, i) for i in range(count)])]
    pallas_call x1 -> x4, Pallas kernels: 7.17 us -> 10.5 us  [the longest x2 8.34 us: per_device(): pl.pallas_call(functools.partial(backward_kernel, dims, band, last), in_s...]
    pallas_call x1, Pallas kernels: 0.67 us -> 2.35 us  [per_device(): pl.pallas_call(functools.partial(stage_kernel, len(held), frames), in_spe...]
    convert_element_type x2 -> x1, other arithmetic: 1.63 us -> 0.82 us  [per_device(): mixed.astype(BF16).reshape(inputs.shape)]
    broadcast_in_dim x1 -> x0, local copies, waits for them, and re-layouts: 0.68 us -> none  [per_device(): jnp.broadcast_to(small[None], (others, tm, lines, LANES)).reshape(-1, LANES)]
    squeeze x0 -> x1, local copies, waits for them, and re-layouts: none -> 0.6 us  [per_device(): lax.dynamic_index_in_dim(small, (me + tm - k) % tm, 0, keepdims=False)]
  transfers between devices with their start and end apart: 5 -> 8, of which waited for: 4 -> 4; matrix products, arithmetic and copies ran while one was open for 6% -> 7% of each run, Pallas kernels for 9% -> 22%
where the time goes in v4:
time: 51 us; the launch traced here: 50.7 us
  starting transfers between devices  16.7 us (33%)
  Pallas kernels  16.6 us (33%)
  waiting for transfers between devices  12.8 us (25%)
  local copies, waits for them, and re-layouts  3.09 us (6%)
  other arithmetic  0.83 us (2%)
  between operations  0.71 us (1%)
    ppermute x7, starting transfers between devices, shifted(): lax.ppermute(value, axis, [((i + step) % count, i) for i in range(count)])  10.3 us
    pallas_call x2, Pallas kernels, per_device(): pl.pallas_call(functools.partial(backward_kernel, dims, band, last), in_s...  8.34 us
    ppermute x7, waiting for transfers between devices, shifted(): lax.ppermute(value, axis, [((i + step) % count, i) for i in range(count)])  7.02 us
    all_to_all x1, starting transfers between devices, per_device(): lax.all_to_all(small.reshape(-1, LANES), ('dp', 'space'), split_axis=0, c...  6.43 us
    all_to_all x1, waiting for transfers between devices, per_device(): lax.all_to_all(small.reshape(-1, LANES), ('dp', 'space'), split_axis=0, c...  5.76 us
    pallas_call x1, Pallas kernels, per_device(): pl.pallas_call(functools.partial(forward_kernel, dims), in_specs=[smem] +...  3.71 us
    pallas_call x1, Pallas kernels, per_device(): pl.pallas_call(functools.partial(stage_kernel, len(held), frames), in_spe...  2.35 us
    pallas_call x1, Pallas kernels, per_device(): pl.pallas_call(functools.partial(sums_kernel, gain_rows, bias_rows), in_s...  1.37 us
  transfers between devices with their start and end apart: 8, of which 4 were waited for; matrix products, arithmetic and copies ran while one was open for 7% of the time, Pallas kernels for 22%

profile of v4, /device:TPU:0, one launch (start us, length us, event | category | flops | bytes accessed | tf_op | source)
XLA Modules:
  0.0 50.7 jit_solution(12771862405746400901)
XLA Ops:
  0.6 3.0 %collective-permute-start = (bf16[320,512]{1,0:T(8,128)(2,1)}, bf16[320,512]{1,0:T(8,128)(2,1)S(1)}, u32[]{:S(2)}, u32[]{:S(2)}) collective-permute-start(bf16[320,512]{1,0:T(8,128)(2,1)} %bitcast.16), channel_id=1, source_target_pairs={{1,0},{0,1},{3,2},{2,3},{5,4},{4,5},{7,6},{6,7},{9,8},{8,9},{11,10... | collective-permute-start | bytes 983048 | tf_op jit(solution)/shard_map/ppermute | solution.py:241
  3.7 1.0 %slice_bitcast_fusion = (bf16[160,512]{1,0:T(8,128)(2,1)S(1)}, bf16[160,512]{1,0:T(8,128)(2,1)S(1)}) fusion(bf16[1,20,16,512]{3,2,1,0:T(8,128)(2,1)} %param.9), kind=kLoop, calls=%fused_computation.1 | loop fusion | bytes 655360 | tf_op jit(solution)/shard_map/reshape | solution.py:260
  4.7 0.1 collective-permute-start.2
  4.8 2.0 %collective-permute-start.1 = (bf16[160,512]{1,0:T(8,128)(2,1)S(1)}, bf16[160,512]{1,0:T(8,128)(2,1)S(1)}, u32[]{:S(2)}, u32[]{:S(2)}) collective-permute-start(bf16[160,512]{1,0:T(8,128)(2,1)S(1)} %get-tuple-element.57.refs_0_), channel_id=1, source_target_pairs={{1,0},{0,1},{3,2},{2,3},{5,4},{4,5},{7,6},{6,7},{9,8},{8,9},{11,10... | collective-permute-start | bytes 491528 | tf_op jit(solution)/shard_map/ppermute | solution.py:241
  6.8 0.8 %broadcast_in_dim.2 = f32[8,39,8]{2,1,0:T(8,128)S(1)} broadcast(f32[8,39]{1,0:T(8,128)} %param.11), dimensions={0,1} | broadcast | bytes 11232 | tf_op jit(solution)/shard_map/broadcast_in_dim | solution.py:265
  7.6 0.1 reshape.44.bias_ref
  7.7 2.4 %stage.1 = (f32[20,8,160]{2,1,0:T(8,128)S(1)}, bf16[320,512]{1,0:T(8,128)(2,1)S(1)}, bf16[1024,512]{1,0:T(8,128)(2,1)S(1)}, bf16[1024,512]{1,0:T(8,128)(2,1)S(1)...) custom-call(f32[8,312]{1,0:T(8,128)S(1)} %reshape.44.bias_ref, ...), custom_call_target="tpu_custom_call" | custom-call | bytes 8000000 | tf_op jit(solution)/shard_map/stage/pallas_call | solution.py:270
  10.0 2.4 %collective-permute-done.refs_1_ = bf16[320,512]{1,0:T(8,128)(2,1)S(1)} collective-permute-done((bf16[320,512]{1,0:T(8,128)(2,1)}, bf16[320,512]{1,0:T(8,128)(2,1)S(1)}, u32[]{:S(2)}, u32[]{:S(2)}) %collective-permute-start) | collective-permute-done | bytes 327712 | tf_op jit(solution)/shard_map/ppermute | solution.py:241
  12.4 3.7 %attend.1 = (bf16[2,160,512]{2,1,0:T(8,128)(2,1)S(1)}, bf16[2,160,512]{2,1,0:T(8,128)(2,1)S(1)}, bf16[2,160,512]{2,1,0:T(8,128)(2,1)S(1)}, bf16[2,8,160,160]{3,2...) custom-call(s32[1]{0:T(128)} %bitcast.me_ref, ...), custom_call_target="tpu_custom_call" | custom-call | flops 4000000000 | bytes 8000000 | tf_op jit(solution)/shard_map/attend/pallas_call | solution.py:284
  16.1 3.7 %attend_back.2 = (f32[160,512]{1,0:T(8,128)S(1)}, bf16[160,512]{1,0:T(8,128)(2,1)S(1)}, f32[1,1024]{1,0:T(1,128)S(1)}, f32[8,20,160]{2,1,0:T(8,128)S(1)}) custom-call(s32[1]{0:T(128)} %bitcast.me_ref, bf16[160,512]{1,0:T(8,128)(2,1)S(1)} %get-tuple-element.56.refs_0_, bf16[160,512]{1,0:T(8,128)(2,1)S(1)} %collective-permute-done.2.refs_1_, ...), custom_call_target="tpu_custom_call" | custom-call | flops 4000000000 | bytes 4000000 | tf_op jit(solution)/shard_map/attend_back/pallas_call | solution.py:314
  19.8 4.7 %attend_back.3 = (f32[160,512]{1,0:T(8,128)S(1)}, bf16[160,512]{1,0:T(8,128)(2,1)S(1)}, f32[16,2,8,128]{3,2,1,0:T(8,128)}) custom-call(s32[1]{0:T(128)} %bitcast.me_ref, bf16[160,512]{1,0:T(8,128)(2,1)S(1)} %get-tuple-element.57.refs_0_, bf16[160,512]{1,0:T(8,128)(2,1)S(1)} %collective-permute-done.1.refs_1_, f32[1,1024]{1,0:T(1,128)S(1)} %get-tuple-element.31.refs_2_, ...), custom_call_target="tpu_custom_call" | custom-call | flops 4000000000 | bytes 4000000 | tf_op jit(solution)/shard_map/attend_back/pallas_call | solution.py:314
  24.5 6.4 %all-to-all-start = ((f32[16,16,128]{2,1,0:T(8,128)}), f32[16,16,128]{2,1,0:T(8,128)S(1)}, u32[]{:S(2)}, u32[]{:S(2)}) async-start(f32[16,16,128]{2,1,0:T(8,128)} %bitcast.7), calls=%async_computation | async-start | bytes 262144 | tf_op jit(solution)/shard_map/all_to_all | solution.py:334
  30.9 1.6 %collective-permute-start.3 = (bf16[320,512]{1,0:T(8,128)(2,1)S(1)}, bf16[320,512]{1,0:T(8,128)(2,1)S(1)}, u32[]{:S(2)}, u32[]{:S(2)}) collective-permute-start(bf16[320,512]{1,0:T(8,128)(2,1)S(1)} %get-tuple-element.47), channel_id=1, source_target_pairs={{1,0},{0,1},{3,2},{2,3},{5,4},{4,5},{7,6},{6,7},{9,8},{8,9},{11,10... | collective-permute-start | bytes 983048 | tf_op jit(solution)/shard_map/ppermute | solution.py:241
  32.5 5.8 %all-to-all-done = f32[16,16,128]{2,1,0:T(8,128)S(1)} async-done(((f32[16,16,128]{2,1,0:T(8,128)}), f32[16,16,128]{2,1,0:T(8,128)S(1)}, u32[]{:S(2)}, u32[]{:S(2)}) %all-to-all-start) | async-done | bytes 131104 | tf_op jit(solution)/shard_map/all_to_all | solution.py:334
  38.3 0.6 %dynamic-slice_bitcast_fusion = (f32[8,128]{1,0:T(8,128)S(1)}, f32[8,128]{1,0:T(8,128)}) fusion(f32[2,8,128]{2,1,0:T(8,128)S(1)} %bitcast.20, s32[]{:T(128)S(6)} %select_n.16, s32[]{:T(128)S(6)} %select_n.14), kind=kLoop, calls=%fused_computation.3 | loop fusion | bytes 16392 | tf_op jit(solution)/shard_map/jit(dynamic_index_in_dim)/squeeze | solution.py:338
  38.9 1.5 %collective-permute-start.6 = (f32[8,128]{1,0:T(8,128)S(1)}, f32[8,128]{1,0:T(8,128)S(1)}, u32[]{:S(2)}, u32[]{:S(2)}) collective-permute-start(f32[8,128]{1,0:T(8,128)S(1)} %get-tuple-element.58), channel_id=1, source_target_pairs={{1,0},{0,1},{3,2},{2,3},{5,4},{4,5},{7,6},{6,7},{9,8},{8,9},{11,10... | collective-permute-start | bytes 12296 | tf_op jit(solution)/shard_map/ppermute | solution.py:241
  40.4 0.5 collective-permute-start.4
  40.9 1.6 %collective-permute-done.6.refs_1_ = f32[8,128]{1,0:T(8,128)S(1)} collective-permute-done((f32[8,128]{1,0:T(8,128)S(1)}, f32[8,128]{1,0:T(8,128)S(1)}, u32[]{:S(2)}, u32[]{:S(2)}) %collective-permute-start.6) | collective-permute-done | bytes 4128 | tf_op jit(solution)/shard_map/ppermute | solution.py:241
  42.5 0.6 %copy-done = f32[8,128]{1,0:T(8,128)} copy-done((f32[8,128]{1,0:T(8,128)}, f32[8,128]{1,0:T(8,128)S(1)}, u32[]{:S(2)}) %copy-start) | copy-done | bytes 4120
  43.1 1.4 %sums.1 = (f32[1,512]{1,0:T(1,128)}, f32[8,39]{1,0:T(8,128)}) custom-call(f32[8,128]{1,0:T(8,128)} %get-tuple-element.59.refs_0_, f32[8,128]{1,0:T(8,128)} %copy-done), custom_call_target="tpu_custom_call" | custom-call | tf_op jit(solution)/shard_map/sums/pallas_call | solution.py:340
  44.5 1.5 %collective-permute-start.5 = (bf16[160,512]{1,0:T(8,128)(2,1)S(1)}, bf16[160,512]{1,0:T(8,128)(2,1)S(1)}, u32[]{:S(2)}, u32[]{:S(2)}) collective-permute-start(bf16[160,512]{1,0:T(8,128)(2,1)S(1)} %get-tuple-element.52), channel_id=1, source_target_pairs={{1,0},{0,1},{3,2},{2,3},{5,4},{4,5},{7,6},{6,7},{9,8},{8,9},{11,10... | collective-permute-start | bytes 491528 | tf_op jit(solution)/shard_map/ppermute | solution.py:241
  46.0 0.8 %add_convert_fusion = bf16[320,512]{1,0:T(8,128)(2,1)} fusion(f32[320,512]{1,0:T(8,128)S(1)} %get-tuple-element.37, bf16[320,512]{1,0:T(8,128)(2,1)S(1)} %collective-permute-done.3), kind=kLoop, calls=%fused_computation | loop fusion | flops 491520 | bytes 1310720 | tf_op jit(solution)/shard_map/convert_element_type | solution.py:359
  46.8 3.1 %collective-permute-done.5.refs_3_ = bf16[160,512]{1,0:T(8,128)(2,1)S(1)} collective-permute-done((bf16[160,512]{1,0:T(8,128)(2,1)S(1)}, bf16[160,512]{1,0:T(8,128)(2,1)S(1)}, u32[]{:S(2)}, u32[]{:S(2)}) %collective-permute-start.5) | collective-permute-done | bytes 163872 | tf_op jit(solution)/shard_map/ppermute | solution.py:241
  49.9 0.8 %finish.1 = bf16[320,512]{1,0:T(8,128)(2,1)} custom-call(f32[160,512]{1,0:T(8,128)S(1)} %get-tuple-element.49.refs_0_, f32[160,512]{1,0:T(8,128)S(1)} %get-tuple-element.50.refs_1_, bf16[160,512]{1,0:T(8,128)(2,1)S(1)} %collective-permute-done.4.refs_2_, bf16[160,512]{1,0:T(8,128)(2,1)S(1)} %collective-permute-done.5.refs_3_), custom_call_target="tpu_custom_call" | custom-call | tf_op jit(solution)/shard_map/finish/pallas_call | solution.py:347
  (6 shorter events, 0.0 us)
Async XLA Ops:
  0.6 11.8 %collective-permute-start = (bf16[320,512]{1,0:T(8,128)(2,1)}, bf16[320,512]{1,0:T(8,128)(2,1)S(1)}, u32[]{:S(2)}, u32[]{:S(2)}) collective-permute-start(bf16[320,512]{1,0:T(8,128)(2,1)} %bitcast.16), channel_id=1, source_target_pairs={{1,0},{0,1},{3,2},{2,3},{5,4},{4,5},{7,6},{6,7},{9,8},{8,9},{11,10... | collective-permute-start | bytes 983048 | tf_op jit(solution)/shard_map/ppermute | solution.py:241
  4.7 11.5 %collective-permute-start.2 = (bf16[160,512]{1,0:T(8,128)(2,1)S(1)}, bf16[160,512]{1,0:T(8,128)(2,1)S(1)}, u32[]{:S(2)}, u32[]{:S(2)}) collective-permute-start(bf16[160,512]{1,0:T(8,128)(2,1)S(1)} %get-tuple-element.56.refs_0_), channel_id=1, source_target_pairs={{1,0},{0,1},{3,2},{2,3},{5,4},{4,5},{7,6},{6,7},{9,8},{8,9},{11,10... | collective-permute-start | bytes 491528 | tf_op jit(solution)/shard_map/ppermute | solution.py:241
  4.8 15.1 %collective-permute-start.1 = (bf16[160,512]{1,0:T(8,128)(2,1)S(1)}, bf16[160,512]{1,0:T(8,128)(2,1)S(1)}, u32[]{:S(2)}, u32[]{:S(2)}) collective-permute-start(bf16[160,512]{1,0:T(8,128)(2,1)S(1)} %get-tuple-element.57.refs_0_), channel_id=1, source_target_pairs={{1,0},{0,1},{3,2},{2,3},{5,4},{4,5},{7,6},{6,7},{9,8},{8,9},{11,10... | collective-permute-start | bytes 491528 | tf_op jit(solution)/shard_map/ppermute | solution.py:241
  24.5 13.8 %all-to-all-start = ((f32[16,16,128]{2,1,0:T(8,128)}), f32[16,16,128]{2,1,0:T(8,128)S(1)}, u32[]{:S(2)}, u32[]{:S(2)}) async-start(f32[16,16,128]{2,1,0:T(8,128)} %bitcast.7), calls=%async_computation | async-start | bytes 262144 | tf_op jit(solution)/shard_map/all_to_all | solution.py:334
  30.9 13.6 %collective-permute-start.3 = (bf16[320,512]{1,0:T(8,128)(2,1)S(1)}, bf16[320,512]{1,0:T(8,128)(2,1)S(1)}, u32[]{:S(2)}, u32[]{:S(2)}) collective-permute-start(bf16[320,512]{1,0:T(8,128)(2,1)S(1)} %get-tuple-element.47), channel_id=1, source_target_pairs={{1,0},{0,1},{3,2},{2,3},{5,4},{4,5},{7,6},{6,7},{9,8},{8,9},{11,10... | collective-permute-start | bytes 983048 | tf_op jit(solution)/shard_map/ppermute | solution.py:241
  38.9 3.6 %collective-permute-start.6 = (f32[8,128]{1,0:T(8,128)S(1)}, f32[8,128]{1,0:T(8,128)S(1)}, u32[]{:S(2)}, u32[]{:S(2)}) collective-permute-start(f32[8,128]{1,0:T(8,128)S(1)} %get-tuple-element.58), channel_id=1, source_target_pairs={{1,0},{0,1},{3,2},{2,3},{5,4},{4,5},{7,6},{6,7},{9,8},{8,9},{11,10... | collective-permute-start | bytes 12296 | tf_op jit(solution)/shard_map/ppermute | solution.py:241
  40.4 6.4 %collective-permute-start.4 = (bf16[160,512]{1,0:T(8,128)(2,1)S(1)}, bf16[160,512]{1,0:T(8,128)(2,1)S(1)}, u32[]{:S(2)}, u32[]{:S(2)}) collective-permute-start(bf16[160,512]{1,0:T(8,128)(2,1)S(1)} %get-tuple-element.51), channel_id=1, source_target_pairs={{1,0},{0,1},{3,2},{2,3},{5,4},{4,5},{7,6},{6,7},{9,8},{8,9},{11,10... | collective-permute-start | bytes 491528 | tf_op jit(solution)/shard_map/ppermute | solution.py:241
  42.5 0.6 %copy-start = (f32[8,128]{1,0:T(8,128)}, f32[8,128]{1,0:T(8,128)S(1)}, u32[]{:S(2)}) copy-start(f32[8,128]{1,0:T(8,128)S(1)} %collective-permute-done.6.refs_1_) | copy-start | bytes 12292
  44.5 5.4 %collective-permute-start.5 = (bf16[160,512]{1,0:T(8,128)(2,1)S(1)}, bf16[160,512]{1,0:T(8,128)(2,1)S(1)}, u32[]{:S(2)}, u32[]{:S(2)}) collective-permute-start(bf16[160,512]{1,0:T(8,128)(2,1)S(1)} %get-tuple-element.52), channel_id=1, source_target_pairs={{1,0},{0,1},{3,2},{2,3},{5,4},{4,5},{7,6},{6,7},{9,8},{8,9},{11,10... | collective-permute-start | bytes 491528 | tf_op jit(solution)/shard_map/ppermute | solution.py:241

commit v5 on v4

v5 whole, which is shorter than its diff:
```python
import functools

import jax
import jax.numpy as jnp
from jax import lax
from jax.experimental import pallas as pl
from jax.experimental.pallas import tpu as pltpu
from jax.sharding import PartitionSpec as P

CHUNK = 4
BAND = 8
LANES = 128
FAR = -1e30
F32, BF16 = jnp.float32, jnp.bfloat16
NT = (((1,), (1,)), ((), ()))
NN = (((1,), (0,)), ((), ()))
TN = (((0,), (0,)), ((), ()))
VMEM_LIMIT = 24 * 1024 * 1024


def mm(a, b, dims=NN):
    return lax.dot_general(a, b, dims, preferred_element_type=F32)


def same_pixel(rows):
    row = lax.broadcasted_iota(jnp.int32, (BAND, rows), 0)
    lane = lax.broadcasted_iota(jnp.int32, (BAND, rows), 1)
    return (lane & (BAND - 1)) == row


def head_lanes(head_dim, rows):
    return lax.broadcasted_iota(jnp.int32, (rows, LANES), 1) // head_dim


def stack_heads(pair, owner, per_pair, factor=None):
    pair = pair if factor is None else pair * jnp.asarray(factor, pair.dtype)
    return jnp.concatenate([jnp.where(owner == h, pair, jnp.zeros_like(pair)) for h in range(per_pair)], 0)


def pick_heads(parts, owner):
    out = parts[0]
    for h in range(1, len(parts)):
        out = jnp.where(owner == h, parts[h], out)
    return out


def stage_kernel(frames, width, bias_ref, x_ref, wq_ref, wk_ref, wv_ref, wo_ref, gain_ref,
                 rel_ref, x_out, proj_out, wo_out, gain_out, sems):
    pairs = [(x_ref, x_out), (wo_ref, wo_out), (gain_ref, gain_out)]
    pairs += [(w, proj_out.at[:, n * width:(n + 1) * width]) for n, w in enumerate((wq_ref, wk_ref, wv_ref))]
    copies = [pltpu.make_async_copy(source, target, sems.at[n]) for n, (source, target) in enumerate(pairs)]
    for copy in copies:
        copy.start()
    rows = rel_ref.shape[2]
    for i in range(frames):
        start = (frames - 1 - i) * BAND
        rel_ref[i] = bias_ref[:, start:start + rows]
    for copy in copies:
        copy.wait()


def forward_kernel(dims, me_ref, *refs):
    tm, frames, pixels, width, group, head_dim, eps = dims
    x_refs = refs[:tm]
    gain_ref, rel_ref, proj_ref, wo_ref = refs[tm:tm + 4]
    qkv_ref, p_ref, xb_ref, inv_ref, own_ref = refs[tm + 4:tm + 9]
    msg_refs = refs[tm + 9:tm + 9 + tm - 1]
    xw_ref, normed_ref = refs[tm + 9 + tm - 1:]
    me = me_ref[0]
    rows = frames * BAND
    bands = pixels // BAND
    per_pair = LANES // head_dim
    scale = head_dim ** -0.5

    def place(k):
        return pl.multiple_of(lax.rem(me + k, tm) * width, width)

    for k in range(tm):
        xw_ref[:, pl.ds(place(k), width)] = x_refs[k][...]
    for f in range(0, frames, 2):
        both = xw_ref[f * pixels:(f + 2) * pixels, :].astype(F32).reshape(2, bands, BAND, -1)
        for band in range(bands):
            x = both[:, band].reshape(2 * BAND, -1)
            inv = lax.rsqrt(jnp.mean(x * x, axis=-1, keepdims=True) + eps)
            at = slice(f * BAND, (f + 2) * BAND)
            normed_ref[band, at, :] = (x * inv * gain_ref[...]).astype(BF16)
            xb_ref[band, at, :] = x.astype(BF16)
            inv_ref[band, at, :] = jnp.broadcast_to(inv, (2 * BAND, LANES))
    same = same_pixel(rows)[None]
    owner = head_lanes(head_dim, rows)
    for band in range(bands):
        qkv_ref[band] = mm(normed_ref[band], proj_ref[...]).astype(BF16)
        att = []
        for pair in range(width // LANES):
            qp, kp, vp = (
                qkv_ref[band, :, n * width + pair * LANES:n * width + (pair + 1) * LANES] for n in range(3)
            )
            scores = mm(stack_heads(qp, owner, per_pair, scale), kp, NT)
            outs = []
            for h in range(per_pair):
                head = pair * per_pair + h
                for f in range(0, frames, CHUNK):
                    at = slice(f * BAND, (f + CHUNK) * BAND)
                    s = scores[h * rows + f * BAND:h * rows + (f + CHUNK) * BAND].reshape(CHUNK, BAND, rows)
                    s = jnp.where(same, s + rel_ref[f:f + CHUNK, head:head + 1, :], FAR)
                    s = s.reshape(CHUNK * BAND, rows)
                    e = jnp.exp(s - jnp.max(s, axis=-1, keepdims=True))
                    p_ref[band, head, at, :] = (e * (1.0 / jnp.sum(e, axis=-1, keepdims=True))).astype(BF16)
                outs.append(mm(p_ref[band, head], vp))
            att.append(pick_heads(outs, owner).astype(BF16))
        att = jnp.concatenate(att, axis=1)
        for k in range(1, tm):
            msg_refs[k - 1][band] = mm(att, wo_ref[:, pl.ds(place(tm - k), width)]).astype(BF16)
        own_ref[band] = mm(att, wo_ref[:, pl.ds(place(0), width)]) + xb_ref[band, :, pl.ds(place(0), width)].astype(F32)


def backward_kernel(dims, band, last, me_ref, *refs):
    tm, frames, pixels, width, group, head_dim, eps = dims
    g_refs = refs[:tm]
    gain_ref, qkv_ref, p_ref, xb_ref, inv_ref, proj_ref, wo_ref = refs[tm:tm + 7]
    rest = list(refs[tm + 7:])
    carried = (rest.pop(0), rest.pop(0)) if band else None
    own_ref = rest.pop(0)
    msg_refs = [rest.pop(0) for _ in range(tm - 1)]
    small_ref = rest.pop(0) if last else None
    gain_out = None if last else rest.pop(0)
    diag_ref = rest.pop() if last else rest.pop(0)
    gw_ref, ds_ref, grad_ref = rest
    me = me_ref[0]
    rows = frames * BAND
    per_pair = LANES // head_dim
    scale = head_dim ** -0.5
    chans = width * tm

    def place(k):
        return pl.multiple_of(lax.rem(me + k, tm) * width, width)

    for k in range(tm):
        gw_ref[:, pl.ds(place(k), width)] = g_refs[k][...]
    owner = head_lanes(head_dim, rows)
    d_att = mm(gw_ref[...], wo_ref[...], NT).astype(BF16)
    grads = [[], [], []]
    for pair in range(width // LANES):
        qp, kp, vp = (
            qkv_ref[band, :, n * width + pair * LANES:n * width + (pair + 1) * LANES] for n in range(3)
        )
        da = d_att[:, pair * LANES:(pair + 1) * LANES]
        d_prob = mm(stack_heads(da, owner, per_pair), vp, NT)
        parts = [[], [], []]
        for h in range(per_pair):
            head = pair * per_pair + h
            for f in range(0, frames, CHUNK):
                at = slice(f * BAND, (f + CHUNK) * BAND)
                full = p_ref[band, head, at, :].astype(F32)
                t = d_prob[h * rows + f * BAND:h * rows + (f + CHUNK) * BAND]
                score = full * (t - jnp.sum(full * t, axis=-1, keepdims=True))
                ds_ref[head, at, :] = (score * scale).astype(BF16)
                part = jnp.sum(score.reshape(CHUNK, BAND, rows), axis=1, keepdims=True)
                if carried is not None:
                    part = part + carried[1][f:f + CHUNK, head:head + 1, :]
                diag_ref[f:f + CHUNK, head:head + 1, :] = part
            probs, score = p_ref[band, head], ds_ref[head]
            parts[0].append(mm(score, kp))
            parts[1].append(mm(score, qp, TN))
            parts[2].append(mm(probs, da, TN))
        for n in range(3):
            grads[n].append(pick_heads(parts[n], owner).astype(BF16))
    grad_ref[...] = mm(jnp.concatenate(grads[0] + grads[1] + grads[2], axis=1), proj_ref[...], NT)
    gain_sum = jnp.zeros((BAND, chans), F32)
    for f in range(0, frames, 2):
        at = slice(f * BAND, (f + 2) * BAND)
        grad, x = grad_ref[at, :], xb_ref[band, at, :].astype(F32)
        inv = inv_ref[band, at, :1]
        scaled = x * inv
        gain_sum = gain_sum + jnp.sum((grad * scaled).reshape(2, BAND, chans), axis=0)
        term = grad * gain_ref[...]
        inner = jnp.mean(term * scaled, axis=-1, keepdims=True)
        grad_ref[at, :] = inv * (term - scaled * inner)
    for k in range(1, tm):
        msg_refs[k - 1][...] = grad_ref[:, pl.ds(place(tm - k), width)].astype(BF16)
    own_ref[...] = grad_ref[:, pl.ds(place(0), width)] + g_refs[0][...].astype(F32)
    gain_sum = jnp.sum(gain_sum, axis=0, keepdims=True)
    if carried is not None:
        gain_sum = gain_sum + carried[0][...]
    if not last:
        gain_out[...] = gain_sum
        return
    small_ref[...] = jnp.zeros_like(small_ref)
    for r in range(chans // LANES):
        small_ref[r:r + 1, :LANES] = gain_sum[:, r * LANES:(r + 1) * LANES]
    span = small_ref.shape[1] - LANES
    bias = jnp.zeros((group, span), F32)
    for i in range(frames):
        before = (frames - 1 - i) * BAND
        bias = bias + jnp.pad(diag_ref[i], ((0, 0), (before, span - before - rows)))
    small_ref[:group, LANES:] = bias


def finish_kernel(bands, frames, own_refs, in_refs, out_ref):
    each = len(in_refs) // bands
    parts = []
    for band in range(bands):
        value = own_refs[band][...]
        for ref in in_refs[band * each:(band + 1) * each]:
            value = value + ref[...].astype(F32)
        parts.append(value.reshape(frames, 1, BAND, value.shape[-1]))
    value = jnp.concatenate(parts, axis=1)
    out_ref[...] = value.reshape(out_ref.shape).astype(out_ref.dtype)


def finish_bands(bands, frames, *refs):
    finish_kernel(bands, frames, refs[:bands], refs[bands:-1], refs[-1])


def finish_whole(bands, frames, own_ref, *refs):
    in_refs = [ref.at[band] for band in range(bands) for ref in refs[:-1]]
    finish_kernel(bands, frames, [own_ref.at[band] for band in range(bands)], in_refs, refs[-1])


def bias_kernel(small_ref, out_ref):
    group, offsets = out_ref.shape
    value = small_ref[:group, LANES:]
    lane = lax.broadcasted_iota(jnp.int32, (value.shape[1], offsets), 0) // BAND
    put = (lane == lax.broadcasted_iota(jnp.int32, (value.shape[1], offsets), 1)).astype(F32)
    out_ref[...] = lax.dot_general(value, put, NN, precision=lax.Precision.HIGHEST, preferred_element_type=F32)


def gain_kernel(me_ref, *refs):
    *tile_refs, out_ref, sum_ref = refs
    total = tile_refs[0][...]
    for ref in tile_refs[1:]:
        total = total + ref[...]
    sum_ref[...] = total
    count = out_ref.shape[1] // LANES
    for r in range(count):
        out_ref[:, r * LANES:(r + 1) * LANES] = sum_ref[pl.ds(me_ref[0] * count + r, 1), :]


def shifted(value, axis, step):
    count = lax.axis_size(axis)
    return lax.ppermute(value, axis, [((i + step) % count, i) for i in range(count)])


def group_sum(value, axis, beside=()):
    count = lax.axis_size(axis)
    stride = 1
    while stride < count:
        left = count // stride
        radix = 4 if left % 4 == 0 else 2 if left % 2 == 0 else left
        parts = [value]
        for step in range(1, radix):
            pairs = []
            for i in range(count):
                digit = i // stride % radix
                other = digit ^ step if radix in (2, 4) else (digit + step) % radix
                pairs.append((i + (other - digit) * stride, i))
            parts.append(lax.ppermute(value, axis, pairs))
        parts, beside = lax.optimization_barrier((parts, beside))
        value = sum(parts[1:], parts[0])
        stride *= radix
    return value, beside


def per_device(inputs, out_grad, norm_gain, pos_bias, w_query, w_key, w_value, w_out):
    clips, frames, pixels, width = inputs.shape
    group = pos_bias.shape[0]
    tm = lax.axis_size("tm")
    me = lax.axis_index("tm")
    chans = width * tm
    head_dim = width // group
    total = frames * pixels
    bands = pixels // BAND
    rows = frames * BAND
    offsets = 2 * frames - 1
    span = -(-offsets * BAND // LANES) * LANES
    lines = -(-max(chans // LANES, group) // BAND) * BAND
    dims = (tm, frames, pixels, width, group, head_dim, 1e-06)
    x0 = inputs.reshape(total, width)
    g_bands = [out_grad[:, :, n * BAND:(n + 1) * BAND].reshape(rows, width) for n in range(bands)]
    x_parts = [x0] + [shifted(x0, "tm", k) for k in range(1, tm)]
    g_parts = [[g] + [shifted(g, "tm", k) for k in range(1, tm)] for g in g_bands]
    me1 = me.astype(jnp.int32).reshape(1)
    gain = norm_gain.reshape(1, chans)
    spread = jnp.broadcast_to(pos_bias[:, :, None], (*pos_bias.shape, BAND)).reshape(group, -1)
    smem, vmem = pl.BlockSpec(memory_space=pltpu.SMEM), pl.BlockSpec(memory_space=pltpu.VMEM)
    params = pltpu.CompilerParams(vmem_limit_bytes=VMEM_LIMIT)
    held = [x0, w_query, w_key, w_value, w_out, gain]
    held = [pltpu.with_memory_space_constraint(h, pltpu.HBM) for h in held]
    rel, x0, proj, w_out, gain = pl.pallas_call(
        functools.partial(stage_kernel, frames, width),
        in_specs=[vmem] + [pl.BlockSpec(memory_space=pltpu.HBM)] * len(held),
        out_specs=[vmem] * 5,
        out_shape=[
            jax.ShapeDtypeStruct((frames, group, rows), F32),
            jax.ShapeDtypeStruct((total, width), BF16),
            jax.ShapeDtypeStruct((chans, 3 * width), BF16),
            jax.ShapeDtypeStruct((width, chans), BF16),
            jax.ShapeDtypeStruct((1, chans), F32),
        ],
        scratch_shapes=[pltpu.SemaphoreType.DMA((len(held),))],
        compiler_params=params,
        cost_estimate=pl.CostEstimate(flops=0, bytes_accessed=8_000_000, transcendentals=0),
        name="stage",
    )(spread, *held)
    x_parts[0] = x0
    qkv, probs, xb, inv, mix_own, *mix_out = pl.pallas_call(
        functools.partial(forward_kernel, dims),
        in_specs=[smem] + [vmem] * (tm + 4),
        out_specs=[vmem] * (5 + tm - 1),
        out_shape=[
            jax.ShapeDtypeStruct((bands, rows, 3 * width), BF16),
            jax.ShapeDtypeStruct((bands, group, rows, rows), BF16),
            jax.ShapeDtypeStruct((bands, rows, chans), BF16),
            jax.ShapeDtypeStruct((bands, rows, LANES), F32),
            jax.ShapeDtypeStruct((bands, rows, width), F32),
        ] + [jax.ShapeDtypeStruct((bands, rows, width), BF16)] * (tm - 1),
        scratch_shapes=[pltpu.VMEM((total, chans), BF16), pltpu.VMEM((bands, rows, chans), BF16)],
        compiler_params=params,
        cost_estimate=pl.CostEstimate(flops=4_000_000_000, bytes_accessed=8_000_000, transcendentals=0),
        name="attend",
    )(me1, *x_parts, gain, rel, proj, w_out)
    mix_in = [shifted(mix_out[k - 1], "tm", k) for k in range(1, tm)]

    owns, ins, carry = [], [], []
    diag = (frames, group, rows)
    for band in range(bands):
        last = band == bands - 1
        scratch = [pltpu.VMEM((rows, chans), BF16), pltpu.VMEM((group, rows, rows), BF16), pltpu.VMEM((rows, chans), F32)]
        if last:
            extra = [jax.ShapeDtypeStruct((lines, LANES + span), F32)]
            scratch.append(pltpu.VMEM(diag, F32))
        else:
            extra = [jax.ShapeDtypeStruct((1, chans), F32), jax.ShapeDtypeStruct(diag, F32)]
        own, *rest = pl.pallas_call(
            functools.partial(backward_kernel, dims, band, last),
            in_specs=[smem] + [vmem] * (tm + 7 + len(carry)),
            out_specs=[vmem] * (tm + len(extra)),
            out_shape=[jax.ShapeDtypeStruct((rows, width), F32)]
            + [jax.ShapeDtypeStruct((rows, width), BF16)] * (tm - 1) + extra,
            scratch_shapes=scratch,
            compiler_params=params,
            cost_estimate=pl.CostEstimate(flops=2_500_000_000, bytes_accessed=0, transcendentals=0),
            name="attend_back",
        )(me1, *g_parts[band], gain, qkv, probs, xb, inv, proj, w_out, *carry)
        sent, carry = rest[:tm - 1], rest[tm - 1:]
        owns.append(own)
        ins += [shifted(sent[k - 1], "tm", k) for k in range(1, tm)]

    small, mix_in = lax.optimization_barrier((carry[0], mix_in))
    small, ins[:-1] = group_sum(small, "dp", ins[:-1])
    small, ins[-1:] = group_sum(small, "space", ins[-1:])
    bias_grad = pl.pallas_call(
        bias_kernel,
        in_specs=[vmem],
        out_specs=vmem,
        out_shape=jax.ShapeDtypeStruct((group, offsets), F32),
        name="bias_sum",
    )(small)
    tile = small[:chans // LANES, :LANES]
    tiles = [tile] + [shifted(tile, "tm", k) for k in range(1, tm)]
    gain_grad = pl.pallas_call(
        gain_kernel,
        in_specs=[smem] + [vmem] * tm,
        out_specs=vmem,
        out_shape=jax.ShapeDtypeStruct((1, width), F32),
        scratch_shapes=[pltpu.VMEM(tile.shape, F32)],
        name="gain_sum",
    )(me1, *tiles)
    result = jax.ShapeDtypeStruct((total, width), BF16)
    block_out = pl.pallas_call(
        functools.partial(finish_whole, bands, frames),
        in_specs=[vmem] * tm,
        out_specs=vmem,
        out_shape=result,
        compiler_params=params,
        cost_estimate=pl.CostEstimate(flops=0, bytes_accessed=1_500_000, transcendentals=0),
        name="finish_out",
    )(mix_own, *mix_in)
    input_grad = pl.pallas_call(
        functools.partial(finish_bands, bands, frames),
        in_specs=[vmem] * (bands * tm),
        out_specs=vmem,
        out_shape=result,
        compiler_params=params,
        cost_estimate=pl.CostEstimate(flops=0, bytes_accessed=1_500_000, transcendentals=0),
        name="finish_grad",
    )(*owns, *ins)
    return (block_out.reshape(inputs.shape), input_grad.reshape(inputs.shape), gain_grad.reshape(width), bias_grad)


def solution(mesh):
    return jax.shard_map(
        per_device,
        mesh=mesh,
        in_specs=(
            P("dp", None, "space", "tm"),
            P("dp", None, "space", "tm"),
            P(),
            P("tm", None),
            P(None, "tm"),
            P(None, "tm"),
            P(None, "tm"),
            P("tm", None),
        ),
        out_specs=(
            P("dp", None, "space", "tm"),
            P("dp", None, "space", "tm"),
            P("tm"),
            P("tm", None),
        ),
        check_vma=False,
    )
```

time: 51 us -> 46.5 us (0.912)
  waiting for transfers between devices: 12.8 us -> 7.61 us
  Pallas kernels: 16.6 us -> 17.9 us
  other arithmetic: 0.83 us -> 0.02 us
  starting transfers between devices: 16.7 us -> 17.5 us
  local copies, waits for them, and re-layouts: 3.09 us -> 2.5 us
    ppermute x0 -> x6, starting transfers between devices: none -> 6.8 us  [group_sum(): parts.append(lax.ppermute(value, axis, pairs))]
    all_to_all x1 -> x0, starting transfers between devices: 6.43 us -> none  [per_device(): lax.all_to_all(small.reshape(-1, LANES), ('dp', 'space'), split_axis=0, c...]
    all_to_all x1 -> x0, waiting for transfers between devices: 5.76 us -> none  [per_device(): lax.all_to_all(small.reshape(-1, LANES), ('dp', 'space'), split_axis=0, c...]
    ppermute x0 -> x6, waiting for transfers between devices: none -> 3.95 us  [group_sum(): parts.append(lax.ppermute(value, axis, pairs))]
    ppermute x7, waiting for transfers between devices: 7.02 us -> 3.66 us  [shifted(): lax.ppermute(value, axis, [((i + step) % count, i) for i in range(count)])]
    pallas_call x3 -> x5, Pallas kernels: 4.5 us -> 6.77 us  [the longest x1 2.36 us: per_device(): pl.pallas_call(functools.partial(stage_kernel, frames, width), in_specs=[...]
    pallas_call x2, Pallas kernels: 8.34 us -> 7.31 us  [per_device(): pl.pallas_call(functools.partial(backward_kernel, dims, band, last), in_s...]
    convert_element_type x1 -> x0, other arithmetic: 0.82 us -> none  [per_device(): mixed.astype(BF16).reshape(inputs.shape)]
  transfers between devices with their start and end apart: 8 -> 13, of which waited for: 4 -> 5; matrix products, arithmetic and copies ran while one was open for 7% -> 4% of each run, Pallas kernels for 22% -> 36%
where the time goes in v5:
time: 46.5 us; the launch traced here: 46.3 us
  Pallas kernels  17.9 us (38%)
  starting transfers between devices  17.5 us (38%)
  waiting for transfers between devices  7.61 us (16%)
  local copies, waits for them, and re-layouts  2.5 us (5%)
  between operations  0.73 us (2%)
    ppermute x7, starting transfers between devices, shifted(): lax.ppermute(value, axis, [((i + step) % count, i) for i in range(count)])  10.7 us
    pallas_call x2, Pallas kernels, per_device(): pl.pallas_call(functools.partial(backward_kernel, dims, band, last), in_s...  7.31 us
    ppermute x6, starting transfers between devices, group_sum(): parts.append(lax.ppermute(value, axis, pairs))  6.8 us
    ppermute x6, waiting for transfers between devices, group_sum(): parts.append(lax.ppermute(value, axis, pairs))  3.95 us
    pallas_call x1, Pallas kernels, per_device(): pl.pallas_call(functools.partial(forward_kernel, dims), in_specs=[smem] +...  3.85 us
    ppermute x7, waiting for transfers between devices, shifted(): lax.ppermute(value, axis, [((i + step) % count, i) for i in range(count)])  3.66 us
    pallas_call x1, Pallas kernels, per_device(): pl.pallas_call(functools.partial(stage_kernel, frames, width), in_specs=[...  2.36 us
    pallas_call x1, Pallas kernels, per_device(): pl.pallas_call(bias_kernel, in_specs=[vmem], out_specs=vmem, out_shape=ja...  1.56 us
  transfers between devices with their start and end apart: 13, of which 5 were waited for; matrix products, arithmetic and copies ran while one was open for 4% of the time, Pallas kernels for 36%

profile of v5, /device:TPU:0, one launch (start us, length us, event | category | flops | bytes accessed | tf_op | source)
XLA Modules:
  0.0 46.3 jit_solution(11162592389513277827)
XLA Ops:
  0.6 3.0 %collective-permute-start = (bf16[320,512]{1,0:T(8,128)(2,1)}, bf16[320,512]{1,0:T(8,128)(2,1)S(1)}, u32[]{:S(2)}, u32[]{:S(2)}) collective-permute-start(bf16[320,512]{1,0:T(8,128)(2,1)} %bitcast.10), channel_id=1, source_target_pairs={{1,0},{0,1},{3,2},{2,3},{5,4},{4,5},{7,6},{6,7},{9,8},{8,9},{11,10... | collective-permute-start | bytes 983048 | tf_op jit(solution)/shard_map/ppermute | solution.py:241
  3.7 1.0 %slice_bitcast_fusion = (bf16[160,512]{1,0:T(8,128)(2,1)S(1)}, bf16[160,512]{1,0:T(8,128)(2,1)S(1)}) fusion(bf16[1,20,16,512]{3,2,1,0:T(8,128)(2,1)} %param.9), kind=kLoop, calls=%fused_computation | loop fusion | bytes 655360 | tf_op jit(solution)/shard_map/reshape | solution.py:279
  4.8 2.0 %collective-permute-start.1 = (bf16[160,512]{1,0:T(8,128)(2,1)S(1)}, bf16[160,512]{1,0:T(8,128)(2,1)S(1)}, u32[]{:S(2)}, u32[]{:S(2)}) collective-permute-start(bf16[160,512]{1,0:T(8,128)(2,1)S(1)} %get-tuple-element.65.refs_0_), channel_id=1, source_target_pairs={{1,0},{0,1},{3,2},{2,3},{5,4},{4,5},{7,6},{6,7},{9,8},{8,9},{11,10... | collective-permute-start | bytes 491528 | tf_op jit(solution)/shard_map/ppermute | solution.py:241
  6.8 0.8 %broadcast_in_dim.2 = f32[8,39,8]{2,1,0:T(8,128)S(1)} broadcast(f32[8,39]{1,0:T(8,128)} %param.11), dimensions={0,1} | broadcast | bytes 11232 | tf_op jit(solution)/shard_map/broadcast_in_dim | solution.py:284
  7.6 0.1 reshape.37.bias_ref
  7.7 2.4 %stage.1 = (f32[20,8,160]{2,1,0:T(8,128)S(1)}, bf16[320,512]{1,0:T(8,128)(2,1)S(1)}, bf16[1024,1536]{1,0:T(8,128)(2,1)S(1)}, bf16[512,1024]{1,0:T(8,128)(2,1)S(1)}, f32[1,1024]{1,0:T(1,128)S(1)}) custom-call(f32[8,312]{1,0:T(8,128)S(1)} %reshape.37.bias_ref, bf16[320,512]{1,0:T(8,128)(2,1)} %bitcast.11, bf16[1024,512]{1,0:T(8,128)(2,1)} %wq_ref.1, ...), custom_call_target="tpu_custom_call" | custom-call | bytes 8000000 | tf_op jit(solution)/shard_map/stage/pallas_call | solution.py:289
  10.0 2.4 %collective-permute-done.refs_1_ = bf16[320,512]{1,0:T(8,128)(2,1)S(1)} collective-permute-done((bf16[320,512]{1,0:T(8,128)(2,1)}, bf16[320,512]{1,0:T(8,128)(2,1)S(1)}, u32[]{:S(2)}, u32[]{:S(2)}) %collective-permute-start) | collective-permute-done | bytes 327712 | tf_op jit(solution)/shard_map/ppermute | solution.py:241
  12.4 3.9 %attend.1 = (bf16[2,160,1536]{2,1,0:T(8,128)(2,1)S(1)}, bf16[2,8,160,160]{3,2,1,0:T(8,128)(2,1)S(1)}, bf16[2,160,1024]{2,1,0:T(8,128)(2,1)S(1)}, f32[2,160,128]{...) custom-call(s32[1]{0:T(128)} %bitcast.me_ref, ...), custom_call_target="tpu_custom_call" | custom-call | flops 4000000000 | bytes 8000000 | tf_op jit(solution)/shard_map/attend/pallas_call | solution.py:306
  16.3 2.1 %collective-permute-start.3 = (bf16[2,160,512]{2,1,0:T(8,128)(2,1)S(1)}, bf16[2,160,512]{2,1,0:T(8,128)(2,1)S(1)}, u32[]{:S(2)}, u32[]{:S(2)}) collective-permute-start(bf16[2,160,512]{2,1,0:T(8,128)(2,1)S(1)} %get-tuple-element.47), channel_id=1, source_target_pairs={{1,0},{0,1},{3,2},{2,3},{5,4},{4,5},{7,6},{6,7},{9,8},{8,9},{11,10... | collective-permute-start | bytes 983048 | tf_op jit(solution)/shard_map/ppermute | solution.py:241
  18.4 3.6 %attend_back.2 = (f32[160,512]{1,0:T(8,128)S(1)}, bf16[160,512]{1,0:T(8,128)(2,1)S(1)}, f32[1,1024]{1,0:T(1,128)S(1)}, f32[20,8,160]{2,1,0:T(8,128)S(1)}) custom-call(s32[1]{0:T(128)} %bitcast.me_ref, bf16[160,512]{1,0:T(8,128)(2,1)S(1)} %get-tuple-element.64.refs_0_, bf16[160,512]{1,0:T(8,128)(2,1)S(1)} %collective-permute-done.2.refs_1_, ...), custom_call_target="tpu_custom_call" | custom-call | flops 2500000000 | tf_op jit(solution)/shard_map/attend_back/pallas_call | solution.py:334
  22.1 3.7 %attend_back.3 = (f32[160,512]{1,0:T(8,128)S(1)}, bf16[160,512]{1,0:T(8,128)(2,1)S(1)}, f32[8,512]{1,0:T(8,128)S(1)}) custom-call(s32[1]{0:T(128)} %bitcast.me_ref, bf16[160,512]{1,0:T(8,128)(2,1)S(1)} %get-tuple-element.65.refs_0_, bf16[160,512]{1,0:T(8,128)(2,1)S(1)} %collective-permute-done.1.refs_1_, f32[1,1024]{1,0:T(1,128)S(1)} %get-tuple-element.35.refs_2_, ...), custom_call_target="tpu_custom_call" | custom-call | flops 2500000000 | tf_op jit(solution)/shard_map/attend_back/pallas_call | solution.py:334
  25.8 1.2 %collective-permute-done.3.refs_0_ = bf16[2,160,512]{2,1,0:T(8,128)(2,1)S(1)} collective-permute-done((bf16[2,160,512]{2,1,0:T(8,128)(2,1)S(1)}, bf16[2,160,512]{2,1,0:T(8,128)(2,1)S(1)}, u32[]{:S(2)}, u32[]{:S(2)}) %collective-permute-start.3) | collective-permute-done | bytes 327712 | tf_op jit(solution)/shard_map/ppermute | solution.py:241
  27.0 2.0 %collective-permute-start.5 = (f32[8,512]{1,0:T(8,128)S(1)}, f32[8,512]{1,0:T(8,128)S(1)}, u32[]{:S(2)}, u32[]{:S(2)}) collective-permute-start(f32[8,512]{1,0:T(8,128)S(1)} %get-tuple-element.54), channel_id=1, source_target_pairs={{16,0},{24,8},{0,16},{8,24},{17,1},{25,9},{1,17},{9,25},{18,2},{26... | collective-permute-start | bytes 49160 | tf_op jit(solution)/shard_map/ppermute | solution.py:257
  29.1 1.8 %collective-permute-start.11 = (bf16[160,512]{1,0:T(8,128)(2,1)S(1)}, bf16[160,512]{1,0:T(8,128)(2,1)S(1)}, u32[]{:S(2)}, u32[]{:S(2)}) collective-permute-start(bf16[160,512]{1,0:T(8,128)(2,1)S(1)} %get-tuple-element.58), channel_id=1, source_target_pairs={{1,0},{0,1},{3,2},{2,3},{5,4},{4,5},{7,6},{6,7},{9,8},{8,9},{11,10... | collective-permute-start | bytes 491528 | tf_op jit(solution)/shard_map/ppermute | solution.py:241
  30.9 4.0 %collective-permute-start.10 = (f32[8,512]{1,0:T(8,128)S(1)}, f32[8,512]{1,0:T(8,128)S(1)}, u32[]{:S(2)}, u32[]{:S(2)}) collective-permute-start(f32[8,512]{1,0:T(8,128)S(1)} %add_add_fusion.1), channel_id=1, source_target_pairs={{6,0},{4,2},{2,4},{0,6},{7,1},{5,3},{3,5},{1,7},{14,8},{12,10},{10... | collective-permute-start | bytes 49160 | tf_op jit(solution)/shard_map/ppermute | solution.py:257
  35.0 0.6 %collective-permute-start.8 = (f32[8,512]{1,0:T(8,128)S(1)}, f32[8,512]{1,0:T(8,128)S(1)}, u32[]{:S(2)}, u32[]{:S(2)}) collective-permute-start(f32[8,512]{1,0:T(8,128)S(1)} %add_add_fusion.1), channel_id=1, source_target_pairs={{2,0},{0,2},{6,4},{4,6},{3,1},{1,3},{7,5},{5,7},{10,8},{8,10},{14,... | collective-permute-start | bytes 49160 | tf_op jit(solution)/shard_map/ppermute | solution.py:257
  35.7 1.0 %collective-permute-done.10 = f32[8,512]{1,0:T(8,128)S(1)} collective-permute-done((f32[8,512]{1,0:T(8,128)S(1)}, f32[8,512]{1,0:T(8,128)S(1)}, u32[]{:S(2)}, u32[]{:S(2)}) %collective-permute-start.10) | collective-permute-done | bytes 16416 | tf_op jit(solution)/shard_map/ppermute | solution.py:257
  36.7 2.9 %collective-permute-done.9 = f32[8,512]{1,0:T(8,128)S(1)} collective-permute-done((f32[8,512]{1,0:T(8,128)S(1)}, f32[8,512]{1,0:T(8,128)S(1)}, u32[]{:S(2)}, u32[]{:S(2)}) %collective-permute-start.9) | collective-permute-done | bytes 16416 | tf_op jit(solution)/shard_map/ppermute | solution.py:257
  39.7 1.6 %collective-permute-start.12 = (f32[8,128]{1,0:T(8,128)S(1)}, f32[8,128]{1,0:T(8,128)S(1)}, u32[]{:S(2)}, u32[]{:S(2)}) collective-permute-start(f32[8,128]{1,0:T(8,128)S(1)} %slice.12.refs_0_), channel_id=1, source_target_pairs={{1,0},{0,1},{3,2},{2,3},{5,4},{4,5},{7,6},{6,7},{9,8},{8,9},{11,10... | collective-permute-start | bytes 12296 | tf_op jit(solution)/shard_map/ppermute | solution.py:241
  41.2 0.8 %finish_out.1 = bf16[320,512]{1,0:T(8,128)(2,1)} custom-call(f32[2,160,512]{2,1,0:T(8,128)S(1)} %get-tuple-element.39.own_ref, bf16[2,160,512]{2,1,0:T(8,128)(2,1)S(1)} %collective-permute-done.3.refs_0_), custom_call_target="tpu_custom_call" | custom-call | bytes 1500000 | tf_op jit(solution)/shard_map/finish_out/pallas_call | solution.py:370
  42.1 1.6 %bias_sum.1 = f32[8,39]{1,0:T(8,128)} custom-call(f32[8,512]{1,0:T(8,128)} %copy-done), custom_call_target="tpu_custom_call" | custom-call | tf_op jit(solution)/shard_map/bias_sum/pallas_call | solution.py:352
  43.6 0.8 %finish_grad.1 = bf16[320,512]{1,0:T(8,128)(2,1)} custom-call(f32[160,512]{1,0:T(8,128)S(1)} %get-tuple-element.49.refs_0_, f32[160,512]{1,0:T(8,128)S(1)} %get-tuple-element.50.refs_1_, bf16[160,512]{1,0:T(8,128)(2,1)S(1)} %collective-permute-done.7.refs_2_, bf16[160,512]{1,0:T(8,128)(2,1)S(1)} %collective-permute-done.11.refs_3_), custom_call_target="tpu_custom_call" | custom-call | bytes 1500000 | tf_op jit(solution)/shard_map/finish_grad/pallas_call | solution.py:379
  44.4 0.6 %copy-done.2 = f32[8,128]{1,0:T(8,128)} copy-done((f32[8,128]{1,0:T(8,128)}, f32[8,128]{1,0:T(8,128)S(1)}, u32[]{:S(2)}) %copy-start.2) | copy-done | bytes 4120
  45.0 1.3 %gain_sum.1 = f32[1,512]{1,0:T(1,128)} custom-call(s32[1]{0:T(128)} %bitcast.me_ref, f32[8,128]{1,0:T(8,128)} %copy-done.1, f32[8,128]{1,0:T(8,128)} %copy-done.2), custom_call_target="tpu_custom_call" | custom-call | tf_op jit(solution)/shard_map/gain_sum/pallas_call | solution.py:361
  (22 shorter events, 0.4 us)
Async XLA Ops:
  0.6 11.8 %collective-permute-start = (bf16[320,512]{1,0:T(8,128)(2,1)}, bf16[320,512]{1,0:T(8,128)(2,1)S(1)}, u32[]{:S(2)}, u32[]{:S(2)}) collective-permute-start(bf16[320,512]{1,0:T(8,128)(2,1)} %bitcast.10), channel_id=1, source_target_pairs={{1,0},{0,1},{3,2},{2,3},{5,4},{4,5},{7,6},{6,7},{9,8},{8,9},{11,10... | collective-permute-start | bytes 983048 | tf_op jit(solution)/shard_map/ppermute | solution.py:241
  4.7 13.7 %collective-permute-start.2 = (bf16[160,512]{1,0:T(8,128)(2,1)S(1)}, bf16[160,512]{1,0:T(8,128)(2,1)S(1)}, u32[]{:S(2)}, u32[]{:S(2)}) collective-permute-start(bf16[160,512]{1,0:T(8,128)(2,1)S(1)} %get-tuple-element.64.refs_0_), channel_id=1, source_target_pairs={{1,0},{0,1},{3,2},{2,3},{5,4},{4,5},{7,6},{6,7},{9,8},{8,9},{11,10... | collective-permute-start | bytes 491528 | tf_op jit(solution)/shard_map/ppermute | solution.py:241
  4.8 17.4 %collective-permute-start.1 = (bf16[160,512]{1,0:T(8,128)(2,1)S(1)}, bf16[160,512]{1,0:T(8,128)(2,1)S(1)}, u32[]{:S(2)}, u32[]{:S(2)}) collective-permute-start(bf16[160,512]{1,0:T(8,128)(2,1)S(1)} %get-tuple-element.65.refs_0_), channel_id=1, source_target_pairs={{1,0},{0,1},{3,2},{2,3},{5,4},{4,5},{7,6},{6,7},{9,8},{8,9},{11,10... | collective-permute-start | bytes 491528 | tf_op jit(solution)/shard_map/ppermute | solution.py:241
  16.3 10.7 %collective-permute-start.3 = (bf16[2,160,512]{2,1,0:T(8,128)(2,1)S(1)}, bf16[2,160,512]{2,1,0:T(8,128)(2,1)S(1)}, u32[]{:S(2)}, u32[]{:S(2)}) collective-permute-start(bf16[2,160,512]{2,1,0:T(8,128)(2,1)S(1)} %get-tuple-element.47), channel_id=1, source_target_pairs={{1,0},{0,1},{3,2},{2,3},{5,4},{4,5},{7,6},{6,7},{9,8},{8,9},{11,10... | collective-permute-start | bytes 983048 | tf_op jit(solution)/shard_map/ppermute | solution.py:241
  22.0 8.9 %collective-permute-start.7 = (bf16[160,512]{1,0:T(8,128)(2,1)S(1)}, bf16[160,512]{1,0:T(8,128)(2,1)S(1)}, u32[]{:S(2)}, u32[]{:S(2)}) collective-permute-start(bf16[160,512]{1,0:T(8,128)(2,1)S(1)} %get-tuple-element.52), channel_id=1, source_target_pairs={{1,0},{0,1},{3,2},{2,3},{5,4},{4,5},{7,6},{6,7},{9,8},{8,9},{11,10... | collective-permute-start | bytes 491528 | tf_op jit(solution)/shard_map/ppermute | solution.py:241
  27.0 3.9 %collective-permute-start.6 = (f32[8,512]{1,0:T(8,128)S(1)}, f32[8,512]{1,0:T(8,128)S(1)}, u32[]{:S(2)}, u32[]{:S(2)}) collective-permute-start(f32[8,512]{1,0:T(8,128)S(1)} %get-tuple-element.54), channel_id=1, source_target_pairs={{24,0},{16,8},{8,16},{0,24},{25,1},{17,9},{9,17},{1,25},{26,2},{18... | collective-permute-start | bytes 49160 | tf_op jit(solution)/shard_map/ppermute | solution.py:257
  27.0 3.9 %collective-permute-start.5 = (f32[8,512]{1,0:T(8,128)S(1)}, f32[8,512]{1,0:T(8,128)S(1)}, u32[]{:S(2)}, u32[]{:S(2)}) collective-permute-start(f32[8,512]{1,0:T(8,128)S(1)} %get-tuple-element.54), channel_id=1, source_target_pairs={{16,0},{24,8},{0,16},{8,24},{17,1},{25,9},{1,17},{9,25},{18,2},{26... | collective-permute-start | bytes 49160 | tf_op jit(solution)/shard_map/ppermute | solution.py:257
  29.1 1.9 %collective-permute-start.4 = (f32[8,512]{1,0:T(8,128)S(1)}, f32[8,512]{1,0:T(8,128)S(1)}, u32[]{:S(2)}, u32[]{:S(2)}) collective-permute-start(f32[8,512]{1,0:T(8,128)S(1)} %get-tuple-element.54), channel_id=1, source_target_pairs={{8,0},{0,8},{24,16},{16,24},{9,1},{1,9},{25,17},{17,25},{10,2},{2,... | collective-permute-start | bytes 49160 | tf_op jit(solution)/shard_map/ppermute | solution.py:257
  29.1 6.5 %collective-permute-start.11 = (bf16[160,512]{1,0:T(8,128)(2,1)S(1)}, bf16[160,512]{1,0:T(8,128)(2,1)S(1)}, u32[]{:S(2)}, u32[]{:S(2)}) collective-permute-start(bf16[160,512]{1,0:T(8,128)(2,1)S(1)} %get-tuple-element.58), channel_id=1, source_target_pairs={{1,0},{0,1},{3,2},{2,3},{5,4},{4,5},{7,6},{6,7},{9,8},{8,9},{11,10... | collective-permute-start | bytes 491528 | tf_op jit(solution)/shard_map/ppermute | solution.py:241
  30.9 5.8 %collective-permute-start.10 = (f32[8,512]{1,0:T(8,128)S(1)}, f32[8,512]{1,0:T(8,128)S(1)}, u32[]{:S(2)}, u32[]{:S(2)}) collective-permute-start(f32[8,512]{1,0:T(8,128)S(1)} %add_add_fusion.1), channel_id=1, source_target_pairs={{6,0},{4,2},{2,4},{0,6},{7,1},{5,3},{3,5},{1,7},{14,8},{12,10},{10... | collective-permute-start | bytes 49160 | tf_op jit(solution)/shard_map/ppermute | solution.py:257
  35.0 4.6 %collective-permute-start.9 = (f32[8,512]{1,0:T(8,128)S(1)}, f32[8,512]{1,0:T(8,128)S(1)}, u32[]{:S(2)}, u32[]{:S(2)}) collective-permute-start(f32[8,512]{1,0:T(8,128)S(1)} %add_add_fusion.1), channel_id=1, source_target_pairs={{4,0},{6,2},{0,4},{2,6},{5,1},{7,3},{1,5},{3,7},{12,8},{14,10},{8,... | collective-permute-start | bytes 49160 | tf_op jit(solution)/shard_map/ppermute | solution.py:257
  35.0 4.6 %collective-permute-start.8 = (f32[8,512]{1,0:T(8,128)S(1)}, f32[8,512]{1,0:T(8,128)S(1)}, u32[]{:S(2)}, u32[]{:S(2)}) collective-permute-start(f32[8,512]{1,0:T(8,128)S(1)} %add_add_fusion.1), channel_id=1, source_target_pairs={{2,0},{0,2},{6,4},{4,6},{3,1},{1,3},{7,5},{5,7},{10,8},{8,10},{14,... | collective-permute-start | bytes 49160 | tf_op jit(solution)/shard_map/ppermute | solution.py:257
  39.6 2.4 %copy-start = (f32[8,512]{1,0:T(8,128)}, f32[8,512]{1,0:T(8,128)S(1)}, u32[]{:S(2)}) copy-start(f32[8,512]{1,0:T(8,128)S(1)} %add_add_fusion.small_ref) | copy-start | bytes 49156
  39.7 4.7 %copy-start.1 = (f32[8,128]{1,0:T(8,128)}, f32[8,128]{1,0:T(8,128)S(1)}, u32[]{:S(2)}) copy-start(f32[8,128]{1,0:T(8,128)S(1)} %slice.12.refs_0_) | copy-start | bytes 12292
  39.7 4.7 %collective-permute-start.12 = (f32[8,128]{1,0:T(8,128)S(1)}, f32[8,128]{1,0:T(8,128)S(1)}, u32[]{:S(2)}, u32[]{:S(2)}) collective-permute-start(f32[8,128]{1,0:T(8,128)S(1)} %slice.12.refs_0_), channel_id=1, source_target_pairs={{1,0},{0,1},{3,2},{2,3},{5,4},{4,5},{7,6},{6,7},{9,8},{8,9},{11,10... | collective-permute-start | bytes 12296 | tf_op jit(solution)/shard_map/ppermute | solution.py:241
  44.4 0.6 %copy-start.2 = (f32[8,128]{1,0:T(8,128)}, f32[8,128]{1,0:T(8,128)S(1)}, u32[]{:S(2)}) copy-start(f32[8,128]{1,0:T(8,128)S(1)} %collective-permute-done.12.refs_1_) | copy-start | bytes 12292

commit v6 on v5

--- a/solution.py
+++ b/solution.py
@@ -65,7 +65,7 @@
     gain_ref, rel_ref, proj_ref, wo_ref = refs[tm:tm + 4]
     qkv_ref, p_ref, xb_ref, inv_ref, own_ref = refs[tm + 4:tm + 9]
     msg_refs = refs[tm + 9:tm + 9 + tm - 1]
-    xw_ref, normed_ref = refs[tm + 9 + tm - 1:]
+    xw_ref, normed_ref, att_ref = refs[tm + 9 + tm - 1:]
     me = me_ref[0]
     rows = frames * BAND
     bands = pixels // BAND
@@ -88,9 +88,10 @@
             inv_ref[band, at, :] = jnp.broadcast_to(inv, (2 * BAND, LANES))
     same = same_pixel(rows)[None]
     owner = head_lanes(head_dim, rows)
+    total = frames * pixels
+    qkv = mm(normed_ref[...].reshape(total, -1), proj_ref[...]).astype(BF16)
+    qkv_ref[...] = qkv.reshape(bands, rows, 3 * width)
     for band in range(bands):
-        qkv_ref[band] = mm(normed_ref[band], proj_ref[...]).astype(BF16)
-        att = []
         for pair in range(width // LANES):
             qp, kp, vp = (
                 qkv_ref[band, :, n * width + pair * LANES:n * width + (pair + 1) * LANES] for n in range(3)
@@ -107,11 +108,13 @@
                     e = jnp.exp(s - jnp.max(s, axis=-1, keepdims=True))
                     p_ref[band, head, at, :] = (e * (1.0 / jnp.sum(e, axis=-1, keepdims=True))).astype(BF16)
                 outs.append(mm(p_ref[band, head], vp))
-            att.append(pick_heads(outs, owner).astype(BF16))
-        att = jnp.concatenate(att, axis=1)
-        for k in range(1, tm):
-            msg_refs[k - 1][band] = mm(att, wo_ref[:, pl.ds(place(tm - k), width)]).astype(BF16)
-        own_ref[band] = mm(att, wo_ref[:, pl.ds(place(0), width)]) + xb_ref[band, :, pl.ds(place(0), width)].astype(F32)
+            att_ref[band, :, pair * LANES:(pair + 1) * LANES] = pick_heads(outs, owner).astype(BF16)
+    att = att_ref[...].reshape(total, width)
+    for k in range(1, tm):
+        part = mm(att, wo_ref[:, pl.ds(place(tm - k), width)]).astype(BF16)
+        msg_refs[k - 1][...] = part.reshape(bands, rows, width)
+    own = mm(att, wo_ref[:, pl.ds(place(0), width)]).reshape(bands, rows, width)
+    own_ref[...] = own + xb_ref[:, :, pl.ds(place(0), width)].astype(F32)
 
 
 def backward_kernel(dims, band, last, me_ref, *refs):
@@ -208,21 +211,25 @@
     out_ref[...] = value.reshape(out_ref.shape).astype(out_ref.dtype)
 
 
-def finish_bands(bands, frames, *refs):
-    finish_kernel(bands, frames, refs[:bands], refs[bands:-1], refs[-1])
-
-
-def finish_whole(bands, frames, own_ref, *refs):
+def finish_grad_kernel(bands, frames, small_ref, *refs):
+    *refs, out_ref, bias_ref = refs
+    finish_kernel(bands, frames, refs[:bands], refs[bands:], out_ref)
+    group, offsets = bias_ref.shape
+    value = small_ref[:, LANES:]
+    high = value.astype(BF16)
+    rest = value - high.astype(F32)
+    middle = rest.astype(BF16)
+    low = (rest - middle.astype(F32)).astype(BF16)
+    span = value.shape[1]
+    lane = lax.broadcasted_iota(jnp.int32, (span, LANES), 0) // BAND
+    put = (lane == lax.broadcasted_iota(jnp.int32, (span, LANES), 1)).astype(F32).astype(BF16)
+    total = mm(high, put) + mm(middle, put) + mm(low, put)
+    bias_ref[...] = total[:group, :offsets]
+
+
+def finish_out_kernel(bands, frames, own_ref, *refs):
     in_refs = [ref.at[band] for band in range(bands) for ref in refs[:-1]]
     finish_kernel(bands, frames, [own_ref.at[band] for band in range(bands)], in_refs, refs[-1])
-
-
-def bias_kernel(small_ref, out_ref):
-    group, offsets = out_ref.shape
-    value = small_ref[:group, LANES:]
-    lane = lax.broadcasted_iota(jnp.int32, (value.shape[1], offsets), 0) // BAND
-    put = (lane == lax.broadcasted_iota(jnp.int32, (value.shape[1], offsets), 1)).astype(F32)
-    out_ref[...] = lax.dot_general(value, put, NN, precision=lax.Precision.HIGHEST, preferred_element_type=F32)
 
 
 def gain_kernel(me_ref, *refs):
@@ -278,7 +285,6 @@
     x0 = inputs.reshape(total, width)
     g_bands = [out_grad[:, :, n * BAND:(n + 1) * BAND].reshape(rows, width) for n in range(bands)]
     x_parts = [x0] + [shifted(x0, "tm", k) for k in range(1, tm)]
-    g_parts = [[g] + [shifted(g, "tm", k) for k in range(1, tm)] for g in g_bands]
     me1 = me.astype(jnp.int32).reshape(1)
     gain = norm_gain.reshape(1, chans)
     spread = jnp.broadcast_to(pos_bias[:, :, None], (*pos_bias.shape, BAND)).reshape(group, -1)
@@ -303,6 +309,8 @@
         name="stage",
     )(spread, *held)
     x_parts[0] = x0
+    g_bands, rel = lax.optimization_barrier((g_bands, rel))
+    g_parts = [[g] + [shifted(g, "tm", k) for k in range(1, tm)] for g in g_bands]
     qkv, probs, xb, inv, mix_own, *mix_out = pl.pallas_call(
         functools.partial(forward_kernel, dims),
         in_specs=[smem] + [vmem] * (tm + 4),
@@ -314,13 +322,15 @@
             jax.ShapeDtypeStruct((bands, rows, LANES), F32),
             jax.ShapeDtypeStruct((bands, rows, width), F32),
         ] + [jax.ShapeDtypeStruct((bands, rows, width), BF16)] * (tm - 1),
-        scratch_shapes=[pltpu.VMEM((total, chans), BF16), pltpu.VMEM((bands, rows, chans), BF16)],
+        scratch_shapes=[
+            pltpu.VMEM((total, chans), BF16),
+            pltpu.VMEM((bands, rows, chans), BF16),
+            pltpu.VMEM((bands, rows, width), BF16),
+        ],
         compiler_params=params,
         cost_estimate=pl.CostEstimate(flops=4_000_000_000, bytes_accessed=8_000_000, transcendentals=0),
         name="attend",
     )(me1, *x_parts, gain, rel, proj, w_out)
-    mix_in = [shifted(mix_out[k - 1], "tm", k) for k in range(1, tm)]
-
     owns, ins, carry = [], [], []
     diag = (frames, group, rows)
     for band in range(bands):
@@ -339,52 +349,50 @@
             + [jax.ShapeDtypeStruct((rows, width), BF16)] * (tm - 1) + extra,
             scratch_shapes=scratch,
             compiler_params=params,
-            cost_estimate=pl.CostEstimate(flops=2_500_000_000, bytes_accessed=0, transcendentals=0),
+            cost_estimate=pl.CostEstimate(flops=4_000_000_000, bytes_accessed=0, transcendentals=0),
             name="attend_back",
         )(me1, *g_parts[band], gain, qkv, probs, xb, inv, proj, w_out, *carry)
         sent, carry = rest[:tm - 1], rest[tm - 1:]
+        if band == 0:
+            sent, mix_out = lax.optimization_barrier((sent, mix_out))
+            mix_in = [shifted(mix_out[k - 1], "tm", k) for k in range(1, tm)]
         owns.append(own)
         ins += [shifted(sent[k - 1], "tm", k) for k in range(1, tm)]
 
-    small, mix_in = lax.optimization_barrier((carry[0], mix_in))
-    small, ins[:-1] = group_sum(small, "dp", ins[:-1])
-    small, ins[-1:] = group_sum(small, "space", ins[-1:])
-    bias_grad = pl.pallas_call(
-        bias_kernel,
-        in_specs=[vmem],
+    result = jax.ShapeDtypeStruct((total, width), BF16)
+    finish_cost = pl.CostEstimate(flops=0, bytes_accessed=1_500_000, transcendentals=0)
+    block_out = pl.pallas_call(
+        functools.partial(finish_out_kernel, bands, frames),
+        in_specs=[vmem] * tm,
         out_specs=vmem,
-        out_shape=jax.ShapeDtypeStruct((group, offsets), F32),
-        name="bias_sum",
-    )(small)
+        out_shape=result,
+        compiler_params=params,
+        cost_estimate=finish_cost,
+        name="finish_out",
+    )(mix_own, *mix_in)
+    small, ins[:-1] = group_sum(carry[0], "dp", ins[:-1])
+    small, (block_out, ins[-1]) = group_sum(small, "space", (block_out, ins[-1]))
     tile = small[:chans // LANES, :LANES]
-    tiles = [tile] + [shifted(tile, "tm", k) for k in range(1, tm)]
+    tiles = [shifted(tile, "tm", k) for k in range(1, tm)]
+    input_grad, bias_grad = pl.pallas_call(
+        functools.partial(finish_grad_kernel, bands, frames),
+        in_specs=[vmem] * (1 + bands * tm),
+        out_specs=[vmem] * 2,
+        out_shape=[result, jax.ShapeDtypeStruct((group, offsets), F32)],
+        compiler_params=params,
+        cost_estimate=finish_cost,
+        name="finish_grad",
+    )(small, *owns, *ins)
+    tiles, input_grad = lax.optimization_barrier((tiles, input_grad))
     gain_grad = pl.pallas_call(
         gain_kernel,
         in_specs=[smem] + [vmem] * tm,
         out_specs=vmem,
         out_shape=jax.ShapeDtypeStruct((1, width), F32),
         scratch_shapes=[pltpu.VMEM(tile.shape, F32)],
+        compiler_params=params,
         name="gain_sum",
-    )(me1, *tiles)
-    result = jax.ShapeDtypeStruct((total, width), BF16)
-    block_out = pl.pallas_call(
-        functools.partial(finish_whole, bands, frames),
-        in_specs=[vmem] * tm,
-        out_specs=vmem,
-        out_shape=result,
-        compiler_params=params,
-        cost_estimate=pl.CostEstimate(flops=0, bytes_accessed=1_500_000, transcendentals=0),
-        name="finish_out",
-    )(mix_own, *mix_in)
-    input_grad = pl.pallas_call(
-        functools.partial(finish_bands, bands, frames),
-        in_specs=[vmem] * (bands * tm),
-        out_specs=vmem,
-        out_shape=result,
-        compiler_params=params,
-        cost_estimate=pl.CostEstimate(flops=0, bytes_accessed=1_500_000, transcendentals=0),
-        name="finish_grad",
-    )(*owns, *ins)
+    )(me1, tile, *tiles)
     return (block_out.reshape(inputs.shape), input_grad.reshape(inputs.shape), gain_grad.reshape(width), bias_grad)
 
 

time: 46.5 us -> 50.8 us (1.092)
  local copies, waits for them, and re-layouts: 2.5 us -> 5.75 us
  waiting for transfers between devices: 7.61 us -> 8.15 us
    unnamed x6 -> x14, local copies, waits for them, and re-layouts: 0.6 us -> 4.84 us
    pallas_call x2, Pallas kernels: 7.31 us -> 9.09 us  [per_device(): pl.pallas_call(functools.partial(backward_kernel, dims, band, last), in_s...]
    ppermute x6, waiting for transfers between devices: 3.95 us -> 5.59 us  [group_sum(): parts.append(lax.ppermute(value, axis, pairs))]
    pallas_call x3 -> x2, Pallas kernels: 3.14 us -> 1.72 us  [the longest x1 0.92 us: per_device(): pl.pallas_call(functools.partial(finish_grad_kernel, bands, frames), in_s...]
    ppermute x7, waiting for transfers between devices: 3.66 us -> 2.56 us  [shifted(): lax.ppermute(value, axis, [((i + step) % count, i) for i in range(count)])]
    reshape x1, local copies, waits for them, and re-layouts: 1.02 us -> 0.02 us  [per_device(): out_grad[:, :, n * BAND:(n + 1) * BAND].reshape(rows, width)]
    pallas_call x1, Pallas kernels: 1.27 us -> 0.59 us  [per_device(): pl.pallas_call(gain_kernel, in_specs=[smem] + [vmem] * tm, out_specs=vmem...]
    pallas_call x1, Pallas kernels: 3.85 us -> 4.5 us  [per_device(): pl.pallas_call(functools.partial(forward_kernel, dims), in_specs=[smem] +...]
  transfers between devices with their start and end apart: 13 -> 13, of which waited for: 5 -> 5; matrix products, arithmetic and copies ran while one was open for 4% -> 2% of each run, Pallas kernels for 36% -> 35%
where the time goes in v6:
time: 50.8 us; the launch traced here: 50.5 us
  Pallas kernels  18.3 us (36%)
  starting transfers between devices  17.5 us (34%)
  waiting for transfers between devices  8.15 us (16%)
  local copies, waits for them, and re-layouts  5.75 us (11%)
  between operations  0.73 us (1%)
    ppermute x7, starting transfers between devices, shifted(): lax.ppermute(value, axis, [((i + step) % count, i) for i in range(count)])  11.1 us
    pallas_call x2, Pallas kernels, per_device(): pl.pallas_call(functools.partial(backward_kernel, dims, band, last), in_s...  9.09 us
    ppermute x6, starting transfers between devices, group_sum(): parts.append(lax.ppermute(value, axis, pairs))  6.38 us
    ppermute x6, waiting for transfers between devices, group_sum(): parts.append(lax.ppermute(value, axis, pairs))  5.59 us
    unnamed x14, local copies, waits for them, and re-layouts  4.84 us
    pallas_call x1, Pallas kernels, per_device(): pl.pallas_call(functools.partial(forward_kernel, dims), in_specs=[smem] +...  4.5 us
    ppermute x7, waiting for transfers between devices, shifted(): lax.ppermute(value, axis, [((i + step) % count, i) for i in range(count)])  2.56 us
    pallas_call x1, Pallas kernels, per_device(): pl.pallas_call(functools.partial(stage_kernel, frames, width), in_specs=[...  2.4 us
  transfers between devices with their start and end apart: 13, of which 5 were waited for; matrix products, arithmetic and copies ran while one was open for 2% of the time, Pallas kernels for 35%

profile of v6, /device:TPU:0, one launch (start us, length us, event | category | flops | bytes accessed | tf_op | source)
XLA Modules:
  0.0 50.5 jit_solution(15300224577227866085)
XLA Ops:
  0.6 3.0 %collective-permute-start.1 = (bf16[320,512]{1,0:T(8,128)(2,1)}, bf16[320,512]{1,0:T(8,128)(2,1)}, u32[]{:S(2)}, u32[]{:S(2)}) collective-permute-start(bf16[320,512]{1,0:T(8,128)(2,1)} %bitcast.10), channel_id=1, source_target_pairs={{1,0},{0,1},{3,2},{2,3},{5,4},{4,5},{7,6},{6,7},{9,8},{8,9},{11,10... | collective-permute-start | bytes 983048 | tf_op jit(solution)/shard_map/ppermute | solution.py:248
  3.7 0.8 %broadcast_in_dim.2 = f32[8,39,8]{2,1,0:T(8,128)S(1)} broadcast(f32[8,39]{1,0:T(8,128)} %param.11), dimensions={0,1} | broadcast | bytes 11232 | tf_op jit(solution)/shard_map/broadcast_in_dim | solution.py:290
  4.6 2.4 %stage.1 = (f32[20,8,160]{2,1,0:T(8,128)S(1)}, bf16[320,512]{1,0:T(8,128)(2,1)S(1)}, bf16[1024,1536]{1,0:T(8,128)(2,1)S(1)}, bf16[512,1024]{1,0:T(8,128)(2,1)S(1)}, f32[1,1024]{1,0:T(1,128)S(1)}) custom-call(f32[8,312]{1,0:T(8,128)S(1)} %reshape.39.bias_ref, bf16[320,512]{1,0:T(8,128)(2,1)} %bitcast.11, bf16[1024,512]{1,0:T(8,128)(2,1)} %wq_ref.1, ...), custom_call_target="tpu_custom_call" | custom-call | bytes 8000000 | tf_op jit(solution)/shard_map/stage/pallas_call | solution.py:295
  7.0 1.0 %copy-done = bf16[512,1024]{1,0:T(8,128)(2,1)} copy-done((bf16[512,1024]{1,0:T(8,128)(2,1)}, bf16[512,1024]{1,0:T(8,128)(2,1)S(1)}, u32[]{:S(2)}) %copy-start) | copy-done | bytes 1048600
  8.8 2.0 %collective-permute-start = (bf16[160,512]{1,0:T(8,128)(2,1)S(1)}, bf16[160,512]{1,0:T(8,128)(2,1)}, u32[]{:S(2)}, u32[]{:S(2)}) collective-permute-start(bf16[160,512]{1,0:T(8,128)(2,1)S(1)} %get-tuple-element.43.refs_0_), channel_id=1, source_target_pairs={{1,0},{0,1},{3,2},{2,3},{5,4},{4,5},{7,6},{6,7},{9,8},{8,9},{11,10... | collective-permute-start | bytes 491528 | tf_op jit(solution)/shard_map/ppermute | solution.py:248
  10.7 1.6 %collective-permute-done.1.refs_1_ = bf16[320,512]{1,0:T(8,128)(2,1)} collective-permute-done((bf16[320,512]{1,0:T(8,128)(2,1)}, bf16[320,512]{1,0:T(8,128)(2,1)}, u32[]{:S(2)}, u32[]{:S(2)}) %collective-permute-start.1) | collective-permute-done | bytes 327712 | tf_op jit(solution)/shard_map/ppermute | solution.py:248
  12.4 1.2 %copy-done.1 = bf16[512,1024]{1,0:T(8,128)(2,1)S(1)} copy-done((bf16[512,1024]{1,0:T(8,128)(2,1)S(1)}, bf16[512,1024]{1,0:T(8,128)(2,1)}, u32[]{:S(2)}) %copy-start.1) | copy-done | bytes 1048600
  13.6 1.0 %copy-done.3 = bf16[320,512]{1,0:T(8,128)(2,1)S(1)} copy-done((bf16[320,512]{1,0:T(8,128)(2,1)S(1)}, bf16[320,512]{1,0:T(8,128)(2,1)}, u32[]{:S(2)}) %copy-start.3) | copy-done | bytes 327704
  14.6 0.9 %copy-done.5 = f32[20,8,160]{2,1,0:T(8,128)S(1)} copy-done((f32[20,8,160]{2,1,0:T(8,128)S(1)}, f32[20,8,160]{2,1,0:T(8,128)}, u32[]{:S(2)}) %copy-start.5) | copy-done | bytes 102424
  15.5 4.5 %attend.1 = (bf16[2,160,1536]{2,1,0:T(8,128)(2,1)S(1)}, bf16[2,8,160,160]{3,2,1,0:T(8,128)(2,1)S(1)}, bf16[2,160,1024]{2,1,0:T(8,128)(2,1)S(1)}, f32[2,160,128]{...) custom-call(s32[1]{0:T(128)} %bitcast.me_ref, bf16[320,512]{1,0:T(8,128)(2,1)S(1)} %copy-done.3, ...), custom_call_target="tpu_custom_call" | custom-call | flops 4000000000 | bytes 8000000 | tf_op jit(solution)/shard_map/attend/pallas_call | solution.py:314
  20.0 4.5 %attend_back.2 = (f32[160,512]{1,0:T(8,128)S(1)}, bf16[160,512]{1,0:T(8,128)(2,1)S(1)}, f32[1,1024]{1,0:T(1,128)S(1)}, f32[20,8,160]{2,1,0:T(8,128)S(1)}) custom-call(s32[1]{0:T(128)} %bitcast.me_ref, bf16[160,512]{1,0:T(8,128)(2,1)S(1)} %get-tuple-element.53.refs_0_, bf16[160,512]{1,0:T(8,128)(2,1)} %collective-permute-done.2.refs_1_, ...), custom_call_target="tpu_custom_call" | custom-call | flops 4000000000 | tf_op jit(solution)/shard_map/attend_back/pallas_call | solution.py:344
  24.5 2.3 %collective-permute-start.10 = (bf16[2,160,512]{2,1,0:T(8,128)(2,1)S(1)}, bf16[2,160,512]{2,1,0:T(8,128)(2,1)S(1)}, u32[]{:S(2)}, u32[]{:S(2)}) collective-permute-start(bf16[2,160,512]{2,1,0:T(8,128)(2,1)S(1)} %get-tuple-element.65), channel_id=1, source_target_pairs={{1,0},{0,1},{3,2},{2,3},{5,4},{4,5},{7,6},{6,7},{9,8},{8,9},{11,10... | collective-permute-start | bytes 983048 | tf_op jit(solution)/shard_map/ppermute | solution.py:248
  26.9 4.5 %attend_back.3 = (f32[160,512]{1,0:T(8,128)S(1)}, bf16[160,512]{1,0:T(8,128)(2,1)S(1)}, f32[8,512]{1,0:T(8,128)S(1)}) custom-call(s32[1]{0:T(128)} %bitcast.me_ref, bf16[160,512]{1,0:T(8,128)(2,1)S(1)} %get-tuple-element.43.refs_0_, bf16[160,512]{1,0:T(8,128)(2,1)} %collective-permute-done.refs_1_, f32[1,1024]{1,0:T(1,128)S(1)} %get-tuple-element.44.refs_2_, ...), custom_call_target="tpu_custom_call" | custom-call | flops 4000000000 | tf_op jit(solution)/shard_map/attend_back/pallas_call | solution.py:344
  31.5 1.7 %collective-permute-start.4 = (f32[8,512]{1,0:T(8,128)S(1)}, f32[8,512]{1,0:T(8,128)S(1)}, u32[]{:S(2)}, u32[]{:S(2)}) collective-permute-start(f32[8,512]{1,0:T(8,128)S(1)} %get-tuple-element.60), channel_id=1, source_target_pairs={{16,0},{24,8},{0,16},{8,24},{17,1},{25,9},{1,17},{9,25},{18,2},{26... | collective-permute-start | bytes 49160 | tf_op jit(solution)/shard_map/ppermute | solution.py:264
  33.4 1.9 %collective-permute-start.11 = (bf16[160,512]{1,0:T(8,128)(2,1)S(1)}, bf16[160,512]{1,0:T(8,128)(2,1)S(1)}, u32[]{:S(2)}, u32[]{:S(2)}) collective-permute-start(bf16[160,512]{1,0:T(8,128)(2,1)S(1)} %get-tuple-element.66), channel_id=1, source_target_pairs={{1,0},{0,1},{3,2},{2,3},{5,4},{4,5},{7,6},{6,7},{9,8},{8,9},{11,10... | collective-permute-start | bytes 491528 | tf_op jit(solution)/shard_map/ppermute | solution.py:248
  35.3 1.1 %collective-permute-done.5 = f32[8,512]{1,0:T(8,128)S(1)} collective-permute-done((f32[8,512]{1,0:T(8,128)S(1)}, f32[8,512]{1,0:T(8,128)S(1)}, u32[]{:S(2)}, u32[]{:S(2)}) %collective-permute-start.5) | collective-permute-done | bytes 16416 | tf_op jit(solution)/shard_map/ppermute | solution.py:264
  36.4 1.7 %collective-permute-start.7 = (f32[8,512]{1,0:T(8,128)S(1)}, f32[8,512]{1,0:T(8,128)S(1)}, u32[]{:S(2)}, u32[]{:S(2)}) collective-permute-start(f32[8,512]{1,0:T(8,128)S(1)} %add_add_fusion.1), channel_id=1, source_target_pairs={{2,0},{0,2},{6,4},{4,6},{3,1},{1,3},{7,5},{5,7},{10,8},{8,10},{14,... | collective-permute-start | bytes 49160 | tf_op jit(solution)/shard_map/ppermute | solution.py:264
  38.1 2.6 %collective-permute-start.8 = (f32[8,512]{1,0:T(8,128)S(1)}, f32[8,512]{1,0:T(8,128)S(1)}, u32[]{:S(2)}, u32[]{:S(2)}) collective-permute-start(f32[8,512]{1,0:T(8,128)S(1)} %add_add_fusion.1), channel_id=1, source_target_pairs={{4,0},{6,2},{0,4},{2,6},{5,1},{7,3},{1,5},{3,7},{12,8},{14,10},{8,... | collective-permute-start | bytes 49160 | tf_op jit(solution)/shard_map/ppermute | solution.py:264
  40.9 0.8 %finish_out.1 = bf16[320,512]{1,0:T(8,128)(2,1)} custom-call(f32[2,160,512]{2,1,0:T(8,128)S(1)} %get-tuple-element.64.own_ref, bf16[2,160,512]{2,1,0:T(8,128)(2,1)S(1)} %collective-permute-done.10.refs_0_), custom_call_target="tpu_custom_call" | custom-call | bytes 1500000 | tf_op jit(solution)/shard_map/finish_out/pallas_call | solution.py:364
  41.7 1.1 %collective-permute-done.8 = f32[8,512]{1,0:T(8,128)S(1)} collective-permute-done((f32[8,512]{1,0:T(8,128)S(1)}, f32[8,512]{1,0:T(8,128)S(1)}, u32[]{:S(2)}, u32[]{:S(2)}) %collective-permute-start.8) | collective-permute-done | bytes 16416 | tf_op jit(solution)/shard_map/ppermute | solution.py:264
  42.8 3.4 %collective-permute-done.9 = f32[8,512]{1,0:T(8,128)S(1)} collective-permute-done((f32[8,512]{1,0:T(8,128)S(1)}, f32[8,512]{1,0:T(8,128)S(1)}, u32[]{:S(2)}, u32[]{:S(2)}) %collective-permute-start.9) | collective-permute-done | bytes 16416 | tf_op jit(solution)/shard_map/ppermute | solution.py:264
  46.2 1.8 %collective-permute-start.12 = (f32[8,128]{1,0:T(8,128)S(1)}, f32[8,128]{1,0:T(8,128)S(1)}, u32[]{:S(2)}, u32[]{:S(2)}) collective-permute-start(f32[8,128]{1,0:T(8,128)S(1)} %slice.12.refs_0_), channel_id=1, source_target_pairs={{1,0},{0,1},{3,2},{2,3},{5,4},{4,5},{7,6},{6,7},{9,8},{8,9},{11,10... | collective-permute-start | bytes 12296 | tf_op jit(solution)/shard_map/ppermute | solution.py:248
  48.0 0.9 %finish_grad.1 = (bf16[320,512]{1,0:T(8,128)(2,1)}, f32[8,39]{1,0:T(8,128)}) custom-call(f32[8,512]{1,0:T(8,128)S(1)} %add_add_fusion.small_ref, f32[160,512]{1,0:T(8,128)S(1)} %get-tuple-element.72.refs_0_, f32[160,512]{1,0:T(8,128)S(1)} %get-tuple-element.73.refs_1_, bf16[160,512]{1,0:T(8,128)(2,1)S(1)} %collective-permute-done.6.refs_2_, ...), custom_call_target="tpu_custom_call" | custom-call | bytes 1500000 | tf_op jit(solution)/shard_map/finish_grad/pallas_call | solution.py:377
  48.9 0.9 %collective-permute-done.12.refs_1_ = f32[8,128]{1,0:T(8,128)S(1)} collective-permute-done((f32[8,128]{1,0:T(8,128)S(1)}, f32[8,128]{1,0:T(8,128)S(1)}, u32[]{:S(2)}, u32[]{:S(2)}) %collective-permute-start.12) | collective-permute-done | bytes 4128 | tf_op jit(solution)/shard_map/ppermute | solution.py:248
  (29 shorter events, 2.0 us)
Async XLA Ops:
  0.6 11.7 %collective-permute-start.1 = (bf16[320,512]{1,0:T(8,128)(2,1)}, bf16[320,512]{1,0:T(8,128)(2,1)}, u32[]{:S(2)}, u32[]{:S(2)}) collective-permute-start(bf16[320,512]{1,0:T(8,128)(2,1)} %bitcast.10), channel_id=1, source_target_pairs={{1,0},{0,1},{3,2},{2,3},{5,4},{4,5},{7,6},{6,7},{9,8},{8,9},{11,10... | collective-permute-start | bytes 983048 | tf_op jit(solution)/shard_map/ppermute | solution.py:248
  4.6 3.4 %copy-start.6 = (bf16[1,20,16,512]{3,2,1,0:T(8,128)(2,1)S(1)}, bf16[1,20,16,512]{3,2,1,0:T(8,128)(2,1)}, u32[]{:S(2)}) copy-start(bf16[1,20,16,512]{3,2,1,0:T(8,128)(2,1)} %param.9) | copy-start | bytes 983044
  7.0 1.0 %copy-start = (bf16[512,1024]{1,0:T(8,128)(2,1)}, bf16[512,1024]{1,0:T(8,128)(2,1)S(1)}, u32[]{:S(2)}) copy-start(bf16[512,1024]{1,0:T(8,128)(2,1)S(1)} %get-tuple-element.48.refs_5_.refs_8_) | copy-start | bytes 3145732
  8.0 0.7 %copy-start.2 = (bf16[320,512]{1,0:T(8,128)(2,1)}, bf16[320,512]{1,0:T(8,128)(2,1)S(1)}, u32[]{:S(2)}) copy-start(bf16[320,512]{1,0:T(8,128)(2,1)S(1)} %get-tuple-element.45.refs_0_) | copy-start | bytes 983044
  8.0 0.8 %copy-start.4 = (f32[20,8,160]{2,1,0:T(8,128)}, f32[20,8,160]{2,1,0:T(8,128)S(1)}, u32[]{:S(2)}) copy-start(f32[20,8,160]{2,1,0:T(8,128)S(1)} %get-tuple-element.46.refs_3_) | copy-start | bytes 307204
  8.7 11.3 %collective-permute-start.2 = (bf16[160,512]{1,0:T(8,128)(2,1)S(1)}, bf16[160,512]{1,0:T(8,128)(2,1)}, u32[]{:S(2)}, u32[]{:S(2)}) collective-permute-start(bf16[160,512]{1,0:T(8,128)(2,1)S(1)} %get-tuple-element.53.refs_0_), channel_id=1, source_target_pairs={{1,0},{0,1},{3,2},{2,3},{5,4},{4,5},{7,6},{6,7},{9,8},{8,9},{11,10... | collective-permute-start | bytes 491528 | tf_op jit(solution)/shard_map/ppermute | solution.py:248
  8.8 18.1 %collective-permute-start = (bf16[160,512]{1,0:T(8,128)(2,1)S(1)}, bf16[160,512]{1,0:T(8,128)(2,1)}, u32[]{:S(2)}, u32[]{:S(2)}) collective-permute-start(bf16[160,512]{1,0:T(8,128)(2,1)S(1)} %get-tuple-element.43.refs_0_), channel_id=1, source_target_pairs={{1,0},{0,1},{3,2},{2,3},{5,4},{4,5},{7,6},{6,7},{9,8},{8,9},{11,10... | collective-permute-start | bytes 491528 | tf_op jit(solution)/shard_map/ppermute | solution.py:248
  12.3 1.2 %copy-start.1 = (bf16[512,1024]{1,0:T(8,128)(2,1)S(1)}, bf16[512,1024]{1,0:T(8,128)(2,1)}, u32[]{:S(2)}) copy-start(bf16[512,1024]{1,0:T(8,128)(2,1)} %copy-done) | copy-start | bytes 3145732
  13.6 1.0 %copy-start.3 = (bf16[320,512]{1,0:T(8,128)(2,1)S(1)}, bf16[320,512]{1,0:T(8,128)(2,1)}, u32[]{:S(2)}) copy-start(bf16[320,512]{1,0:T(8,128)(2,1)} %copy-done.2) | copy-start | bytes 983044
  14.5 0.9 %copy-start.5 = (f32[20,8,160]{2,1,0:T(8,128)S(1)}, f32[20,8,160]{2,1,0:T(8,128)}, u32[]{:S(2)}) copy-start(f32[20,8,160]{2,1,0:T(8,128)} %copy-done.4) | copy-start | bytes 307204
  24.5 16.3 %collective-permute-start.10 = (bf16[2,160,512]{2,1,0:T(8,128)(2,1)S(1)}, bf16[2,160,512]{2,1,0:T(8,128)(2,1)S(1)}, u32[]{:S(2)}, u32[]{:S(2)}) collective-permute-start(bf16[2,160,512]{2,1,0:T(8,128)(2,1)S(1)} %get-tuple-element.65), channel_id=1, source_target_pairs={{1,0},{0,1},{3,2},{2,3},{5,4},{4,5},{7,6},{6,7},{9,8},{8,9},{11,10... | collective-permute-start | bytes 983048 | tf_op jit(solution)/shard_map/ppermute | solution.py:248
  26.8 9.6 %collective-permute-start.6 = (bf16[160,512]{1,0:T(8,128)(2,1)S(1)}, bf16[160,512]{1,0:T(8,128)(2,1)S(1)}, u32[]{:S(2)}, u32[]{:S(2)}) collective-permute-start(bf16[160,512]{1,0:T(8,128)(2,1)S(1)} %get-tuple-element.59), channel_id=1, source_target_pairs={{1,0},{0,1},{3,2},{2,3},{5,4},{4,5},{7,6},{6,7},{9,8},{8,9},{11,10... | collective-permute-start | bytes 491528 | tf_op jit(solution)/shard_map/ppermute | solution.py:248
  31.4 1.9 %collective-permute-start.3 = (f32[8,512]{1,0:T(8,128)S(1)}, f32[8,512]{1,0:T(8,128)S(1)}, u32[]{:S(2)}, u32[]{:S(2)}) collective-permute-start(f32[8,512]{1,0:T(8,128)S(1)} %get-tuple-element.60), channel_id=1, source_target_pairs={{8,0},{0,8},{24,16},{16,24},{9,1},{1,9},{25,17},{17,25},{10,2},{2,... | collective-permute-start | bytes 49160 | tf_op jit(solution)/shard_map/ppermute | solution.py:264
  31.5 3.8 %collective-permute-start.4 = (f32[8,512]{1,0:T(8,128)S(1)}, f32[8,512]{1,0:T(8,128)S(1)}, u32[]{:S(2)}, u32[]{:S(2)}) collective-permute-start(f32[8,512]{1,0:T(8,128)S(1)} %get-tuple-element.60), channel_id=1, source_target_pairs={{16,0},{24,8},{0,16},{8,24},{17,1},{25,9},{1,17},{9,25},{18,2},{26... | collective-permute-start | bytes 49160 | tf_op jit(solution)/shard_map/ppermute | solution.py:264
  33.2 3.2 %collective-permute-start.5 = (f32[8,512]{1,0:T(8,128)S(1)}, f32[8,512]{1,0:T(8,128)S(1)}, u32[]{:S(2)}, u32[]{:S(2)}) collective-permute-start(f32[8,512]{1,0:T(8,128)S(1)} %get-tuple-element.60), channel_id=1, source_target_pairs={{24,0},{16,8},{8,16},{0,24},{25,1},{17,9},{9,17},{1,25},{26,2},{18... | collective-permute-start | bytes 49160 | tf_op jit(solution)/shard_map/ppermute | solution.py:264
  33.4 8.3 %collective-permute-start.11 = (bf16[160,512]{1,0:T(8,128)(2,1)S(1)}, bf16[160,512]{1,0:T(8,128)(2,1)S(1)}, u32[]{:S(2)}, u32[]{:S(2)}) collective-permute-start(bf16[160,512]{1,0:T(8,128)(2,1)S(1)} %get-tuple-element.66), channel_id=1, source_target_pairs={{1,0},{0,1},{3,2},{2,3},{5,4},{4,5},{7,6},{6,7},{9,8},{8,9},{11,10... | collective-permute-start | bytes 491528 | tf_op jit(solution)/shard_map/ppermute | solution.py:248
  36.4 5.3 %collective-permute-start.7 = (f32[8,512]{1,0:T(8,128)S(1)}, f32[8,512]{1,0:T(8,128)S(1)}, u32[]{:S(2)}, u32[]{:S(2)}) collective-permute-start(f32[8,512]{1,0:T(8,128)S(1)} %add_add_fusion.1), channel_id=1, source_target_pairs={{2,0},{0,2},{6,4},{4,6},{3,1},{1,3},{7,5},{5,7},{10,8},{8,10},{14,... | collective-permute-start | bytes 49160 | tf_op jit(solution)/shard_map/ppermute | solution.py:264
  38.1 4.7 %collective-permute-start.8 = (f32[8,512]{1,0:T(8,128)S(1)}, f32[8,512]{1,0:T(8,128)S(1)}, u32[]{:S(2)}, u32[]{:S(2)}) collective-permute-start(f32[8,512]{1,0:T(8,128)S(1)} %add_add_fusion.1), channel_id=1, source_target_pairs={{4,0},{6,2},{0,4},{2,6},{5,1},{7,3},{1,5},{3,7},{12,8},{14,10},{8,... | collective-permute-start | bytes 49160 | tf_op jit(solution)/shard_map/ppermute | solution.py:264
  40.7 5.5 %collective-permute-start.9 = (f32[8,512]{1,0:T(8,128)S(1)}, f32[8,512]{1,0:T(8,128)S(1)}, u32[]{:S(2)}, u32[]{:S(2)}) collective-permute-start(f32[8,512]{1,0:T(8,128)S(1)} %add_add_fusion.1), channel_id=1, source_target_pairs={{6,0},{4,2},{2,4},{0,6},{7,1},{5,3},{3,5},{1,7},{14,8},{12,10},{10... | collective-permute-start | bytes 49160 | tf_op jit(solution)/shard_map/ppermute | solution.py:264
  46.2 3.7 %collective-permute-start.12 = (f32[8,128]{1,0:T(8,128)S(1)}, f32[8,128]{1,0:T(8,128)S(1)}, u32[]{:S(2)}, u32[]{:S(2)}) collective-permute-start(f32[8,128]{1,0:T(8,128)S(1)} %slice.12.refs_0_), channel_id=1, source_target_pairs={{1,0},{0,1},{3,2},{2,3},{5,4},{4,5},{7,6},{6,7},{9,8},{8,9},{11,10... | collective-permute-start | bytes 12296 | tf_op jit(solution)/shard_map/ppermute | solution.py:248

commit v7 on v6

--- a/solution.py
+++ b/solution.py
@@ -285,6 +285,7 @@
     x0 = inputs.reshape(total, width)
     g_bands = [out_grad[:, :, n * BAND:(n + 1) * BAND].reshape(rows, width) for n in range(bands)]
     x_parts = [x0] + [shifted(x0, "tm", k) for k in range(1, tm)]
+    g_parts = [[g] + [shifted(g, "tm", k) for k in range(1, tm)] for g in g_bands]
     me1 = me.astype(jnp.int32).reshape(1)
     gain = norm_gain.reshape(1, chans)
     spread = jnp.broadcast_to(pos_bias[:, :, None], (*pos_bias.shape, BAND)).reshape(group, -1)
@@ -297,11 +298,11 @@
         in_specs=[vmem] + [pl.BlockSpec(memory_space=pltpu.HBM)] * len(held),
         out_specs=[vmem] * 5,
         out_shape=[
-            jax.ShapeDtypeStruct((frames, group, rows), F32),
-            jax.ShapeDtypeStruct((total, width), BF16),
-            jax.ShapeDtypeStruct((chans, 3 * width), BF16),
-            jax.ShapeDtypeStruct((width, chans), BF16),
-            jax.ShapeDtypeStruct((1, chans), F32),
+            pltpu.VMEM((frames, group, rows), F32),
+            pltpu.VMEM((total, width), BF16),
+            pltpu.VMEM((chans, 3 * width), BF16),
+            pltpu.VMEM((width, chans), BF16),
+            pltpu.VMEM((1, chans), F32),
         ],
         scratch_shapes=[pltpu.SemaphoreType.DMA((len(held),))],
         compiler_params=params,
@@ -309,19 +310,17 @@
         name="stage",
     )(spread, *held)
     x_parts[0] = x0
-    g_bands, rel = lax.optimization_barrier((g_bands, rel))
-    g_parts = [[g] + [shifted(g, "tm", k) for k in range(1, tm)] for g in g_bands]
     qkv, probs, xb, inv, mix_own, *mix_out = pl.pallas_call(
         functools.partial(forward_kernel, dims),
         in_specs=[smem] + [vmem] * (tm + 4),
         out_specs=[vmem] * (5 + tm - 1),
         out_shape=[
-            jax.ShapeDtypeStruct((bands, rows, 3 * width), BF16),
-            jax.ShapeDtypeStruct((bands, group, rows, rows), BF16),
-            jax.ShapeDtypeStruct((bands, rows, chans), BF16),
-            jax.ShapeDtypeStruct((bands, rows, LANES), F32),
-            jax.ShapeDtypeStruct((bands, rows, width), F32),
-        ] + [jax.ShapeDtypeStruct((bands, rows, width), BF16)] * (tm - 1),
+            pltpu.VMEM((bands, rows, 3 * width), BF16),
+            pltpu.VMEM((bands, group, rows, rows), BF16),
+            pltpu.VMEM((bands, rows, chans), BF16),
+            pltpu.VMEM((bands, rows, LANES), F32),
+            pltpu.VMEM((bands, rows, width), F32),
+        ] + [pltpu.VMEM((bands, rows, width), BF16)] * (tm - 1),
         scratch_shapes=[
             pltpu.VMEM((total, chans), BF16),
             pltpu.VMEM((bands, rows, chans), BF16),
@@ -331,6 +330,7 @@
         cost_estimate=pl.CostEstimate(flops=4_000_000_000, bytes_accessed=8_000_000, transcendentals=0),
         name="attend",
     )(me1, *x_parts, gain, rel, proj, w_out)
+    mix_in = [shifted(mix_out[k - 1], "tm", k) for k in range(1, tm)]
     owns, ins, carry = [], [], []
     diag = (frames, group, rows)
     for band in range(bands):
@@ -349,18 +349,16 @@
             + [jax.ShapeDtypeStruct((rows, width), BF16)] * (tm - 1) + extra,
             scratch_shapes=scratch,
             compiler_params=params,
-            cost_estimate=pl.CostEstimate(flops=4_000_000_000, bytes_accessed=0, transcendentals=0),
+            cost_estimate=pl.CostEstimate(flops=2_500_000_000, bytes_accessed=0, transcendentals=0),
             name="attend_back",
         )(me1, *g_parts[band], gain, qkv, probs, xb, inv, proj, w_out, *carry)
         sent, carry = rest[:tm - 1], rest[tm - 1:]
-        if band == 0:
-            sent, mix_out = lax.optimization_barrier((sent, mix_out))
-            mix_in = [shifted(mix_out[k - 1], "tm", k) for k in range(1, tm)]
         owns.append(own)
         ins += [shifted(sent[k - 1], "tm", k) for k in range(1, tm)]
 
     result = jax.ShapeDtypeStruct((total, width), BF16)
     finish_cost = pl.CostEstimate(flops=0, bytes_accessed=1_500_000, transcendentals=0)
+    small, (ins[:-1], mix_in) = group_sum(carry[0], "dp", (ins[:-1], mix_in))
     block_out = pl.pallas_call(
         functools.partial(finish_out_kernel, bands, frames),
         in_specs=[vmem] * tm,
@@ -370,7 +368,6 @@
         cost_estimate=finish_cost,
         name="finish_out",
     )(mix_own, *mix_in)
-    small, ins[:-1] = group_sum(carry[0], "dp", ins[:-1])
     small, (block_out, ins[-1]) = group_sum(small, "space", (block_out, ins[-1]))
     tile = small[:chans // LANES, :LANES]
     tiles = [shifted(tile, "tm", k) for k in range(1, tm)]

time: 50.8 us -> 43.7 us (0.86)
  local copies, waits for them, and re-layouts: 5.75 us -> 1.9 us
  Pallas kernels: 18.3 us -> 15.6 us
  starting transfers between devices: 17.5 us -> 16.6 us
  waiting for transfers between devices: 8.15 us -> 8.68 us
    unnamed x14 -> x0, local copies, waits for them, and re-layouts: 4.84 us -> none
    ppermute x7, waiting for transfers between devices: 2.56 us -> 4.55 us  [shifted(): lax.ppermute(value, axis, [((i + step) % count, i) for i in range(count)])]
    pallas_call x2, Pallas kernels: 9.09 us -> 7.32 us  [per_device(): pl.pallas_call(functools.partial(backward_kernel, dims, band, last), in_s...]
    ppermute x6, waiting for transfers between devices: 5.59 us -> 4.13 us  [group_sum(): parts.append(lax.ppermute(value, axis, pairs))]
    ppermute x7, starting transfers between devices: 11.1 us -> 10 us  [shifted(): lax.ppermute(value, axis, [((i + step) % count, i) for i in range(count)])]
    reshape x1, local copies, waits for them, and re-layouts: 0.02 us -> 1.02 us  [per_device(): out_grad[:, :, n * BAND:(n + 1) * BAND].reshape(rows, width)]
    pallas_call x1, Pallas kernels: 4.5 us -> 3.56 us  [per_device(): pl.pallas_call(functools.partial(forward_kernel, dims), in_specs=[smem] +...]
  transfers between devices with their start and end apart: 13 -> 13, of which waited for: 5 -> 5; matrix products, arithmetic and copies ran while one was open for 2% -> 4% of each run, Pallas kernels for 35% -> 34%
where the time goes in v7:
time: 43.7 us; the launch traced here: 43.5 us
  starting transfers between devices  16.6 us (38%)
  Pallas kernels  15.6 us (36%)
  waiting for transfers between devices  8.68 us (20%)
  local copies, waits for them, and re-layouts  1.9 us (4%)
  between operations  0.72 us (2%)
    ppermute x7, starting transfers between devices, shifted(): lax.ppermute(value, axis, [((i + step) % count, i) for i in range(count)])  10 us
    pallas_call x2, Pallas kernels, per_device(): pl.pallas_call(functools.partial(backward_kernel, dims, band, last), in_s...  7.32 us
    ppermute x6, starting transfers between devices, group_sum(): parts.append(lax.ppermute(value, axis, pairs))  6.6 us
    ppermute x7, waiting for transfers between devices, shifted(): lax.ppermute(value, axis, [((i + step) % count, i) for i in range(count)])  4.55 us
    ppermute x6, waiting for transfers between devices, group_sum(): parts.append(lax.ppermute(value, axis, pairs))  4.13 us
    pallas_call x1, Pallas kernels, per_device(): pl.pallas_call(functools.partial(forward_kernel, dims), in_specs=[smem] +...  3.56 us
    pallas_call x1, Pallas kernels, per_device(): pl.pallas_call(functools.partial(stage_kernel, frames, width), in_specs=[...  2.36 us
    reshape x1, local copies, waits for them, and re-layouts, per_device(): out_grad[:, :, n * BAND:(n + 1) * BAND].reshape(rows, width)  1.02 us
  transfers between devices with their start and end apart: 13, of which 5 were waited for; matrix products, arithmetic and copies ran while one was open for 4% of the time, Pallas kernels for 34%

profile of v7, /device:TPU:0, one launch (start us, length us, event | category | flops | bytes accessed | tf_op | source)
XLA Modules:
  0.0 43.5 jit_solution(8744337693954638649)
XLA Ops:
  0.6 3.0 %collective-permute-start.1 = (bf16[320,512]{1,0:T(8,128)(2,1)}, bf16[320,512]{1,0:T(8,128)(2,1)S(1)}, u32[]{:S(2)}, u32[]{:S(2)}) collective-permute-start(bf16[320,512]{1,0:T(8,128)(2,1)} %bitcast.10), channel_id=1, source_target_pairs={{1,0},{0,1},{3,2},{2,3},{5,4},{4,5},{7,6},{6,7},{9,8},{8,9},{11,10... | collective-permute-start | bytes 983048 | tf_op jit(solution)/shard_map/ppermute | solution.py:248
  3.7 1.0 %slice_bitcast_fusion = (bf16[160,512]{1,0:T(8,128)(2,1)S(1)}, bf16[160,512]{1,0:T(8,128)(2,1)S(1)}) fusion(bf16[1,20,16,512]{3,2,1,0:T(8,128)(2,1)} %param.9), kind=kLoop, calls=%fused_computation | loop fusion | bytes 655360 | tf_op jit(solution)/shard_map/reshape | solution.py:286
  4.7 0.1 collective-permute-start.2
  4.8 2.0 %collective-permute-start = (bf16[160,512]{1,0:T(8,128)(2,1)S(1)}, bf16[160,512]{1,0:T(8,128)(2,1)S(1)}, u32[]{:S(2)}, u32[]{:S(2)}) collective-permute-start(bf16[160,512]{1,0:T(8,128)(2,1)S(1)} %get-tuple-element.73.refs_0_), channel_id=1, source_target_pairs={{1,0},{0,1},{3,2},{2,3},{5,4},{4,5},{7,6},{6,7},{9,8},{8,9},{11,10... | collective-permute-start | bytes 491528 | tf_op jit(solution)/shard_map/ppermute | solution.py:248
  6.8 0.8 %broadcast_in_dim.2 = f32[8,39,8]{2,1,0:T(8,128)S(1)} broadcast(f32[8,39]{1,0:T(8,128)} %param.11), dimensions={0,1} | broadcast | bytes 11232 | tf_op jit(solution)/shard_map/broadcast_in_dim | solution.py:291
  7.6 0.1 reshape.38.bias_ref
  7.7 2.4 %stage.1 = (f32[20,8,160]{2,1,0:T(8,128)S(1)}, bf16[320,512]{1,0:T(8,128)(2,1)S(1)}, bf16[1024,1536]{1,0:T(8,128)(2,1)S(1)}, bf16[512,1024]{1,0:T(8,128)(2,1)S(1)}, f32[1,1024]{1,0:T(1,128)S(1)}) custom-call(f32[8,312]{1,0:T(8,128)S(1)} %reshape.38.bias_ref, bf16[320,512]{1,0:T(8,128)(2,1)} %bitcast.11, bf16[1024,512]{1,0:T(8,128)(2,1)} %wq_ref.1, ...), custom_call_target="tpu_custom_call" | custom-call | bytes 8000000 | tf_op jit(solution)/shard_map/stage/pallas_call | solution.py:296
  10.0 2.4 %collective-permute-done.1.refs_1_ = bf16[320,512]{1,0:T(8,128)(2,1)S(1)} collective-permute-done((bf16[320,512]{1,0:T(8,128)(2,1)}, bf16[320,512]{1,0:T(8,128)(2,1)S(1)}, u32[]{:S(2)}, u32[]{:S(2)}) %collective-permute-start.1) | collective-permute-done | bytes 327712 | tf_op jit(solution)/shard_map/ppermute | solution.py:248
  12.4 3.6 %attend.1 = (bf16[2,160,1536]{2,1,0:T(8,128)(2,1)S(1)}, bf16[2,8,160,160]{3,2,1,0:T(8,128)(2,1)S(1)}, bf16[2,160,1024]{2,1,0:T(8,128)(2,1)S(1)}, f32[2,160,128]{...) custom-call(s32[1]{0:T(128)} %bitcast.me_ref, ...), custom_call_target="tpu_custom_call" | custom-call | flops 4000000000 | bytes 8000000 | tf_op jit(solution)/shard_map/attend/pallas_call | solution.py:313
  16.0 2.1 %collective-permute-start.7 = (bf16[2,160,512]{2,1,0:T(8,128)(2,1)S(1)}, bf16[2,160,512]{2,1,0:T(8,128)(2,1)S(1)}, u32[]{:S(2)}, u32[]{:S(2)}) collective-permute-start(bf16[2,160,512]{2,1,0:T(8,128)(2,1)S(1)} %get-tuple-element.51), channel_id=1, source_target_pairs={{1,0},{0,1},{3,2},{2,3},{5,4},{4,5},{7,6},{6,7},{9,8},{8,9},{11,10... | collective-permute-start | bytes 983048 | tf_op jit(solution)/shard_map/ppermute | solution.py:248
  18.1 3.7 %attend_back.2 = (f32[160,512]{1,0:T(8,128)S(1)}, bf16[160,512]{1,0:T(8,128)(2,1)S(1)}, f32[1,1024]{1,0:T(1,128)S(1)}, f32[20,8,160]{2,1,0:T(8,128)S(1)}) custom-call(s32[1]{0:T(128)} %bitcast.me_ref, bf16[160,512]{1,0:T(8,128)(2,1)S(1)} %get-tuple-element.72.refs_0_, bf16[160,512]{1,0:T(8,128)(2,1)S(1)} %collective-permute-done.2.refs_1_, ...), custom_call_target="tpu_custom_call" | custom-call | flops 2500000000 | tf_op jit(solution)/shard_map/attend_back/pallas_call | solution.py:344
  21.8 3.7 %attend_back.3 = (f32[160,512]{1,0:T(8,128)S(1)}, bf16[160,512]{1,0:T(8,128)(2,1)S(1)}, f32[8,512]{1,0:T(8,128)S(1)}) custom-call(s32[1]{0:T(128)} %bitcast.me_ref, bf16[160,512]{1,0:T(8,128)(2,1)S(1)} %get-tuple-element.73.refs_0_, bf16[160,512]{1,0:T(8,128)(2,1)S(1)} %collective-permute-done.refs_1_, f32[1,1024]{1,0:T(1,128)S(1)} %get-tuple-element.38.refs_2_, ...), custom_call_target="tpu_custom_call" | custom-call | flops 2500000000 | tf_op jit(solution)/shard_map/attend_back/pallas_call | solution.py:344
  25.6 2.0 %collective-permute-start.4 = (f32[8,512]{1,0:T(8,128)S(1)}, f32[8,512]{1,0:T(8,128)S(1)}, u32[]{:S(2)}, u32[]{:S(2)}) collective-permute-start(f32[8,512]{1,0:T(8,128)S(1)} %get-tuple-element.52), channel_id=1, source_target_pairs={{16,0},{24,8},{0,16},{8,24},{17,1},{25,9},{1,17},{9,25},{18,2},{26... | collective-permute-start | bytes 49160 | tf_op jit(solution)/shard_map/ppermute | solution.py:264
  27.7 1.1 %collective-permute-done.5 = f32[8,512]{1,0:T(8,128)S(1)} collective-permute-done((f32[8,512]{1,0:T(8,128)S(1)}, f32[8,512]{1,0:T(8,128)S(1)}, u32[]{:S(2)}, u32[]{:S(2)}) %collective-permute-start.5) | collective-permute-done | bytes 16416 | tf_op jit(solution)/shard_map/ppermute | solution.py:264
  28.7 2.1 %collective-permute-start.11 = (bf16[160,512]{1,0:T(8,128)(2,1)S(1)}, bf16[160,512]{1,0:T(8,128)(2,1)S(1)}, u32[]{:S(2)}, u32[]{:S(2)}) collective-permute-start(bf16[160,512]{1,0:T(8,128)(2,1)S(1)} %get-tuple-element.58), channel_id=1, source_target_pairs={{1,0},{0,1},{3,2},{2,3},{5,4},{4,5},{7,6},{6,7},{9,8},{8,9},{11,10... | collective-permute-start | bytes 491528 | tf_op jit(solution)/shard_map/ppermute | solution.py:248
  30.9 3.7 %collective-permute-start.10 = (f32[8,512]{1,0:T(8,128)S(1)}, f32[8,512]{1,0:T(8,128)S(1)}, u32[]{:S(2)}, u32[]{:S(2)}) collective-permute-start(f32[8,512]{1,0:T(8,128)S(1)} %add_add_fusion.1), channel_id=1, source_target_pairs={{6,0},{4,2},{2,4},{0,6},{7,1},{5,3},{3,5},{1,7},{14,8},{12,10},{10... | collective-permute-start | bytes 49160 | tf_op jit(solution)/shard_map/ppermute | solution.py:264
  34.6 0.8 %collective-permute-start.8 = (f32[8,512]{1,0:T(8,128)S(1)}, f32[8,512]{1,0:T(8,128)S(1)}, u32[]{:S(2)}, u32[]{:S(2)}) collective-permute-start(f32[8,512]{1,0:T(8,128)S(1)} %add_add_fusion.1), channel_id=1, source_target_pairs={{2,0},{0,2},{6,4},{4,6},{3,1},{1,3},{7,5},{5,7},{10,8},{8,10},{14,... | collective-permute-start | bytes 49160 | tf_op jit(solution)/shard_map/ppermute | solution.py:264
  35.4 0.8 %finish_out.1 = bf16[320,512]{1,0:T(8,128)(2,1)} custom-call(f32[2,160,512]{2,1,0:T(8,128)S(1)} %get-tuple-element.56.own_ref, bf16[2,160,512]{2,1,0:T(8,128)(2,1)S(1)} %collective-permute-done.7.refs_0_), custom_call_target="tpu_custom_call" | custom-call | bytes 1500000 | tf_op jit(solution)/shard_map/finish_out/pallas_call | solution.py:362
  36.2 0.3 collective-permute-done.10
  36.5 2.7 %collective-permute-done.9 = f32[8,512]{1,0:T(8,128)S(1)} collective-permute-done((f32[8,512]{1,0:T(8,128)S(1)}, f32[8,512]{1,0:T(8,128)S(1)}, u32[]{:S(2)}, u32[]{:S(2)}) %collective-permute-start.9) | collective-permute-done | bytes 16416 | tf_op jit(solution)/shard_map/ppermute | solution.py:264
  39.2 0.6 %collective-permute-start.12 = (f32[8,128]{1,0:T(8,128)S(1)}, f32[8,128]{1,0:T(8,128)S(1)}, u32[]{:S(2)}, u32[]{:S(2)}) collective-permute-start(f32[8,128]{1,0:T(8,128)S(1)} %slice.12.refs_0_), channel_id=1, source_target_pairs={{1,0},{0,1},{3,2},{2,3},{5,4},{4,5},{7,6},{6,7},{9,8},{8,9},{11,10... | collective-permute-start | bytes 12296 | tf_op jit(solution)/shard_map/ppermute | solution.py:248
  39.8 0.9 %finish_grad.1 = (bf16[320,512]{1,0:T(8,128)(2,1)}, f32[8,39]{1,0:T(8,128)}) custom-call(f32[8,512]{1,0:T(8,128)S(1)} %add_add_fusion.small_ref, f32[160,512]{1,0:T(8,128)S(1)} %get-tuple-element.64.refs_0_, f32[160,512]{1,0:T(8,128)S(1)} %get-tuple-element.65.refs_1_, bf16[160,512]{1,0:T(8,128)(2,1)S(1)} %collective-permute-done.6.refs_2_, ...), custom_call_target="tpu_custom_call" | custom-call | bytes 1500000 | tf_op jit(solution)/shard_map/finish_grad/pallas_call | solution.py:374
  40.7 2.2 %collective-permute-done.12.refs_1_ = f32[8,128]{1,0:T(8,128)S(1)} collective-permute-done((f32[8,128]{1,0:T(8,128)S(1)}, f32[8,128]{1,0:T(8,128)S(1)}, u32[]{:S(2)}, u32[]{:S(2)}) %collective-permute-start.12) | collective-permute-done | bytes 4128 | tf_op jit(solution)/shard_map/ppermute | solution.py:248
  42.9 0.6 %gain_sum.1 = f32[1,512]{1,0:T(1,128)} custom-call(s32[1]{0:T(128)} %bitcast.me_ref, f32[8,128]{1,0:T(8,128)S(1)} %slice.12.refs_0_, f32[8,128]{1,0:T(8,128)S(1)} %collective-permute-done.12.refs_1_), custom_call_target="tpu_custom_call" | custom-call | tf_op jit(solution)/shard_map/gain_sum/pallas_call | solution.py:384
  (15 shorter events, 0.2 us)
Async XLA Ops:
  0.6 11.8 %collective-permute-start.1 = (bf16[320,512]{1,0:T(8,128)(2,1)}, bf16[320,512]{1,0:T(8,128)(2,1)S(1)}, u32[]{:S(2)}, u32[]{:S(2)}) collective-permute-start(bf16[320,512]{1,0:T(8,128)(2,1)} %bitcast.10), channel_id=1, source_target_pairs={{1,0},{0,1},{3,2},{2,3},{5,4},{4,5},{7,6},{6,7},{9,8},{8,9},{11,10... | collective-permute-start | bytes 983048 | tf_op jit(solution)/shard_map/ppermute | solution.py:248
  4.7 13.4 %collective-permute-start.2 = (bf16[160,512]{1,0:T(8,128)(2,1)S(1)}, bf16[160,512]{1,0:T(8,128)(2,1)S(1)}, u32[]{:S(2)}, u32[]{:S(2)}) collective-permute-start(bf16[160,512]{1,0:T(8,128)(2,1)S(1)} %get-tuple-element.72.refs_0_), channel_id=1, source_target_pairs={{1,0},{0,1},{3,2},{2,3},{5,4},{4,5},{7,6},{6,7},{9,8},{8,9},{11,10... | collective-permute-start | bytes 491528 | tf_op jit(solution)/shard_map/ppermute | solution.py:248
  4.8 17.1 %collective-permute-start = (bf16[160,512]{1,0:T(8,128)(2,1)S(1)}, bf16[160,512]{1,0:T(8,128)(2,1)S(1)}, u32[]{:S(2)}, u32[]{:S(2)}) collective-permute-start(bf16[160,512]{1,0:T(8,128)(2,1)S(1)} %get-tuple-element.73.refs_0_), channel_id=1, source_target_pairs={{1,0},{0,1},{3,2},{2,3},{5,4},{4,5},{7,6},{6,7},{9,8},{8,9},{11,10... | collective-permute-start | bytes 491528 | tf_op jit(solution)/shard_map/ppermute | solution.py:248
  16.0 14.9 %collective-permute-start.7 = (bf16[2,160,512]{2,1,0:T(8,128)(2,1)S(1)}, bf16[2,160,512]{2,1,0:T(8,128)(2,1)S(1)}, u32[]{:S(2)}, u32[]{:S(2)}) collective-permute-start(bf16[2,160,512]{2,1,0:T(8,128)(2,1)S(1)} %get-tuple-element.51), channel_id=1, source_target_pairs={{1,0},{0,1},{3,2},{2,3},{5,4},{4,5},{7,6},{6,7},{9,8},{8,9},{11,10... | collective-permute-start | bytes 983048 | tf_op jit(solution)/shard_map/ppermute | solution.py:248
  21.8 9.1 %collective-permute-start.6 = (bf16[160,512]{1,0:T(8,128)(2,1)S(1)}, bf16[160,512]{1,0:T(8,128)(2,1)S(1)}, u32[]{:S(2)}, u32[]{:S(2)}) collective-permute-start(bf16[160,512]{1,0:T(8,128)(2,1)S(1)} %get-tuple-element.50), channel_id=1, source_target_pairs={{1,0},{0,1},{3,2},{2,3},{5,4},{4,5},{7,6},{6,7},{9,8},{8,9},{11,10... | collective-permute-start | bytes 491528 | tf_op jit(solution)/shard_map/ppermute | solution.py:248
  25.5 3.2 %collective-permute-start.5 = (f32[8,512]{1,0:T(8,128)S(1)}, f32[8,512]{1,0:T(8,128)S(1)}, u32[]{:S(2)}, u32[]{:S(2)}) collective-permute-start(f32[8,512]{1,0:T(8,128)S(1)} %get-tuple-element.52), channel_id=1, source_target_pairs={{24,0},{16,8},{8,16},{0,24},{25,1},{17,9},{9,17},{1,25},{26,2},{18... | collective-permute-start | bytes 49160 | tf_op jit(solution)/shard_map/ppermute | solution.py:264
  25.6 5.3 %collective-permute-start.4 = (f32[8,512]{1,0:T(8,128)S(1)}, f32[8,512]{1,0:T(8,128)S(1)}, u32[]{:S(2)}, u32[]{:S(2)}) collective-permute-start(f32[8,512]{1,0:T(8,128)S(1)} %get-tuple-element.52), channel_id=1, source_target_pairs={{16,0},{24,8},{0,16},{8,24},{17,1},{25,9},{1,17},{9,25},{18,2},{26... | collective-permute-start | bytes 49160 | tf_op jit(solution)/shard_map/ppermute | solution.py:264
  27.6 3.2 %collective-permute-start.3 = (f32[8,512]{1,0:T(8,128)S(1)}, f32[8,512]{1,0:T(8,128)S(1)}, u32[]{:S(2)}, u32[]{:S(2)}) collective-permute-start(f32[8,512]{1,0:T(8,128)S(1)} %get-tuple-element.52), channel_id=1, source_target_pairs={{8,0},{0,8},{24,16},{16,24},{9,1},{1,9},{25,17},{17,25},{10,2},{2,... | collective-permute-start | bytes 49160 | tf_op jit(solution)/shard_map/ppermute | solution.py:264
  28.7 7.4 %collective-permute-start.11 = (bf16[160,512]{1,0:T(8,128)(2,1)S(1)}, bf16[160,512]{1,0:T(8,128)(2,1)S(1)}, u32[]{:S(2)}, u32[]{:S(2)}) collective-permute-start(bf16[160,512]{1,0:T(8,128)(2,1)S(1)} %get-tuple-element.58), channel_id=1, source_target_pairs={{1,0},{0,1},{3,2},{2,3},{5,4},{4,5},{7,6},{6,7},{9,8},{8,9},{11,10... | collective-permute-start | bytes 491528 | tf_op jit(solution)/shard_map/ppermute | solution.py:248
  30.9 5.6 %collective-permute-start.10 = (f32[8,512]{1,0:T(8,128)S(1)}, f32[8,512]{1,0:T(8,128)S(1)}, u32[]{:S(2)}, u32[]{:S(2)}) collective-permute-start(f32[8,512]{1,0:T(8,128)S(1)} %add_add_fusion.1), channel_id=1, source_target_pairs={{6,0},{4,2},{2,4},{0,6},{7,1},{5,3},{3,5},{1,7},{14,8},{12,10},{10... | collective-permute-start | bytes 49160 | tf_op jit(solution)/shard_map/ppermute | solution.py:264
  34.6 4.6 %collective-permute-start.9 = (f32[8,512]{1,0:T(8,128)S(1)}, f32[8,512]{1,0:T(8,128)S(1)}, u32[]{:S(2)}, u32[]{:S(2)}) collective-permute-start(f32[8,512]{1,0:T(8,128)S(1)} %add_add_fusion.1), channel_id=1, source_target_pairs={{4,0},{6,2},{0,4},{2,6},{5,1},{7,3},{1,5},{3,7},{12,8},{14,10},{8,... | collective-permute-start | bytes 49160 | tf_op jit(solution)/shard_map/ppermute | solution.py:264
  34.6 4.6 %collective-permute-start.8 = (f32[8,512]{1,0:T(8,128)S(1)}, f32[8,512]{1,0:T(8,128)S(1)}, u32[]{:S(2)}, u32[]{:S(2)}) collective-permute-start(f32[8,512]{1,0:T(8,128)S(1)} %add_add_fusion.1), channel_id=1, source_target_pairs={{2,0},{0,2},{6,4},{4,6},{3,1},{1,3},{7,5},{5,7},{10,8},{8,10},{14,... | collective-permute-start | bytes 49160 | tf_op jit(solution)/shard_map/ppermute | solution.py:264
  39.2 3.7 %collective-permute-start.12 = (f32[8,128]{1,0:T(8,128)S(1)}, f32[8,128]{1,0:T(8,128)S(1)}, u32[]{:S(2)}, u32[]{:S(2)}) collective-permute-start(f32[8,128]{1,0:T(8,128)S(1)} %slice.12.refs_0_), channel_id=1, source_target_pairs={{1,0},{0,1},{3,2},{2,3},{5,4},{4,5},{7,6},{6,7},{9,8},{8,9},{11,10... | collective-permute-start | bytes 12296 | tf_op jit(solution)/shard_map/ppermute | solution.py:248

commit v8 on v7

--- a/solution.py
+++ b/solution.py
@@ -117,23 +117,20 @@
     own_ref[...] = own + xb_ref[:, :, pl.ds(place(0), width)].astype(F32)
 
 
-def backward_kernel(dims, band, last, me_ref, *refs):
+def backward_kernel(dims, me_ref, *refs):
     tm, frames, pixels, width, group, head_dim, eps = dims
     g_refs = refs[:tm]
     gain_ref, qkv_ref, p_ref, xb_ref, inv_ref, proj_ref, wo_ref = refs[tm:tm + 7]
-    rest = list(refs[tm + 7:])
-    carried = (rest.pop(0), rest.pop(0)) if band else None
-    own_ref = rest.pop(0)
-    msg_refs = [rest.pop(0) for _ in range(tm - 1)]
-    small_ref = rest.pop(0) if last else None
-    gain_out = None if last else rest.pop(0)
-    diag_ref = rest.pop() if last else rest.pop(0)
-    gw_ref, ds_ref, grad_ref = rest
+    own_ref, small_ref = refs[tm + 7:tm + 9]
+    msg_refs = refs[tm + 9:tm + 9 + tm - 1]
+    gw_ref, da_ref, ds_ref, dqkv_ref, grad_ref, diag_ref = refs[tm + 9 + tm - 1:]
     me = me_ref[0]
     rows = frames * BAND
+    bands = pixels // BAND
     per_pair = LANES // head_dim
     scale = head_dim ** -0.5
     chans = width * tm
+    total = frames * pixels
 
     def place(k):
         return pl.multiple_of(lax.rem(me + k, tm) * width, width)
@@ -141,53 +138,56 @@
     for k in range(tm):
         gw_ref[:, pl.ds(place(k), width)] = g_refs[k][...]
     owner = head_lanes(head_dim, rows)
-    d_att = mm(gw_ref[...], wo_ref[...], NT).astype(BF16)
-    grads = [[], [], []]
-    for pair in range(width // LANES):
-        qp, kp, vp = (
-            qkv_ref[band, :, n * width + pair * LANES:n * width + (pair + 1) * LANES] for n in range(3)
-        )
-        da = d_att[:, pair * LANES:(pair + 1) * LANES]
-        d_prob = mm(stack_heads(da, owner, per_pair), vp, NT)
-        parts = [[], [], []]
-        for h in range(per_pair):
-            head = pair * per_pair + h
-            for f in range(0, frames, CHUNK):
-                at = slice(f * BAND, (f + CHUNK) * BAND)
-                full = p_ref[band, head, at, :].astype(F32)
-                t = d_prob[h * rows + f * BAND:h * rows + (f + CHUNK) * BAND]
-                score = full * (t - jnp.sum(full * t, axis=-1, keepdims=True))
-                ds_ref[head, at, :] = (score * scale).astype(BF16)
-                part = jnp.sum(score.reshape(CHUNK, BAND, rows), axis=1, keepdims=True)
-                if carried is not None:
-                    part = part + carried[1][f:f + CHUNK, head:head + 1, :]
-                diag_ref[f:f + CHUNK, head:head + 1, :] = part
-            probs, score = p_ref[band, head], ds_ref[head]
-            parts[0].append(mm(score, kp))
-            parts[1].append(mm(score, qp, TN))
-            parts[2].append(mm(probs, da, TN))
-        for n in range(3):
-            grads[n].append(pick_heads(parts[n], owner).astype(BF16))
-    grad_ref[...] = mm(jnp.concatenate(grads[0] + grads[1] + grads[2], axis=1), proj_ref[...], NT)
+    d_att = mm(gw_ref[...], wo_ref[...], NT).reshape(frames, bands, BAND, width)
+    for band in range(bands):
+        da_ref[band] = d_att[:, band].reshape(rows, width).astype(BF16)
+    for band in range(bands):
+        for pair in range(width // LANES):
+            cols = [slice(n * width + pair * LANES, n * width + (pair + 1) * LANES) for n in range(3)]
+            qp, kp, vp = (qkv_ref[band, :, c] for c in cols)
+            da = da_ref[band, :, pair * LANES:(pair + 1) * LANES]
+            d_prob = mm(stack_heads(da, owner, per_pair), vp, NT)
+            parts = [[], [], []]
+            for h in range(per_pair):
+                head = pair * per_pair + h
+                for f in range(0, frames, CHUNK):
+                    at = slice(f * BAND, (f + CHUNK) * BAND)
+                    full = p_ref[band, head, at, :].astype(F32)
+                    t = d_prob[h * rows + f * BAND:h * rows + (f + CHUNK) * BAND]
+                    score = full * (t - jnp.sum(full * t, axis=-1, keepdims=True))
+                    ds_ref[band, head, at, :] = (score * scale).astype(BF16)
+                    part = jnp.sum(score.reshape(CHUNK, BAND, rows), axis=1, keepdims=True)
+                    if band:
+                        part = part + diag_ref[f:f + CHUNK, head:head + 1, :]
+                    diag_ref[f:f + CHUNK, head:head + 1, :] = part
+                probs, score = p_ref[band, head], ds_ref[band, head]
+                parts[0].append(mm(score, kp))
+                parts[1].append(mm(score, qp, TN))
+                parts[2].append(mm(probs, da, TN))
+            for n in range(3):
+                dqkv_ref[band, :, cols[n]] = pick_heads(parts[n], owner).astype(BF16)
+    grad = mm(dqkv_ref[...].reshape(total, 3 * width), proj_ref[...], NT)
+    grad_ref[...] = grad.reshape(bands, rows, chans)
     gain_sum = jnp.zeros((BAND, chans), F32)
     for f in range(0, frames, 2):
         at = slice(f * BAND, (f + 2) * BAND)
-        grad, x = grad_ref[at, :], xb_ref[band, at, :].astype(F32)
-        inv = inv_ref[band, at, :1]
-        scaled = x * inv
-        gain_sum = gain_sum + jnp.sum((grad * scaled).reshape(2, BAND, chans), axis=0)
-        term = grad * gain_ref[...]
-        inner = jnp.mean(term * scaled, axis=-1, keepdims=True)
-        grad_ref[at, :] = inv * (term - scaled * inner)
+        for band in range(bands):
+            grad, x = grad_ref[band, at, :], xb_ref[band, at, :].astype(F32)
+            inv = inv_ref[band, at, :1]
+            scaled = x * inv
+            gain_sum = gain_sum + jnp.sum((grad * scaled).reshape(2, BAND, chans), axis=0)
+            term = grad * gain_ref[...]
+            inner = jnp.mean(term * scaled, axis=-1, keepdims=True)
+            grad_ref[band, at, :] = inv * (term - scaled * inner)
     for k in range(1, tm):
-        msg_refs[k - 1][...] = grad_ref[:, pl.ds(place(tm - k), width)].astype(BF16)
-    own_ref[...] = grad_ref[:, pl.ds(place(0), width)] + g_refs[0][...].astype(F32)
+        msg_refs[k - 1][...] = grad_ref[:, :, pl.ds(place(tm - k), width)].astype(BF16)
+    for f in range(0, frames, 2):
+        at = slice(f * BAND, (f + 2) * BAND)
+        both = g_refs[0][f * pixels:(f + 2) * pixels, :].astype(F32).reshape(2, bands, BAND, width)
+        for band in range(bands):
+            own = grad_ref[band, at, pl.ds(place(0), width)]
+            own_ref[band, at, :] = own + both[:, band].reshape(2 * BAND, width)
     gain_sum = jnp.sum(gain_sum, axis=0, keepdims=True)
-    if carried is not None:
-        gain_sum = gain_sum + carried[0][...]
-    if not last:
-        gain_out[...] = gain_sum
-        return
     small_ref[...] = jnp.zeros_like(small_ref)
     for r in range(chans // LANES):
         small_ref[r:r + 1, :LANES] = gain_sum[:, r * LANES:(r + 1) * LANES]
@@ -199,21 +199,22 @@
     small_ref[:group, LANES:] = bias
 
 
-def finish_kernel(bands, frames, own_refs, in_refs, out_ref):
-    each = len(in_refs) // bands
+def finish_kernel(own_ref, in_refs, out_ref):
+    bands, rows, width = own_ref.shape
+    frames = rows // BAND
     parts = []
     for band in range(bands):
-        value = own_refs[band][...]
-        for ref in in_refs[band * each:(band + 1) * each]:
-            value = value + ref[...].astype(F32)
-        parts.append(value.reshape(frames, 1, BAND, value.shape[-1]))
+        value = own_ref[band]
+        for ref in in_refs:
+            value = value + ref[band].astype(F32)
+        parts.append(value.reshape(frames, 1, BAND, width))
     value = jnp.concatenate(parts, axis=1)
     out_ref[...] = value.reshape(out_ref.shape).astype(out_ref.dtype)
 
 
-def finish_grad_kernel(bands, frames, small_ref, *refs):
-    *refs, out_ref, bias_ref = refs
-    finish_kernel(bands, frames, refs[:bands], refs[bands:], out_ref)
+def finish_grad_kernel(small_ref, own_ref, *refs):
+    *in_refs, out_ref, bias_ref = refs
+    finish_kernel(own_ref, in_refs, out_ref)
     group, offsets = bias_ref.shape
     value = small_ref[:, LANES:]
     high = value.astype(BF16)
@@ -227,9 +228,8 @@
     bias_ref[...] = total[:group, :offsets]
 
 
-def finish_out_kernel(bands, frames, own_ref, *refs):
-    in_refs = [ref.at[band] for band in range(bands) for ref in refs[:-1]]
-    finish_kernel(bands, frames, [own_ref.at[band] for band in range(bands)], in_refs, refs[-1])
+def finish_out_kernel(own_ref, *refs):
+    finish_kernel(own_ref, refs[:-1], refs[-1])
 
 
 def gain_kernel(me_ref, *refs):
@@ -248,24 +248,17 @@
     return lax.ppermute(value, axis, [((i + step) % count, i) for i in range(count)])
 
 
-def group_sum(value, axis, beside=()):
+def group_sum(value, axis):
     count = lax.axis_size(axis)
-    stride = 1
-    while stride < count:
-        left = count // stride
-        radix = 4 if left % 4 == 0 else 2 if left % 2 == 0 else left
-        parts = [value]
-        for step in range(1, radix):
-            pairs = []
-            for i in range(count):
-                digit = i // stride % radix
-                other = digit ^ step if radix in (2, 4) else (digit + step) % radix
-                pairs.append((i + (other - digit) * stride, i))
-            parts.append(lax.ppermute(value, axis, pairs))
-        parts, beside = lax.optimization_barrier((parts, beside))
-        value = sum(parts[1:], parts[0])
-        stride *= radix
-    return value, beside
+    step = 1
+    while count % (2 * step) == 0:
+        value = value + lax.ppermute(value, axis, [(i ^ step, i) for i in range(count)])
+        step *= 2
+    odd = count // step
+    if odd > 1:
+        pairs = [[((i + k * step) % count, i) for i in range(count)] for k in range(1, odd)]
+        value = sum((lax.ppermute(value, axis, p) for p in pairs), value)
+    return value
 
 
 def per_device(inputs, out_grad, norm_gain, pos_bias, w_query, w_key, w_value, w_out):
@@ -282,10 +275,9 @@
     span = -(-offsets * BAND // LANES) * LANES
     lines = -(-max(chans // LANES, group) // BAND) * BAND
     dims = (tm, frames, pixels, width, group, head_dim, 1e-06)
-    x0 = inputs.reshape(total, width)
-    g_bands = [out_grad[:, :, n * BAND:(n + 1) * BAND].reshape(rows, width) for n in range(bands)]
+    x0, g0 = inputs.reshape(total, width), out_grad.reshape(total, width)
     x_parts = [x0] + [shifted(x0, "tm", k) for k in range(1, tm)]
-    g_parts = [[g] + [shifted(g, "tm", k) for k in range(1, tm)] for g in g_bands]
+    g_parts = [g0] + [shifted(g0, "tm", k) for k in range(1, tm)]
     me1 = me.astype(jnp.int32).reshape(1)
     gain = norm_gain.reshape(1, chans)
     spread = jnp.broadcast_to(pos_bias[:, :, None], (*pos_bias.shape, BAND)).reshape(group, -1)
@@ -331,36 +323,31 @@
         name="attend",
     )(me1, *x_parts, gain, rel, proj, w_out)
     mix_in = [shifted(mix_out[k - 1], "tm", k) for k in range(1, tm)]
-    owns, ins, carry = [], [], []
-    diag = (frames, group, rows)
-    for band in range(bands):
-        last = band == bands - 1
-        scratch = [pltpu.VMEM((rows, chans), BF16), pltpu.VMEM((group, rows, rows), BF16), pltpu.VMEM((rows, chans), F32)]
-        if last:
-            extra = [jax.ShapeDtypeStruct((lines, LANES + span), F32)]
-            scratch.append(pltpu.VMEM(diag, F32))
-        else:
-            extra = [jax.ShapeDtypeStruct((1, chans), F32), jax.ShapeDtypeStruct(diag, F32)]
-        own, *rest = pl.pallas_call(
-            functools.partial(backward_kernel, dims, band, last),
-            in_specs=[smem] + [vmem] * (tm + 7 + len(carry)),
-            out_specs=[vmem] * (tm + len(extra)),
-            out_shape=[jax.ShapeDtypeStruct((rows, width), F32)]
-            + [jax.ShapeDtypeStruct((rows, width), BF16)] * (tm - 1) + extra,
-            scratch_shapes=scratch,
-            compiler_params=params,
-            cost_estimate=pl.CostEstimate(flops=2_500_000_000, bytes_accessed=0, transcendentals=0),
-            name="attend_back",
-        )(me1, *g_parts[band], gain, qkv, probs, xb, inv, proj, w_out, *carry)
-        sent, carry = rest[:tm - 1], rest[tm - 1:]
-        owns.append(own)
-        ins += [shifted(sent[k - 1], "tm", k) for k in range(1, tm)]
-
+    grad_own, small, *grad_out = pl.pallas_call(
+        functools.partial(backward_kernel, dims),
+        in_specs=[smem] + [vmem] * (tm + 7),
+        out_specs=[vmem] * (2 + tm - 1),
+        out_shape=[
+            pltpu.VMEM((bands, rows, width), F32),
+            pltpu.VMEM((lines, LANES + span), F32),
+        ] + [pltpu.VMEM((bands, rows, width), BF16)] * (tm - 1),
+        scratch_shapes=[
+            pltpu.VMEM((total, chans), BF16),
+            pltpu.VMEM((bands, rows, width), BF16),
+            pltpu.VMEM((bands, group, rows, rows), BF16),
+            pltpu.VMEM((bands, rows, 3 * width), BF16),
+            pltpu.VMEM((bands, rows, chans), F32),
+            pltpu.VMEM((frames, group, rows), F32),
+        ],
+        compiler_params=params,
+        cost_estimate=pl.CostEstimate(flops=6_000_000_000, bytes_accessed=0, transcendentals=0),
+        name="attend_back",
+    )(me1, *g_parts, gain, qkv, probs, xb, inv, proj, w_out)
+    grad_in = [shifted(grad_out[k - 1], "tm", k) for k in range(1, tm)]
     result = jax.ShapeDtypeStruct((total, width), BF16)
     finish_cost = pl.CostEstimate(flops=0, bytes_accessed=1_500_000, transcendentals=0)
-    small, (ins[:-1], mix_in) = group_sum(carry[0], "dp", (ins[:-1], mix_in))
     block_out = pl.pallas_call(
-        functools.partial(finish_out_kernel, bands, frames),
+        finish_out_kernel,
         in_specs=[vmem] * tm,
         out_specs=vmem,
         out_shape=result,
@@ -368,18 +355,19 @@
         cost_estimate=finish_cost,
         name="finish_out",
     )(mix_own, *mix_in)
-    small, (block_out, ins[-1]) = group_sum(small, "space", (block_out, ins[-1]))
+    small, mix_in = lax.optimization_barrier((group_sum(small, "dp"), mix_in))
+    small, block_out, grad_in = lax.optimization_barrier((group_sum(small, "space"), block_out, grad_in))
     tile = small[:chans // LANES, :LANES]
     tiles = [shifted(tile, "tm", k) for k in range(1, tm)]
     input_grad, bias_grad = pl.pallas_call(
-        functools.partial(finish_grad_kernel, bands, frames),
-        in_specs=[vmem] * (1 + bands * tm),
+        finish_grad_kernel,
+        in_specs=[vmem] * (1 + tm),
         out_specs=[vmem] * 2,
         out_shape=[result, jax.ShapeDtypeStruct((group, offsets), F32)],
         compiler_params=params,
         cost_estimate=finish_cost,
         name="finish_grad",
-    )(small, *owns, *ins)
+    )(small, grad_own, *grad_in)
     tiles, input_grad = lax.optimization_barrier((tiles, input_grad))
     gain_grad = pl.pallas_call(
         gain_kernel,

time: 43.7 us -> 45.4 us (1.039)
  waiting for transfers between devices: 8.68 us -> 16.1 us
  starting transfers between devices: 16.6 us -> 13.3 us
  Pallas kernels: 15.6 us -> 14.2 us
  local copies, waits for them, and re-layouts: 1.9 us -> 0.89 us
    ppermute x7 -> x5, waiting for transfers between devices: 4.55 us -> 9.23 us  [shifted(): lax.ppermute(value, axis, [((i + step) % count, i) for i in range(count)])]
    ppermute x6 -> x4, waiting for transfers between devices: 4.13 us -> 6.85 us  [group_sum(): lax.ppermute(value, axis, [(i ^ step, i) for i in range(count)])]
    ppermute x7 -> x5, starting transfers between devices: 10 us -> 7.58 us  [shifted(): lax.ppermute(value, axis, [((i + step) % count, i) for i in range(count)])]
    pallas_call x4 -> x3, Pallas kernels: 9.04 us -> 7.73 us  [the longest x1 6.04 us: per_device(): pl.pallas_call(functools.partial(backward_kernel, dims), in_specs=[smem]...]
    reshape x1 -> x0, local copies, waits for them, and re-layouts: 1.02 us -> none  [per_device(): out_grad[:, :, n * BAND:(n + 1) * BAND].reshape(rows, width)]
    ppermute x6 -> x4, starting transfers between devices: 6.6 us -> 5.73 us  [group_sum(): lax.ppermute(value, axis, [(i ^ step, i) for i in range(count)])]
  transfers between devices with their start and end apart: 13 -> 9, of which waited for: 5 -> 7; matrix products, arithmetic and copies ran while one was open for 4% -> 2% of each run, Pallas kernels for 34% -> 30%
where the time goes in v8:
time: 45.4 us; the launch traced here: 45.2 us
  waiting for transfers between devices  16.1 us (35%)
  Pallas kernels  14.2 us (31%)
  starting transfers between devices  13.3 us (29%)
  local copies, waits for them, and re-layouts  0.89 us (2%)
  between operations  0.69 us (2%)
    ppermute x5, waiting for transfers between devices, shifted(): lax.ppermute(value, axis, [((i + step) % count, i) for i in range(count)])  9.23 us
    ppermute x5, starting transfers between devices, shifted(): lax.ppermute(value, axis, [((i + step) % count, i) for i in range(count)])  7.58 us
    ppermute x4, waiting for transfers between devices, group_sum(): lax.ppermute(value, axis, [(i ^ step, i) for i in range(count)])  6.85 us
    pallas_call x1, Pallas kernels, per_device(): pl.pallas_call(functools.partial(backward_kernel, dims), in_specs=[smem]...  6.04 us
    ppermute x4, starting transfers between devices, group_sum(): lax.ppermute(value, axis, [(i ^ step, i) for i in range(count)])  5.73 us
    pallas_call x1, Pallas kernels, per_device(): pl.pallas_call(functools.partial(forward_kernel, dims), in_specs=[smem] +...  3.55 us
    pallas_call x1, Pallas kernels, per_device(): pl.pallas_call(functools.partial(stage_kernel, frames, width), in_specs=[...  2.36 us
    pallas_call x1, Pallas kernels, per_device(): pl.pallas_call(finish_grad_kernel, in_specs=[vmem] * (1 + tm), out_specs=...  0.92 us
  transfers between devices with their start and end apart: 9, of which 7 were waited for; matrix products, arithmetic and copies ran while one was open for 2% of the time, Pallas kernels for 30%

profile of v8, /device:TPU:0, one launch (start us, length us, event | category | flops | bytes accessed | tf_op | source)
XLA Modules:
  0.0 45.2 jit_solution(5231353879859891206)
XLA Ops:
  0.6 3.0 %collective-permute-start.1 = (bf16[320,512]{1,0:T(8,128)(2,1)}, bf16[320,512]{1,0:T(8,128)(2,1)S(1)}, u32[]{:S(2)}, u32[]{:S(2)}) collective-permute-start(bf16[320,512]{1,0:T(8,128)(2,1)} %bitcast.9), channel_id=1, source_target_pairs={{1,0},{0,1},{3,2},{2,3},{5,4},{4,5},{7,6},{6,7},{9,8},{8,9},{11,10... | collective-permute-start | bytes 983048 | tf_op jit(solution)/shard_map/ppermute | solution.py:248
  3.7 0.1 collective-permute-start
  3.7 0.8 %broadcast_in_dim.2 = f32[8,39,8]{2,1,0:T(8,128)S(1)} broadcast(f32[8,39]{1,0:T(8,128)} %param.11), dimensions={0,1} | broadcast | bytes 11232 | tf_op jit(solution)/shard_map/broadcast_in_dim | solution.py:283
  4.5 0.1 reshape.35.bias_ref
  4.6 2.4 %stage.1 = (f32[20,8,160]{2,1,0:T(8,128)S(1)}, bf16[320,512]{1,0:T(8,128)(2,1)S(1)}, bf16[1024,1536]{1,0:T(8,128)(2,1)S(1)}, bf16[512,1024]{1,0:T(8,128)(2,1)S(1)}, f32[1,1024]{1,0:T(1,128)S(1)}) custom-call(f32[8,312]{1,0:T(8,128)S(1)} %reshape.35.bias_ref, bf16[320,512]{1,0:T(8,128)(2,1)} %bitcast.10, bf16[1024,512]{1,0:T(8,128)(2,1)} %wq_ref.1, ...), custom_call_target="tpu_custom_call" | custom-call | bytes 8000000 | tf_op jit(solution)/shard_map/stage/pallas_call | solution.py:288
  7.0 5.4 %collective-permute-done.1.refs_1_ = bf16[320,512]{1,0:T(8,128)(2,1)S(1)} collective-permute-done((bf16[320,512]{1,0:T(8,128)(2,1)}, bf16[320,512]{1,0:T(8,128)(2,1)S(1)}, u32[]{:S(2)}, u32[]{:S(2)}) %collective-permute-start.1) | collective-permute-done | bytes 327712 | tf_op jit(solution)/shard_map/ppermute | solution.py:248
  12.4 3.5 %attend.1 = (bf16[2,160,1536]{2,1,0:T(8,128)(2,1)S(1)}, bf16[2,8,160,160]{3,2,1,0:T(8,128)(2,1)S(1)}, bf16[2,160,1024]{2,1,0:T(8,128)(2,1)S(1)}, f32[2,160,128]{...) custom-call(s32[1]{0:T(128)} %bitcast.me_ref, ...), custom_call_target="tpu_custom_call" | custom-call | flops 4000000000 | bytes 8000000 | tf_op jit(solution)/shard_map/attend/pallas_call | solution.py:305
  16.0 2.1 %collective-permute-start.4 = (bf16[2,160,512]{2,1,0:T(8,128)(2,1)S(1)}, bf16[2,160,512]{2,1,0:T(8,128)(2,1)S(1)}, u32[]{:S(2)}, u32[]{:S(2)}) collective-permute-start(bf16[2,160,512]{2,1,0:T(8,128)(2,1)S(1)} %get-tuple-element.36), channel_id=1, source_target_pairs={{1,0},{0,1},{3,2},{2,3},{5,4},{4,5},{7,6},{6,7},{9,8},{8,9},{11,10... | collective-permute-start | bytes 983048 | tf_op jit(solution)/shard_map/ppermute | solution.py:248
  18.1 1.4 %collective-permute-done.refs_1_ = bf16[320,512]{1,0:T(8,128)(2,1)S(1)} collective-permute-done((bf16[320,512]{1,0:T(8,128)(2,1)}, bf16[320,512]{1,0:T(8,128)(2,1)S(1)}, u32[]{:S(2)}, u32[]{:S(2)}) %collective-permute-start) | collective-permute-done | bytes 327712 | tf_op jit(solution)/shard_map/ppermute | solution.py:248
  19.4 6.0 %attend_back.1 = (f32[2,160,512]{2,1,0:T(8,128)S(1)}, f32[8,512]{1,0:T(8,128)S(1)}, bf16[2,160,512]{2,1,0:T(8,128)(2,1)S(1)}) custom-call(s32[1]{0:T(128)} %bitcast.me_ref, bf16[320,512]{1,0:T(8,128)(2,1)S(1)} %bitcast.8, bf16[320,512]{1,0:T(8,128)(2,1)S(1)} %collective-permute-done.refs_1_, f32[1,1024]{1,0:T(1,128)S(1)} %get-tuple-element.26.refs_2_, ...), custom_call_target="tpu_custom_call" | custom-call | flops 6000000000 | tf_op jit(solution)/shard_map/attend_back/pallas_call | solution.py:326
  25.5 2.1 %collective-permute-start.7 = (bf16[2,160,512]{2,1,0:T(8,128)(2,1)S(1)}, bf16[2,160,512]{2,1,0:T(8,128)(2,1)S(1)}, u32[]{:S(2)}, u32[]{:S(2)}) collective-permute-start(bf16[2,160,512]{2,1,0:T(8,128)(2,1)S(1)} %get-tuple-element.39), channel_id=1, source_target_pairs={{1,0},{0,1},{3,2},{2,3},{5,4},{4,5},{7,6},{6,7},{9,8},{8,9},{11,10... | collective-permute-start | bytes 983048 | tf_op jit(solution)/shard_map/ppermute | solution.py:248
  27.6 0.0 collective-permute-start.2
  27.6 1.2 %collective-permute-done.2 = f32[8,512]{1,0:T(8,128)S(1)} collective-permute-done((f32[8,512]{1,0:T(8,128)S(1)}, f32[8,512]{1,0:T(8,128)S(1)}, u32[]{:S(2)}, u32[]{:S(2)}) %collective-permute-start.2) | collective-permute-done | bytes 16416 | tf_op jit(solution)/shard_map/ppermute | solution.py:255
  28.7 1.5 %collective-permute-start.3 = (f32[8,512]{1,0:T(8,128)S(1)}, f32[8,512]{1,0:T(8,128)S(1)}, u32[]{:S(2)}, u32[]{:S(2)}) collective-permute-start(f32[8,512]{1,0:T(8,128)S(1)} %add.12), channel_id=1, source_target_pairs={{16,0},{24,8},{0,16},{8,24},{17,1},{25,9},{1,17},{9,25},{18,2},{26... | collective-permute-start | bytes 49160 | tf_op jit(solution)/shard_map/ppermute | solution.py:255
  30.2 2.2 %collective-permute-done.3 = f32[8,512]{1,0:T(8,128)S(1)} collective-permute-done((f32[8,512]{1,0:T(8,128)S(1)}, f32[8,512]{1,0:T(8,128)S(1)}, u32[]{:S(2)}, u32[]{:S(2)}) %collective-permute-start.3) | collective-permute-done | bytes 16416 | tf_op jit(solution)/shard_map/ppermute | solution.py:255
  32.5 1.6 %collective-permute-start.5 = (f32[8,512]{1,0:T(8,128)S(1)}, f32[8,512]{1,0:T(8,128)S(1)}, u32[]{:S(2)}, u32[]{:S(2)}) collective-permute-start(f32[8,512]{1,0:T(8,128)S(1)} %add.13), channel_id=1, source_target_pairs={{2,0},{0,2},{6,4},{4,6},{3,1},{1,3},{7,5},{5,7},{10,8},{8,10},{14,... | collective-permute-start | bytes 49160 | tf_op jit(solution)/shard_map/ppermute | solution.py:255
  34.1 2.2 %collective-permute-done.5 = f32[8,512]{1,0:T(8,128)S(1)} collective-permute-done((f32[8,512]{1,0:T(8,128)S(1)}, f32[8,512]{1,0:T(8,128)S(1)}, u32[]{:S(2)}, u32[]{:S(2)}) %collective-permute-start.5) | collective-permute-done | bytes 16416 | tf_op jit(solution)/shard_map/ppermute | solution.py:255
  36.3 2.6 %collective-permute-start.6 = (f32[8,512]{1,0:T(8,128)S(1)}, f32[8,512]{1,0:T(8,128)S(1)}, u32[]{:S(2)}, u32[]{:S(2)}) collective-permute-start(f32[8,512]{1,0:T(8,128)S(1)} %add.14), channel_id=1, source_target_pairs={{4,0},{6,2},{0,4},{2,6},{5,1},{7,3},{1,5},{3,7},{12,8},{14,10},{8,... | collective-permute-start | bytes 49160 | tf_op jit(solution)/shard_map/ppermute | solution.py:255
  38.9 0.8 %finish_out.1 = bf16[320,512]{1,0:T(8,128)(2,1)} custom-call(f32[2,160,512]{2,1,0:T(8,128)S(1)} %get-tuple-element.38.own_ref, bf16[2,160,512]{2,1,0:T(8,128)(2,1)S(1)} %collective-permute-done.4.refs_0_), custom_call_target="tpu_custom_call" | custom-call | bytes 1500000 | tf_op jit(solution)/shard_map/finish_out/pallas_call | solution.py:349
  39.7 1.3 %collective-permute-done.6 = f32[8,512]{1,0:T(8,128)S(1)} collective-permute-done((f32[8,512]{1,0:T(8,128)S(1)}, f32[8,512]{1,0:T(8,128)S(1)}, u32[]{:S(2)}, u32[]{:S(2)}) %collective-permute-start.6) | collective-permute-done | bytes 16416 | tf_op jit(solution)/shard_map/ppermute | solution.py:255
  41.0 0.3 collective-permute-start.8
  41.2 0.9 %finish_grad.1 = (bf16[320,512]{1,0:T(8,128)(2,1)}, f32[8,39]{1,0:T(8,128)}) custom-call(f32[8,512]{1,0:T(8,128)S(1)} %add.15.small_ref, f32[2,160,512]{2,1,0:T(8,128)S(1)} %get-tuple-element.42.own_ref, bf16[2,160,512]{2,1,0:T(8,128)(2,1)S(1)} %collective-permute-done.7.refs_0_), custom_call_target="tpu_custom_call" | custom-call | bytes 1500000 | tf_op jit(solution)/shard_map/finish_grad/pallas_call | solution.py:362
  42.2 2.5 %collective-permute-done.8.refs_1_ = f32[8,128]{1,0:T(8,128)S(1)} collective-permute-done((f32[8,128]{1,0:T(8,128)S(1)}, f32[8,128]{1,0:T(8,128)S(1)}, u32[]{:S(2)}, u32[]{:S(2)}) %collective-permute-start.8) | collective-permute-done | bytes 4128 | tf_op jit(solution)/shard_map/ppermute | solution.py:248
  44.6 0.6 %gain_sum.1 = f32[1,512]{1,0:T(1,128)} custom-call(s32[1]{0:T(128)} %bitcast.me_ref, f32[8,128]{1,0:T(8,128)S(1)} %slice.3.refs_0_, f32[8,128]{1,0:T(8,128)S(1)} %collective-permute-done.8.refs_1_), custom_call_target="tpu_custom_call" | custom-call | tf_op jit(solution)/shard_map/gain_sum/pallas_call | solution.py:372
  (9 shorter events, 0.0 us)
Async XLA Ops:
  0.6 11.8 %collective-permute-start.1 = (bf16[320,512]{1,0:T(8,128)(2,1)}, bf16[320,512]{1,0:T(8,128)(2,1)S(1)}, u32[]{:S(2)}, u32[]{:S(2)}) collective-permute-start(bf16[320,512]{1,0:T(8,128)(2,1)} %bitcast.9), channel_id=1, source_target_pairs={{1,0},{0,1},{3,2},{2,3},{5,4},{4,5},{7,6},{6,7},{9,8},{8,9},{11,10... | collective-permute-start | bytes 983048 | tf_op jit(solution)/shard_map/ppermute | solution.py:248
  3.7 15.8 %collective-permute-start = (bf16[320,512]{1,0:T(8,128)(2,1)}, bf16[320,512]{1,0:T(8,128)(2,1)S(1)}, u32[]{:S(2)}, u32[]{:S(2)}) collective-permute-start(bf16[320,512]{1,0:T(8,128)(2,1)} %bitcast.7), channel_id=1, source_target_pairs={{1,0},{0,1},{3,2},{2,3},{5,4},{4,5},{7,6},{6,7},{9,8},{8,9},{11,10... | collective-permute-start | bytes 983048 | tf_op jit(solution)/shard_map/ppermute | solution.py:248
  12.4 7.0 %copy-start = (bf16[1,20,16,512]{3,2,1,0:T(8,128)(2,1)S(1)}, bf16[1,20,16,512]{3,2,1,0:T(8,128)(2,1)}, u32[]{:S(2)}) copy-start(bf16[1,20,16,512]{3,2,1,0:T(8,128)(2,1)} %param.9) | copy-start | bytes 983044
  16.0 16.5 %collective-permute-start.4 = (bf16[2,160,512]{2,1,0:T(8,128)(2,1)S(1)}, bf16[2,160,512]{2,1,0:T(8,128)(2,1)S(1)}, u32[]{:S(2)}, u32[]{:S(2)}) collective-permute-start(bf16[2,160,512]{2,1,0:T(8,128)(2,1)S(1)} %get-tuple-element.36), channel_id=1, source_target_pairs={{1,0},{0,1},{3,2},{2,3},{5,4},{4,5},{7,6},{6,7},{9,8},{8,9},{11,10... | collective-permute-start | bytes 983048 | tf_op jit(solution)/shard_map/ppermute | solution.py:248
  25.5 15.5 %collective-permute-start.7 = (bf16[2,160,512]{2,1,0:T(8,128)(2,1)S(1)}, bf16[2,160,512]{2,1,0:T(8,128)(2,1)S(1)}, u32[]{:S(2)}, u32[]{:S(2)}) collective-permute-start(bf16[2,160,512]{2,1,0:T(8,128)(2,1)S(1)} %get-tuple-element.39), channel_id=1, source_target_pairs={{1,0},{0,1},{3,2},{2,3},{5,4},{4,5},{7,6},{6,7},{9,8},{8,9},{11,10... | collective-permute-start | bytes 983048 | tf_op jit(solution)/shard_map/ppermute | solution.py:248
  27.6 1.2 %collective-permute-start.2 = (f32[8,512]{1,0:T(8,128)S(1)}, f32[8,512]{1,0:T(8,128)S(1)}, u32[]{:S(2)}, u32[]{:S(2)}) collective-permute-start(f32[8,512]{1,0:T(8,128)S(1)} %get-tuple-element.35), channel_id=1, source_target_pairs={{8,0},{0,8},{24,16},{16,24},{9,1},{1,9},{25,17},{17,25},{10,2},{2,... | collective-permute-start | bytes 49160 | tf_op jit(solution)/shard_map/ppermute | solution.py:255
  28.7 3.7 %collective-permute-start.3 = (f32[8,512]{1,0:T(8,128)S(1)}, f32[8,512]{1,0:T(8,128)S(1)}, u32[]{:S(2)}, u32[]{:S(2)}) collective-permute-start(f32[8,512]{1,0:T(8,128)S(1)} %add.12), channel_id=1, source_target_pairs={{16,0},{24,8},{0,16},{8,24},{17,1},{25,9},{1,17},{9,25},{18,2},{26... | collective-permute-start | bytes 49160 | tf_op jit(solution)/shard_map/ppermute | solution.py:255
  32.5 3.8 %collective-permute-start.5 = (f32[8,512]{1,0:T(8,128)S(1)}, f32[8,512]{1,0:T(8,128)S(1)}, u32[]{:S(2)}, u32[]{:S(2)}) collective-permute-start(f32[8,512]{1,0:T(8,128)S(1)} %add.13), channel_id=1, source_target_pairs={{2,0},{0,2},{6,4},{4,6},{3,1},{1,3},{7,5},{5,7},{10,8},{8,10},{14,... | collective-permute-start | bytes 49160 | tf_op jit(solution)/shard_map/ppermute | solution.py:255
  36.3 4.6 %collective-permute-start.6 = (f32[8,512]{1,0:T(8,128)S(1)}, f32[8,512]{1,0:T(8,128)S(1)}, u32[]{:S(2)}, u32[]{:S(2)}) collective-permute-start(f32[8,512]{1,0:T(8,128)S(1)} %add.14), channel_id=1, source_target_pairs={{4,0},{6,2},{0,4},{2,6},{5,1},{7,3},{1,5},{3,7},{12,8},{14,10},{8,... | collective-permute-start | bytes 49160 | tf_op jit(solution)/shard_map/ppermute | solution.py:255
  41.0 3.7 %collective-permute-start.8 = (f32[8,128]{1,0:T(8,128)S(1)}, f32[8,128]{1,0:T(8,128)S(1)}, u32[]{:S(2)}, u32[]{:S(2)}) collective-permute-start(f32[8,128]{1,0:T(8,128)S(1)} %slice.3.refs_0_), channel_id=1, source_target_pairs={{1,0},{0,1},{3,2},{2,3},{5,4},{4,5},{7,6},{6,7},{9,8},{8,9},{11,10... | collective-permute-start | bytes 12296 | tf_op jit(solution)/shard_map/ppermute | solution.py:248

commit v9 on v8

--- a/solution.py
+++ b/solution.py
@@ -120,10 +120,8 @@
 def backward_kernel(dims, me_ref, *refs):
     tm, frames, pixels, width, group, head_dim, eps = dims
     g_refs = refs[:tm]
-    gain_ref, qkv_ref, p_ref, xb_ref, inv_ref, proj_ref, wo_ref = refs[tm:tm + 7]
-    own_ref, small_ref = refs[tm + 7:tm + 9]
-    msg_refs = refs[tm + 9:tm + 9 + tm - 1]
-    gw_ref, da_ref, ds_ref, dqkv_ref, grad_ref, diag_ref = refs[tm + 9 + tm - 1:]
+    qkv_ref, p_ref, xb_ref, inv_ref, proj_ref, wo_ref = refs[tm:tm + 6]
+    grad_ref, tile_ref, bias_ref, gw_ref, da_ref, ds_ref, dqkv_ref, diag_ref = refs[tm + 6:]
     me = me_ref[0]
     rows = frames * BAND
     bands = pixels // BAND
@@ -169,34 +167,46 @@
     grad = mm(dqkv_ref[...].reshape(total, 3 * width), proj_ref[...], NT)
     grad_ref[...] = grad.reshape(bands, rows, chans)
     gain_sum = jnp.zeros((BAND, chans), F32)
-    for f in range(0, frames, 2):
-        at = slice(f * BAND, (f + 2) * BAND)
-        for band in range(bands):
-            grad, x = grad_ref[band, at, :], xb_ref[band, at, :].astype(F32)
-            inv = inv_ref[band, at, :1]
-            scaled = x * inv
-            gain_sum = gain_sum + jnp.sum((grad * scaled).reshape(2, BAND, chans), axis=0)
-            term = grad * gain_ref[...]
-            inner = jnp.mean(term * scaled, axis=-1, keepdims=True)
-            grad_ref[band, at, :] = inv * (term - scaled * inner)
-    for k in range(1, tm):
-        msg_refs[k - 1][...] = grad_ref[:, :, pl.ds(place(tm - k), width)].astype(BF16)
-    for f in range(0, frames, 2):
-        at = slice(f * BAND, (f + 2) * BAND)
-        both = g_refs[0][f * pixels:(f + 2) * pixels, :].astype(F32).reshape(2, bands, BAND, width)
-        for band in range(bands):
-            own = grad_ref[band, at, pl.ds(place(0), width)]
-            own_ref[band, at, :] = own + both[:, band].reshape(2 * BAND, width)
+    for band in range(bands):
+        for f in range(0, frames, 2):
+            at = slice(f * BAND, (f + 2) * BAND)
+            scaled = xb_ref[band, at, :].astype(F32) * inv_ref[band, at, :1]
+            gain_sum = gain_sum + jnp.sum((grad_ref[band, at, :] * scaled).reshape(2, BAND, chans), axis=0)
     gain_sum = jnp.sum(gain_sum, axis=0, keepdims=True)
-    small_ref[...] = jnp.zeros_like(small_ref)
+    tile_ref[...] = jnp.zeros_like(tile_ref)
     for r in range(chans // LANES):
-        small_ref[r:r + 1, :LANES] = gain_sum[:, r * LANES:(r + 1) * LANES]
-    span = small_ref.shape[1] - LANES
+        tile_ref[r:r + 1, :] = gain_sum[:, r * LANES:(r + 1) * LANES]
+    span = bias_ref.shape[1]
     bias = jnp.zeros((group, span), F32)
     for i in range(frames):
         before = (frames - 1 - i) * BAND
         bias = bias + jnp.pad(diag_ref[i], ((0, 0), (before, span - before - rows)))
-    small_ref[:group, LANES:] = bias
+    bias_ref[...] = jnp.zeros_like(bias_ref)
+    bias_ref[:group, :] = bias
+
+
+def share_kernel(dims, me_ref, g_ref, gain_ref, grad_ref, xb_ref, inv_ref, own_ref, *refs):
+    tm, frames, pixels, width = dims[:4]
+    bands = pixels // BAND
+    *msg_refs, term_ref = refs
+    me = me_ref[0]
+
+    def place(k):
+        return pl.multiple_of(lax.rem(me + k, tm) * width, width)
+
+    for f in range(0, frames, 2):
+        at = slice(f * BAND, (f + 2) * BAND)
+        both = g_ref[f * pixels:(f + 2) * pixels, :].astype(F32).reshape(2, bands, BAND, width)
+        for band in range(bands):
+            inv = inv_ref[band, at, :1]
+            scaled = xb_ref[band, at, :].astype(F32) * inv
+            term = grad_ref[band, at, :] * gain_ref[...]
+            inner = jnp.mean(term * scaled, axis=-1, keepdims=True)
+            term_ref[band, at, :] = inv * (term - scaled * inner)
+            own = term_ref[band, at, pl.ds(place(0), width)]
+            own_ref[band, at, :] = own + both[:, band].reshape(2 * BAND, width)
+    for k in range(1, tm):
+        msg_refs[k - 1][...] = term_ref[:, :, pl.ds(place(tm - k), width)].astype(BF16)
 
 
 def finish_kernel(own_ref, in_refs, out_ref):
@@ -212,11 +222,20 @@
     out_ref[...] = value.reshape(out_ref.shape).astype(out_ref.dtype)
 
 
-def finish_grad_kernel(small_ref, own_ref, *refs):
-    *in_refs, out_ref, bias_ref = refs
-    finish_kernel(own_ref, in_refs, out_ref)
+def finish_shares(own_ref, *refs):
+    finish_kernel(own_ref, refs[:-1], refs[-1])
+
+
+def sums_kernel(me_ref, parts_ref, gain_ref, bias_ref, sum_ref):
+    total = parts_ref[0]
+    for n in range(1, parts_ref.shape[0]):
+        total = total + parts_ref[n]
+    sum_ref[...] = total[:, :LANES]
+    count = gain_ref.shape[1] // LANES
+    for r in range(count):
+        gain_ref[:, r * LANES:(r + 1) * LANES] = sum_ref[pl.ds(me_ref[0] * count + r, 1), :]
     group, offsets = bias_ref.shape
-    value = small_ref[:, LANES:]
+    value = total[:, LANES:]
     high = value.astype(BF16)
     rest = value - high.astype(F32)
     middle = rest.astype(BF16)
@@ -224,23 +243,8 @@
     span = value.shape[1]
     lane = lax.broadcasted_iota(jnp.int32, (span, LANES), 0) // BAND
     put = (lane == lax.broadcasted_iota(jnp.int32, (span, LANES), 1)).astype(F32).astype(BF16)
-    total = mm(high, put) + mm(middle, put) + mm(low, put)
-    bias_ref[...] = total[:group, :offsets]
-
-
-def finish_out_kernel(own_ref, *refs):
-    finish_kernel(own_ref, refs[:-1], refs[-1])
-
-
-def gain_kernel(me_ref, *refs):
-    *tile_refs, out_ref, sum_ref = refs
-    total = tile_refs[0][...]
-    for ref in tile_refs[1:]:
-        total = total + ref[...]
-    sum_ref[...] = total
-    count = out_ref.shape[1] // LANES
-    for r in range(count):
-        out_ref[:, r * LANES:(r + 1) * LANES] = sum_ref[pl.ds(me_ref[0] * count + r, 1), :]
+    summed = mm(high, put) + mm(middle, put) + mm(low, put)
+    bias_ref[...] = summed[:group, :offsets]
 
 
 def shifted(value, axis, step):
@@ -248,17 +252,10 @@
     return lax.ppermute(value, axis, [((i + step) % count, i) for i in range(count)])
 
 
-def group_sum(value, axis):
+def to_all(value, axis):
     count = lax.axis_size(axis)
-    step = 1
-    while count % (2 * step) == 0:
-        value = value + lax.ppermute(value, axis, [(i ^ step, i) for i in range(count)])
-        step *= 2
-    odd = count // step
-    if odd > 1:
-        pairs = [[((i + k * step) % count, i) for i in range(count)] for k in range(1, odd)]
-        value = sum((lax.ppermute(value, axis, p) for p in pairs), value)
-    return value
+    copies = jnp.broadcast_to(value[None], (count, *value.shape))
+    return lax.all_to_all(copies, axis, split_axis=0, concat_axis=0, tiled=True)
 
 
 def per_device(inputs, out_grad, norm_gain, pos_bias, w_query, w_key, w_value, w_out):
@@ -323,61 +320,65 @@
         name="attend",
     )(me1, *x_parts, gain, rel, proj, w_out)
     mix_in = [shifted(mix_out[k - 1], "tm", k) for k in range(1, tm)]
-    grad_own, small, *grad_out = pl.pallas_call(
+    grad, tile, bias = pl.pallas_call(
         functools.partial(backward_kernel, dims),
-        in_specs=[smem] + [vmem] * (tm + 7),
-        out_specs=[vmem] * (2 + tm - 1),
+        in_specs=[smem] + [vmem] * (tm + 6),
+        out_specs=[vmem] * 3,
         out_shape=[
-            pltpu.VMEM((bands, rows, width), F32),
-            pltpu.VMEM((lines, LANES + span), F32),
-        ] + [pltpu.VMEM((bands, rows, width), BF16)] * (tm - 1),
+            pltpu.VMEM((bands, rows, chans), F32),
+            pltpu.VMEM((lines, LANES), F32),
+            pltpu.VMEM((lines, span), F32),
+        ],
         scratch_shapes=[
             pltpu.VMEM((total, chans), BF16),
             pltpu.VMEM((bands, rows, width), BF16),
             pltpu.VMEM((bands, group, rows, rows), BF16),
             pltpu.VMEM((bands, rows, 3 * width), BF16),
-            pltpu.VMEM((bands, rows, chans), F32),
             pltpu.VMEM((frames, group, rows), F32),
         ],
         compiler_params=params,
         cost_estimate=pl.CostEstimate(flops=6_000_000_000, bytes_accessed=0, transcendentals=0),
         name="attend_back",
-    )(me1, *g_parts, gain, qkv, probs, xb, inv, proj, w_out)
+    )(me1, *g_parts, qkv, probs, xb, inv, proj, w_out)
+    grad_own, *grad_out = pl.pallas_call(
+        functools.partial(share_kernel, dims),
+        in_specs=[smem] + [vmem] * 5,
+        out_specs=[vmem] * tm,
+        out_shape=[pltpu.VMEM((bands, rows, width), F32)] + [pltpu.VMEM((bands, rows, width), BF16)] * (tm - 1),
+        scratch_shapes=[pltpu.VMEM((bands, rows, chans), F32)],
+        compiler_params=params,
+        cost_estimate=pl.CostEstimate(flops=2_000_000_000, bytes_accessed=0, transcendentals=0),
+        name="share",
+    )(me1, g0, gain, grad, xb, inv)
+    tiles = [shifted(tile, "tm", k) for k in range(1, tm)]
+    tiles, grad_out, mix_in = lax.optimization_barrier((tiles, grad_out, mix_in))
     grad_in = [shifted(grad_out[k - 1], "tm", k) for k in range(1, tm)]
-    result = jax.ShapeDtypeStruct((total, width), BF16)
-    finish_cost = pl.CostEstimate(flops=0, bytes_accessed=1_500_000, transcendentals=0)
-    block_out = pl.pallas_call(
-        finish_out_kernel,
-        in_specs=[vmem] * tm,
-        out_specs=vmem,
-        out_shape=result,
-        compiler_params=params,
-        cost_estimate=finish_cost,
-        name="finish_out",
-    )(mix_own, *mix_in)
-    small, mix_in = lax.optimization_barrier((group_sum(small, "dp"), mix_in))
-    small, block_out, grad_in = lax.optimization_barrier((group_sum(small, "space"), block_out, grad_in))
-    tile = small[:chans // LANES, :LANES]
-    tiles = [shifted(tile, "tm", k) for k in range(1, tm)]
-    input_grad, bias_grad = pl.pallas_call(
-        finish_grad_kernel,
-        in_specs=[vmem] * (1 + tm),
+
+    def finish(mine, others):
+        return pl.pallas_call(
+            finish_shares,
+            in_specs=[vmem] * tm,
+            out_specs=vmem,
+            out_shape=jax.ShapeDtypeStruct((total, width), BF16),
+            compiler_params=params,
+            cost_estimate=pl.CostEstimate(flops=0, bytes_accessed=1_500_000, transcendentals=0),
+            name="finish",
+        )(mine, *others)
+
+    small = jnp.concatenate([sum(tiles, tile), bias], axis=1)
+    small, mix_in = lax.optimization_barrier((jnp.sum(to_all(small, "dp"), axis=0), mix_in))
+    block_out, input_grad = finish(mix_own, mix_in), finish(grad_own, grad_in)
+    parts = to_all(small, "space")
+    parts, block_out, input_grad = lax.optimization_barrier((parts, block_out, input_grad))
+    gain_grad, bias_grad = pl.pallas_call(
+        sums_kernel,
+        in_specs=[smem, vmem],
         out_specs=[vmem] * 2,
-        out_shape=[result, jax.ShapeDtypeStruct((group, offsets), F32)],
-        compiler_params=params,
-        cost_estimate=finish_cost,
-        name="finish_grad",
-    )(small, grad_own, *grad_in)
-    tiles, input_grad = lax.optimization_barrier((tiles, input_grad))
-    gain_grad = pl.pallas_call(
-        gain_kernel,
-        in_specs=[smem] + [vmem] * tm,
-        out_specs=vmem,
-        out_shape=jax.ShapeDtypeStruct((1, width), F32),
+        out_shape=[jax.ShapeDtypeStruct((1, width), F32), jax.ShapeDtypeStruct((group, offsets), F32)],
         scratch_shapes=[pltpu.VMEM(tile.shape, F32)],
         compiler_params=params,
-        name="gain_sum",
-    )(me1, tile, *tiles)
+        name="sums",
+    )(me1, parts)
     return (block_out.reshape(inputs.shape), input_grad.reshape(inputs.shape), gain_grad.reshape(width), bias_grad)
 
 

time: 45.4 us -> 49.8 us (1.097)
  blocking collectives: 0 us -> 6.68 us
  waiting for transfers between devices: 16.1 us -> 11 us
  Pallas kernels: 14.2 us -> 15.4 us
  starting transfers between devices: 13.3 us -> 14.2 us
  local copies, waits for them, and re-layouts: 0.89 us -> 1.53 us
    ppermute x4 -> x0, waiting for transfers between devices: 6.85 us -> none  [group_sum(): lax.ppermute(value, axis, [(i ^ step, i) for i in range(count)])]
    all_to_all x0 -> x1, blocking collectives: none -> 6.68 us  [to_all(): return lax.all_to_all(copies, axis, split_axis=0, concat_axis=0, tiled=True)]
    ppermute x4 -> x0, starting transfers between devices: 5.73 us -> none  [group_sum(): lax.ppermute(value, axis, [(i ^ step, i) for i in range(count)])]
    all_to_all x0 -> x1, starting transfers between devices: none -> 4.87 us  [to_all(): return lax.all_to_all(copies, axis, split_axis=0, concat_axis=0, tiled=True)]
    all_to_all x0 -> x1, waiting for transfers between devices: none -> 4.18 us  [to_all(): return lax.all_to_all(copies, axis, split_axis=0, concat_axis=0, tiled=True)]
    ppermute x5, waiting for transfers between devices: 9.23 us -> 6.79 us  [shifted(): lax.ppermute(value, axis, [((i + step) % count, i) for i in range(count)])]
    ppermute x5, starting transfers between devices: 7.58 us -> 9.37 us  [shifted(): lax.ppermute(value, axis, [((i + step) % count, i) for i in range(count)])]
    pallas_call x3 -> x4, Pallas kernels: 2.28 us -> 3.83 us  [the longest x2 1.56 us: finish(): pl.pallas_call(finish_shares, in_specs=[vmem] * tm, out_specs=vmem, out_s...]
  transfers between devices with their start and end apart: 9 -> 6, of which waited for: 7 -> 4; matrix products, arithmetic and copies ran while one was open for 2% -> 3% of each run, Pallas kernels for 30% -> 30%
where the time goes in v9:
time: 49.8 us; the launch traced here: 49.5 us
  Pallas kernels  15.4 us (31%)
  starting transfers between devices  14.2 us (29%)
  waiting for transfers between devices  11 us (22%)
  blocking collectives  6.68 us (13%)
  local copies, waits for them, and re-layouts  1.53 us (3%)
  between operations  0.69 us (1%)
    ppermute x5, starting transfers between devices, shifted(): lax.ppermute(value, axis, [((i + step) % count, i) for i in range(count)])  9.37 us
    ppermute x5, waiting for transfers between devices, shifted(): lax.ppermute(value, axis, [((i + step) % count, i) for i in range(count)])  6.79 us
    all_to_all x1, blocking collectives, to_all(): return lax.all_to_all(copies, axis, split_axis=0, concat_axis=0, tiled=True)  6.68 us
    pallas_call x1, Pallas kernels, per_device(): pl.pallas_call(functools.partial(backward_kernel, dims), in_specs=[smem]...  5.59 us
    all_to_all x1, starting transfers between devices, to_all(): return lax.all_to_all(copies, axis, split_axis=0, concat_axis=0, tiled=True)  4.87 us
    all_to_all x1, waiting for transfers between devices, to_all(): return lax.all_to_all(copies, axis, split_axis=0, concat_axis=0, tiled=True)  4.18 us
    pallas_call x1, Pallas kernels, per_device(): pl.pallas_call(functools.partial(forward_kernel, dims), in_specs=[smem] +...  3.6 us
    pallas_call x1, Pallas kernels, per_device(): pl.pallas_call(functools.partial(stage_kernel, frames, width), in_specs=[...  2.36 us
  transfers between devices with their start and end apart: 6, of which 4 were waited for; matrix products, arithmetic and copies ran while one was open for 3% of the time, Pallas kernels for 30%

profile of v9, /device:TPU:0, one launch (start us, length us, event | category | flops | bytes accessed | tf_op | source)
XLA Modules:
  0.0 49.5 jit_solution(3033199471443481601)
XLA Ops:
  0.6 3.0 %collective-permute-start.1 = (bf16[320,512]{1,0:T(8,128)(2,1)}, bf16[320,512]{1,0:T(8,128)(2,1)S(1)}, u32[]{:S(2)}, u32[]{:S(2)}) collective-permute-start(bf16[320,512]{1,0:T(8,128)(2,1)} %bitcast.10), channel_id=1, source_target_pairs={{1,0},{0,1},{3,2},{2,3},{5,4},{4,5},{7,6},{6,7},{9,8},{8,9},{11,10... | collective-permute-start | bytes 983048 | tf_op jit(solution)/shard_map/ppermute | solution.py:252
  3.7 0.1 collective-permute-start
  3.7 0.8 %broadcast_in_dim.6 = f32[8,39,8]{2,1,0:T(8,128)S(1)} broadcast(f32[8,39]{1,0:T(8,128)} %param.11), dimensions={0,1} | broadcast | bytes 11232 | tf_op jit(solution)/shard_map/broadcast_in_dim | solution.py:280
  4.5 0.1 reshape.37.bias_ref
  4.6 2.4 %stage.1 = (f32[20,8,160]{2,1,0:T(8,128)S(1)}, bf16[320,512]{1,0:T(8,128)(2,1)S(1)}, bf16[1024,1536]{1,0:T(8,128)(2,1)S(1)}, bf16[512,1024]{1,0:T(8,128)(2,1)S(1)}, f32[1,1024]{1,0:T(1,128)S(1)}) custom-call(f32[8,312]{1,0:T(8,128)S(1)} %reshape.37.bias_ref, bf16[320,512]{1,0:T(8,128)(2,1)} %bitcast.11, bf16[1024,512]{1,0:T(8,128)(2,1)} %wq_ref.1, ...), custom_call_target="tpu_custom_call" | custom-call | bytes 8000000 | tf_op jit(solution)/shard_map/stage/pallas_call | solution.py:285
  7.0 5.4 %collective-permute-done.1.refs_1_ = bf16[320,512]{1,0:T(8,128)(2,1)S(1)} collective-permute-done((bf16[320,512]{1,0:T(8,128)(2,1)}, bf16[320,512]{1,0:T(8,128)(2,1)S(1)}, u32[]{:S(2)}, u32[]{:S(2)}) %collective-permute-start.1) | collective-permute-done | bytes 327712 | tf_op jit(solution)/shard_map/ppermute | solution.py:252
  12.4 3.6 %attend.1 = (bf16[2,160,1536]{2,1,0:T(8,128)(2,1)S(1)}, bf16[2,8,160,160]{3,2,1,0:T(8,128)(2,1)S(1)}, bf16[2,160,1024]{2,1,0:T(8,128)(2,1)S(1)}, f32[2,160,128]{...) custom-call(s32[1]{0:T(128)} %bitcast.me_ref, ...), custom_call_target="tpu_custom_call" | custom-call | flops 4000000000 | bytes 8000000 | tf_op jit(solution)/shard_map/attend/pallas_call | solution.py:302
  16.0 2.1 %collective-permute-start.3 = (bf16[2,160,512]{2,1,0:T(8,128)(2,1)S(1)}, bf16[2,160,512]{2,1,0:T(8,128)(2,1)S(1)}, u32[]{:S(2)}, u32[]{:S(2)}) collective-permute-start(bf16[2,160,512]{2,1,0:T(8,128)(2,1)S(1)} %get-tuple-element.42), channel_id=1, source_target_pairs={{1,0},{0,1},{3,2},{2,3},{5,4},{4,5},{7,6},{6,7},{9,8},{8,9},{11,10... | collective-permute-start | bytes 983048 | tf_op jit(solution)/shard_map/ppermute | solution.py:252
  18.1 1.3 %collective-permute-done.refs_1_ = bf16[320,512]{1,0:T(8,128)(2,1)S(1)} collective-permute-done((bf16[320,512]{1,0:T(8,128)(2,1)}, bf16[320,512]{1,0:T(8,128)(2,1)S(1)}, u32[]{:S(2)}, u32[]{:S(2)}) %collective-permute-start) | collective-permute-done | bytes 327712 | tf_op jit(solution)/shard_map/ppermute | solution.py:252
  19.4 0.0 copy-done
  19.4 5.6 %attend_back.1 = (f32[2,160,1024]{2,1,0:T(8,128)S(1)}, f32[8,128]{1,0:T(8,128)S(1)}, f32[8,384]{1,0:T(8,128)S(1)}) custom-call(s32[1]{0:T(128)} %bitcast.me_ref, bf16[320,512]{1,0:T(8,128)(2,1)S(1)} %bitcast.8, bf16[320,512]{1,0:T(8,128)(2,1)S(1)} %collective-permute-done.refs_1_, bf16[2,160,1536]{2,1,0:T(8,128)(2,1)S(1)} %get-tuple-element.35.refs_2_, ...), custom_call_target="tpu_custom_call" | custom-call | flops 6000000000 | tf_op jit(solution)/shard_map/attend_back/pallas_call | solution.py:323
  25.0 2.1 %collective-permute-start.2 = (f32[8,128]{1,0:T(8,128)S(1)}, f32[8,128]{1,0:T(8,128)S(1)}, u32[]{:S(2)}, u32[]{:S(2)}) collective-permute-start(f32[8,128]{1,0:T(8,128)S(1)} %get-tuple-element.39), channel_id=1, source_target_pairs={{1,0},{0,1},{3,2},{2,3},{5,4},{4,5},{7,6},{6,7},{9,8},{8,9},{11,10... | collective-permute-start | bytes 12296 | tf_op jit(solution)/shard_map/ppermute | solution.py:252
  27.2 1.5 %share.1 = (f32[2,160,512]{2,1,0:T(8,128)S(1)}, bf16[2,160,512]{2,1,0:T(8,128)(2,1)S(1)}) custom-call(s32[1]{0:T(128)} %bitcast.me_ref, bf16[320,512]{1,0:T(8,128)(2,1)S(1)} %bitcast.9, f32[1,1024]{1,0:T(1,128)S(1)} %get-tuple-element.31.refs_2_.gain_ref, f32[2,160,1024]{2,1,0:T(8,128)S(1)} %get-tuple-element.40.grad_ref, ...), custom_call_target="tpu_custom_call" | custom-call | flops 2000000000 | tf_op jit(solution)/shard_map/share/pallas_call | solution.py:343
  28.6 0.1 collective-permute-done.2
  28.7 0.0 collective-permute-done.3.refs_0_
  28.7 2.0 %collective-permute-start.4 = (bf16[2,160,512]{2,1,0:T(8,128)(2,1)S(1)}, bf16[2,160,512]{2,1,0:T(8,128)(2,1)S(1)}, u32[]{:S(2)}, u32[]{:S(2)}) collective-permute-start(bf16[2,160,512]{2,1,0:T(8,128)(2,1)S(1)} %get-tuple-element.50), channel_id=1, source_target_pairs={{1,0},{0,1},{3,2},{2,3},{5,4},{4,5},{7,6},{6,7},{9,8},{8,9},{11,10... | collective-permute-start | bytes 983048 | tf_op jit(solution)/shard_map/ppermute | solution.py:252
  30.8 6.7 %all_to_all.10 = f32[4,8,512]{2,1,0:T(8,128)S(1)} all-to-all(f32[4,8,512]{2,1,0:T(8,128)S(1)} %broadcast_in_dim.7), channel_id=1, replica_groups=mesh['dp'=4,'space'=4,'tm'=2] {'dp'}, dimensions={0} | all-to-all | bytes 131072 | tf_op jit(solution)/shard_map/all_to_all | solution.py:258
  37.5 0.6 %broadcast_in_dim.8 = f32[4,8,512]{2,1,0:T(8,128)} broadcast(f32[8,512]{1,0:T(8,128)S(1)} %reduce_sum.9), dimensions={1,2} | broadcast | bytes 81920 | tf_op jit(solution)/shard_map/broadcast_in_dim | solution.py:257
  38.1 4.9 %all-to-all-start.1 = ((f32[4,8,512]{2,1,0:T(8,128)}), f32[4,8,512]{2,1,0:T(8,128)S(1)}, u32[]{:S(2)}, u32[]{:S(2)}) async-start(f32[4,8,512]{2,1,0:T(8,128)} %broadcast_in_dim.8), calls=%async_computation.1 | async-start | bytes 131072 | tf_op jit(solution)/shard_map/all_to_all | solution.py:258
  43.0 0.8 %finish.2 = bf16[320,512]{1,0:T(8,128)(2,1)} custom-call(f32[2,160,512]{2,1,0:T(8,128)S(1)} %get-tuple-element.47.own_ref, bf16[2,160,512]{2,1,0:T(8,128)(2,1)S(1)} %collective-permute-done.3.refs_0_), custom_call_target="tpu_custom_call" | custom-call | bytes 1500000 | tf_op jit(solution)/shard_map/finish/pallas_call | solution.py:358
  43.8 0.0 collective-permute-done.4.refs_0_
  43.8 0.8 %finish.3 = bf16[320,512]{1,0:T(8,128)(2,1)} custom-call(f32[2,160,512]{2,1,0:T(8,128)S(1)} %get-tuple-element.49.own_ref, bf16[2,160,512]{2,1,0:T(8,128)(2,1)S(1)} %collective-permute-done.4.refs_0_), custom_call_target="tpu_custom_call" | custom-call | bytes 1500000 | tf_op jit(solution)/shard_map/finish/pallas_call | solution.py:358
  44.5 4.2 %all-to-all-done.1.parts_ref = f32[4,8,512]{2,1,0:T(8,128)S(1)} async-done(((f32[4,8,512]{2,1,0:T(8,128)}), f32[4,8,512]{2,1,0:T(8,128)S(1)}, u32[]{:S(2)}, u32[]{:S(2)}) %all-to-all-start.1) | async-done | bytes 65568 | tf_op jit(solution)/shard_map/all_to_all | solution.py:258
  48.7 0.8 %sums.1 = (f32[1,512]{1,0:T(1,128)}, f32[8,39]{1,0:T(8,128)}) custom-call(s32[1]{0:T(128)} %bitcast.me_ref, f32[4,8,512]{2,1,0:T(8,128)S(1)} %all-to-all-done.1.parts_ref), custom_call_target="tpu_custom_call" | custom-call | tf_op jit(solution)/shard_map/sums/pallas_call | solution.py:373
  (5 shorter events, 0.0 us)
Async XLA Ops:
  0.6 11.8 %collective-permute-start.1 = (bf16[320,512]{1,0:T(8,128)(2,1)}, bf16[320,512]{1,0:T(8,128)(2,1)S(1)}, u32[]{:S(2)}, u32[]{:S(2)}) collective-permute-start(bf16[320,512]{1,0:T(8,128)(2,1)} %bitcast.10), channel_id=1, source_target_pairs={{1,0},{0,1},{3,2},{2,3},{5,4},{4,5},{7,6},{6,7},{9,8},{8,9},{11,10... | collective-permute-start | bytes 983048 | tf_op jit(solution)/shard_map/ppermute | solution.py:252
  3.7 15.8 %collective-permute-start = (bf16[320,512]{1,0:T(8,128)(2,1)}, bf16[320,512]{1,0:T(8,128)(2,1)S(1)}, u32[]{:S(2)}, u32[]{:S(2)}) collective-permute-start(bf16[320,512]{1,0:T(8,128)(2,1)} %bitcast.7), channel_id=1, source_target_pairs={{1,0},{0,1},{3,2},{2,3},{5,4},{4,5},{7,6},{6,7},{9,8},{8,9},{11,10... | collective-permute-start | bytes 983048 | tf_op jit(solution)/shard_map/ppermute | solution.py:252
  12.4 7.0 %copy-start = (bf16[1,20,16,512]{3,2,1,0:T(8,128)(2,1)S(1)}, bf16[1,20,16,512]{3,2,1,0:T(8,128)(2,1)}, u32[]{:S(2)}) copy-start(bf16[1,20,16,512]{3,2,1,0:T(8,128)(2,1)} %param.9) | copy-start | bytes 983044
  16.0 12.7 %collective-permute-start.3 = (bf16[2,160,512]{2,1,0:T(8,128)(2,1)S(1)}, bf16[2,160,512]{2,1,0:T(8,128)(2,1)S(1)}, u32[]{:S(2)}, u32[]{:S(2)}) collective-permute-start(bf16[2,160,512]{2,1,0:T(8,128)(2,1)S(1)} %get-tuple-element.42), channel_id=1, source_target_pairs={{1,0},{0,1},{3,2},{2,3},{5,4},{4,5},{7,6},{6,7},{9,8},{8,9},{11,10... | collective-permute-start | bytes 983048 | tf_op jit(solution)/shard_map/ppermute | solution.py:252
  25.0 3.7 %collective-permute-start.2 = (f32[8,128]{1,0:T(8,128)S(1)}, f32[8,128]{1,0:T(8,128)S(1)}, u32[]{:S(2)}, u32[]{:S(2)}) collective-permute-start(f32[8,128]{1,0:T(8,128)S(1)} %get-tuple-element.39), channel_id=1, source_target_pairs={{1,0},{0,1},{3,2},{2,3},{5,4},{4,5},{7,6},{6,7},{9,8},{8,9},{11,10... | collective-permute-start | bytes 12296 | tf_op jit(solution)/shard_map/ppermute | solution.py:252
  28.7 15.0 %collective-permute-start.4 = (bf16[2,160,512]{2,1,0:T(8,128)(2,1)S(1)}, bf16[2,160,512]{2,1,0:T(8,128)(2,1)S(1)}, u32[]{:S(2)}, u32[]{:S(2)}) collective-permute-start(bf16[2,160,512]{2,1,0:T(8,128)(2,1)S(1)} %get-tuple-element.50), channel_id=1, source_target_pairs={{1,0},{0,1},{3,2},{2,3},{5,4},{4,5},{7,6},{6,7},{9,8},{8,9},{11,10... | collective-permute-start | bytes 983048 | tf_op jit(solution)/shard_map/ppermute | solution.py:252
  38.1 10.6 %all-to-all-start.1 = ((f32[4,8,512]{2,1,0:T(8,128)}), f32[4,8,512]{2,1,0:T(8,128)S(1)}, u32[]{:S(2)}, u32[]{:S(2)}) async-start(f32[4,8,512]{2,1,0:T(8,128)} %broadcast_in_dim.8), calls=%async_computation.1 | async-start | bytes 131072 | tf_op jit(solution)/shard_map/all_to_all | solution.py:258

commit v10 on v7

--- a/solution.py
+++ b/solution.py
@@ -42,6 +42,14 @@
     for h in range(1, len(parts)):
         out = jnp.where(owner == h, parts[h], out)
     return out
+
+
+def row_sums(value):
+    return mm(value.astype(BF16), jnp.ones((value.shape[1], LANES), BF16))
+
+
+def over_lanes(tile, lanes):
+    return jnp.concatenate([tile] * (lanes // LANES) + [tile[:, :lanes % LANES]], axis=1)
 
 
 def stage_kernel(frames, width, bias_ref, x_ref, wq_ref, wk_ref, wv_ref, wo_ref, gain_ref,
@@ -106,7 +114,7 @@
                     s = jnp.where(same, s + rel_ref[f:f + CHUNK, head:head + 1, :], FAR)
                     s = s.reshape(CHUNK * BAND, rows)
                     e = jnp.exp(s - jnp.max(s, axis=-1, keepdims=True))
-                    p_ref[band, head, at, :] = (e * (1.0 / jnp.sum(e, axis=-1, keepdims=True))).astype(BF16)
+                    p_ref[band, head, at, :] = (e * over_lanes(1.0 / row_sums(e), rows)).astype(BF16)
                 outs.append(mm(p_ref[band, head], vp))
             att_ref[band, :, pair * LANES:(pair + 1) * LANES] = pick_heads(outs, owner).astype(BF16)
     att = att_ref[...].reshape(total, width)
@@ -149,6 +157,7 @@
         )
         da = d_att[:, pair * LANES:(pair + 1) * LANES]
         d_prob = mm(stack_heads(da, owner, per_pair), vp, NT)
+        q_turned, da_turned = qp.T, da.T
         parts = [[], [], []]
         for h in range(per_pair):
             head = pair * per_pair + h
@@ -163,11 +172,13 @@
                     part = part + carried[1][f:f + CHUNK, head:head + 1, :]
                 diag_ref[f:f + CHUNK, head:head + 1, :] = part
             probs, score = p_ref[band, head], ds_ref[head]
+            own = slice(h * head_dim, (h + 1) * head_dim)
             parts[0].append(mm(score, kp))
-            parts[1].append(mm(score, qp, TN))
-            parts[2].append(mm(probs, da, TN))
-        for n in range(3):
-            grads[n].append(pick_heads(parts[n], owner).astype(BF16))
+            parts[1].append(mm(q_turned[own], score))
+            parts[2].append(mm(da_turned[own], probs))
+        grads[0].append(pick_heads(parts[0], owner).astype(BF16))
+        for n in (1, 2):
+            grads[n].append(jnp.concatenate(parts[n], axis=0).astype(BF16).T)
     grad_ref[...] = mm(jnp.concatenate(grads[0] + grads[1] + grads[2], axis=1), proj_ref[...], NT)
     gain_sum = jnp.zeros((BAND, chans), F32)
     for f in range(0, frames, 2):

time: 43.7 us -> 45.4 us (1.039)
  Pallas kernels: 15.6 us -> 17.2 us
    pallas_call x1, Pallas kernels: 3.56 us -> 5.97 us  [per_device(): pl.pallas_call(functools.partial(forward_kernel, dims), in_specs=[smem] +...]
    pallas_call x2, Pallas kernels: 7.32 us -> 6.58 us  [per_device(): pl.pallas_call(functools.partial(backward_kernel, dims, band, last), in_s...]
  transfers between devices with their start and end apart: 13 -> 13, of which waited for: 5 -> 5; matrix products, arithmetic and copies ran while one was open for 4% -> 4% of each run, Pallas kernels for 34% -> 37%
where the time goes in v10:
time: 45.4 us; the launch traced here: 45.2 us
  Pallas kernels  17.2 us (38%)
  starting transfers between devices  16.7 us (37%)
  waiting for transfers between devices  8.67 us (19%)
  local copies, waits for them, and re-layouts  1.9 us (4%)
  between operations  0.72 us (2%)
    ppermute x7, starting transfers between devices, shifted(): lax.ppermute(value, axis, [((i + step) % count, i) for i in range(count)])  10.1 us
    ppermute x6, starting transfers between devices, group_sum(): parts.append(lax.ppermute(value, axis, pairs))  6.61 us
    pallas_call x2, Pallas kernels, per_device(): pl.pallas_call(functools.partial(backward_kernel, dims, band, last), in_s...  6.58 us
    pallas_call x1, Pallas kernels, per_device(): pl.pallas_call(functools.partial(forward_kernel, dims), in_specs=[smem] +...  5.97 us
    ppermute x7, waiting for transfers between devices, shifted(): lax.ppermute(value, axis, [((i + step) % count, i) for i in range(count)])  4.55 us
    ppermute x6, waiting for transfers between devices, group_sum(): parts.append(lax.ppermute(value, axis, pairs))  4.12 us
    pallas_call x1, Pallas kernels, per_device(): pl.pallas_call(functools.partial(stage_kernel, frames, width), in_specs=[...  2.36 us
    reshape x1, local copies, waits for them, and re-layouts, per_device(): out_grad[:, :, n * BAND:(n + 1) * BAND].reshape(rows, width)  1.02 us
  transfers between devices with their start and end apart: 13, of which 5 were waited for; matrix products, arithmetic and copies ran while one was open for 4% of the time, Pallas kernels for 37%

profile of v10, /device:TPU:0, one launch (start us, length us, event | category | flops | bytes accessed | tf_op | source)
XLA Modules:
  0.0 45.2 jit_solution(8168904695562751674)
XLA Ops:
  0.6 3.0 %collective-permute-start.1 = (bf16[320,512]{1,0:T(8,128)(2,1)}, bf16[320,512]{1,0:T(8,128)(2,1)S(1)}, u32[]{:S(2)}, u32[]{:S(2)}) collective-permute-start(bf16[320,512]{1,0:T(8,128)(2,1)} %bitcast.10), channel_id=1, source_target_pairs={{1,0},{0,1},{3,2},{2,3},{5,4},{4,5},{7,6},{6,7},{9,8},{8,9},{11,10... | collective-permute-start | bytes 983048 | tf_op jit(solution)/shard_map/ppermute | solution.py:259
  3.7 1.0 %slice_bitcast_fusion = (bf16[160,512]{1,0:T(8,128)(2,1)S(1)}, bf16[160,512]{1,0:T(8,128)(2,1)S(1)}) fusion(bf16[1,20,16,512]{3,2,1,0:T(8,128)(2,1)} %param.9), kind=kLoop, calls=%fused_computation | loop fusion | bytes 655360 | tf_op jit(solution)/shard_map/reshape | solution.py:297
  4.8 2.0 %collective-permute-start = (bf16[160,512]{1,0:T(8,128)(2,1)S(1)}, bf16[160,512]{1,0:T(8,128)(2,1)S(1)}, u32[]{:S(2)}, u32[]{:S(2)}) collective-permute-start(bf16[160,512]{1,0:T(8,128)(2,1)S(1)} %get-tuple-element.73.refs_0_), channel_id=1, source_target_pairs={{1,0},{0,1},{3,2},{2,3},{5,4},{4,5},{7,6},{6,7},{9,8},{8,9},{11,10... | collective-permute-start | bytes 491528 | tf_op jit(solution)/shard_map/ppermute | solution.py:259
  6.8 0.8 %broadcast_in_dim.2 = f32[8,39,8]{2,1,0:T(8,128)S(1)} broadcast(f32[8,39]{1,0:T(8,128)} %param.11), dimensions={0,1} | broadcast | bytes 11232 | tf_op jit(solution)/shard_map/broadcast_in_dim | solution.py:302
  7.6 0.1 reshape.38.bias_ref
  7.7 2.4 %stage.1 = (f32[20,8,160]{2,1,0:T(8,128)S(1)}, bf16[320,512]{1,0:T(8,128)(2,1)S(1)}, bf16[1024,1536]{1,0:T(8,128)(2,1)S(1)}, bf16[512,1024]{1,0:T(8,128)(2,1)S(1)}, f32[1,1024]{1,0:T(1,128)S(1)}) custom-call(f32[8,312]{1,0:T(8,128)S(1)} %reshape.38.bias_ref, bf16[320,512]{1,0:T(8,128)(2,1)} %bitcast.11, bf16[1024,512]{1,0:T(8,128)(2,1)} %wq_ref.1, ...), custom_call_target="tpu_custom_call" | custom-call | bytes 8000000 | tf_op jit(solution)/shard_map/stage/pallas_call | solution.py:307
  10.0 2.4 %collective-permute-done.1.refs_1_ = bf16[320,512]{1,0:T(8,128)(2,1)S(1)} collective-permute-done((bf16[320,512]{1,0:T(8,128)(2,1)}, bf16[320,512]{1,0:T(8,128)(2,1)S(1)}, u32[]{:S(2)}, u32[]{:S(2)}) %collective-permute-start.1) | collective-permute-done | bytes 327712 | tf_op jit(solution)/shard_map/ppermute | solution.py:259
  12.4 6.0 %attend.1 = (bf16[2,160,1536]{2,1,0:T(8,128)(2,1)S(1)}, bf16[2,8,160,160]{3,2,1,0:T(8,128)(2,1)S(1)}, bf16[2,160,1024]{2,1,0:T(8,128)(2,1)S(1)}, f32[2,160,128]{...) custom-call(s32[1]{0:T(128)} %bitcast.me_ref, ...), custom_call_target="tpu_custom_call" | custom-call | flops 4000000000 | bytes 8000000 | tf_op jit(solution)/shard_map/attend/pallas_call | solution.py:324
  18.4 2.1 %collective-permute-start.7 = (bf16[2,160,512]{2,1,0:T(8,128)(2,1)S(1)}, bf16[2,160,512]{2,1,0:T(8,128)(2,1)S(1)}, u32[]{:S(2)}, u32[]{:S(2)}) collective-permute-start(bf16[2,160,512]{2,1,0:T(8,128)(2,1)S(1)} %get-tuple-element.51), channel_id=1, source_target_pairs={{1,0},{0,1},{3,2},{2,3},{5,4},{4,5},{7,6},{6,7},{9,8},{8,9},{11,10... | collective-permute-start | bytes 983048 | tf_op jit(solution)/shard_map/ppermute | solution.py:259
  20.5 3.3 %attend_back.2 = (f32[160,512]{1,0:T(8,128)S(1)}, bf16[160,512]{1,0:T(8,128)(2,1)S(1)}, f32[1,1024]{1,0:T(1,128)S(1)}, f32[20,8,160]{2,1,0:T(8,128)S(1)}) custom-call(s32[1]{0:T(128)} %bitcast.me_ref, bf16[160,512]{1,0:T(8,128)(2,1)S(1)} %get-tuple-element.72.refs_0_, bf16[160,512]{1,0:T(8,128)(2,1)S(1)} %collective-permute-done.2.refs_1_, ...), custom_call_target="tpu_custom_call" | custom-call | flops 2500000000 | tf_op jit(solution)/shard_map/attend_back/pallas_call | solution.py:355
  23.8 0.1 collective-permute-start.6
  23.9 3.3 %attend_back.3 = (f32[160,512]{1,0:T(8,128)S(1)}, bf16[160,512]{1,0:T(8,128)(2,1)S(1)}, f32[8,512]{1,0:T(8,128)S(1)}) custom-call(s32[1]{0:T(128)} %bitcast.me_ref, bf16[160,512]{1,0:T(8,128)(2,1)S(1)} %get-tuple-element.73.refs_0_, bf16[160,512]{1,0:T(8,128)(2,1)S(1)} %collective-permute-done.refs_1_, f32[1,1024]{1,0:T(1,128)S(1)} %get-tuple-element.38.refs_2_, ...), custom_call_target="tpu_custom_call" | custom-call | flops 2500000000 | tf_op jit(solution)/shard_map/attend_back/pallas_call | solution.py:355
  27.3 2.0 %collective-permute-start.4 = (f32[8,512]{1,0:T(8,128)S(1)}, f32[8,512]{1,0:T(8,128)S(1)}, u32[]{:S(2)}, u32[]{:S(2)}) collective-permute-start(f32[8,512]{1,0:T(8,128)S(1)} %get-tuple-element.52), channel_id=1, source_target_pairs={{16,0},{24,8},{0,16},{8,24},{17,1},{25,9},{1,17},{9,25},{18,2},{26... | collective-permute-start | bytes 49160 | tf_op jit(solution)/shard_map/ppermute | solution.py:275
  29.4 1.1 %collective-permute-done.5 = f32[8,512]{1,0:T(8,128)S(1)} collective-permute-done((f32[8,512]{1,0:T(8,128)S(1)}, f32[8,512]{1,0:T(8,128)S(1)}, u32[]{:S(2)}, u32[]{:S(2)}) %collective-permute-start.5) | collective-permute-done | bytes 16416 | tf_op jit(solution)/shard_map/ppermute | solution.py:275
  30.4 2.1 %collective-permute-start.11 = (bf16[160,512]{1,0:T(8,128)(2,1)S(1)}, bf16[160,512]{1,0:T(8,128)(2,1)S(1)}, u32[]{:S(2)}, u32[]{:S(2)}) collective-permute-start(bf16[160,512]{1,0:T(8,128)(2,1)S(1)} %get-tuple-element.58), channel_id=1, source_target_pairs={{1,0},{0,1},{3,2},{2,3},{5,4},{4,5},{7,6},{6,7},{9,8},{8,9},{11,10... | collective-permute-start | bytes 491528 | tf_op jit(solution)/shard_map/ppermute | solution.py:259
  32.6 3.7 %collective-permute-start.10 = (f32[8,512]{1,0:T(8,128)S(1)}, f32[8,512]{1,0:T(8,128)S(1)}, u32[]{:S(2)}, u32[]{:S(2)}) collective-permute-start(f32[8,512]{1,0:T(8,128)S(1)} %add_add_fusion.1), channel_id=1, source_target_pairs={{6,0},{4,2},{2,4},{0,6},{7,1},{5,3},{3,5},{1,7},{14,8},{12,10},{10... | collective-permute-start | bytes 49160 | tf_op jit(solution)/shard_map/ppermute | solution.py:275
  36.3 0.8 %collective-permute-start.8 = (f32[8,512]{1,0:T(8,128)S(1)}, f32[8,512]{1,0:T(8,128)S(1)}, u32[]{:S(2)}, u32[]{:S(2)}) collective-permute-start(f32[8,512]{1,0:T(8,128)S(1)} %add_add_fusion.1), channel_id=1, source_target_pairs={{2,0},{0,2},{6,4},{4,6},{3,1},{1,3},{7,5},{5,7},{10,8},{8,10},{14,... | collective-permute-start | bytes 49160 | tf_op jit(solution)/shard_map/ppermute | solution.py:275
  37.1 0.8 %finish_out.1 = bf16[320,512]{1,0:T(8,128)(2,1)} custom-call(f32[2,160,512]{2,1,0:T(8,128)S(1)} %get-tuple-element.56.own_ref, bf16[2,160,512]{2,1,0:T(8,128)(2,1)S(1)} %collective-permute-done.7.refs_0_), custom_call_target="tpu_custom_call" | custom-call | bytes 1500000 | tf_op jit(solution)/shard_map/finish_out/pallas_call | solution.py:373
  37.9 0.3 collective-permute-done.10
  38.2 2.7 %collective-permute-done.9 = f32[8,512]{1,0:T(8,128)S(1)} collective-permute-done((f32[8,512]{1,0:T(8,128)S(1)}, f32[8,512]{1,0:T(8,128)S(1)}, u32[]{:S(2)}, u32[]{:S(2)}) %collective-permute-start.9) | collective-permute-done | bytes 16416 | tf_op jit(solution)/shard_map/ppermute | solution.py:275
  40.9 0.6 %collective-permute-start.12 = (f32[8,128]{1,0:T(8,128)S(1)}, f32[8,128]{1,0:T(8,128)S(1)}, u32[]{:S(2)}, u32[]{:S(2)}) collective-permute-start(f32[8,128]{1,0:T(8,128)S(1)} %slice.12.refs_0_), channel_id=1, source_target_pairs={{1,0},{0,1},{3,2},{2,3},{5,4},{4,5},{7,6},{6,7},{9,8},{8,9},{11,10... | collective-permute-start | bytes 12296 | tf_op jit(solution)/shard_map/ppermute | solution.py:259
  41.5 0.9 %finish_grad.1 = (bf16[320,512]{1,0:T(8,128)(2,1)}, f32[8,39]{1,0:T(8,128)}) custom-call(f32[8,512]{1,0:T(8,128)S(1)} %add_add_fusion.small_ref, f32[160,512]{1,0:T(8,128)S(1)} %get-tuple-element.64.refs_0_, f32[160,512]{1,0:T(8,128)S(1)} %get-tuple-element.65.refs_1_, bf16[160,512]{1,0:T(8,128)(2,1)S(1)} %collective-permute-done.6.refs_2_, ...), custom_call_target="tpu_custom_call" | custom-call | bytes 1500000 | tf_op jit(solution)/shard_map/finish_grad/pallas_call | solution.py:385
  42.4 2.2 %collective-permute-done.12.refs_1_ = f32[8,128]{1,0:T(8,128)S(1)} collective-permute-done((f32[8,128]{1,0:T(8,128)S(1)}, f32[8,128]{1,0:T(8,128)S(1)}, u32[]{:S(2)}, u32[]{:S(2)}) %collective-permute-start.12) | collective-permute-done | bytes 4128 | tf_op jit(solution)/shard_map/ppermute | solution.py:259
  44.6 0.6 %gain_sum.1 = f32[1,512]{1,0:T(1,128)} custom-call(s32[1]{0:T(128)} %bitcast.me_ref, f32[8,128]{1,0:T(8,128)S(1)} %slice.12.refs_0_, f32[8,128]{1,0:T(8,128)S(1)} %collective-permute-done.12.refs_1_), custom_call_target="tpu_custom_call" | custom-call | tf_op jit(solution)/shard_map/gain_sum/pallas_call | solution.py:395
  (15 shorter events, 0.2 us)
Async XLA Ops:
  0.6 11.8 %collective-permute-start.1 = (bf16[320,512]{1,0:T(8,128)(2,1)}, bf16[320,512]{1,0:T(8,128)(2,1)S(1)}, u32[]{:S(2)}, u32[]{:S(2)}) collective-permute-start(bf16[320,512]{1,0:T(8,128)(2,1)} %bitcast.10), channel_id=1, source_target_pairs={{1,0},{0,1},{3,2},{2,3},{5,4},{4,5},{7,6},{6,7},{9,8},{8,9},{11,10... | collective-permute-start | bytes 983048 | tf_op jit(solution)/shard_map/ppermute | solution.py:259
  4.7 15.8 %collective-permute-start.2 = (bf16[160,512]{1,0:T(8,128)(2,1)S(1)}, bf16[160,512]{1,0:T(8,128)(2,1)S(1)}, u32[]{:S(2)}, u32[]{:S(2)}) collective-permute-start(bf16[160,512]{1,0:T(8,128)(2,1)S(1)} %get-tuple-element.72.refs_0_), channel_id=1, source_target_pairs={{1,0},{0,1},{3,2},{2,3},{5,4},{4,5},{7,6},{6,7},{9,8},{8,9},{11,10... | collective-permute-start | bytes 491528 | tf_op jit(solution)/shard_map/ppermute | solution.py:259
  4.8 19.1 %collective-permute-start = (bf16[160,512]{1,0:T(8,128)(2,1)S(1)}, bf16[160,512]{1,0:T(8,128)(2,1)S(1)}, u32[]{:S(2)}, u32[]{:S(2)}) collective-permute-start(bf16[160,512]{1,0:T(8,128)(2,1)S(1)} %get-tuple-element.73.refs_0_), channel_id=1, source_target_pairs={{1,0},{0,1},{3,2},{2,3},{5,4},{4,5},{7,6},{6,7},{9,8},{8,9},{11,10... | collective-permute-start | bytes 491528 | tf_op jit(solution)/shard_map/ppermute | solution.py:259
  18.4 14.2 %collective-permute-start.7 = (bf16[2,160,512]{2,1,0:T(8,128)(2,1)S(1)}, bf16[2,160,512]{2,1,0:T(8,128)(2,1)S(1)}, u32[]{:S(2)}, u32[]{:S(2)}) collective-permute-start(bf16[2,160,512]{2,1,0:T(8,128)(2,1)S(1)} %get-tuple-element.51), channel_id=1, source_target_pairs={{1,0},{0,1},{3,2},{2,3},{5,4},{4,5},{7,6},{6,7},{9,8},{8,9},{11,10... | collective-permute-start | bytes 983048 | tf_op jit(solution)/shard_map/ppermute | solution.py:259
  23.8 8.8 %collective-permute-start.6 = (bf16[160,512]{1,0:T(8,128)(2,1)S(1)}, bf16[160,512]{1,0:T(8,128)(2,1)S(1)}, u32[]{:S(2)}, u32[]{:S(2)}) collective-permute-start(bf16[160,512]{1,0:T(8,128)(2,1)S(1)} %get-tuple-element.50), channel_id=1, source_target_pairs={{1,0},{0,1},{3,2},{2,3},{5,4},{4,5},{7,6},{6,7},{9,8},{8,9},{11,10... | collective-permute-start | bytes 491528 | tf_op jit(solution)/shard_map/ppermute | solution.py:259
  27.2 3.2 %collective-permute-start.5 = (f32[8,512]{1,0:T(8,128)S(1)}, f32[8,512]{1,0:T(8,128)S(1)}, u32[]{:S(2)}, u32[]{:S(2)}) collective-permute-start(f32[8,512]{1,0:T(8,128)S(1)} %get-tuple-element.52), channel_id=1, source_target_pairs={{24,0},{16,8},{8,16},{0,24},{25,1},{17,9},{9,17},{1,25},{26,2},{18... | collective-permute-start | bytes 49160 | tf_op jit(solution)/shard_map/ppermute | solution.py:275
  27.3 5.3 %collective-permute-start.4 = (f32[8,512]{1,0:T(8,128)S(1)}, f32[8,512]{1,0:T(8,128)S(1)}, u32[]{:S(2)}, u32[]{:S(2)}) collective-permute-start(f32[8,512]{1,0:T(8,128)S(1)} %get-tuple-element.52), channel_id=1, source_target_pairs={{16,0},{24,8},{0,16},{8,24},{17,1},{25,9},{1,17},{9,25},{18,2},{26... | collective-permute-start | bytes 49160 | tf_op jit(solution)/shard_map/ppermute | solution.py:275
  29.3 3.3 %collective-permute-start.3 = (f32[8,512]{1,0:T(8,128)S(1)}, f32[8,512]{1,0:T(8,128)S(1)}, u32[]{:S(2)}, u32[]{:S(2)}) collective-permute-start(f32[8,512]{1,0:T(8,128)S(1)} %get-tuple-element.52), channel_id=1, source_target_pairs={{8,0},{0,8},{24,16},{16,24},{9,1},{1,9},{25,17},{17,25},{10,2},{2,... | collective-permute-start | bytes 49160 | tf_op jit(solution)/shard_map/ppermute | solution.py:275
  30.4 7.4 %collective-permute-start.11 = (bf16[160,512]{1,0:T(8,128)(2,1)S(1)}, bf16[160,512]{1,0:T(8,128)(2,1)S(1)}, u32[]{:S(2)}, u32[]{:S(2)}) collective-permute-start(bf16[160,512]{1,0:T(8,128)(2,1)S(1)} %get-tuple-element.58), channel_id=1, source_target_pairs={{1,0},{0,1},{3,2},{2,3},{5,4},{4,5},{7,6},{6,7},{9,8},{8,9},{11,10... | collective-permute-start | bytes 491528 | tf_op jit(solution)/shard_map/ppermute | solution.py:259
  32.6 5.6 %collective-permute-start.10 = (f32[8,512]{1,0:T(8,128)S(1)}, f32[8,512]{1,0:T(8,128)S(1)}, u32[]{:S(2)}, u32[]{:S(2)}) collective-permute-start(f32[8,512]{1,0:T(8,128)S(1)} %add_add_fusion.1), channel_id=1, source_target_pairs={{6,0},{4,2},{2,4},{0,6},{7,1},{5,3},{3,5},{1,7},{14,8},{12,10},{10... | collective-permute-start | bytes 49160 | tf_op jit(solution)/shard_map/ppermute | solution.py:275
  36.3 4.6 %collective-permute-start.9 = (f32[8,512]{1,0:T(8,128)S(1)}, f32[8,512]{1,0:T(8,128)S(1)}, u32[]{:S(2)}, u32[]{:S(2)}) collective-permute-start(f32[8,512]{1,0:T(8,128)S(1)} %add_add_fusion.1), channel_id=1, source_target_pairs={{4,0},{6,2},{0,4},{2,6},{5,1},{7,3},{1,5},{3,7},{12,8},{14,10},{8,... | collective-permute-start | bytes 49160 | tf_op jit(solution)/shard_map/ppermute | solution.py:275
  36.3 4.6 %collective-permute-start.8 = (f32[8,512]{1,0:T(8,128)S(1)}, f32[8,512]{1,0:T(8,128)S(1)}, u32[]{:S(2)}, u32[]{:S(2)}) collective-permute-start(f32[8,512]{1,0:T(8,128)S(1)} %add_add_fusion.1), channel_id=1, source_target_pairs={{2,0},{0,2},{6,4},{4,6},{3,1},{1,3},{7,5},{5,7},{10,8},{8,10},{14,... | collective-permute-start | bytes 49160 | tf_op jit(solution)/shard_map/ppermute | solution.py:275
  40.9 3.7 %collective-permute-start.12 = (f32[8,128]{1,0:T(8,128)S(1)}, f32[8,128]{1,0:T(8,128)S(1)}, u32[]{:S(2)}, u32[]{:S(2)}) collective-permute-start(f32[8,128]{1,0:T(8,128)S(1)} %slice.12.refs_0_), channel_id=1, source_target_pairs={{1,0},{0,1},{3,2},{2,3},{5,4},{4,5},{7,6},{6,7},{9,8},{8,9},{11,10... | collective-permute-start | bytes 12296 | tf_op jit(solution)/shard_map/ppermute | solution.py:259

commit v11 on v7

--- a/solution.py
+++ b/solution.py
@@ -65,7 +65,7 @@
     gain_ref, rel_ref, proj_ref, wo_ref = refs[tm:tm + 4]
     qkv_ref, p_ref, xb_ref, inv_ref, own_ref = refs[tm + 4:tm + 9]
     msg_refs = refs[tm + 9:tm + 9 + tm - 1]
-    xw_ref, normed_ref, att_ref = refs[tm + 9 + tm - 1:]
+    xw_ref, normed_ref, att_ref, score_ref = refs[tm + 9 + tm - 1:]
     me = me_ref[0]
     rows = frames * BAND
     bands = pixels // BAND
@@ -91,24 +91,28 @@
     total = frames * pixels
     qkv = mm(normed_ref[...].reshape(total, -1), proj_ref[...]).astype(BF16)
     qkv_ref[...] = qkv.reshape(bands, rows, 3 * width)
-    for band in range(bands):
-        for pair in range(width // LANES):
-            qp, kp, vp = (
-                qkv_ref[band, :, n * width + pair * LANES:n * width + (pair + 1) * LANES] for n in range(3)
-            )
-            scores = mm(stack_heads(qp, owner, per_pair, scale), kp, NT)
-            outs = []
-            for h in range(per_pair):
-                head = pair * per_pair + h
-                for f in range(0, frames, CHUNK):
-                    at = slice(f * BAND, (f + CHUNK) * BAND)
-                    s = scores[h * rows + f * BAND:h * rows + (f + CHUNK) * BAND].reshape(CHUNK, BAND, rows)
-                    s = jnp.where(same, s + rel_ref[f:f + CHUNK, head:head + 1, :], FAR)
-                    s = s.reshape(CHUNK * BAND, rows)
-                    e = jnp.exp(s - jnp.max(s, axis=-1, keepdims=True))
-                    p_ref[band, head, at, :] = (e * (1.0 / jnp.sum(e, axis=-1, keepdims=True))).astype(BF16)
-                outs.append(mm(p_ref[band, head], vp))
-            att_ref[band, :, pair * LANES:(pair + 1) * LANES] = pick_heads(outs, owner).astype(BF16)
+    pairs = [(band, pair) for band in range(bands) for pair in range(width // LANES)]
+
+    def cols(n, pair):
+        return slice(n * width + pair * LANES, n * width + (pair + 1) * LANES)
+
+    for band, pair in pairs:
+        stacked = stack_heads(qkv_ref[band, :, cols(0, pair)], owner, per_pair, scale)
+        score_ref[band, pair] = mm(stacked, qkv_ref[band, :, cols(1, pair)], NT)
+    for band, pair in pairs:
+        for h in range(per_pair):
+            head = pair * per_pair + h
+            for f in range(0, frames, CHUNK):
+                at = slice(f * BAND, (f + CHUNK) * BAND)
+                s = score_ref[band, pair, h * rows + f * BAND:h * rows + (f + CHUNK) * BAND, :]
+                s = s.reshape(CHUNK, BAND, rows)
+                s = jnp.where(same, s + rel_ref[f:f + CHUNK, head:head + 1, :], FAR)
+                s = s.reshape(CHUNK * BAND, rows)
+                e = jnp.exp(s - jnp.max(s, axis=-1, keepdims=True))
+                p_ref[band, head, at, :] = (e * (1.0 / jnp.sum(e, axis=-1, keepdims=True))).astype(BF16)
+    for band, pair in pairs:
+        outs = [mm(p_ref[band, pair * per_pair + h], qkv_ref[band, :, cols(2, pair)]) for h in range(per_pair)]
+        att_ref[band, :, pair * LANES:(pair + 1) * LANES] = pick_heads(outs, owner).astype(BF16)
     att = att_ref[...].reshape(total, width)
     for k in range(1, tm):
         part = mm(att, wo_ref[:, pl.ds(place(tm - k), width)]).astype(BF16)
@@ -123,12 +127,13 @@
     gain_ref, qkv_ref, p_ref, xb_ref, inv_ref, proj_ref, wo_ref = refs[tm:tm + 7]
     rest = list(refs[tm + 7:])
     carried = (rest.pop(0), rest.pop(0)) if band else None
+    earlier = [rest.pop(0) for _ in range(band * (tm - 1))]
     own_ref = rest.pop(0)
     msg_refs = [rest.pop(0) for _ in range(tm - 1)]
     small_ref = rest.pop(0) if last else None
     gain_out = None if last else rest.pop(0)
     diag_ref = rest.pop() if last else rest.pop(0)
-    gw_ref, ds_ref, grad_ref = rest
+    gw_ref, dp_ref, ds_ref, grad_ref = rest
     me = me_ref[0]
     rows = frames * BAND
     per_pair = LANES // head_dim
@@ -142,32 +147,42 @@
         gw_ref[:, pl.ds(place(k), width)] = g_refs[k][...]
     owner = head_lanes(head_dim, rows)
     d_att = mm(gw_ref[...], wo_ref[...], NT).astype(BF16)
-    grads = [[], [], []]
-    for pair in range(width // LANES):
-        qp, kp, vp = (
-            qkv_ref[band, :, n * width + pair * LANES:n * width + (pair + 1) * LANES] for n in range(3)
-        )
-        da = d_att[:, pair * LANES:(pair + 1) * LANES]
-        d_prob = mm(stack_heads(da, owner, per_pair), vp, NT)
-        parts = [[], [], []]
+    pairs = range(width // LANES)
+
+    def part(n, pair):
+        return qkv_ref[band, :, n * width + pair * LANES:n * width + (pair + 1) * LANES]
+
+    def out_rows(pair):
+        return d_att[:, pair * LANES:(pair + 1) * LANES]
+
+    for pair in pairs:
+        dp_ref[pair] = mm(stack_heads(out_rows(pair), owner, per_pair), part(2, pair), NT)
+    for pair in pairs:
         for h in range(per_pair):
             head = pair * per_pair + h
             for f in range(0, frames, CHUNK):
                 at = slice(f * BAND, (f + CHUNK) * BAND)
                 full = p_ref[band, head, at, :].astype(F32)
-                t = d_prob[h * rows + f * BAND:h * rows + (f + CHUNK) * BAND]
+                t = dp_ref[pair, h * rows + f * BAND:h * rows + (f + CHUNK) * BAND, :]
                 score = full * (t - jnp.sum(full * t, axis=-1, keepdims=True))
                 ds_ref[head, at, :] = (score * scale).astype(BF16)
-                part = jnp.sum(score.reshape(CHUNK, BAND, rows), axis=1, keepdims=True)
+                folded = jnp.sum(score.reshape(CHUNK, BAND, rows), axis=1, keepdims=True)
                 if carried is not None:
-                    part = part + carried[1][f:f + CHUNK, head:head + 1, :]
-                diag_ref[f:f + CHUNK, head:head + 1, :] = part
-            probs, score = p_ref[band, head], ds_ref[head]
-            parts[0].append(mm(score, kp))
-            parts[1].append(mm(score, qp, TN))
-            parts[2].append(mm(probs, da, TN))
-        for n in range(3):
-            grads[n].append(pick_heads(parts[n], owner).astype(BF16))
+                    folded = folded + carried[1][f:f + CHUNK, head:head + 1, :]
+                diag_ref[f:f + CHUNK, head:head + 1, :] = folded
+    grads = [[], [], []]
+    for pair in pairs:
+        turned = [None, part(0, pair).T, out_rows(pair).T]
+        products = [[], [], []]
+        for h in range(per_pair):
+            head = pair * per_pair + h
+            own = slice(h * head_dim, (h + 1) * head_dim)
+            products[0].append(mm(ds_ref[head], part(1, pair)))
+            products[1].append(mm(turned[1][own], ds_ref[head]))
+            products[2].append(mm(turned[2][own], p_ref[band, head]))
+        grads[0].append(pick_heads(products[0], owner).astype(BF16))
+        for n in (1, 2):
+            grads[n].append(jnp.concatenate(products[n], axis=0).astype(BF16).T)
     grad_ref[...] = mm(jnp.concatenate(grads[0] + grads[1] + grads[2], axis=1), proj_ref[...], NT)
     gain_sum = jnp.zeros((BAND, chans), F32)
     for f in range(0, frames, 2):
@@ -180,7 +195,13 @@
         inner = jnp.mean(term * scaled, axis=-1, keepdims=True)
         grad_ref[at, :] = inv * (term - scaled * inner)
     for k in range(1, tm):
-        msg_refs[k - 1][...] = grad_ref[:, pl.ds(place(tm - k), width)].astype(BF16)
+        share = grad_ref[:, pl.ds(place(tm - k), width)].astype(BF16)
+        if last:
+            for n in range(band):
+                msg_refs[k - 1][n] = earlier[n * (tm - 1) + k - 1][...]
+            msg_refs[k - 1][band] = share
+        else:
+            msg_refs[k - 1][...] = share
     own_ref[...] = grad_ref[:, pl.ds(place(0), width)] + g_refs[0][...].astype(F32)
     gain_sum = jnp.sum(gain_sum, axis=0, keepdims=True)
     if carried is not None:
@@ -213,7 +234,8 @@
 
 def finish_grad_kernel(bands, frames, small_ref, *refs):
     *refs, out_ref, bias_ref = refs
-    finish_kernel(bands, frames, refs[:bands], refs[bands:], out_ref)
+    in_refs = [ref.at[band] for band in range(bands) for ref in refs[bands:]]
+    finish_kernel(bands, frames, refs[:bands], in_refs, out_ref)
     group, offsets = bias_ref.shape
     value = small_ref[:, LANES:]
     high = value.astype(BF16)
@@ -325,17 +347,23 @@
             pltpu.VMEM((total, chans), BF16),
             pltpu.VMEM((bands, rows, chans), BF16),
             pltpu.VMEM((bands, rows, width), BF16),
+            pltpu.VMEM((bands, width // LANES, LANES // head_dim * rows, rows), F32),
         ],
         compiler_params=params,
         cost_estimate=pl.CostEstimate(flops=4_000_000_000, bytes_accessed=8_000_000, transcendentals=0),
         name="attend",
     )(me1, *x_parts, gain, rel, proj, w_out)
     mix_in = [shifted(mix_out[k - 1], "tm", k) for k in range(1, tm)]
-    owns, ins, carry = [], [], []
+    owns, sent, carry = [], [], []
     diag = (frames, group, rows)
     for band in range(bands):
         last = band == bands - 1
-        scratch = [pltpu.VMEM((rows, chans), BF16), pltpu.VMEM((group, rows, rows), BF16), pltpu.VMEM((rows, chans), F32)]
+        scratch = [
+            pltpu.VMEM((rows, chans), BF16),
+            pltpu.VMEM((width // LANES, LANES // head_dim * rows, rows), F32),
+            pltpu.VMEM((group, rows, rows), BF16),
+            pltpu.VMEM((rows, chans), F32),
+        ]
         if last:
             extra = [jax.ShapeDtypeStruct((lines, LANES + span), F32)]
             scratch.append(pltpu.VMEM(diag, F32))
@@ -343,22 +371,22 @@
             extra = [jax.ShapeDtypeStruct((1, chans), F32), jax.ShapeDtypeStruct(diag, F32)]
         own, *rest = pl.pallas_call(
             functools.partial(backward_kernel, dims, band, last),
-            in_specs=[smem] + [vmem] * (tm + 7 + len(carry)),
+            in_specs=[smem] + [vmem] * (tm + 7 + len(carry) + len(sent)),
             out_specs=[vmem] * (tm + len(extra)),
-            out_shape=[jax.ShapeDtypeStruct((rows, width), F32)]
-            + [jax.ShapeDtypeStruct((rows, width), BF16)] * (tm - 1) + extra,
+            out_shape=[pltpu.VMEM((rows, width), F32)]
+            + [pltpu.VMEM((bands, rows, width) if last else (rows, width), BF16)] * (tm - 1) + extra,
             scratch_shapes=scratch,
             compiler_params=params,
             cost_estimate=pl.CostEstimate(flops=2_500_000_000, bytes_accessed=0, transcendentals=0),
             name="attend_back",
-        )(me1, *g_parts[band], gain, qkv, probs, xb, inv, proj, w_out, *carry)
-        sent, carry = rest[:tm - 1], rest[tm - 1:]
+        )(me1, *g_parts[band], gain, qkv, probs, xb, inv, proj, w_out, *carry, *sent)
+        sent, carry = (rest[:tm - 1] if last else sent + rest[:tm - 1]), rest[tm - 1:]
         owns.append(own)
-        ins += [shifted(sent[k - 1], "tm", k) for k in range(1, tm)]
+    grad_in = [shifted(sent[k - 1], "tm", k) for k in range(1, tm)]
 
     result = jax.ShapeDtypeStruct((total, width), BF16)
     finish_cost = pl.CostEstimate(flops=0, bytes_accessed=1_500_000, transcendentals=0)
-    small, (ins[:-1], mix_in) = group_sum(carry[0], "dp", (ins[:-1], mix_in))
+    small, mix_in = group_sum(carry[0], "dp", mix_in)
     block_out = pl.pallas_call(
         functools.partial(finish_out_kernel, bands, frames),
         in_specs=[vmem] * tm,
@@ -368,18 +396,18 @@
         cost_estimate=finish_cost,
         name="finish_out",
     )(mix_own, *mix_in)
-    small, (block_out, ins[-1]) = group_sum(small, "space", (block_out, ins[-1]))
+    small, block_out = group_sum(small, "space", block_out)
     tile = small[:chans // LANES, :LANES]
     tiles = [shifted(tile, "tm", k) for k in range(1, tm)]
     input_grad, bias_grad = pl.pallas_call(
         functools.partial(finish_grad_kernel, bands, frames),
-        in_specs=[vmem] * (1 + bands * tm),
+        in_specs=[vmem] * (bands + tm),
         out_specs=[vmem] * 2,
         out_shape=[result, jax.ShapeDtypeStruct((group, offsets), F32)],
         compiler_params=params,
         cost_estimate=finish_cost,
         name="finish_grad",
-    )(small, *owns, *ins)
+    )(small, *owns, *grad_in)
     tiles, input_grad = lax.optimization_barrier((tiles, input_grad))
     gain_grad = pl.pallas_call(
         gain_kernel,

time: 43.7 us -> 40.2 us (0.920)
  Pallas kernels: 15.6 us -> 13.6 us
  starting transfers between devices: 16.6 us -> 15.6 us
  waiting for transfers between devices: 8.68 us -> 8.14 us
    pallas_call x2, Pallas kernels: 7.32 us -> 5.69 us  [per_device(): pl.pallas_call(functools.partial(backward_kernel, dims, band, last), in_s...]
    ppermute x7 -> x6, starting transfers between devices: 10 us -> 9.25 us  [shifted(): lax.ppermute(value, axis, [((i + step) % count, i) for i in range(count)])]
    ppermute x7 -> x6, waiting for transfers between devices: 4.55 us -> 4.1 us  [shifted(): lax.ppermute(value, axis, [((i + step) % count, i) for i in range(count)])]
  transfers between devices with their start and end apart: 13 -> 12, of which waited for: 5 -> 6; matrix products, arithmetic and copies ran while one was open for 4% -> 5% of each run, Pallas kernels for 34% -> 32%
where the time goes in v11:
time: 40.2 us; the launch traced here: 40 us
  starting transfers between devices  15.6 us (39%)
  Pallas kernels  13.6 us (34%)
  waiting for transfers between devices  8.14 us (20%)
  local copies, waits for them, and re-layouts  1.9 us (5%)
  between operations  0.71 us (2%)
    ppermute x6, starting transfers between devices, shifted(): lax.ppermute(value, axis, [((i + step) % count, i) for i in range(count)])  9.25 us
    ppermute x6, starting transfers between devices, group_sum(): parts.append(lax.ppermute(value, axis, pairs))  6.39 us
    pallas_call x2, Pallas kernels, per_device(): pl.pallas_call(functools.partial(backward_kernel, dims, band, last), in_s...  5.69 us
    ppermute x6, waiting for transfers between devices, shifted(): lax.ppermute(value, axis, [((i + step) % count, i) for i in range(count)])  4.1 us
    ppermute x6, waiting for transfers between devices, group_sum(): parts.append(lax.ppermute(value, axis, pairs))  4.04 us
    pallas_call x1, Pallas kernels, per_device(): pl.pallas_call(functools.partial(forward_kernel, dims), in_specs=[smem] +...  3.22 us
    pallas_call x1, Pallas kernels, per_device(): pl.pallas_call(functools.partial(stage_kernel, frames, width), in_specs=[...  2.36 us
    reshape x1, local copies, waits for them, and re-layouts, per_device(): out_grad[:, :, n * BAND:(n + 1) * BAND].reshape(rows, width)  1.02 us
  transfers between devices with their start and end apart: 12, of which 6 were waited for; matrix products, arithmetic and copies ran while one was open for 5% of the time, Pallas kernels for 32%

profile of v11, /device:TPU:0, one launch (start us, length us, event | category | flops | bytes accessed | tf_op | source)
XLA Modules:
  0.0 40.0 jit_solution(17712477542473429636)
XLA Ops:
  0.6 3.0 %collective-permute-start.1 = (bf16[320,512]{1,0:T(8,128)(2,1)}, bf16[320,512]{1,0:T(8,128)(2,1)S(1)}, u32[]{:S(2)}, u32[]{:S(2)}) collective-permute-start(bf16[320,512]{1,0:T(8,128)(2,1)} %bitcast.10), channel_id=1, source_target_pairs={{1,0},{0,1},{3,2},{2,3},{5,4},{4,5},{7,6},{6,7},{9,8},{8,9},{11,10... | collective-permute-start | bytes 983048 | tf_op jit(solution)/shard_map/ppermute | solution.py:270
  3.7 1.0 %slice_bitcast_fusion = (bf16[160,512]{1,0:T(8,128)(2,1)S(1)}, bf16[160,512]{1,0:T(8,128)(2,1)S(1)}) fusion(bf16[1,20,16,512]{3,2,1,0:T(8,128)(2,1)} %param.9), kind=kLoop, calls=%fused_computation | loop fusion | bytes 655360 | tf_op jit(solution)/shard_map/reshape | solution.py:308
  4.8 2.0 %collective-permute-start = (bf16[160,512]{1,0:T(8,128)(2,1)S(1)}, bf16[160,512]{1,0:T(8,128)(2,1)S(1)}, u32[]{:S(2)}, u32[]{:S(2)}) collective-permute-start(bf16[160,512]{1,0:T(8,128)(2,1)S(1)} %get-tuple-element.69.refs_0_), channel_id=1, source_target_pairs={{1,0},{0,1},{3,2},{2,3},{5,4},{4,5},{7,6},{6,7},{9,8},{8,9},{11,10... | collective-permute-start | bytes 491528 | tf_op jit(solution)/shard_map/ppermute | solution.py:270
  6.8 0.8 %broadcast_in_dim.2 = f32[8,39,8]{2,1,0:T(8,128)S(1)} broadcast(f32[8,39]{1,0:T(8,128)} %param.11), dimensions={0,1} | broadcast | bytes 11232 | tf_op jit(solution)/shard_map/broadcast_in_dim | solution.py:313
  7.7 2.4 %stage.1 = (f32[20,8,160]{2,1,0:T(8,128)S(1)}, bf16[320,512]{1,0:T(8,128)(2,1)S(1)}, bf16[1024,1536]{1,0:T(8,128)(2,1)S(1)}, bf16[512,1024]{1,0:T(8,128)(2,1)S(1)}, f32[1,1024]{1,0:T(1,128)S(1)}) custom-call(f32[8,312]{1,0:T(8,128)S(1)} %reshape.38.bias_ref, bf16[320,512]{1,0:T(8,128)(2,1)} %bitcast.11, bf16[1024,512]{1,0:T(8,128)(2,1)} %wq_ref.1, ...), custom_call_target="tpu_custom_call" | custom-call | bytes 8000000 | tf_op jit(solution)/shard_map/stage/pallas_call | solution.py:318
  10.0 2.4 %collective-permute-done.1.refs_1_ = bf16[320,512]{1,0:T(8,128)(2,1)S(1)} collective-permute-done((bf16[320,512]{1,0:T(8,128)(2,1)}, bf16[320,512]{1,0:T(8,128)(2,1)S(1)}, u32[]{:S(2)}, u32[]{:S(2)}) %collective-permute-start.1) | collective-permute-done | bytes 327712 | tf_op jit(solution)/shard_map/ppermute | solution.py:270
  12.4 3.2 %attend.1 = (bf16[2,160,1536]{2,1,0:T(8,128)(2,1)S(1)}, bf16[2,8,160,160]{3,2,1,0:T(8,128)(2,1)S(1)}, bf16[2,160,1024]{2,1,0:T(8,128)(2,1)S(1)}, f32[2,160,128]{...) custom-call(s32[1]{0:T(128)} %bitcast.me_ref, ...), custom_call_target="tpu_custom_call" | custom-call | flops 4000000000 | bytes 8000000 | tf_op jit(solution)/shard_map/attend/pallas_call | solution.py:335
  15.6 2.1 %collective-permute-start.6 = (bf16[2,160,512]{2,1,0:T(8,128)(2,1)S(1)}, bf16[2,160,512]{2,1,0:T(8,128)(2,1)S(1)}, u32[]{:S(2)}, u32[]{:S(2)}) collective-permute-start(bf16[2,160,512]{2,1,0:T(8,128)(2,1)S(1)} %get-tuple-element.49), channel_id=1, source_target_pairs={{1,0},{0,1},{3,2},{2,3},{5,4},{4,5},{7,6},{6,7},{9,8},{8,9},{11,10... | collective-permute-start | bytes 983048 | tf_op jit(solution)/shard_map/ppermute | solution.py:270
  17.8 2.7 %attend_back.2 = (f32[160,512]{1,0:T(8,128)S(1)}, bf16[160,512]{1,0:T(8,128)(2,1)S(1)}, f32[1,1024]{1,0:T(1,128)S(1)}, f32[20,8,160]{2,1,0:T(8,128)S(1)}) custom-call(s32[1]{0:T(128)} %bitcast.me_ref, bf16[160,512]{1,0:T(8,128)(2,1)S(1)} %get-tuple-element.68.refs_0_, bf16[160,512]{1,0:T(8,128)(2,1)S(1)} %collective-permute-done.2.refs_1_, ...), custom_call_target="tpu_custom_call" | custom-call | flops 2500000000 | tf_op jit(solution)/shard_map/attend_back/pallas_call | solution.py:372
  20.5 3.0 %attend_back.3 = (f32[160,512]{1,0:T(8,128)S(1)}, bf16[2,160,512]{2,1,0:T(8,128)(2,1)S(1)}, f32[8,512]{1,0:T(8,128)S(1)}) custom-call(s32[1]{0:T(128)} %bitcast.me_ref, bf16[160,512]{1,0:T(8,128)(2,1)S(1)} %get-tuple-element.69.refs_0_, bf16[160,512]{1,0:T(8,128)(2,1)S(1)} %collective-permute-done.refs_1_, f32[1,1024]{1,0:T(1,128)S(1)} %get-tuple-element.36.refs_2_, ...), custom_call_target="tpu_custom_call" | custom-call | flops 2500000000 | tf_op jit(solution)/shard_map/attend_back/pallas_call | solution.py:372
  23.6 1.6 %collective-permute-start.4 = (f32[8,512]{1,0:T(8,128)S(1)}, f32[8,512]{1,0:T(8,128)S(1)}, u32[]{:S(2)}, u32[]{:S(2)}) collective-permute-start(f32[8,512]{1,0:T(8,128)S(1)} %get-tuple-element.50), channel_id=1, source_target_pairs={{16,0},{24,8},{0,16},{8,24},{17,1},{25,9},{1,17},{9,25},{18,2},{26... | collective-permute-start | bytes 49160 | tf_op jit(solution)/shard_map/ppermute | solution.py:286
  25.1 0.3 collective-permute-start.3
  25.4 1.0 %collective-permute-start.11 = (bf16[2,160,512]{2,1,0:T(8,128)(2,1)S(1)}, bf16[2,160,512]{2,1,0:T(8,128)(2,1)S(1)}, u32[]{:S(2)}, u32[]{:S(2)}) collective-permute-start(bf16[2,160,512]{2,1,0:T(8,128)(2,1)S(1)} %get-tuple-element.63), channel_id=1, source_target_pairs={{1,0},{0,1},{3,2},{2,3},{5,4},{4,5},{7,6},{6,7},{9,8},{8,9},{11,10... | collective-permute-start | bytes 983048 | tf_op jit(solution)/shard_map/ppermute | solution.py:270
  26.4 0.5 %collective-permute-done.5 = f32[8,512]{1,0:T(8,128)S(1)} collective-permute-done((f32[8,512]{1,0:T(8,128)S(1)}, f32[8,512]{1,0:T(8,128)S(1)}, u32[]{:S(2)}, u32[]{:S(2)}) %collective-permute-start.5) | collective-permute-done | bytes 16416 | tf_op jit(solution)/shard_map/ppermute | solution.py:286
  26.8 0.5 %collective-permute-done.4 = f32[8,512]{1,0:T(8,128)S(1)} collective-permute-done((f32[8,512]{1,0:T(8,128)S(1)}, f32[8,512]{1,0:T(8,128)S(1)}, u32[]{:S(2)}, u32[]{:S(2)}) %collective-permute-start.4) | collective-permute-done | bytes 16416 | tf_op jit(solution)/shard_map/ppermute | solution.py:286
  27.4 3.7 %collective-permute-start.9 = (f32[8,512]{1,0:T(8,128)S(1)}, f32[8,512]{1,0:T(8,128)S(1)}, u32[]{:S(2)}, u32[]{:S(2)}) collective-permute-start(f32[8,512]{1,0:T(8,128)S(1)} %add_add_fusion.1), channel_id=1, source_target_pairs={{6,0},{4,2},{2,4},{0,6},{7,1},{5,3},{3,5},{1,7},{14,8},{12,10},{10... | collective-permute-start | bytes 49160 | tf_op jit(solution)/shard_map/ppermute | solution.py:286
  31.1 0.8 %collective-permute-start.7 = (f32[8,512]{1,0:T(8,128)S(1)}, f32[8,512]{1,0:T(8,128)S(1)}, u32[]{:S(2)}, u32[]{:S(2)}) collective-permute-start(f32[8,512]{1,0:T(8,128)S(1)} %add_add_fusion.1), channel_id=1, source_target_pairs={{2,0},{0,2},{6,4},{4,6},{3,1},{1,3},{7,5},{5,7},{10,8},{8,10},{14,... | collective-permute-start | bytes 49160 | tf_op jit(solution)/shard_map/ppermute | solution.py:286
  31.8 0.8 %finish_out.1 = bf16[320,512]{1,0:T(8,128)(2,1)} custom-call(f32[2,160,512]{2,1,0:T(8,128)S(1)} %get-tuple-element.54.own_ref, bf16[2,160,512]{2,1,0:T(8,128)(2,1)S(1)} %collective-permute-done.6.refs_0_), custom_call_target="tpu_custom_call" | custom-call | bytes 1500000 | tf_op jit(solution)/shard_map/finish_out/pallas_call | solution.py:390
  32.7 0.3 collective-permute-done.9
  33.0 2.7 %collective-permute-done.8 = f32[8,512]{1,0:T(8,128)S(1)} collective-permute-done((f32[8,512]{1,0:T(8,128)S(1)}, f32[8,512]{1,0:T(8,128)S(1)}, u32[]{:S(2)}, u32[]{:S(2)}) %collective-permute-start.8) | collective-permute-done | bytes 16416 | tf_op jit(solution)/shard_map/ppermute | solution.py:286
  35.7 1.0 %collective-permute-start.10 = (f32[8,128]{1,0:T(8,128)S(1)}, f32[8,128]{1,0:T(8,128)S(1)}, u32[]{:S(2)}, u32[]{:S(2)}) collective-permute-start(f32[8,128]{1,0:T(8,128)S(1)} %slice.12.refs_0_), channel_id=1, source_target_pairs={{1,0},{0,1},{3,2},{2,3},{5,4},{4,5},{7,6},{6,7},{9,8},{8,9},{11,10... | collective-permute-start | bytes 12296 | tf_op jit(solution)/shard_map/ppermute | solution.py:270
  36.8 0.9 %finish_grad.1 = (bf16[320,512]{1,0:T(8,128)(2,1)}, f32[8,39]{1,0:T(8,128)}) custom-call(f32[8,512]{1,0:T(8,128)S(1)} %add_add_fusion.small_ref, f32[160,512]{1,0:T(8,128)S(1)} %get-tuple-element.61.refs_0_, f32[160,512]{1,0:T(8,128)S(1)} %get-tuple-element.62.refs_1_, bf16[2,160,512]{2,1,0:T(8,128)(2,1)S(1)} %collective-permute-done.11.refs_2_), custom_call_target="tpu_custom_call" | custom-call | bytes 1500000 | tf_op jit(solution)/shard_map/finish_grad/pallas_call | solution.py:402
  37.7 1.7 %collective-permute-done.10.refs_1_ = f32[8,128]{1,0:T(8,128)S(1)} collective-permute-done((f32[8,128]{1,0:T(8,128)S(1)}, f32[8,128]{1,0:T(8,128)S(1)}, u32[]{:S(2)}, u32[]{:S(2)}) %collective-permute-start.10) | collective-permute-done | bytes 4128 | tf_op jit(solution)/shard_map/ppermute | solution.py:270
  39.4 0.6 %gain_sum.1 = f32[1,512]{1,0:T(1,128)} custom-call(s32[1]{0:T(128)} %bitcast.me_ref, f32[8,128]{1,0:T(8,128)S(1)} %slice.12.refs_0_, f32[8,128]{1,0:T(8,128)S(1)} %collective-permute-done.10.refs_1_), custom_call_target="tpu_custom_call" | custom-call | tf_op jit(solution)/shard_map/gain_sum/pallas_call | solution.py:412
  (13 shorter events, 0.3 us)
Async XLA Ops:
  0.6 11.8 %collective-permute-start.1 = (bf16[320,512]{1,0:T(8,128)(2,1)}, bf16[320,512]{1,0:T(8,128)(2,1)S(1)}, u32[]{:S(2)}, u32[]{:S(2)}) collective-permute-start(bf16[320,512]{1,0:T(8,128)(2,1)} %bitcast.10), channel_id=1, source_target_pairs={{1,0},{0,1},{3,2},{2,3},{5,4},{4,5},{7,6},{6,7},{9,8},{8,9},{11,10... | collective-permute-start | bytes 983048 | tf_op jit(solution)/shard_map/ppermute | solution.py:270
  4.7 13.1 %collective-permute-start.2 = (bf16[160,512]{1,0:T(8,128)(2,1)S(1)}, bf16[160,512]{1,0:T(8,128)(2,1)S(1)}, u32[]{:S(2)}, u32[]{:S(2)}) collective-permute-start(bf16[160,512]{1,0:T(8,128)(2,1)S(1)} %get-tuple-element.68.refs_0_), channel_id=1, source_target_pairs={{1,0},{0,1},{3,2},{2,3},{5,4},{4,5},{7,6},{6,7},{9,8},{8,9},{11,10... | collective-permute-start | bytes 491528 | tf_op jit(solution)/shard_map/ppermute | solution.py:270
  4.8 15.7 %collective-permute-start = (bf16[160,512]{1,0:T(8,128)(2,1)S(1)}, bf16[160,512]{1,0:T(8,128)(2,1)S(1)}, u32[]{:S(2)}, u32[]{:S(2)}) collective-permute-start(bf16[160,512]{1,0:T(8,128)(2,1)S(1)} %get-tuple-element.69.refs_0_), channel_id=1, source_target_pairs={{1,0},{0,1},{3,2},{2,3},{5,4},{4,5},{7,6},{6,7},{9,8},{8,9},{11,10... | collective-permute-start | bytes 491528 | tf_op jit(solution)/shard_map/ppermute | solution.py:270
  15.6 11.7 %collective-permute-start.6 = (bf16[2,160,512]{2,1,0:T(8,128)(2,1)S(1)}, bf16[2,160,512]{2,1,0:T(8,128)(2,1)S(1)}, u32[]{:S(2)}, u32[]{:S(2)}) collective-permute-start(bf16[2,160,512]{2,1,0:T(8,128)(2,1)S(1)} %get-tuple-element.49), channel_id=1, source_target_pairs={{1,0},{0,1},{3,2},{2,3},{5,4},{4,5},{7,6},{6,7},{9,8},{8,9},{11,10... | collective-permute-start | bytes 983048 | tf_op jit(solution)/shard_map/ppermute | solution.py:270
  23.5 3.4 %collective-permute-start.5 = (f32[8,512]{1,0:T(8,128)S(1)}, f32[8,512]{1,0:T(8,128)S(1)}, u32[]{:S(2)}, u32[]{:S(2)}) collective-permute-start(f32[8,512]{1,0:T(8,128)S(1)} %get-tuple-element.50), channel_id=1, source_target_pairs={{24,0},{16,8},{8,16},{0,24},{25,1},{17,9},{9,17},{1,25},{26,2},{18... | collective-permute-start | bytes 49160 | tf_op jit(solution)/shard_map/ppermute | solution.py:286
  23.6 3.8 %collective-permute-start.4 = (f32[8,512]{1,0:T(8,128)S(1)}, f32[8,512]{1,0:T(8,128)S(1)}, u32[]{:S(2)}, u32[]{:S(2)}) collective-permute-start(f32[8,512]{1,0:T(8,128)S(1)} %get-tuple-element.50), channel_id=1, source_target_pairs={{16,0},{24,8},{0,16},{8,24},{17,1},{25,9},{1,17},{9,25},{18,2},{26... | collective-permute-start | bytes 49160 | tf_op jit(solution)/shard_map/ppermute | solution.py:286
  25.1 2.3 %collective-permute-start.3 = (f32[8,512]{1,0:T(8,128)S(1)}, f32[8,512]{1,0:T(8,128)S(1)}, u32[]{:S(2)}, u32[]{:S(2)}) collective-permute-start(f32[8,512]{1,0:T(8,128)S(1)} %get-tuple-element.50), channel_id=1, source_target_pairs={{8,0},{0,8},{24,16},{16,24},{9,1},{1,9},{25,17},{17,25},{10,2},{2,... | collective-permute-start | bytes 49160 | tf_op jit(solution)/shard_map/ppermute | solution.py:286
  25.4 11.4 %collective-permute-start.11 = (bf16[2,160,512]{2,1,0:T(8,128)(2,1)S(1)}, bf16[2,160,512]{2,1,0:T(8,128)(2,1)S(1)}, u32[]{:S(2)}, u32[]{:S(2)}) collective-permute-start(bf16[2,160,512]{2,1,0:T(8,128)(2,1)S(1)} %get-tuple-element.63), channel_id=1, source_target_pairs={{1,0},{0,1},{3,2},{2,3},{5,4},{4,5},{7,6},{6,7},{9,8},{8,9},{11,10... | collective-permute-start | bytes 983048 | tf_op jit(solution)/shard_map/ppermute | solution.py:270
  27.4 5.6 %collective-permute-start.9 = (f32[8,512]{1,0:T(8,128)S(1)}, f32[8,512]{1,0:T(8,128)S(1)}, u32[]{:S(2)}, u32[]{:S(2)}) collective-permute-start(f32[8,512]{1,0:T(8,128)S(1)} %add_add_fusion.1), channel_id=1, source_target_pairs={{6,0},{4,2},{2,4},{0,6},{7,1},{5,3},{3,5},{1,7},{14,8},{12,10},{10... | collective-permute-start | bytes 49160 | tf_op jit(solution)/shard_map/ppermute | solution.py:286
  31.1 4.6 %collective-permute-start.8 = (f32[8,512]{1,0:T(8,128)S(1)}, f32[8,512]{1,0:T(8,128)S(1)}, u32[]{:S(2)}, u32[]{:S(2)}) collective-permute-start(f32[8,512]{1,0:T(8,128)S(1)} %add_add_fusion.1), channel_id=1, source_target_pairs={{4,0},{6,2},{0,4},{2,6},{5,1},{7,3},{1,5},{3,7},{12,8},{14,10},{8,... | collective-permute-start | bytes 49160 | tf_op jit(solution)/shard_map/ppermute | solution.py:286
  31.1 4.6 %collective-permute-start.7 = (f32[8,512]{1,0:T(8,128)S(1)}, f32[8,512]{1,0:T(8,128)S(1)}, u32[]{:S(2)}, u32[]{:S(2)}) collective-permute-start(f32[8,512]{1,0:T(8,128)S(1)} %add_add_fusion.1), channel_id=1, source_target_pairs={{2,0},{0,2},{6,4},{4,6},{3,1},{1,3},{7,5},{5,7},{10,8},{8,10},{14,... | collective-permute-start | bytes 49160 | tf_op jit(solution)/shard_map/ppermute | solution.py:286
  35.7 3.7 %collective-permute-start.10 = (f32[8,128]{1,0:T(8,128)S(1)}, f32[8,128]{1,0:T(8,128)S(1)}, u32[]{:S(2)}, u32[]{:S(2)}) collective-permute-start(f32[8,128]{1,0:T(8,128)S(1)} %slice.12.refs_0_), channel_id=1, source_target_pairs={{1,0},{0,1},{3,2},{2,3},{5,4},{4,5},{7,6},{6,7},{9,8},{8,9},{11,10... | collective-permute-start | bytes 12296 | tf_op jit(solution)/shard_map/ppermute | solution.py:270

commit v12 on v11

--- a/solution.py
+++ b/solution.py
@@ -45,7 +45,7 @@
 
 
 def stage_kernel(frames, width, bias_ref, x_ref, wq_ref, wk_ref, wv_ref, wo_ref, gain_ref,
-                 rel_ref, x_out, proj_out, wo_out, gain_out, sems):
+                 rel_ref, x_out, proj_out, wo_out, gain_out, proj_turned, wo_turned, sems):
     pairs = [(x_ref, x_out), (wo_ref, wo_out), (gain_ref, gain_out)]
     pairs += [(w, proj_out.at[:, n * width:(n + 1) * width]) for n, w in enumerate((wq_ref, wk_ref, wv_ref))]
     copies = [pltpu.make_async_copy(source, target, sems.at[n]) for n, (source, target) in enumerate(pairs)]
@@ -57,6 +57,9 @@
         rel_ref[i] = bias_ref[:, start:start + rows]
     for copy in copies:
         copy.wait()
+    for source, target in ((proj_out, proj_turned), (wo_out, wo_turned)):
+        for start in range(0, source.shape[1], 2 * LANES):
+            target[start:start + 2 * LANES, :] = source[:, start:start + 2 * LANES].T
 
 
 def forward_kernel(dims, me_ref, *refs):
@@ -146,7 +149,7 @@
     for k in range(tm):
         gw_ref[:, pl.ds(place(k), width)] = g_refs[k][...]
     owner = head_lanes(head_dim, rows)
-    d_att = mm(gw_ref[...], wo_ref[...], NT).astype(BF16)
+    d_att = mm(gw_ref[...], wo_ref[...]).astype(BF16)
     pairs = range(width // LANES)
 
     def part(n, pair):
@@ -183,7 +186,7 @@
         grads[0].append(pick_heads(products[0], owner).astype(BF16))
         for n in (1, 2):
             grads[n].append(jnp.concatenate(products[n], axis=0).astype(BF16).T)
-    grad_ref[...] = mm(jnp.concatenate(grads[0] + grads[1] + grads[2], axis=1), proj_ref[...], NT)
+    grad_ref[...] = mm(jnp.concatenate(grads[0] + grads[1] + grads[2], axis=1), proj_ref[...])
     gain_sum = jnp.zeros((BAND, chans), F32)
     for f in range(0, frames, 2):
         at = slice(f * BAND, (f + 2) * BAND)
@@ -284,9 +287,10 @@
                 other = digit ^ step if radix in (2, 4) else (digit + step) % radix
                 pairs.append((i + (other - digit) * stride, i))
             parts.append(lax.ppermute(value, axis, pairs))
-        parts, beside = lax.optimization_barrier((parts, beside))
+        stride *= radix
+        if stride == count:
+            parts, beside = lax.optimization_barrier((parts, beside))
         value = sum(parts[1:], parts[0])
-        stride *= radix
     return value, beside
 
 
@@ -315,16 +319,18 @@
     params = pltpu.CompilerParams(vmem_limit_bytes=VMEM_LIMIT)
     held = [x0, w_query, w_key, w_value, w_out, gain]
     held = [pltpu.with_memory_space_constraint(h, pltpu.HBM) for h in held]
-    rel, x0, proj, w_out, gain = pl.pallas_call(
+    rel, x0, proj, w_out, gain, proj_turned, out_turned = pl.pallas_call(
         functools.partial(stage_kernel, frames, width),
         in_specs=[vmem] + [pl.BlockSpec(memory_space=pltpu.HBM)] * len(held),
-        out_specs=[vmem] * 5,
+        out_specs=[vmem] * 7,
         out_shape=[
             pltpu.VMEM((frames, group, rows), F32),
             pltpu.VMEM((total, width), BF16),
             pltpu.VMEM((chans, 3 * width), BF16),
             pltpu.VMEM((width, chans), BF16),
             pltpu.VMEM((1, chans), F32),
+            pltpu.VMEM((3 * width, chans), BF16),
+            pltpu.VMEM((chans, width), BF16),
         ],
         scratch_shapes=[pltpu.SemaphoreType.DMA((len(held),))],
         compiler_params=params,
@@ -379,14 +385,14 @@
             compiler_params=params,
             cost_estimate=pl.CostEstimate(flops=2_500_000_000, bytes_accessed=0, transcendentals=0),
             name="attend_back",
-        )(me1, *g_parts[band], gain, qkv, probs, xb, inv, proj, w_out, *carry, *sent)
+        )(me1, *g_parts[band], gain, qkv, probs, xb, inv, proj_turned, out_turned, *carry, *sent)
         sent, carry = (rest[:tm - 1] if last else sent + rest[:tm - 1]), rest[tm - 1:]
         owns.append(own)
-    grad_in = [shifted(sent[k - 1], "tm", k) for k in range(1, tm)]
 
     result = jax.ShapeDtypeStruct((total, width), BF16)
     finish_cost = pl.CostEstimate(flops=0, bytes_accessed=1_500_000, transcendentals=0)
     small, mix_in = group_sum(carry[0], "dp", mix_in)
+    grad_in = [shifted(sent[k - 1], "tm", k) for k in range(1, tm)]
     block_out = pl.pallas_call(
         functools.partial(finish_out_kernel, bands, frames),
         in_specs=[vmem] * tm,
@@ -397,6 +403,7 @@
         name="finish_out",
     )(mix_own, *mix_in)
     small, block_out = group_sum(small, "space", block_out)
+
     tile = small[:chans // LANES, :LANES]
     tiles = [shifted(tile, "tm", k) for k in range(1, tm)]
     input_grad, bias_grad = pl.pallas_call(

time: 40.2 us -> 41.6 us (1.035)
  starting transfers between devices: 15.6 us -> 16.4 us
    ppermute x6, waiting for transfers between devices: 4.04 us -> 6.01 us  [group_sum(): parts.append(lax.ppermute(value, axis, pairs))]
    ppermute x6, waiting for transfers between devices: 4.1 us -> 2.52 us  [shifted(): lax.ppermute(value, axis, [((i + step) % count, i) for i in range(count)])]
    pallas_call x1, Pallas kernels: 2.36 us -> 3.56 us  [per_device(): pl.pallas_call(functools.partial(stage_kernel, frames, width), in_specs=[...]
    pallas_call x2, Pallas kernels: 5.69 us -> 4.72 us  [per_device(): pl.pallas_call(functools.partial(backward_kernel, dims, band, last), in_s...]
    ppermute x6, starting transfers between devices: 9.25 us -> 10 us  [shifted(): lax.ppermute(value, axis, [((i + step) % count, i) for i in range(count)])]
where the time goes in v12:
time: 41.6 us; the launch traced here: 41.4 us
  starting transfers between devices  16.4 us (39%)
  Pallas kernels  13.8 us (33%)
  waiting for transfers between devices  8.53 us (21%)
  local copies, waits for them, and re-layouts  1.9 us (5%)
  between operations  0.71 us (2%)
    ppermute x6, starting transfers between devices, shifted(): lax.ppermute(value, axis, [((i + step) % count, i) for i in range(count)])  10 us
    ppermute x6, starting transfers between devices, group_sum(): parts.append(lax.ppermute(value, axis, pairs))  6.38 us
    ppermute x6, waiting for transfers between devices, group_sum(): parts.append(lax.ppermute(value, axis, pairs))  6.01 us
    pallas_call x2, Pallas kernels, per_device(): pl.pallas_call(functools.partial(backward_kernel, dims, band, last), in_s...  4.72 us
    pallas_call x1, Pallas kernels, per_device(): pl.pallas_call(functools.partial(stage_kernel, frames, width), in_specs=[...  3.56 us
    pallas_call x1, Pallas kernels, per_device(): pl.pallas_call(functools.partial(forward_kernel, dims), in_specs=[smem] +...  3.24 us
    ppermute x6, waiting for transfers between devices, shifted(): lax.ppermute(value, axis, [((i + step) % count, i) for i in range(count)])  2.52 us
    reshape x1, local copies, waits for them, and re-layouts, per_device(): out_grad[:, :, n * BAND:(n + 1) * BAND].reshape(rows, width)  1.02 us
  transfers between devices with their start and end apart: 12, of which 6 were waited for; matrix products, arithmetic and copies ran while one was open for 5% of the time, Pallas kernels for 32%

profile of v12, /device:TPU:0, one launch (start us, length us, event | category | flops | bytes accessed | tf_op | source)
XLA Modules:
  0.0 41.4 jit_solution(8854637853874361984)
XLA Ops:
  0.6 3.0 %collective-permute-start.1 = (bf16[320,512]{1,0:T(8,128)(2,1)}, bf16[320,512]{1,0:T(8,128)(2,1)S(1)}, u32[]{:S(2)}, u32[]{:S(2)}) collective-permute-start(bf16[320,512]{1,0:T(8,128)(2,1)} %bitcast.10), channel_id=1, source_target_pairs={{1,0},{0,1},{3,2},{2,3},{5,4},{4,5},{7,6},{6,7},{9,8},{8,9},{11,10... | collective-permute-start | bytes 983048 | tf_op jit(solution)/shard_map/ppermute | solution.py:273
  3.7 1.0 %slice_bitcast_fusion = (bf16[160,512]{1,0:T(8,128)(2,1)S(1)}, bf16[160,512]{1,0:T(8,128)(2,1)S(1)}) fusion(bf16[1,20,16,512]{3,2,1,0:T(8,128)(2,1)} %param.9), kind=kLoop, calls=%fused_computation | loop fusion | bytes 655360 | tf_op jit(solution)/shard_map/reshape | solution.py:312
  4.8 2.0 %collective-permute-start = (bf16[160,512]{1,0:T(8,128)(2,1)S(1)}, bf16[160,512]{1,0:T(8,128)(2,1)S(1)}, u32[]{:S(2)}, u32[]{:S(2)}) collective-permute-start(bf16[160,512]{1,0:T(8,128)(2,1)S(1)} %get-tuple-element.73.refs_0_), channel_id=1, source_target_pairs={{1,0},{0,1},{3,2},{2,3},{5,4},{4,5},{7,6},{6,7},{9,8},{8,9},{11,10... | collective-permute-start | bytes 491528 | tf_op jit(solution)/shard_map/ppermute | solution.py:273
  6.8 0.8 %broadcast_in_dim.2 = f32[8,39,8]{2,1,0:T(8,128)S(1)} broadcast(f32[8,39]{1,0:T(8,128)} %param.11), dimensions={0,1} | broadcast | bytes 11232 | tf_op jit(solution)/shard_map/broadcast_in_dim | solution.py:317
  7.7 3.6 %stage.1 = (f32[20,8,160]{2,1,0:T(8,128)S(1)}, bf16[320,512]{1,0:T(8,128)(2,1)S(1)}, bf16[1024,1536]{1,0:T(8,128)(2,1)S(1)}, bf16[512,1024]{1,0:T(8,128)(2,1)S(1...) custom-call(f32[8,312]{1,0:T(8,128)S(1)} %reshape.38.bias_ref, ...), custom_call_target="tpu_custom_call" | custom-call | bytes 8000000 | tf_op jit(solution)/shard_map/stage/pallas_call | solution.py:322
  11.2 1.2 %collective-permute-done.1.refs_1_ = bf16[320,512]{1,0:T(8,128)(2,1)S(1)} collective-permute-done((bf16[320,512]{1,0:T(8,128)(2,1)}, bf16[320,512]{1,0:T(8,128)(2,1)S(1)}, u32[]{:S(2)}, u32[]{:S(2)}) %collective-permute-start.1) | collective-permute-done | bytes 327712 | tf_op jit(solution)/shard_map/ppermute | solution.py:273
  12.4 3.2 %attend.1 = (bf16[2,160,1536]{2,1,0:T(8,128)(2,1)S(1)}, bf16[2,8,160,160]{3,2,1,0:T(8,128)(2,1)S(1)}, bf16[2,160,1024]{2,1,0:T(8,128)(2,1)S(1)}, f32[2,160,128]{...) custom-call(s32[1]{0:T(128)} %bitcast.me_ref, ...), custom_call_target="tpu_custom_call" | custom-call | flops 4000000000 | bytes 8000000 | tf_op jit(solution)/shard_map/attend/pallas_call | solution.py:341
  15.7 2.1 %collective-permute-start.6 = (bf16[2,160,512]{2,1,0:T(8,128)(2,1)S(1)}, bf16[2,160,512]{2,1,0:T(8,128)(2,1)S(1)}, u32[]{:S(2)}, u32[]{:S(2)}) collective-permute-start(bf16[2,160,512]{2,1,0:T(8,128)(2,1)S(1)} %get-tuple-element.53), channel_id=1, source_target_pairs={{1,0},{0,1},{3,2},{2,3},{5,4},{4,5},{7,6},{6,7},{9,8},{8,9},{11,10... | collective-permute-start | bytes 983048 | tf_op jit(solution)/shard_map/ppermute | solution.py:273
  17.8 2.3 %attend_back.2 = (f32[160,512]{1,0:T(8,128)S(1)}, bf16[160,512]{1,0:T(8,128)(2,1)S(1)}, f32[1,1024]{1,0:T(1,128)S(1)}, f32[20,8,160]{2,1,0:T(8,128)S(1)}) custom-call(s32[1]{0:T(128)} %bitcast.me_ref, bf16[160,512]{1,0:T(8,128)(2,1)S(1)} %get-tuple-element.72.refs_0_, bf16[160,512]{1,0:T(8,128)(2,1)S(1)} %collective-permute-done.2.refs_1_, ...), custom_call_target="tpu_custom_call" | custom-call | flops 2500000000 | tf_op jit(solution)/shard_map/attend_back/pallas_call | solution.py:378
  20.1 2.4 %attend_back.3 = (f32[160,512]{1,0:T(8,128)S(1)}, bf16[2,160,512]{2,1,0:T(8,128)(2,1)S(1)}, f32[8,512]{1,0:T(8,128)S(1)}) custom-call(s32[1]{0:T(128)} %bitcast.me_ref, bf16[160,512]{1,0:T(8,128)(2,1)S(1)} %get-tuple-element.73.refs_0_, bf16[160,512]{1,0:T(8,128)(2,1)S(1)} %collective-permute-done.refs_1_, f32[1,1024]{1,0:T(1,128)S(1)} %get-tuple-element.38.refs_2_, ...), custom_call_target="tpu_custom_call" | custom-call | flops 2500000000 | tf_op jit(solution)/shard_map/attend_back/pallas_call | solution.py:378
  22.6 1.6 %collective-permute-start.4 = (f32[8,512]{1,0:T(8,128)S(1)}, f32[8,512]{1,0:T(8,128)S(1)}, u32[]{:S(2)}, u32[]{:S(2)}) collective-permute-start(f32[8,512]{1,0:T(8,128)S(1)} %get-tuple-element.54), channel_id=1, source_target_pairs={{16,0},{24,8},{0,16},{8,24},{17,1},{25,9},{1,17},{9,25},{18,2},{26... | collective-permute-start | bytes 49160 | tf_op jit(solution)/shard_map/ppermute | solution.py:289
  24.2 0.3 collective-permute-start.5
  24.5 1.4 %collective-permute-start.11 = (bf16[2,160,512]{2,1,0:T(8,128)(2,1)S(1)}, bf16[2,160,512]{2,1,0:T(8,128)(2,1)S(1)}, u32[]{:S(2)}, u32[]{:S(2)}) collective-permute-start(bf16[2,160,512]{2,1,0:T(8,128)(2,1)S(1)} %get-tuple-element.67), channel_id=1, source_target_pairs={{1,0},{0,1},{3,2},{2,3},{5,4},{4,5},{7,6},{6,7},{9,8},{8,9},{11,10... | collective-permute-start | bytes 983048 | tf_op jit(solution)/shard_map/ppermute | solution.py:273
  25.8 0.6 %collective-permute-done.4 = f32[8,512]{1,0:T(8,128)S(1)} collective-permute-done((f32[8,512]{1,0:T(8,128)S(1)}, f32[8,512]{1,0:T(8,128)S(1)}, u32[]{:S(2)}, u32[]{:S(2)}) %collective-permute-start.4) | collective-permute-done | bytes 16416 | tf_op jit(solution)/shard_map/ppermute | solution.py:289
  26.4 0.9 %collective-permute-done.5 = f32[8,512]{1,0:T(8,128)S(1)} collective-permute-done((f32[8,512]{1,0:T(8,128)S(1)}, f32[8,512]{1,0:T(8,128)S(1)}, u32[]{:S(2)}, u32[]{:S(2)}) %collective-permute-start.5) | collective-permute-done | bytes 16416 | tf_op jit(solution)/shard_map/ppermute | solution.py:289
  27.3 1.6 %collective-permute-start.7 = (f32[8,512]{1,0:T(8,128)S(1)}, f32[8,512]{1,0:T(8,128)S(1)}, u32[]{:S(2)}, u32[]{:S(2)}) collective-permute-start(f32[8,512]{1,0:T(8,128)S(1)} %add_add_fusion.1), channel_id=1, source_target_pairs={{2,0},{0,2},{6,4},{4,6},{3,1},{1,3},{7,5},{5,7},{10,8},{8,10},{14,... | collective-permute-start | bytes 49160 | tf_op jit(solution)/shard_map/ppermute | solution.py:289
  29.0 2.6 %collective-permute-start.8 = (f32[8,512]{1,0:T(8,128)S(1)}, f32[8,512]{1,0:T(8,128)S(1)}, u32[]{:S(2)}, u32[]{:S(2)}) collective-permute-start(f32[8,512]{1,0:T(8,128)S(1)} %add_add_fusion.1), channel_id=1, source_target_pairs={{4,0},{6,2},{0,4},{2,6},{5,1},{7,3},{1,5},{3,7},{12,8},{14,10},{8,... | collective-permute-start | bytes 49160 | tf_op jit(solution)/shard_map/ppermute | solution.py:289
  31.8 0.8 %finish_out.1 = bf16[320,512]{1,0:T(8,128)(2,1)} custom-call(f32[2,160,512]{2,1,0:T(8,128)S(1)} %get-tuple-element.58.own_ref, bf16[2,160,512]{2,1,0:T(8,128)(2,1)S(1)} %collective-permute-done.6.refs_0_), custom_call_target="tpu_custom_call" | custom-call | bytes 1500000 | tf_op jit(solution)/shard_map/finish_out/pallas_call | solution.py:396
  32.6 1.1 %collective-permute-done.8 = f32[8,512]{1,0:T(8,128)S(1)} collective-permute-done((f32[8,512]{1,0:T(8,128)S(1)}, f32[8,512]{1,0:T(8,128)S(1)}, u32[]{:S(2)}, u32[]{:S(2)}) %collective-permute-start.8) | collective-permute-done | bytes 16416 | tf_op jit(solution)/shard_map/ppermute | solution.py:289
  33.7 3.4 %collective-permute-done.9 = f32[8,512]{1,0:T(8,128)S(1)} collective-permute-done((f32[8,512]{1,0:T(8,128)S(1)}, f32[8,512]{1,0:T(8,128)S(1)}, u32[]{:S(2)}, u32[]{:S(2)}) %collective-permute-start.9) | collective-permute-done | bytes 16416 | tf_op jit(solution)/shard_map/ppermute | solution.py:289
  37.1 1.4 %collective-permute-start.10 = (f32[8,128]{1,0:T(8,128)S(1)}, f32[8,128]{1,0:T(8,128)S(1)}, u32[]{:S(2)}, u32[]{:S(2)}) collective-permute-start(f32[8,128]{1,0:T(8,128)S(1)} %slice.12.refs_0_), channel_id=1, source_target_pairs={{1,0},{0,1},{3,2},{2,3},{5,4},{4,5},{7,6},{6,7},{9,8},{8,9},{11,10... | collective-permute-start | bytes 12296 | tf_op jit(solution)/shard_map/ppermute | solution.py:273
  38.6 0.9 %finish_grad.1 = (bf16[320,512]{1,0:T(8,128)(2,1)}, f32[8,39]{1,0:T(8,128)}) custom-call(f32[8,512]{1,0:T(8,128)S(1)} %add_add_fusion.small_ref, f32[160,512]{1,0:T(8,128)S(1)} %get-tuple-element.65.refs_0_, f32[160,512]{1,0:T(8,128)S(1)} %get-tuple-element.66.refs_1_, bf16[2,160,512]{2,1,0:T(8,128)(2,1)S(1)} %collective-permute-done.11.refs_2_), custom_call_target="tpu_custom_call" | custom-call | bytes 1500000 | tf_op jit(solution)/shard_map/finish_grad/pallas_call | solution.py:409
  39.5 1.3 %collective-permute-done.10.refs_1_ = f32[8,128]{1,0:T(8,128)S(1)} collective-permute-done((f32[8,128]{1,0:T(8,128)S(1)}, f32[8,128]{1,0:T(8,128)S(1)}, u32[]{:S(2)}, u32[]{:S(2)}) %collective-permute-start.10) | collective-permute-done | bytes 4128 | tf_op jit(solution)/shard_map/ppermute | solution.py:273
  40.8 0.6 %gain_sum.1 = f32[1,512]{1,0:T(1,128)} custom-call(s32[1]{0:T(128)} %bitcast.me_ref, f32[8,128]{1,0:T(8,128)S(1)} %slice.12.refs_0_, f32[8,128]{1,0:T(8,128)S(1)} %collective-permute-done.10.refs_1_), custom_call_target="tpu_custom_call" | custom-call | tf_op jit(solution)/shard_map/gain_sum/pallas_call | solution.py:419
  (13 shorter events, 0.5 us)
Async XLA Ops:
  0.6 11.8 %collective-permute-start.1 = (bf16[320,512]{1,0:T(8,128)(2,1)}, bf16[320,512]{1,0:T(8,128)(2,1)S(1)}, u32[]{:S(2)}, u32[]{:S(2)}) collective-permute-start(bf16[320,512]{1,0:T(8,128)(2,1)} %bitcast.10), channel_id=1, source_target_pairs={{1,0},{0,1},{3,2},{2,3},{5,4},{4,5},{7,6},{6,7},{9,8},{8,9},{11,10... | collective-permute-start | bytes 983048 | tf_op jit(solution)/shard_map/ppermute | solution.py:273
  4.7 13.1 %collective-permute-start.2 = (bf16[160,512]{1,0:T(8,128)(2,1)S(1)}, bf16[160,512]{1,0:T(8,128)(2,1)S(1)}, u32[]{:S(2)}, u32[]{:S(2)}) collective-permute-start(bf16[160,512]{1,0:T(8,128)(2,1)S(1)} %get-tuple-element.72.refs_0_), channel_id=1, source_target_pairs={{1,0},{0,1},{3,2},{2,3},{5,4},{4,5},{7,6},{6,7},{9,8},{8,9},{11,10... | collective-permute-start | bytes 491528 | tf_op jit(solution)/shard_map/ppermute | solution.py:273
  4.8 15.3 %collective-permute-start = (bf16[160,512]{1,0:T(8,128)(2,1)S(1)}, bf16[160,512]{1,0:T(8,128)(2,1)S(1)}, u32[]{:S(2)}, u32[]{:S(2)}) collective-permute-start(bf16[160,512]{1,0:T(8,128)(2,1)S(1)} %get-tuple-element.73.refs_0_), channel_id=1, source_target_pairs={{1,0},{0,1},{3,2},{2,3},{5,4},{4,5},{7,6},{6,7},{9,8},{8,9},{11,10... | collective-permute-start | bytes 491528 | tf_op jit(solution)/shard_map/ppermute | solution.py:273
  15.7 11.7 %collective-permute-start.6 = (bf16[2,160,512]{2,1,0:T(8,128)(2,1)S(1)}, bf16[2,160,512]{2,1,0:T(8,128)(2,1)S(1)}, u32[]{:S(2)}, u32[]{:S(2)}) collective-permute-start(bf16[2,160,512]{2,1,0:T(8,128)(2,1)S(1)} %get-tuple-element.53), channel_id=1, source_target_pairs={{1,0},{0,1},{3,2},{2,3},{5,4},{4,5},{7,6},{6,7},{9,8},{8,9},{11,10... | collective-permute-start | bytes 983048 | tf_op jit(solution)/shard_map/ppermute | solution.py:273
  22.5 3.3 %collective-permute-start.3 = (f32[8,512]{1,0:T(8,128)S(1)}, f32[8,512]{1,0:T(8,128)S(1)}, u32[]{:S(2)}, u32[]{:S(2)}) collective-permute-start(f32[8,512]{1,0:T(8,128)S(1)} %get-tuple-element.54), channel_id=1, source_target_pairs={{8,0},{0,8},{24,16},{16,24},{9,1},{1,9},{25,17},{17,25},{10,2},{2,... | collective-permute-start | bytes 49160 | tf_op jit(solution)/shard_map/ppermute | solution.py:289
  22.6 3.8 %collective-permute-start.4 = (f32[8,512]{1,0:T(8,128)S(1)}, f32[8,512]{1,0:T(8,128)S(1)}, u32[]{:S(2)}, u32[]{:S(2)}) collective-permute-start(f32[8,512]{1,0:T(8,128)S(1)} %get-tuple-element.54), channel_id=1, source_target_pairs={{16,0},{24,8},{0,16},{8,24},{17,1},{25,9},{1,17},{9,25},{18,2},{26... | collective-permute-start | bytes 49160 | tf_op jit(solution)/shard_map/ppermute | solution.py:289
  24.2 3.2 %collective-permute-start.5 = (f32[8,512]{1,0:T(8,128)S(1)}, f32[8,512]{1,0:T(8,128)S(1)}, u32[]{:S(2)}, u32[]{:S(2)}) collective-permute-start(f32[8,512]{1,0:T(8,128)S(1)} %get-tuple-element.54), channel_id=1, source_target_pairs={{24,0},{16,8},{8,16},{0,24},{25,1},{17,9},{9,17},{1,25},{26,2},{18... | collective-permute-start | bytes 49160 | tf_op jit(solution)/shard_map/ppermute | solution.py:289
  24.5 14.1 %collective-permute-start.11 = (bf16[2,160,512]{2,1,0:T(8,128)(2,1)S(1)}, bf16[2,160,512]{2,1,0:T(8,128)(2,1)S(1)}, u32[]{:S(2)}, u32[]{:S(2)}) collective-permute-start(bf16[2,160,512]{2,1,0:T(8,128)(2,1)S(1)} %get-tuple-element.67), channel_id=1, source_target_pairs={{1,0},{0,1},{3,2},{2,3},{5,4},{4,5},{7,6},{6,7},{9,8},{8,9},{11,10... | collective-permute-start | bytes 983048 | tf_op jit(solution)/shard_map/ppermute | solution.py:273
  27.3 5.3 %collective-permute-start.7 = (f32[8,512]{1,0:T(8,128)S(1)}, f32[8,512]{1,0:T(8,128)S(1)}, u32[]{:S(2)}, u32[]{:S(2)}) collective-permute-start(f32[8,512]{1,0:T(8,128)S(1)} %add_add_fusion.1), channel_id=1, source_target_pairs={{2,0},{0,2},{6,4},{4,6},{3,1},{1,3},{7,5},{5,7},{10,8},{8,10},{14,... | collective-permute-start | bytes 49160 | tf_op jit(solution)/shard_map/ppermute | solution.py:289
  29.0 4.7 %collective-permute-start.8 = (f32[8,512]{1,0:T(8,128)S(1)}, f32[8,512]{1,0:T(8,128)S(1)}, u32[]{:S(2)}, u32[]{:S(2)}) collective-permute-start(f32[8,512]{1,0:T(8,128)S(1)} %add_add_fusion.1), channel_id=1, source_target_pairs={{4,0},{6,2},{0,4},{2,6},{5,1},{7,3},{1,5},{3,7},{12,8},{14,10},{8,... | collective-permute-start | bytes 49160 | tf_op jit(solution)/shard_map/ppermute | solution.py:289
  31.6 5.5 %collective-permute-start.9 = (f32[8,512]{1,0:T(8,128)S(1)}, f32[8,512]{1,0:T(8,128)S(1)}, u32[]{:S(2)}, u32[]{:S(2)}) collective-permute-start(f32[8,512]{1,0:T(8,128)S(1)} %add_add_fusion.1), channel_id=1, source_target_pairs={{6,0},{4,2},{2,4},{0,6},{7,1},{5,3},{3,5},{1,7},{14,8},{12,10},{10... | collective-permute-start | bytes 49160 | tf_op jit(solution)/shard_map/ppermute | solution.py:289
  37.1 3.7 %collective-permute-start.10 = (f32[8,128]{1,0:T(8,128)S(1)}, f32[8,128]{1,0:T(8,128)S(1)}, u32[]{:S(2)}, u32[]{:S(2)}) collective-permute-start(f32[8,128]{1,0:T(8,128)S(1)} %slice.12.refs_0_), channel_id=1, source_target_pairs={{1,0},{0,1},{3,2},{2,3},{5,4},{4,5},{7,6},{6,7},{9,8},{8,9},{11,10... | collective-permute-start | bytes 12296 | tf_op jit(solution)/shard_map/ppermute | solution.py:273

commit v13 on v12

--- a/solution.py
+++ b/solution.py
@@ -280,7 +280,7 @@
         left = count // stride
         radix = 4 if left % 4 == 0 else 2 if left % 2 == 0 else left
         parts = [value]
-        for step in range(1, radix):
+        for step in reversed(range(1, radix)):
             pairs = []
             for i in range(count):
                 digit = i // stride % radix

time: 41.6 us -> 39.2 us (0.942)
  waiting for transfers between devices: 8.53 us -> 6.17 us
    ppermute x6, waiting for transfers between devices: 6.01 us -> 3.65 us  [group_sum(): parts.append(lax.ppermute(value, axis, pairs))]
  transfers between devices with their start and end apart: 12 -> 12, of which waited for: 6 -> 6; matrix products, arithmetic and copies ran while one was open for 5% -> 5% of each run, Pallas kernels for 32% -> 34%
where the time goes in v13:
time: 39.2 us; the launch traced here: 39 us
  starting transfers between devices  16.4 us (42%)
  Pallas kernels  13.8 us (35%)
  waiting for transfers between devices  6.17 us (16%)
  local copies, waits for them, and re-layouts  1.9 us (5%)
  between operations  0.72 us (2%)
    ppermute x6, starting transfers between devices, shifted(): lax.ppermute(value, axis, [((i + step) % count, i) for i in range(count)])  10 us
    ppermute x6, starting transfers between devices, group_sum(): parts.append(lax.ppermute(value, axis, pairs))  6.39 us
    pallas_call x2, Pallas kernels, per_device(): pl.pallas_call(functools.partial(backward_kernel, dims, band, last), in_s...  4.72 us
    ppermute x6, waiting for transfers between devices, group_sum(): parts.append(lax.ppermute(value, axis, pairs))  3.65 us
    pallas_call x1, Pallas kernels, per_device(): pl.pallas_call(functools.partial(stage_kernel, frames, width), in_specs=[...  3.56 us
    pallas_call x1, Pallas kernels, per_device(): pl.pallas_call(functools.partial(forward_kernel, dims), in_specs=[smem] +...  3.24 us
    ppermute x6, waiting for transfers between devices, shifted(): lax.ppermute(value, axis, [((i + step) % count, i) for i in range(count)])  2.51 us
    reshape x1, local copies, waits for them, and re-layouts, per_device(): out_grad[:, :, n * BAND:(n + 1) * BAND].reshape(rows, width)  1.02 us
  transfers between devices with their start and end apart: 12, of which 6 were waited for; matrix products, arithmetic and copies ran while one was open for 5% of the time, Pallas kernels for 34%

profile of v13, /device:TPU:0, one launch (start us, length us, event | category | flops | bytes accessed | tf_op | source)
XLA Modules:
  0.0 39.0 jit_solution(17781344806642843031)
XLA Ops:
  0.6 3.0 %collective-permute-start.1 = (bf16[320,512]{1,0:T(8,128)(2,1)}, bf16[320,512]{1,0:T(8,128)(2,1)S(1)}, u32[]{:S(2)}, u32[]{:S(2)}) collective-permute-start(bf16[320,512]{1,0:T(8,128)(2,1)} %bitcast.10), channel_id=1, source_target_pairs={{1,0},{0,1},{3,2},{2,3},{5,4},{4,5},{7,6},{6,7},{9,8},{8,9},{11,10... | collective-permute-start | bytes 983048 | tf_op jit(solution)/shard_map/ppermute | solution.py:273
  3.7 1.0 %slice_bitcast_fusion = (bf16[160,512]{1,0:T(8,128)(2,1)S(1)}, bf16[160,512]{1,0:T(8,128)(2,1)S(1)}) fusion(bf16[1,20,16,512]{3,2,1,0:T(8,128)(2,1)} %param.9), kind=kLoop, calls=%fused_computation | loop fusion | bytes 655360 | tf_op jit(solution)/shard_map/reshape | solution.py:312
  4.8 2.0 %collective-permute-start = (bf16[160,512]{1,0:T(8,128)(2,1)S(1)}, bf16[160,512]{1,0:T(8,128)(2,1)S(1)}, u32[]{:S(2)}, u32[]{:S(2)}) collective-permute-start(bf16[160,512]{1,0:T(8,128)(2,1)S(1)} %get-tuple-element.73.refs_0_), channel_id=1, source_target_pairs={{1,0},{0,1},{3,2},{2,3},{5,4},{4,5},{7,6},{6,7},{9,8},{8,9},{11,10... | collective-permute-start | bytes 491528 | tf_op jit(solution)/shard_map/ppermute | solution.py:273
  6.8 0.8 %broadcast_in_dim.2 = f32[8,39,8]{2,1,0:T(8,128)S(1)} broadcast(f32[8,39]{1,0:T(8,128)} %param.11), dimensions={0,1} | broadcast | bytes 11232 | tf_op jit(solution)/shard_map/broadcast_in_dim | solution.py:317
  7.6 0.1 reshape.38.bias_ref
  7.7 3.6 %stage.1 = (f32[20,8,160]{2,1,0:T(8,128)S(1)}, bf16[320,512]{1,0:T(8,128)(2,1)S(1)}, bf16[1024,1536]{1,0:T(8,128)(2,1)S(1)}, bf16[512,1024]{1,0:T(8,128)(2,1)S(1...) custom-call(f32[8,312]{1,0:T(8,128)S(1)} %reshape.38.bias_ref, ...), custom_call_target="tpu_custom_call" | custom-call | bytes 8000000 | tf_op jit(solution)/shard_map/stage/pallas_call | solution.py:322
  11.2 1.2 %collective-permute-done.1.refs_1_ = bf16[320,512]{1,0:T(8,128)(2,1)S(1)} collective-permute-done((bf16[320,512]{1,0:T(8,128)(2,1)}, bf16[320,512]{1,0:T(8,128)(2,1)S(1)}, u32[]{:S(2)}, u32[]{:S(2)}) %collective-permute-start.1) | collective-permute-done | bytes 327712 | tf_op jit(solution)/shard_map/ppermute | solution.py:273
  12.4 3.2 %attend.1 = (bf16[2,160,1536]{2,1,0:T(8,128)(2,1)S(1)}, bf16[2,8,160,160]{3,2,1,0:T(8,128)(2,1)S(1)}, bf16[2,160,1024]{2,1,0:T(8,128)(2,1)S(1)}, f32[2,160,128]{...) custom-call(s32[1]{0:T(128)} %bitcast.me_ref, ...), custom_call_target="tpu_custom_call" | custom-call | flops 4000000000 | bytes 8000000 | tf_op jit(solution)/shard_map/attend/pallas_call | solution.py:341
  15.7 2.1 %collective-permute-start.6 = (bf16[2,160,512]{2,1,0:T(8,128)(2,1)S(1)}, bf16[2,160,512]{2,1,0:T(8,128)(2,1)S(1)}, u32[]{:S(2)}, u32[]{:S(2)}) collective-permute-start(bf16[2,160,512]{2,1,0:T(8,128)(2,1)S(1)} %get-tuple-element.53), channel_id=1, source_target_pairs={{1,0},{0,1},{3,2},{2,3},{5,4},{4,5},{7,6},{6,7},{9,8},{8,9},{11,10... | collective-permute-start | bytes 983048 | tf_op jit(solution)/shard_map/ppermute | solution.py:273
  17.8 2.3 %attend_back.2 = (f32[160,512]{1,0:T(8,128)S(1)}, bf16[160,512]{1,0:T(8,128)(2,1)S(1)}, f32[1,1024]{1,0:T(1,128)S(1)}, f32[20,8,160]{2,1,0:T(8,128)S(1)}) custom-call(s32[1]{0:T(128)} %bitcast.me_ref, bf16[160,512]{1,0:T(8,128)(2,1)S(1)} %get-tuple-element.72.refs_0_, bf16[160,512]{1,0:T(8,128)(2,1)S(1)} %collective-permute-done.2.refs_1_, ...), custom_call_target="tpu_custom_call" | custom-call | flops 2500000000 | tf_op jit(solution)/shard_map/attend_back/pallas_call | solution.py:378
  20.1 2.4 %attend_back.3 = (f32[160,512]{1,0:T(8,128)S(1)}, bf16[2,160,512]{2,1,0:T(8,128)(2,1)S(1)}, f32[8,512]{1,0:T(8,128)S(1)}) custom-call(s32[1]{0:T(128)} %bitcast.me_ref, bf16[160,512]{1,0:T(8,128)(2,1)S(1)} %get-tuple-element.73.refs_0_, bf16[160,512]{1,0:T(8,128)(2,1)S(1)} %collective-permute-done.refs_1_, f32[1,1024]{1,0:T(1,128)S(1)} %get-tuple-element.38.refs_2_, ...), custom_call_target="tpu_custom_call" | custom-call | flops 2500000000 | tf_op jit(solution)/shard_map/attend_back/pallas_call | solution.py:378
  22.6 1.6 %collective-permute-start.4 = (f32[8,512]{1,0:T(8,128)S(1)}, f32[8,512]{1,0:T(8,128)S(1)}, u32[]{:S(2)}, u32[]{:S(2)}) collective-permute-start(f32[8,512]{1,0:T(8,128)S(1)} %get-tuple-element.54), channel_id=1, source_target_pairs={{16,0},{24,8},{0,16},{8,24},{17,1},{25,9},{1,17},{9,25},{18,2},{26... | collective-permute-start | bytes 49160 | tf_op jit(solution)/shard_map/ppermute | solution.py:289
  24.2 0.3 collective-permute-start.5
  24.5 1.4 %collective-permute-start.11 = (bf16[2,160,512]{2,1,0:T(8,128)(2,1)S(1)}, bf16[2,160,512]{2,1,0:T(8,128)(2,1)S(1)}, u32[]{:S(2)}, u32[]{:S(2)}) collective-permute-start(bf16[2,160,512]{2,1,0:T(8,128)(2,1)S(1)} %get-tuple-element.67), channel_id=1, source_target_pairs={{1,0},{0,1},{3,2},{2,3},{5,4},{4,5},{7,6},{6,7},{9,8},{8,9},{11,10... | collective-permute-start | bytes 983048 | tf_op jit(solution)/shard_map/ppermute | solution.py:273
  25.9 0.5 %collective-permute-done.4 = f32[8,512]{1,0:T(8,128)S(1)} collective-permute-done((f32[8,512]{1,0:T(8,128)S(1)}, f32[8,512]{1,0:T(8,128)S(1)}, u32[]{:S(2)}, u32[]{:S(2)}) %collective-permute-start.4) | collective-permute-done | bytes 16416 | tf_op jit(solution)/shard_map/ppermute | solution.py:289
  26.4 3.7 %collective-permute-start.7 = (f32[8,512]{1,0:T(8,128)S(1)}, f32[8,512]{1,0:T(8,128)S(1)}, u32[]{:S(2)}, u32[]{:S(2)}) collective-permute-start(f32[8,512]{1,0:T(8,128)S(1)} %add_add_fusion.1), channel_id=1, source_target_pairs={{6,0},{4,2},{2,4},{0,6},{7,1},{5,3},{3,5},{1,7},{14,8},{12,10},{10... | collective-permute-start | bytes 49160 | tf_op jit(solution)/shard_map/ppermute | solution.py:289
  30.1 0.8 %collective-permute-start.9 = (f32[8,512]{1,0:T(8,128)S(1)}, f32[8,512]{1,0:T(8,128)S(1)}, u32[]{:S(2)}, u32[]{:S(2)}) collective-permute-start(f32[8,512]{1,0:T(8,128)S(1)} %add_add_fusion.1), channel_id=1, source_target_pairs={{2,0},{0,2},{6,4},{4,6},{3,1},{1,3},{7,5},{5,7},{10,8},{8,10},{14,... | collective-permute-start | bytes 49160 | tf_op jit(solution)/shard_map/ppermute | solution.py:289
  30.9 0.8 %finish_out.1 = bf16[320,512]{1,0:T(8,128)(2,1)} custom-call(f32[2,160,512]{2,1,0:T(8,128)S(1)} %get-tuple-element.58.own_ref, bf16[2,160,512]{2,1,0:T(8,128)(2,1)S(1)} %collective-permute-done.6.refs_0_), custom_call_target="tpu_custom_call" | custom-call | bytes 1500000 | tf_op jit(solution)/shard_map/finish_out/pallas_call | solution.py:396
  31.7 0.3 collective-permute-done.7
  32.1 2.7 %collective-permute-done.8 = f32[8,512]{1,0:T(8,128)S(1)} collective-permute-done((f32[8,512]{1,0:T(8,128)S(1)}, f32[8,512]{1,0:T(8,128)S(1)}, u32[]{:S(2)}, u32[]{:S(2)}) %collective-permute-start.8) | collective-permute-done | bytes 16416 | tf_op jit(solution)/shard_map/ppermute | solution.py:289
  34.8 1.4 %collective-permute-start.10 = (f32[8,128]{1,0:T(8,128)S(1)}, f32[8,128]{1,0:T(8,128)S(1)}, u32[]{:S(2)}, u32[]{:S(2)}) collective-permute-start(f32[8,128]{1,0:T(8,128)S(1)} %slice.12.refs_0_), channel_id=1, source_target_pairs={{1,0},{0,1},{3,2},{2,3},{5,4},{4,5},{7,6},{6,7},{9,8},{8,9},{11,10... | collective-permute-start | bytes 12296 | tf_op jit(solution)/shard_map/ppermute | solution.py:273
  36.2 0.9 %finish_grad.1 = (bf16[320,512]{1,0:T(8,128)(2,1)}, f32[8,39]{1,0:T(8,128)}) custom-call(f32[8,512]{1,0:T(8,128)S(1)} %add_add_fusion.small_ref, f32[160,512]{1,0:T(8,128)S(1)} %get-tuple-element.65.refs_0_, f32[160,512]{1,0:T(8,128)S(1)} %get-tuple-element.66.refs_1_, bf16[2,160,512]{2,1,0:T(8,128)(2,1)S(1)} %collective-permute-done.11.refs_2_), custom_call_target="tpu_custom_call" | custom-call | bytes 1500000 | tf_op jit(solution)/shard_map/finish_grad/pallas_call | solution.py:409
  37.1 1.3 %collective-permute-done.10.refs_1_ = f32[8,128]{1,0:T(8,128)S(1)} collective-permute-done((f32[8,128]{1,0:T(8,128)S(1)}, f32[8,128]{1,0:T(8,128)S(1)}, u32[]{:S(2)}, u32[]{:S(2)}) %collective-permute-start.10) | collective-permute-done | bytes 4128 | tf_op jit(solution)/shard_map/ppermute | solution.py:273
  38.5 0.6 %gain_sum.1 = f32[1,512]{1,0:T(1,128)} custom-call(s32[1]{0:T(128)} %bitcast.me_ref, f32[8,128]{1,0:T(8,128)S(1)} %slice.12.refs_0_, f32[8,128]{1,0:T(8,128)S(1)} %collective-permute-done.10.refs_1_), custom_call_target="tpu_custom_call" | custom-call | tf_op jit(solution)/shard_map/gain_sum/pallas_call | solution.py:419
  (13 shorter events, 0.3 us)
Async XLA Ops:
  0.6 11.8 %collective-permute-start.1 = (bf16[320,512]{1,0:T(8,128)(2,1)}, bf16[320,512]{1,0:T(8,128)(2,1)S(1)}, u32[]{:S(2)}, u32[]{:S(2)}) collective-permute-start(bf16[320,512]{1,0:T(8,128)(2,1)} %bitcast.10), channel_id=1, source_target_pairs={{1,0},{0,1},{3,2},{2,3},{5,4},{4,5},{7,6},{6,7},{9,8},{8,9},{11,10... | collective-permute-start | bytes 983048 | tf_op jit(solution)/shard_map/ppermute | solution.py:273
  4.7 13.1 %collective-permute-start.2 = (bf16[160,512]{1,0:T(8,128)(2,1)S(1)}, bf16[160,512]{1,0:T(8,128)(2,1)S(1)}, u32[]{:S(2)}, u32[]{:S(2)}) collective-permute-start(bf16[160,512]{1,0:T(8,128)(2,1)S(1)} %get-tuple-element.72.refs_0_), channel_id=1, source_target_pairs={{1,0},{0,1},{3,2},{2,3},{5,4},{4,5},{7,6},{6,7},{9,8},{8,9},{11,10... | collective-permute-start | bytes 491528 | tf_op jit(solution)/shard_map/ppermute | solution.py:273
  4.8 15.3 %collective-permute-start = (bf16[160,512]{1,0:T(8,128)(2,1)S(1)}, bf16[160,512]{1,0:T(8,128)(2,1)S(1)}, u32[]{:S(2)}, u32[]{:S(2)}) collective-permute-start(bf16[160,512]{1,0:T(8,128)(2,1)S(1)} %get-tuple-element.73.refs_0_), channel_id=1, source_target_pairs={{1,0},{0,1},{3,2},{2,3},{5,4},{4,5},{7,6},{6,7},{9,8},{8,9},{11,10... | collective-permute-start | bytes 491528 | tf_op jit(solution)/shard_map/ppermute | solution.py:273
  15.7 10.8 %collective-permute-start.6 = (bf16[2,160,512]{2,1,0:T(8,128)(2,1)S(1)}, bf16[2,160,512]{2,1,0:T(8,128)(2,1)S(1)}, u32[]{:S(2)}, u32[]{:S(2)}) collective-permute-start(bf16[2,160,512]{2,1,0:T(8,128)(2,1)S(1)} %get-tuple-element.53), channel_id=1, source_target_pairs={{1,0},{0,1},{3,2},{2,3},{5,4},{4,5},{7,6},{6,7},{9,8},{8,9},{11,10... | collective-permute-start | bytes 983048 | tf_op jit(solution)/shard_map/ppermute | solution.py:273
  22.5 3.4 %collective-permute-start.3 = (f32[8,512]{1,0:T(8,128)S(1)}, f32[8,512]{1,0:T(8,128)S(1)}, u32[]{:S(2)}, u32[]{:S(2)}) collective-permute-start(f32[8,512]{1,0:T(8,128)S(1)} %get-tuple-element.54), channel_id=1, source_target_pairs={{24,0},{16,8},{8,16},{0,24},{25,1},{17,9},{9,17},{1,25},{26,2},{18... | collective-permute-start | bytes 49160 | tf_op jit(solution)/shard_map/ppermute | solution.py:289
  22.6 3.8 %collective-permute-start.4 = (f32[8,512]{1,0:T(8,128)S(1)}, f32[8,512]{1,0:T(8,128)S(1)}, u32[]{:S(2)}, u32[]{:S(2)}) collective-permute-start(f32[8,512]{1,0:T(8,128)S(1)} %get-tuple-element.54), channel_id=1, source_target_pairs={{16,0},{24,8},{0,16},{8,24},{17,1},{25,9},{1,17},{9,25},{18,2},{26... | collective-permute-start | bytes 49160 | tf_op jit(solution)/shard_map/ppermute | solution.py:289
  24.2 2.3 %collective-permute-start.5 = (f32[8,512]{1,0:T(8,128)S(1)}, f32[8,512]{1,0:T(8,128)S(1)}, u32[]{:S(2)}, u32[]{:S(2)}) collective-permute-start(f32[8,512]{1,0:T(8,128)S(1)} %get-tuple-element.54), channel_id=1, source_target_pairs={{8,0},{0,8},{24,16},{16,24},{9,1},{1,9},{25,17},{17,25},{10,2},{2,... | collective-permute-start | bytes 49160 | tf_op jit(solution)/shard_map/ppermute | solution.py:289
  24.5 11.7 %collective-permute-start.11 = (bf16[2,160,512]{2,1,0:T(8,128)(2,1)S(1)}, bf16[2,160,512]{2,1,0:T(8,128)(2,1)S(1)}, u32[]{:S(2)}, u32[]{:S(2)}) collective-permute-start(bf16[2,160,512]{2,1,0:T(8,128)(2,1)S(1)} %get-tuple-element.67), channel_id=1, source_target_pairs={{1,0},{0,1},{3,2},{2,3},{5,4},{4,5},{7,6},{6,7},{9,8},{8,9},{11,10... | collective-permute-start | bytes 983048 | tf_op jit(solution)/shard_map/ppermute | solution.py:273
  26.4 5.6 %collective-permute-start.7 = (f32[8,512]{1,0:T(8,128)S(1)}, f32[8,512]{1,0:T(8,128)S(1)}, u32[]{:S(2)}, u32[]{:S(2)}) collective-permute-start(f32[8,512]{1,0:T(8,128)S(1)} %add_add_fusion.1), channel_id=1, source_target_pairs={{6,0},{4,2},{2,4},{0,6},{7,1},{5,3},{3,5},{1,7},{14,8},{12,10},{10... | collective-permute-start | bytes 49160 | tf_op jit(solution)/shard_map/ppermute | solution.py:289
  30.1 4.6 %collective-permute-start.8 = (f32[8,512]{1,0:T(8,128)S(1)}, f32[8,512]{1,0:T(8,128)S(1)}, u32[]{:S(2)}, u32[]{:S(2)}) collective-permute-start(f32[8,512]{1,0:T(8,128)S(1)} %add_add_fusion.1), channel_id=1, source_target_pairs={{4,0},{6,2},{0,4},{2,6},{5,1},{7,3},{1,5},{3,7},{12,8},{14,10},{8,... | collective-permute-start | bytes 49160 | tf_op jit(solution)/shard_map/ppermute | solution.py:289
  30.1 4.6 %collective-permute-start.9 = (f32[8,512]{1,0:T(8,128)S(1)}, f32[8,512]{1,0:T(8,128)S(1)}, u32[]{:S(2)}, u32[]{:S(2)}) collective-permute-start(f32[8,512]{1,0:T(8,128)S(1)} %add_add_fusion.1), channel_id=1, source_target_pairs={{2,0},{0,2},{6,4},{4,6},{3,1},{1,3},{7,5},{5,7},{10,8},{8,10},{14,... | collective-permute-start | bytes 49160 | tf_op jit(solution)/shard_map/ppermute | solution.py:289
  34.8 3.7 %collective-permute-start.10 = (f32[8,128]{1,0:T(8,128)S(1)}, f32[8,128]{1,0:T(8,128)S(1)}, u32[]{:S(2)}, u32[]{:S(2)}) collective-permute-start(f32[8,128]{1,0:T(8,128)S(1)} %slice.12.refs_0_), channel_id=1, source_target_pairs={{1,0},{0,1},{3,2},{2,3},{5,4},{4,5},{7,6},{6,7},{9,8},{8,9},{11,10... | collective-permute-start | bytes 12296 | tf_op jit(solution)/shard_map/ppermute | solution.py:273

commit v14 on v13

--- a/solution.py
+++ b/solution.py
@@ -402,7 +402,7 @@
         cost_estimate=finish_cost,
         name="finish_out",
     )(mix_own, *mix_in)
-    small, block_out = group_sum(small, "space", block_out)
+    small, (block_out, grad_in) = group_sum(small, "space", (block_out, grad_in))
 
     tile = small[:chans // LANES, :LANES]
     tiles = [shifted(tile, "tm", k) for k in range(1, tm)]

time: 39.2 us -> 40.5 us (1.033)
  waiting for transfers between devices: 6.17 us -> 8.08 us
  starting transfers between devices: 16.4 us -> 15.8 us
    ppermute x6, waiting for transfers between devices: 3.65 us -> 4.96 us  [group_sum(): parts.append(lax.ppermute(value, axis, pairs))]
    ppermute x6, waiting for transfers between devices: 2.51 us -> 3.12 us  [shifted(): lax.ppermute(value, axis, [((i + step) % count, i) for i in range(count)])]
    ppermute x6, starting transfers between devices: 10 us -> 9.49 us  [shifted(): lax.ppermute(value, axis, [((i + step) % count, i) for i in range(count)])]
  transfers between devices with their start and end apart: 12 -> 12, of which waited for: 6 -> 6; matrix products, arithmetic and copies ran while one was open for 5% -> 5% of each run, Pallas kernels for 34% -> 33%
where the time goes in v14:
time: 40.5 us; the launch traced here: 40.3 us
  starting transfers between devices  15.8 us (39%)
  Pallas kernels  13.8 us (34%)
  waiting for transfers between devices  8.08 us (20%)
  local copies, waits for them, and re-layouts  1.9 us (5%)
  between operations  0.72 us (2%)
    ppermute x6, starting transfers between devices, shifted(): lax.ppermute(value, axis, [((i + step) % count, i) for i in range(count)])  9.49 us
    ppermute x6, starting transfers between devices, group_sum(): parts.append(lax.ppermute(value, axis, pairs))  6.31 us
    ppermute x6, waiting for transfers between devices, group_sum(): parts.append(lax.ppermute(value, axis, pairs))  4.96 us
    pallas_call x2, Pallas kernels, per_device(): pl.pallas_call(functools.partial(backward_kernel, dims, band, last), in_s...  4.72 us
    pallas_call x1, Pallas kernels, per_device(): pl.pallas_call(functools.partial(stage_kernel, frames, width), in_specs=[...  3.56 us
    pallas_call x1, Pallas kernels, per_device(): pl.pallas_call(functools.partial(forward_kernel, dims), in_specs=[smem] +...  3.24 us
    ppermute x6, waiting for transfers between devices, shifted(): lax.ppermute(value, axis, [((i + step) % count, i) for i in range(count)])  3.12 us
    reshape x1, local copies, waits for them, and re-layouts, per_device(): out_grad[:, :, n * BAND:(n + 1) * BAND].reshape(rows, width)  1.02 us
  transfers between devices with their start and end apart: 12, of which 6 were waited for; matrix products, arithmetic and copies ran while one was open for 5% of the time, Pallas kernels for 33%

profile of v14, /device:TPU:0, one launch (start us, length us, event | category | flops | bytes accessed | tf_op | source)
XLA Modules:
  0.0 40.3 jit_solution(13337613348473610905)
XLA Ops:
  0.6 3.0 %collective-permute-start.1 = (bf16[320,512]{1,0:T(8,128)(2,1)}, bf16[320,512]{1,0:T(8,128)(2,1)S(1)}, u32[]{:S(2)}, u32[]{:S(2)}) collective-permute-start(bf16[320,512]{1,0:T(8,128)(2,1)} %bitcast.10), channel_id=1, source_target_pairs={{1,0},{0,1},{3,2},{2,3},{5,4},{4,5},{7,6},{6,7},{9,8},{8,9},{11,10... | collective-permute-start | bytes 983048 | tf_op jit(solution)/shard_map/ppermute | solution.py:273
  3.7 1.0 %slice_bitcast_fusion = (bf16[160,512]{1,0:T(8,128)(2,1)S(1)}, bf16[160,512]{1,0:T(8,128)(2,1)S(1)}) fusion(bf16[1,20,16,512]{3,2,1,0:T(8,128)(2,1)} %param.9), kind=kLoop, calls=%fused_computation | loop fusion | bytes 655360 | tf_op jit(solution)/shard_map/reshape | solution.py:312
  4.8 2.0 %collective-permute-start = (bf16[160,512]{1,0:T(8,128)(2,1)S(1)}, bf16[160,512]{1,0:T(8,128)(2,1)S(1)}, u32[]{:S(2)}, u32[]{:S(2)}) collective-permute-start(bf16[160,512]{1,0:T(8,128)(2,1)S(1)} %get-tuple-element.75.refs_0_), channel_id=1, source_target_pairs={{1,0},{0,1},{3,2},{2,3},{5,4},{4,5},{7,6},{6,7},{9,8},{8,9},{11,10... | collective-permute-start | bytes 491528 | tf_op jit(solution)/shard_map/ppermute | solution.py:273
  6.8 0.8 %broadcast_in_dim.2 = f32[8,39,8]{2,1,0:T(8,128)S(1)} broadcast(f32[8,39]{1,0:T(8,128)} %param.11), dimensions={0,1} | broadcast | bytes 11232 | tf_op jit(solution)/shard_map/broadcast_in_dim | solution.py:317
  7.7 3.6 %stage.1 = (f32[20,8,160]{2,1,0:T(8,128)S(1)}, bf16[320,512]{1,0:T(8,128)(2,1)S(1)}, bf16[1024,1536]{1,0:T(8,128)(2,1)S(1)}, bf16[512,1024]{1,0:T(8,128)(2,1)S(1...) custom-call(f32[8,312]{1,0:T(8,128)S(1)} %reshape.38.bias_ref, ...), custom_call_target="tpu_custom_call" | custom-call | bytes 8000000 | tf_op jit(solution)/shard_map/stage/pallas_call | solution.py:322
  11.2 1.2 %collective-permute-done.1.refs_1_ = bf16[320,512]{1,0:T(8,128)(2,1)S(1)} collective-permute-done((bf16[320,512]{1,0:T(8,128)(2,1)}, bf16[320,512]{1,0:T(8,128)(2,1)S(1)}, u32[]{:S(2)}, u32[]{:S(2)}) %collective-permute-start.1) | collective-permute-done | bytes 327712 | tf_op jit(solution)/shard_map/ppermute | solution.py:273
  12.4 3.2 %attend.1 = (bf16[2,160,1536]{2,1,0:T(8,128)(2,1)S(1)}, bf16[2,8,160,160]{3,2,1,0:T(8,128)(2,1)S(1)}, bf16[2,160,1024]{2,1,0:T(8,128)(2,1)S(1)}, f32[2,160,128]{...) custom-call(s32[1]{0:T(128)} %bitcast.me_ref, ...), custom_call_target="tpu_custom_call" | custom-call | flops 4000000000 | bytes 8000000 | tf_op jit(solution)/shard_map/attend/pallas_call | solution.py:341
  15.7 2.1 %collective-permute-start.6 = (bf16[2,160,512]{2,1,0:T(8,128)(2,1)S(1)}, bf16[2,160,512]{2,1,0:T(8,128)(2,1)S(1)}, u32[]{:S(2)}, u32[]{:S(2)}) collective-permute-start(bf16[2,160,512]{2,1,0:T(8,128)(2,1)S(1)} %get-tuple-element.54), channel_id=1, source_target_pairs={{1,0},{0,1},{3,2},{2,3},{5,4},{4,5},{7,6},{6,7},{9,8},{8,9},{11,10... | collective-permute-start | bytes 983048 | tf_op jit(solution)/shard_map/ppermute | solution.py:273
  17.8 2.3 %attend_back.2 = (f32[160,512]{1,0:T(8,128)S(1)}, bf16[160,512]{1,0:T(8,128)(2,1)S(1)}, f32[1,1024]{1,0:T(1,128)S(1)}, f32[20,8,160]{2,1,0:T(8,128)S(1)}) custom-call(s32[1]{0:T(128)} %bitcast.me_ref, bf16[160,512]{1,0:T(8,128)(2,1)S(1)} %get-tuple-element.74.refs_0_, bf16[160,512]{1,0:T(8,128)(2,1)S(1)} %collective-permute-done.2.refs_1_, ...), custom_call_target="tpu_custom_call" | custom-call | flops 2500000000 | tf_op jit(solution)/shard_map/attend_back/pallas_call | solution.py:378
  20.1 2.4 %attend_back.3 = (f32[160,512]{1,0:T(8,128)S(1)}, bf16[2,160,512]{2,1,0:T(8,128)(2,1)S(1)}, f32[8,512]{1,0:T(8,128)S(1)}) custom-call(s32[1]{0:T(128)} %bitcast.me_ref, bf16[160,512]{1,0:T(8,128)(2,1)S(1)} %get-tuple-element.75.refs_0_, bf16[160,512]{1,0:T(8,128)(2,1)S(1)} %collective-permute-done.refs_1_, f32[1,1024]{1,0:T(1,128)S(1)} %get-tuple-element.39.refs_2_, ...), custom_call_target="tpu_custom_call" | custom-call | flops 2500000000 | tf_op jit(solution)/shard_map/attend_back/pallas_call | solution.py:378
  22.5 1.4 %collective-permute-start.10 = (bf16[2,160,512]{2,1,0:T(8,128)(2,1)S(1)}, bf16[2,160,512]{2,1,0:T(8,128)(2,1)S(1)}, u32[]{:S(2)}, u32[]{:S(2)}) collective-permute-start(bf16[2,160,512]{2,1,0:T(8,128)(2,1)S(1)} %get-tuple-element.61), channel_id=1, source_target_pairs={{1,0},{0,1},{3,2},{2,3},{5,4},{4,5},{7,6},{6,7},{9,8},{8,9},{11,10... | collective-permute-start | bytes 983048 | tf_op jit(solution)/shard_map/ppermute | solution.py:273
  24.0 1.5 %collective-permute-start.4 = (f32[8,512]{1,0:T(8,128)S(1)}, f32[8,512]{1,0:T(8,128)S(1)}, u32[]{:S(2)}, u32[]{:S(2)}) collective-permute-start(f32[8,512]{1,0:T(8,128)S(1)} %get-tuple-element.55), channel_id=1, source_target_pairs={{16,0},{24,8},{0,16},{8,24},{17,1},{25,9},{1,17},{9,25},{18,2},{26... | collective-permute-start | bytes 49160 | tf_op jit(solution)/shard_map/ppermute | solution.py:289
  25.5 0.3 collective-permute-start.5
  25.8 1.4 %collective-permute-done.3 = f32[8,512]{1,0:T(8,128)S(1)} collective-permute-done((f32[8,512]{1,0:T(8,128)S(1)}, f32[8,512]{1,0:T(8,128)S(1)}, u32[]{:S(2)}, u32[]{:S(2)}) %collective-permute-start.3) | collective-permute-done | bytes 16416 | tf_op jit(solution)/shard_map/ppermute | solution.py:289
  27.2 0.5 %collective-permute-done.4 = f32[8,512]{1,0:T(8,128)S(1)} collective-permute-done((f32[8,512]{1,0:T(8,128)S(1)}, f32[8,512]{1,0:T(8,128)S(1)}, u32[]{:S(2)}, u32[]{:S(2)}) %collective-permute-start.4) | collective-permute-done | bytes 16416 | tf_op jit(solution)/shard_map/ppermute | solution.py:289
  27.7 3.7 %collective-permute-start.7 = (f32[8,512]{1,0:T(8,128)S(1)}, f32[8,512]{1,0:T(8,128)S(1)}, u32[]{:S(2)}, u32[]{:S(2)}) collective-permute-start(f32[8,512]{1,0:T(8,128)S(1)} %add_add_fusion.1), channel_id=1, source_target_pairs={{6,0},{4,2},{2,4},{0,6},{7,1},{5,3},{3,5},{1,7},{14,8},{12,10},{10... | collective-permute-start | bytes 49160 | tf_op jit(solution)/shard_map/ppermute | solution.py:289
  31.4 0.8 %collective-permute-start.9 = (f32[8,512]{1,0:T(8,128)S(1)}, f32[8,512]{1,0:T(8,128)S(1)}, u32[]{:S(2)}, u32[]{:S(2)}) collective-permute-start(f32[8,512]{1,0:T(8,128)S(1)} %add_add_fusion.1), channel_id=1, source_target_pairs={{2,0},{0,2},{6,4},{4,6},{3,1},{1,3},{7,5},{5,7},{10,8},{8,10},{14,... | collective-permute-start | bytes 49160 | tf_op jit(solution)/shard_map/ppermute | solution.py:289
  32.2 0.8 %finish_out.1 = bf16[320,512]{1,0:T(8,128)(2,1)} custom-call(f32[2,160,512]{2,1,0:T(8,128)S(1)} %get-tuple-element.59.own_ref, bf16[2,160,512]{2,1,0:T(8,128)(2,1)S(1)} %collective-permute-done.6.refs_0_), custom_call_target="tpu_custom_call" | custom-call | bytes 1500000 | tf_op jit(solution)/shard_map/finish_out/pallas_call | solution.py:396
  33.0 0.3 collective-permute-done.7
  33.3 2.7 %collective-permute-done.8 = f32[8,512]{1,0:T(8,128)S(1)} collective-permute-done((f32[8,512]{1,0:T(8,128)S(1)}, f32[8,512]{1,0:T(8,128)S(1)}, u32[]{:S(2)}, u32[]{:S(2)}) %collective-permute-start.8) | collective-permute-done | bytes 16416 | tf_op jit(solution)/shard_map/ppermute | solution.py:289
  36.1 0.8 %collective-permute-start.11 = (f32[8,128]{1,0:T(8,128)S(1)}, f32[8,128]{1,0:T(8,128)S(1)}, u32[]{:S(2)}, u32[]{:S(2)}) collective-permute-start(f32[8,128]{1,0:T(8,128)S(1)} %slice.12.refs_0_), channel_id=1, source_target_pairs={{1,0},{0,1},{3,2},{2,3},{5,4},{4,5},{7,6},{6,7},{9,8},{8,9},{11,10... | collective-permute-start | bytes 12296 | tf_op jit(solution)/shard_map/ppermute | solution.py:273
  36.9 0.9 %finish_grad.1 = (bf16[320,512]{1,0:T(8,128)(2,1)}, f32[8,39]{1,0:T(8,128)}) custom-call(f32[8,512]{1,0:T(8,128)S(1)} %add_add_fusion.small_ref, f32[160,512]{1,0:T(8,128)S(1)} %get-tuple-element.67.refs_0_, f32[160,512]{1,0:T(8,128)S(1)} %get-tuple-element.68.refs_1_, bf16[2,160,512]{2,1,0:T(8,128)(2,1)S(1)} %collective-permute-done.10.refs_2_), custom_call_target="tpu_custom_call" | custom-call | bytes 1500000 | tf_op jit(solution)/shard_map/finish_grad/pallas_call | solution.py:409
  37.8 1.9 %collective-permute-done.11.refs_1_ = f32[8,128]{1,0:T(8,128)S(1)} collective-permute-done((f32[8,128]{1,0:T(8,128)S(1)}, f32[8,128]{1,0:T(8,128)S(1)}, u32[]{:S(2)}, u32[]{:S(2)}) %collective-permute-start.11) | collective-permute-done | bytes 4128 | tf_op jit(solution)/shard_map/ppermute | solution.py:273
  39.8 0.6 %gain_sum.1 = f32[1,512]{1,0:T(1,128)} custom-call(s32[1]{0:T(128)} %bitcast.me_ref, f32[8,128]{1,0:T(8,128)S(1)} %slice.12.refs_0_, f32[8,128]{1,0:T(8,128)S(1)} %collective-permute-done.11.refs_1_), custom_call_target="tpu_custom_call" | custom-call | tf_op jit(solution)/shard_map/gain_sum/pallas_call | solution.py:419
  (13 shorter events, 0.2 us)
Async XLA Ops:
  0.6 11.8 %collective-permute-start.1 = (bf16[320,512]{1,0:T(8,128)(2,1)}, bf16[320,512]{1,0:T(8,128)(2,1)S(1)}, u32[]{:S(2)}, u32[]{:S(2)}) collective-permute-start(bf16[320,512]{1,0:T(8,128)(2,1)} %bitcast.10), channel_id=1, source_target_pairs={{1,0},{0,1},{3,2},{2,3},{5,4},{4,5},{7,6},{6,7},{9,8},{8,9},{11,10... | collective-permute-start | bytes 983048 | tf_op jit(solution)/shard_map/ppermute | solution.py:273
  4.7 13.1 %collective-permute-start.2 = (bf16[160,512]{1,0:T(8,128)(2,1)S(1)}, bf16[160,512]{1,0:T(8,128)(2,1)S(1)}, u32[]{:S(2)}, u32[]{:S(2)}) collective-permute-start(bf16[160,512]{1,0:T(8,128)(2,1)S(1)} %get-tuple-element.74.refs_0_), channel_id=1, source_target_pairs={{1,0},{0,1},{3,2},{2,3},{5,4},{4,5},{7,6},{6,7},{9,8},{8,9},{11,10... | collective-permute-start | bytes 491528 | tf_op jit(solution)/shard_map/ppermute | solution.py:273
  4.8 15.3 %collective-permute-start = (bf16[160,512]{1,0:T(8,128)(2,1)S(1)}, bf16[160,512]{1,0:T(8,128)(2,1)S(1)}, u32[]{:S(2)}, u32[]{:S(2)}) collective-permute-start(bf16[160,512]{1,0:T(8,128)(2,1)S(1)} %get-tuple-element.75.refs_0_), channel_id=1, source_target_pairs={{1,0},{0,1},{3,2},{2,3},{5,4},{4,5},{7,6},{6,7},{9,8},{8,9},{11,10... | collective-permute-start | bytes 491528 | tf_op jit(solution)/shard_map/ppermute | solution.py:273
  15.7 12.1 %collective-permute-start.6 = (bf16[2,160,512]{2,1,0:T(8,128)(2,1)S(1)}, bf16[2,160,512]{2,1,0:T(8,128)(2,1)S(1)}, u32[]{:S(2)}, u32[]{:S(2)}) collective-permute-start(bf16[2,160,512]{2,1,0:T(8,128)(2,1)S(1)} %get-tuple-element.54), channel_id=1, source_target_pairs={{1,0},{0,1},{3,2},{2,3},{5,4},{4,5},{7,6},{6,7},{9,8},{8,9},{11,10... | collective-permute-start | bytes 983048 | tf_op jit(solution)/shard_map/ppermute | solution.py:273
  22.5 10.5 %collective-permute-start.10 = (bf16[2,160,512]{2,1,0:T(8,128)(2,1)S(1)}, bf16[2,160,512]{2,1,0:T(8,128)(2,1)S(1)}, u32[]{:S(2)}, u32[]{:S(2)}) collective-permute-start(bf16[2,160,512]{2,1,0:T(8,128)(2,1)S(1)} %get-tuple-element.61), channel_id=1, source_target_pairs={{1,0},{0,1},{3,2},{2,3},{5,4},{4,5},{7,6},{6,7},{9,8},{8,9},{11,10... | collective-permute-start | bytes 983048 | tf_op jit(solution)/shard_map/ppermute | solution.py:273
  24.0 3.3 %collective-permute-start.3 = (f32[8,512]{1,0:T(8,128)S(1)}, f32[8,512]{1,0:T(8,128)S(1)}, u32[]{:S(2)}, u32[]{:S(2)}) collective-permute-start(f32[8,512]{1,0:T(8,128)S(1)} %get-tuple-element.55), channel_id=1, source_target_pairs={{24,0},{16,8},{8,16},{0,24},{25,1},{17,9},{9,17},{1,25},{26,2},{18... | collective-permute-start | bytes 49160 | tf_op jit(solution)/shard_map/ppermute | solution.py:289
  24.0 3.8 %collective-permute-start.4 = (f32[8,512]{1,0:T(8,128)S(1)}, f32[8,512]{1,0:T(8,128)S(1)}, u32[]{:S(2)}, u32[]{:S(2)}) collective-permute-start(f32[8,512]{1,0:T(8,128)S(1)} %get-tuple-element.55), channel_id=1, source_target_pairs={{16,0},{24,8},{0,16},{8,24},{17,1},{25,9},{1,17},{9,25},{18,2},{26... | collective-permute-start | bytes 49160 | tf_op jit(solution)/shard_map/ppermute | solution.py:289
  25.5 2.2 %collective-permute-start.5 = (f32[8,512]{1,0:T(8,128)S(1)}, f32[8,512]{1,0:T(8,128)S(1)}, u32[]{:S(2)}, u32[]{:S(2)}) collective-permute-start(f32[8,512]{1,0:T(8,128)S(1)} %get-tuple-element.55), channel_id=1, source_target_pairs={{8,0},{0,8},{24,16},{16,24},{9,1},{1,9},{25,17},{17,25},{10,2},{2,... | collective-permute-start | bytes 49160 | tf_op jit(solution)/shard_map/ppermute | solution.py:289
  27.7 5.6 %collective-permute-start.7 = (f32[8,512]{1,0:T(8,128)S(1)}, f32[8,512]{1,0:T(8,128)S(1)}, u32[]{:S(2)}, u32[]{:S(2)}) collective-permute-start(f32[8,512]{1,0:T(8,128)S(1)} %add_add_fusion.1), channel_id=1, source_target_pairs={{6,0},{4,2},{2,4},{0,6},{7,1},{5,3},{3,5},{1,7},{14,8},{12,10},{10... | collective-permute-start | bytes 49160 | tf_op jit(solution)/shard_map/ppermute | solution.py:289
  31.4 4.6 %collective-permute-start.8 = (f32[8,512]{1,0:T(8,128)S(1)}, f32[8,512]{1,0:T(8,128)S(1)}, u32[]{:S(2)}, u32[]{:S(2)}) collective-permute-start(f32[8,512]{1,0:T(8,128)S(1)} %add_add_fusion.1), channel_id=1, source_target_pairs={{4,0},{6,2},{0,4},{2,6},{5,1},{7,3},{1,5},{3,7},{12,8},{14,10},{8,... | collective-permute-start | bytes 49160 | tf_op jit(solution)/shard_map/ppermute | solution.py:289
  31.4 4.6 %collective-permute-start.9 = (f32[8,512]{1,0:T(8,128)S(1)}, f32[8,512]{1,0:T(8,128)S(1)}, u32[]{:S(2)}, u32[]{:S(2)}) collective-permute-start(f32[8,512]{1,0:T(8,128)S(1)} %add_add_fusion.1), channel_id=1, source_target_pairs={{2,0},{0,2},{6,4},{4,6},{3,1},{1,3},{7,5},{5,7},{10,8},{8,10},{14,... | collective-permute-start | bytes 49160 | tf_op jit(solution)/shard_map/ppermute | solution.py:289
  36.1 3.7 %collective-permute-start.11 = (f32[8,128]{1,0:T(8,128)S(1)}, f32[8,128]{1,0:T(8,128)S(1)}, u32[]{:S(2)}, u32[]{:S(2)}) collective-permute-start(f32[8,128]{1,0:T(8,128)S(1)} %slice.12.refs_0_), channel_id=1, source_target_pairs={{1,0},{0,1},{3,2},{2,3},{5,4},{4,5},{7,6},{6,7},{9,8},{8,9},{11,10... | collective-permute-start | bytes 12296 | tf_op jit(solution)/shard_map/ppermute | solution.py:273

commit v15 on v13

--- a/solution.py
+++ b/solution.py
@@ -280,7 +280,7 @@
         left = count // stride
         radix = 4 if left % 4 == 0 else 2 if left % 2 == 0 else left
         parts = [value]
-        for step in reversed(range(1, radix)):
+        for step in (2, 3, 1) if radix == 4 else range(1, radix):
             pairs = []
             for i in range(count):
                 digit = i // stride % radix

time: 39.2 us -> 39.9 us (1.018)
  waiting for transfers between devices: 6.17 us -> 6.82 us
    ppermute x6, waiting for transfers between devices: 3.65 us -> 4.31 us  [group_sum(): parts.append(lax.ppermute(value, axis, pairs))]
  transfers between devices with their start and end apart: 12 -> 12, of which waited for: 6 -> 5; matrix products, arithmetic and copies ran while one was open for 5% -> 5% of each run, Pallas kernels for 34% -> 33%
where the time goes in v15:
time: 39.9 us; the launch traced here: 39.7 us
  starting transfers between devices  16.5 us (41%)
  Pallas kernels  13.8 us (35%)
  waiting for transfers between devices  6.82 us (17%)
  local copies, waits for them, and re-layouts  1.9 us (5%)
  between operations  0.72 us (2%)
    ppermute x6, starting transfers between devices, shifted(): lax.ppermute(value, axis, [((i + step) % count, i) for i in range(count)])  10 us
    ppermute x6, starting transfers between devices, group_sum(): parts.append(lax.ppermute(value, axis, pairs))  6.44 us
    pallas_call x2, Pallas kernels, per_device(): pl.pallas_call(functools.partial(backward_kernel, dims, band, last), in_s...  4.72 us
    ppermute x6, waiting for transfers between devices, group_sum(): parts.append(lax.ppermute(value, axis, pairs))  4.31 us
    pallas_call x1, Pallas kernels, per_device(): pl.pallas_call(functools.partial(stage_kernel, frames, width), in_specs=[...  3.56 us
    pallas_call x1, Pallas kernels, per_device(): pl.pallas_call(functools.partial(forward_kernel, dims), in_specs=[smem] +...  3.24 us
    ppermute x6, waiting for transfers between devices, shifted(): lax.ppermute(value, axis, [((i + step) % count, i) for i in range(count)])  2.51 us
    reshape x1, local copies, waits for them, and re-layouts, per_device(): out_grad[:, :, n * BAND:(n + 1) * BAND].reshape(rows, width)  1.02 us
  transfers between devices with their start and end apart: 12, of which 5 were waited for; matrix products, arithmetic and copies ran while one was open for 5% of the time, Pallas kernels for 33%

profile of v15, /device:TPU:0, one launch (start us, length us, event | category | flops | bytes accessed | tf_op | source)
XLA Modules:
  0.0 39.7 jit_solution(12997297400048833113)
XLA Ops:
  0.6 3.0 %collective-permute-start.1 = (bf16[320,512]{1,0:T(8,128)(2,1)}, bf16[320,512]{1,0:T(8,128)(2,1)S(1)}, u32[]{:S(2)}, u32[]{:S(2)}) collective-permute-start(bf16[320,512]{1,0:T(8,128)(2,1)} %bitcast.10), channel_id=1, source_target_pairs={{1,0},{0,1},{3,2},{2,3},{5,4},{4,5},{7,6},{6,7},{9,8},{8,9},{11,10... | collective-permute-start | bytes 983048 | tf_op jit(solution)/shard_map/ppermute | solution.py:273
  3.7 1.0 %slice_bitcast_fusion = (bf16[160,512]{1,0:T(8,128)(2,1)S(1)}, bf16[160,512]{1,0:T(8,128)(2,1)S(1)}) fusion(bf16[1,20,16,512]{3,2,1,0:T(8,128)(2,1)} %param.9), kind=kLoop, calls=%fused_computation | loop fusion | bytes 655360 | tf_op jit(solution)/shard_map/reshape | solution.py:312
  4.8 2.0 %collective-permute-start = (bf16[160,512]{1,0:T(8,128)(2,1)S(1)}, bf16[160,512]{1,0:T(8,128)(2,1)S(1)}, u32[]{:S(2)}, u32[]{:S(2)}) collective-permute-start(bf16[160,512]{1,0:T(8,128)(2,1)S(1)} %get-tuple-element.73.refs_0_), channel_id=1, source_target_pairs={{1,0},{0,1},{3,2},{2,3},{5,4},{4,5},{7,6},{6,7},{9,8},{8,9},{11,10... | collective-permute-start | bytes 491528 | tf_op jit(solution)/shard_map/ppermute | solution.py:273
  6.8 0.8 %broadcast_in_dim.2 = f32[8,39,8]{2,1,0:T(8,128)S(1)} broadcast(f32[8,39]{1,0:T(8,128)} %param.11), dimensions={0,1} | broadcast | bytes 11232 | tf_op jit(solution)/shard_map/broadcast_in_dim | solution.py:317
  7.7 3.6 %stage.1 = (f32[20,8,160]{2,1,0:T(8,128)S(1)}, bf16[320,512]{1,0:T(8,128)(2,1)S(1)}, bf16[1024,1536]{1,0:T(8,128)(2,1)S(1)}, bf16[512,1024]{1,0:T(8,128)(2,1)S(1...) custom-call(f32[8,312]{1,0:T(8,128)S(1)} %reshape.38.bias_ref, ...), custom_call_target="tpu_custom_call" | custom-call | bytes 8000000 | tf_op jit(solution)/shard_map/stage/pallas_call | solution.py:322
  11.2 1.2 %collective-permute-done.1.refs_1_ = bf16[320,512]{1,0:T(8,128)(2,1)S(1)} collective-permute-done((bf16[320,512]{1,0:T(8,128)(2,1)}, bf16[320,512]{1,0:T(8,128)(2,1)S(1)}, u32[]{:S(2)}, u32[]{:S(2)}) %collective-permute-start.1) | collective-permute-done | bytes 327712 | tf_op jit(solution)/shard_map/ppermute | solution.py:273
  12.4 3.2 %attend.1 = (bf16[2,160,1536]{2,1,0:T(8,128)(2,1)S(1)}, bf16[2,8,160,160]{3,2,1,0:T(8,128)(2,1)S(1)}, bf16[2,160,1024]{2,1,0:T(8,128)(2,1)S(1)}, f32[2,160,128]{...) custom-call(s32[1]{0:T(128)} %bitcast.me_ref, ...), custom_call_target="tpu_custom_call" | custom-call | flops 4000000000 | bytes 8000000 | tf_op jit(solution)/shard_map/attend/pallas_call | solution.py:341
  15.7 2.1 %collective-permute-start.6 = (bf16[2,160,512]{2,1,0:T(8,128)(2,1)S(1)}, bf16[2,160,512]{2,1,0:T(8,128)(2,1)S(1)}, u32[]{:S(2)}, u32[]{:S(2)}) collective-permute-start(bf16[2,160,512]{2,1,0:T(8,128)(2,1)S(1)} %get-tuple-element.53), channel_id=1, source_target_pairs={{1,0},{0,1},{3,2},{2,3},{5,4},{4,5},{7,6},{6,7},{9,8},{8,9},{11,10... | collective-permute-start | bytes 983048 | tf_op jit(solution)/shard_map/ppermute | solution.py:273
  17.8 2.3 %attend_back.2 = (f32[160,512]{1,0:T(8,128)S(1)}, bf16[160,512]{1,0:T(8,128)(2,1)S(1)}, f32[1,1024]{1,0:T(1,128)S(1)}, f32[20,8,160]{2,1,0:T(8,128)S(1)}) custom-call(s32[1]{0:T(128)} %bitcast.me_ref, bf16[160,512]{1,0:T(8,128)(2,1)S(1)} %get-tuple-element.72.refs_0_, bf16[160,512]{1,0:T(8,128)(2,1)S(1)} %collective-permute-done.2.refs_1_, ...), custom_call_target="tpu_custom_call" | custom-call | flops 2500000000 | tf_op jit(solution)/shard_map/attend_back/pallas_call | solution.py:378
  20.1 2.4 %attend_back.3 = (f32[160,512]{1,0:T(8,128)S(1)}, bf16[2,160,512]{2,1,0:T(8,128)(2,1)S(1)}, f32[8,512]{1,0:T(8,128)S(1)}) custom-call(s32[1]{0:T(128)} %bitcast.me_ref, bf16[160,512]{1,0:T(8,128)(2,1)S(1)} %get-tuple-element.73.refs_0_, bf16[160,512]{1,0:T(8,128)(2,1)S(1)} %collective-permute-done.refs_1_, f32[1,1024]{1,0:T(1,128)S(1)} %get-tuple-element.38.refs_2_, ...), custom_call_target="tpu_custom_call" | custom-call | flops 2500000000 | tf_op jit(solution)/shard_map/attend_back/pallas_call | solution.py:378
  22.5 1.6 %collective-permute-start.3 = (f32[8,512]{1,0:T(8,128)S(1)}, f32[8,512]{1,0:T(8,128)S(1)}, u32[]{:S(2)}, u32[]{:S(2)}) collective-permute-start(f32[8,512]{1,0:T(8,128)S(1)} %get-tuple-element.54), channel_id=1, source_target_pairs={{16,0},{24,8},{0,16},{8,24},{17,1},{25,9},{1,17},{9,25},{18,2},{26... | collective-permute-start | bytes 49160 | tf_op jit(solution)/shard_map/ppermute | solution.py:289
  24.1 0.6 %collective-permute-start.5 = (f32[8,512]{1,0:T(8,128)S(1)}, f32[8,512]{1,0:T(8,128)S(1)}, u32[]{:S(2)}, u32[]{:S(2)}) collective-permute-start(f32[8,512]{1,0:T(8,128)S(1)} %get-tuple-element.54), channel_id=1, source_target_pairs={{8,0},{0,8},{24,16},{16,24},{9,1},{1,9},{25,17},{17,25},{10,2},{2,... | collective-permute-start | bytes 49160 | tf_op jit(solution)/shard_map/ppermute | solution.py:289
  24.7 1.4 %collective-permute-start.11 = (bf16[2,160,512]{2,1,0:T(8,128)(2,1)S(1)}, bf16[2,160,512]{2,1,0:T(8,128)(2,1)S(1)}, u32[]{:S(2)}, u32[]{:S(2)}) collective-permute-start(bf16[2,160,512]{2,1,0:T(8,128)(2,1)S(1)} %get-tuple-element.67), channel_id=1, source_target_pairs={{1,0},{0,1},{3,2},{2,3},{5,4},{4,5},{7,6},{6,7},{9,8},{8,9},{11,10... | collective-permute-start | bytes 983048 | tf_op jit(solution)/shard_map/ppermute | solution.py:273
  26.1 0.2 collective-permute-done.3
  26.3 0.9 %collective-permute-done.4 = f32[8,512]{1,0:T(8,128)S(1)} collective-permute-done((f32[8,512]{1,0:T(8,128)S(1)}, f32[8,512]{1,0:T(8,128)S(1)}, u32[]{:S(2)}, u32[]{:S(2)}) %collective-permute-start.4) | collective-permute-done | bytes 16416 | tf_op jit(solution)/shard_map/ppermute | solution.py:289
  27.3 2.7 %collective-permute-start.7 = (f32[8,512]{1,0:T(8,128)S(1)}, f32[8,512]{1,0:T(8,128)S(1)}, u32[]{:S(2)}, u32[]{:S(2)}) collective-permute-start(f32[8,512]{1,0:T(8,128)S(1)} %add_add_fusion.1), channel_id=1, source_target_pairs={{4,0},{6,2},{0,4},{2,6},{5,1},{7,3},{1,5},{3,7},{12,8},{14,10},{8,... | collective-permute-start | bytes 49160 | tf_op jit(solution)/shard_map/ppermute | solution.py:289
  29.9 1.3 %collective-permute-start.8 = (f32[8,512]{1,0:T(8,128)S(1)}, f32[8,512]{1,0:T(8,128)S(1)}, u32[]{:S(2)}, u32[]{:S(2)}) collective-permute-start(f32[8,512]{1,0:T(8,128)S(1)} %add_add_fusion.1), channel_id=1, source_target_pairs={{6,0},{4,2},{2,4},{0,6},{7,1},{5,3},{3,5},{1,7},{14,8},{12,10},{10... | collective-permute-start | bytes 49160 | tf_op jit(solution)/shard_map/ppermute | solution.py:289
  31.3 0.2 collective-permute-start.9
  31.5 0.8 %finish_out.1 = bf16[320,512]{1,0:T(8,128)(2,1)} custom-call(f32[2,160,512]{2,1,0:T(8,128)S(1)} %get-tuple-element.58.own_ref, bf16[2,160,512]{2,1,0:T(8,128)(2,1)S(1)} %collective-permute-done.6.refs_0_), custom_call_target="tpu_custom_call" | custom-call | bytes 1500000 | tf_op jit(solution)/shard_map/finish_out/pallas_call | solution.py:396
  32.3 3.1 %collective-permute-done.8 = f32[8,512]{1,0:T(8,128)S(1)} collective-permute-done((f32[8,512]{1,0:T(8,128)S(1)}, f32[8,512]{1,0:T(8,128)S(1)}, u32[]{:S(2)}, u32[]{:S(2)}) %collective-permute-start.8) | collective-permute-done | bytes 16416 | tf_op jit(solution)/shard_map/ppermute | solution.py:289
  35.5 1.4 %collective-permute-start.10 = (f32[8,128]{1,0:T(8,128)S(1)}, f32[8,128]{1,0:T(8,128)S(1)}, u32[]{:S(2)}, u32[]{:S(2)}) collective-permute-start(f32[8,128]{1,0:T(8,128)S(1)} %slice.12.refs_0_), channel_id=1, source_target_pairs={{1,0},{0,1},{3,2},{2,3},{5,4},{4,5},{7,6},{6,7},{9,8},{8,9},{11,10... | collective-permute-start | bytes 12296 | tf_op jit(solution)/shard_map/ppermute | solution.py:273
  36.9 0.9 %finish_grad.1 = (bf16[320,512]{1,0:T(8,128)(2,1)}, f32[8,39]{1,0:T(8,128)}) custom-call(f32[8,512]{1,0:T(8,128)S(1)} %add_add_fusion.small_ref, f32[160,512]{1,0:T(8,128)S(1)} %get-tuple-element.65.refs_0_, f32[160,512]{1,0:T(8,128)S(1)} %get-tuple-element.66.refs_1_, bf16[2,160,512]{2,1,0:T(8,128)(2,1)S(1)} %collective-permute-done.11.refs_2_), custom_call_target="tpu_custom_call" | custom-call | bytes 1500000 | tf_op jit(solution)/shard_map/finish_grad/pallas_call | solution.py:409
  37.8 1.3 %collective-permute-done.10.refs_1_ = f32[8,128]{1,0:T(8,128)S(1)} collective-permute-done((f32[8,128]{1,0:T(8,128)S(1)}, f32[8,128]{1,0:T(8,128)S(1)}, u32[]{:S(2)}, u32[]{:S(2)}) %collective-permute-start.10) | collective-permute-done | bytes 4128 | tf_op jit(solution)/shard_map/ppermute | solution.py:273
  39.2 0.6 %gain_sum.1 = f32[1,512]{1,0:T(1,128)} custom-call(s32[1]{0:T(128)} %bitcast.me_ref, f32[8,128]{1,0:T(8,128)S(1)} %slice.12.refs_0_, f32[8,128]{1,0:T(8,128)S(1)} %collective-permute-done.10.refs_1_), custom_call_target="tpu_custom_call" | custom-call | tf_op jit(solution)/shard_map/gain_sum/pallas_call | solution.py:419
  (13 shorter events, 0.2 us)
Async XLA Ops:
  0.6 11.8 %collective-permute-start.1 = (bf16[320,512]{1,0:T(8,128)(2,1)}, bf16[320,512]{1,0:T(8,128)(2,1)S(1)}, u32[]{:S(2)}, u32[]{:S(2)}) collective-permute-start(bf16[320,512]{1,0:T(8,128)(2,1)} %bitcast.10), channel_id=1, source_target_pairs={{1,0},{0,1},{3,2},{2,3},{5,4},{4,5},{7,6},{6,7},{9,8},{8,9},{11,10... | collective-permute-start | bytes 983048 | tf_op jit(solution)/shard_map/ppermute | solution.py:273
  4.7 13.1 %collective-permute-start.2 = (bf16[160,512]{1,0:T(8,128)(2,1)S(1)}, bf16[160,512]{1,0:T(8,128)(2,1)S(1)}, u32[]{:S(2)}, u32[]{:S(2)}) collective-permute-start(bf16[160,512]{1,0:T(8,128)(2,1)S(1)} %get-tuple-element.72.refs_0_), channel_id=1, source_target_pairs={{1,0},{0,1},{3,2},{2,3},{5,4},{4,5},{7,6},{6,7},{9,8},{8,9},{11,10... | collective-permute-start | bytes 491528 | tf_op jit(solution)/shard_map/ppermute | solution.py:273
  4.8 15.3 %collective-permute-start = (bf16[160,512]{1,0:T(8,128)(2,1)S(1)}, bf16[160,512]{1,0:T(8,128)(2,1)S(1)}, u32[]{:S(2)}, u32[]{:S(2)}) collective-permute-start(bf16[160,512]{1,0:T(8,128)(2,1)S(1)} %get-tuple-element.73.refs_0_), channel_id=1, source_target_pairs={{1,0},{0,1},{3,2},{2,3},{5,4},{4,5},{7,6},{6,7},{9,8},{8,9},{11,10... | collective-permute-start | bytes 491528 | tf_op jit(solution)/shard_map/ppermute | solution.py:273
  15.7 11.6 %collective-permute-start.6 = (bf16[2,160,512]{2,1,0:T(8,128)(2,1)S(1)}, bf16[2,160,512]{2,1,0:T(8,128)(2,1)S(1)}, u32[]{:S(2)}, u32[]{:S(2)}) collective-permute-start(bf16[2,160,512]{2,1,0:T(8,128)(2,1)S(1)} %get-tuple-element.53), channel_id=1, source_target_pairs={{1,0},{0,1},{3,2},{2,3},{5,4},{4,5},{7,6},{6,7},{9,8},{8,9},{11,10... | collective-permute-start | bytes 983048 | tf_op jit(solution)/shard_map/ppermute | solution.py:273
  22.5 3.8 %collective-permute-start.3 = (f32[8,512]{1,0:T(8,128)S(1)}, f32[8,512]{1,0:T(8,128)S(1)}, u32[]{:S(2)}, u32[]{:S(2)}) collective-permute-start(f32[8,512]{1,0:T(8,128)S(1)} %get-tuple-element.54), channel_id=1, source_target_pairs={{16,0},{24,8},{0,16},{8,24},{17,1},{25,9},{1,17},{9,25},{18,2},{26... | collective-permute-start | bytes 49160 | tf_op jit(solution)/shard_map/ppermute | solution.py:289
  24.1 3.2 %collective-permute-start.4 = (f32[8,512]{1,0:T(8,128)S(1)}, f32[8,512]{1,0:T(8,128)S(1)}, u32[]{:S(2)}, u32[]{:S(2)}) collective-permute-start(f32[8,512]{1,0:T(8,128)S(1)} %get-tuple-element.54), channel_id=1, source_target_pairs={{24,0},{16,8},{8,16},{0,24},{25,1},{17,9},{9,17},{1,25},{26,2},{18... | collective-permute-start | bytes 49160 | tf_op jit(solution)/shard_map/ppermute | solution.py:289
  24.1 3.2 %collective-permute-start.5 = (f32[8,512]{1,0:T(8,128)S(1)}, f32[8,512]{1,0:T(8,128)S(1)}, u32[]{:S(2)}, u32[]{:S(2)}) collective-permute-start(f32[8,512]{1,0:T(8,128)S(1)} %get-tuple-element.54), channel_id=1, source_target_pairs={{8,0},{0,8},{24,16},{16,24},{9,1},{1,9},{25,17},{17,25},{10,2},{2,... | collective-permute-start | bytes 49160 | tf_op jit(solution)/shard_map/ppermute | solution.py:289
  24.7 12.2 %collective-permute-start.11 = (bf16[2,160,512]{2,1,0:T(8,128)(2,1)S(1)}, bf16[2,160,512]{2,1,0:T(8,128)(2,1)S(1)}, u32[]{:S(2)}, u32[]{:S(2)}) collective-permute-start(bf16[2,160,512]{2,1,0:T(8,128)(2,1)S(1)} %get-tuple-element.67), channel_id=1, source_target_pairs={{1,0},{0,1},{3,2},{2,3},{5,4},{4,5},{7,6},{6,7},{9,8},{8,9},{11,10... | collective-permute-start | bytes 983048 | tf_op jit(solution)/shard_map/ppermute | solution.py:273
  27.3 5.0 %collective-permute-start.7 = (f32[8,512]{1,0:T(8,128)S(1)}, f32[8,512]{1,0:T(8,128)S(1)}, u32[]{:S(2)}, u32[]{:S(2)}) collective-permute-start(f32[8,512]{1,0:T(8,128)S(1)} %add_add_fusion.1), channel_id=1, source_target_pairs={{4,0},{6,2},{0,4},{2,6},{5,1},{7,3},{1,5},{3,7},{12,8},{14,10},{8,... | collective-permute-start | bytes 49160 | tf_op jit(solution)/shard_map/ppermute | solution.py:289
  29.9 5.5 %collective-permute-start.8 = (f32[8,512]{1,0:T(8,128)S(1)}, f32[8,512]{1,0:T(8,128)S(1)}, u32[]{:S(2)}, u32[]{:S(2)}) collective-permute-start(f32[8,512]{1,0:T(8,128)S(1)} %add_add_fusion.1), channel_id=1, source_target_pairs={{6,0},{4,2},{2,4},{0,6},{7,1},{5,3},{3,5},{1,7},{14,8},{12,10},{10... | collective-permute-start | bytes 49160 | tf_op jit(solution)/shard_map/ppermute | solution.py:289
  31.3 4.2 %collective-permute-start.9 = (f32[8,512]{1,0:T(8,128)S(1)}, f32[8,512]{1,0:T(8,128)S(1)}, u32[]{:S(2)}, u32[]{:S(2)}) collective-permute-start(f32[8,512]{1,0:T(8,128)S(1)} %add_add_fusion.1), channel_id=1, source_target_pairs={{2,0},{0,2},{6,4},{4,6},{3,1},{1,3},{7,5},{5,7},{10,8},{8,10},{14,... | collective-permute-start | bytes 49160 | tf_op jit(solution)/shard_map/ppermute | solution.py:289
  35.5 3.7 %collective-permute-start.10 = (f32[8,128]{1,0:T(8,128)S(1)}, f32[8,128]{1,0:T(8,128)S(1)}, u32[]{:S(2)}, u32[]{:S(2)}) collective-permute-start(f32[8,128]{1,0:T(8,128)S(1)} %slice.12.refs_0_), channel_id=1, source_target_pairs={{1,0},{0,1},{3,2},{2,3},{5,4},{4,5},{7,6},{6,7},{9,8},{8,9},{11,10... | collective-permute-start | bytes 12296 | tf_op jit(solution)/shard_map/ppermute | solution.py:273
